TPU v7x, 512 devices: a whole 4x4x16 slice. The times are simulated.
512 devices in a mesh: kp: 128 (over y, z_lo, x, core), own: 4 (over z_hi).
Axes of the slice: x: 4, y: 4, z: 16 (z_hi: 4, z_lo: 4; z = z_hi * 4 + z_lo), core: 2. Of those that a mesh axis runs over, the one named last changes fastest.
Arguments:
- pair_density: bfloat16 [256, 256, 2, 2048], P('kp', None, None, 'own'), may hold values from -6 to 6
- coulomb: float32 [2048], P('own'), may hold values from 0.1 to 10
Outputs:
- kernel: bfloat16 [4, 65536, 2, 512], P(None, ('kp', 'own'))
All inputs are finite; a program needn't handle non-finite values.
Results may differ from a plain program's by a relative error of at most 0.013.
Values may be sent and summed in bfloat16 or wider, within the bound.
No kernel may reach another device: no remote copies, remote signals or barrier semaphores. Data moves between devices by JAX's collectives and lax.ppermute only.
A program may use at most 64 MiB of HBM per device.

v0:
```python
import math

import jax
import jax.numpy as jnp
from jax import lax
from jax.sharding import PartitionSpec as P

ROUNDS = 2
BLOCK = 32


def passed_along(value, axis, steps):
    count = lax.axis_size(axis)
    pairs = [(source, (source + steps) % count) for source in range(count)]
    return lax.ppermute(value, axis, pairs)


def paired_rhs(partner_rows):
    half_width = partner_rows.shape[1] // 2
    real_part = partner_rows[:, :half_width]
    imag_part = partner_rows[:, half_width:]
    lower_half = jnp.concatenate([imag_part, -real_part], axis=1)
    return jnp.concatenate([partner_rows, lower_half], axis=0)


def body(pair_density, coulomb):
    row_total = pair_density.shape[0] * pair_density.shape[1]
    g_local = pair_density.shape[3]
    owners = lax.axis_size("own")
    scale_factor = 1.0 / math.sqrt(g_local * owners)
    own_rows = row_total // owners
    block_count = own_rows // BLOCK
    weighted = (pair_density.astype(jnp.float32) * jnp.sqrt(coulomb)).astype(jnp.bfloat16)
    weighted = weighted.reshape(row_total, 2 * g_local)
    ordered = (
        weighted.reshape(block_count, owners, BLOCK, 2 * g_local)
        .transpose(1, 0, 2, 3)
        .reshape(row_total, 2 * g_local)
    )
    sign_pair = jnp.array([1.0, -1.0], jnp.bfloat16).reshape(1, 2, 1)
    backward = []
    forward = []
    for offset in range(1, ROUNDS + 1):
        partner = passed_along(weighted, "kp", offset)
        right_side = paired_rhs(partner)
        product = lax.dot_general(
            ordered, right_side, (((1,), (1,)), ((), ())), preferred_element_type=jnp.float32
        )
        summed = lax.psum_scatter(
            (product * scale_factor).astype(jnp.bfloat16), "own", scatter_dimension=0, tiled=True
        )
        behind = summed.reshape(own_rows, 2, row_total)
        backward.append(behind)
        flipped = behind * sign_pair
        split_view = (
            flipped.reshape(own_rows, 2, block_count, owners, BLOCK)
            .transpose(3, 2, 4, 1, 0)
            .reshape(owners, own_rows, 2, own_rows)
        )
        swapped = lax.all_to_all(split_view, "own", split_axis=0, concat_axis=0, tiled=True)
        arranged = (
            swapped.reshape(owners, own_rows, 2, block_count, BLOCK)
            .transpose(1, 2, 3, 0, 4)
            .reshape(own_rows, 2, row_total)
        )
        ahead = passed_along(arranged, "kp", -offset)
        forward.append(ahead)
    return jnp.stack(backward + forward, axis=0)


def solution(mesh):
    placed = (P("kp", None, None, "own"), P("own"))
    return jax.shard_map(
        body,
        mesh=mesh,
        in_specs=placed,
        out_specs=P(None, ("kp", "own"), None, None),
        check_vma=False,
    )
```

profile of v0, /device:TPU:7, one launch (start us, length us, event | category | flops | bytes accessed | tf_op | source)
XLA Modules:
  0.0 239.1 jit_solution(7894912586409461160)
XLA Ops:
  6.5 0.0 reduce-scatter.5.cloned.1.call-start
  6.5 0.7 sqrt.3
  7.2 2.0 multiply_convert_fusion.2
  9.3 0.2 copy.29
  9.5 3.5 %collective-permute-start.1 = (bf16[512,1024]{1,0:T(8,128)(2,1)S(1)}, bf16[512,1024]{1,0:T(8,128)(2,1)}, u32[]{:S(2)}, u32[]{:S(2)}) collective-permute-start(bf16[512,1024]{1,0:T(8,128)(2,1)S(1)} %bitcast.35), channel_id=1, source_target_pairs={{0,8},{4,12},{8,16},{12,20},{16,24},{20,28},{24,32},{28,36},{32,40... | collective-permute-start | bytes 3145736 | tf_op jit(solution)/shard_map/ppermute | solution.py:15
  13.0 0.8 reshape_reshape.3
  13.8 0.1 copy.15
  13.9 21.7 %collective-permute-done.1 = bf16[512,1024]{1,0:T(8,128)(2,1)} collective-permute-done((bf16[512,1024]{1,0:T(8,128)(2,1)S(1)}, bf16[512,1024]{1,0:T(8,128)(2,1)}, u32[]{:S(2)}, u32[]{:S(2)}) %collective-permute-start.1) | collective-permute-done | bytes 1048608 | tf_op jit(solution)/shard_map/ppermute | solution.py:15
  35.5 1.3 fusion.19
  36.8 3.5 %multiply_convert_fusion = bf16[512,1024]{1,0:T(8,128)(2,1)} fusion(bf16[512,1024]{1,0:T(8,128)(2,1)S(1)} %bitcast.33, bf16[512,512]{1,0:T(8,128)(2,1)S(1)} %get-tuple-element.8, bf16[512,512]{1,0:T(8,128)(2,1)S(1)} %get-tuple-element.7, bf16[512,1024]{1,0:T(8,128)(2,1)} %collective-permute-done.1), kind=kOutput, calls=%fused_computation.12 | convolution fusion | flops 1081081856 | bytes 4194304 | tf_op jit(solution)/shard_map/dot_general | solution.py:46
  40.3 0.0 reduce-scatter.5.cloned.1.call-update
  40.3 0.0 reduce-scatter.3.cloned.1.call-start
  40.4 7.0 %collective-permute-start = (bf16[512,1024]{1,0:T(8,128)(2,1)S(1)}, bf16[512,1024]{1,0:T(8,128)(2,1)S(1)}, u32[]{:S(2)}, u32[]{:S(2)}) collective-permute-start(bf16[512,1024]{1,0:T(8,128)(2,1)S(1)} %bitcast.36), channel_id=1, source_target_pairs={{0,4},{4,8},{8,12},{12,16},{16,20},{20,24},{24,28},{28,32},{32,36}... | collective-permute-start | bytes 3145736 | tf_op jit(solution)/shard_map/ppermute | solution.py:15
  47.4 11.7 %collective-permute-done = bf16[512,1024]{1,0:T(8,128)(2,1)S(1)} collective-permute-done((bf16[512,1024]{1,0:T(8,128)(2,1)S(1)}, bf16[512,1024]{1,0:T(8,128)(2,1)S(1)}, u32[]{:S(2)}, u32[]{:S(2)}) %collective-permute-start) | collective-permute-done | bytes 1048608 | tf_op jit(solution)/shard_map/ppermute | solution.py:15
  59.1 0.1 fusion.18
  59.2 2.3 multiply_convert_fusion.1
  61.5 0.0 copy-start
  61.5 0.0 reduce-scatter.3.cloned.1.call-update
  61.5 39.1 %reduce-scatter.5.cloned.1.call-done = bf16[128,1024]{1,0:T(8,128)(2,1)} async-done(((bf16[512,1024]{1,0:T(8,128)(2,1)}), bf16[128,1024]{1,0:T(8,128)(2,1)}) %reduce-scatter.5.cloned.1.call-update) | async-done | bytes 262160 | tf_op jit(solution)/shard_map/reduce_scatter | solution.py:49
  100.7 1.1 copy.28
  101.8 69.5 %reduce-scatter.3.cloned.1.call-done = bf16[128,1024]{1,0:T(8,128)(2,1)} async-done(((bf16[512,1024]{1,0:T(8,128)(2,1)}), bf16[128,1024]{1,0:T(8,128)(2,1)}) %reduce-scatter.3.cloned.1.call-update) | async-done | bytes 262160 | tf_op jit(solution)/shard_map/reduce_scatter | solution.py:49
  171.3 1.1 copy.27
  172.4 0.0 copy-done
  172.4 0.1 multiply_bitcast_fusion.1
  172.6 0.7 copy.17
  173.3 6.4 %all-to-all-start = ((bf16[4,128,2,128]{3,1,2,0:T(8,128)(2,1)}), bf16[4,128,2,128]{3,1,2,0:T(8,128)(2,1)S(1)}, u32[]{:S(2)}, u32[]{:S(2)}) async-start(bf16[4,128,2,128]{3,1,2,0:T(8,128)(2,1)} %bitcast.6), calls=%async_computation.2 | async-start | bytes 524288 | tf_op jit(solution)/shard_map/all_to_all | solution.py:60
  179.7 0.7 copy.21
  180.4 12.5 %all-to-all-done = bf16[4,128,2,128]{3,1,2,0:T(8,128)(2,1)S(1)} async-done(((bf16[4,128,2,128]{3,1,2,0:T(8,128)(2,1)}), bf16[4,128,2,128]{3,1,2,0:T(8,128)(2,1)S(1)}, u32[]{:S(2)}, u32[]{:S(2)}) %all-to-all-start) | async-done | bytes 262176 | tf_op jit(solution)/shard_map/all_to_all | solution.py:60
  192.9 7.6 %all-to-all-start.1 = ((bf16[4,128,2,128]{3,1,2,0:T(8,128)(2,1)}), bf16[4,128,2,128]{3,1,2,0:T(8,128)(2,1)S(1)}, u32[]{:S(2)}, u32[]{:S(2)}) async-start(bf16[4,128,2,128]{3,1,2,0:T(8,128)(2,1)} %bitcast.13), calls=%async_computation.3 | async-start | bytes 524288 | tf_op jit(solution)/shard_map/all_to_all | solution.py:60
  200.5 0.2 copy.18
  200.7 14.1 %all-to-all-done.1 = bf16[4,128,2,128]{3,1,2,0:T(8,128)(2,1)S(1)} async-done(((bf16[4,128,2,128]{3,1,2,0:T(8,128)(2,1)}), bf16[4,128,2,128]{3,1,2,0:T(8,128)(2,1)S(1)}, u32[]{:S(2)}, u32[]{:S(2)}) %all-to-all-start.1) | async-done | bytes 262176 | tf_op jit(solution)/shard_map/all_to_all | solution.py:60
  214.8 0.2 copy.22
  215.0 2.6 %collective-permute-start.3 = (bf16[128,2,512]{0,2,1:T(8,128)(2,1)S(1)}, bf16[128,2,512]{0,2,1:T(8,128)(2,1)S(1)}, u32[]{:S(2)}, u32[]{:S(2)}) collective-permute-start(bf16[128,2,512]{0,2,1:T(8,128)(2,1)S(1)} %bitcast.40), channel_id=1, source_target_pairs={{0,504},{4,508},{8,0},{12,4},{16,8},{20,12},{24,16},{28,20},{32,24... | collective-permute-start | bytes 786440 | tf_op jit(solution)/shard_map/ppermute | solution.py:15
  217.5 4.6 %collective-permute-start.2 = (bf16[128,2,512]{0,2,1:T(8,128)(2,1)S(1)}, bf16[128,2,512]{0,2,1:T(8,128)(2,1)S(1)}, u32[]{:S(2)}, u32[]{:S(2)}) collective-permute-start(bf16[128,2,512]{0,2,1:T(8,128)(2,1)S(1)} %bitcast.39), channel_id=1, source_target_pairs={{0,508},{4,0},{8,4},{12,8},{16,12},{20,16},{24,20},{28,24},{32,28}... | collective-permute-start | bytes 786440 | tf_op jit(solution)/shard_map/ppermute | solution.py:15
  222.1 2.1 collective-permute-done.3
  224.2 5.9 %collective-permute-done.2 = bf16[128,2,512]{0,2,1:T(8,128)(2,1)S(1)} collective-permute-done((bf16[128,2,512]{0,2,1:T(8,128)(2,1)S(1)}, bf16[128,2,512]{0,2,1:T(8,128)(2,1)S(1)}, u32[]{:S(2)}, u32[]{:S(2)}) %collective-permute-start.2) | collective-permute-done | bytes 262176 | tf_op jit(solution)/shard_map/ppermute | solution.py:15
  230.1 0.1 pad_maximum_fusion
  230.3 2.0 copy.26
  (2 shorter events, 0.0 us)
Async XLA Ops:
  6.5 94.1 %reduce-scatter.5.cloned.1.call-start = ((), (), s32[]{:S(2)}) async-start(), calls=%async_computation.5 | async-start | bytes 1310720 | tf_op jit(solution)/shard_map/reduce_scatter | solution.py:49
  9.5 26.0 %collective-permute-start.1 = (bf16[512,1024]{1,0:T(8,128)(2,1)S(1)}, bf16[512,1024]{1,0:T(8,128)(2,1)}, u32[]{:S(2)}, u32[]{:S(2)}) collective-permute-start(bf16[512,1024]{1,0:T(8,128)(2,1)S(1)} %bitcast.35), channel_id=1, source_target_pairs={{0,8},{4,12},{8,16},{12,20},{16,24},{20,28},{24,32},{28,36},{32,40... | collective-permute-start | bytes 3145736 | tf_op jit(solution)/shard_map/ppermute | solution.py:15
  40.3 131.0 %reduce-scatter.3.cloned.1.call-start = ((), (), s32[]{:S(2)}) async-start(), calls=%async_computation.4 | async-start | bytes 1310720 | tf_op jit(solution)/shard_map/reduce_scatter | solution.py:49
  40.4 18.7 %collective-permute-start = (bf16[512,1024]{1,0:T(8,128)(2,1)S(1)}, bf16[512,1024]{1,0:T(8,128)(2,1)S(1)}, u32[]{:S(2)}, u32[]{:S(2)}) collective-permute-start(bf16[512,1024]{1,0:T(8,128)(2,1)S(1)} %bitcast.36), channel_id=1, source_target_pairs={{0,4},{4,8},{8,12},{12,16},{16,20},{20,24},{24,28},{28,32},{32,36}... | collective-permute-start | bytes 3145736 | tf_op jit(solution)/shard_map/ppermute | solution.py:15
  61.5 111.0 %copy-start = (bf16[2]{0:T(256)(128)(2,1)S(1)}, bf16[2]{0:T(256)(128)(2,1)}, u32[]{:S(2)}) copy-start(bf16[2]{0:T(256)(128)(2,1)} %constant.4.clone) | copy-start | bytes 16
  173.3 19.6 %all-to-all-start = ((bf16[4,128,2,128]{3,1,2,0:T(8,128)(2,1)}), bf16[4,128,2,128]{3,1,2,0:T(8,128)(2,1)S(1)}, u32[]{:S(2)}, u32[]{:S(2)}) async-start(bf16[4,128,2,128]{3,1,2,0:T(8,128)(2,1)} %bitcast.6), calls=%async_computation.2 | async-start | bytes 524288 | tf_op jit(solution)/shard_map/all_to_all | solution.py:60
  192.9 21.8 %all-to-all-start.1 = ((bf16[4,128,2,128]{3,1,2,0:T(8,128)(2,1)}), bf16[4,128,2,128]{3,1,2,0:T(8,128)(2,1)S(1)}, u32[]{:S(2)}, u32[]{:S(2)}) async-start(bf16[4,128,2,128]{3,1,2,0:T(8,128)(2,1)} %bitcast.13), calls=%async_computation.3 | async-start | bytes 524288 | tf_op jit(solution)/shard_map/all_to_all | solution.py:60
  215.0 9.2 %collective-permute-start.3 = (bf16[128,2,512]{0,2,1:T(8,128)(2,1)S(1)}, bf16[128,2,512]{0,2,1:T(8,128)(2,1)S(1)}, u32[]{:S(2)}, u32[]{:S(2)}) collective-permute-start(bf16[128,2,512]{0,2,1:T(8,128)(2,1)S(1)} %bitcast.40), channel_id=1, source_target_pairs={{0,504},{4,508},{8,0},{12,4},{16,8},{20,12},{24,16},{28,20},{32,24... | collective-permute-start | bytes 786440 | tf_op jit(solution)/shard_map/ppermute | solution.py:15
  217.5 12.6 %collective-permute-start.2 = (bf16[128,2,512]{0,2,1:T(8,128)(2,1)S(1)}, bf16[128,2,512]{0,2,1:T(8,128)(2,1)S(1)}, u32[]{:S(2)}, u32[]{:S(2)}) collective-permute-start(bf16[128,2,512]{0,2,1:T(8,128)(2,1)S(1)} %bitcast.39), channel_id=1, source_target_pairs={{0,508},{4,0},{8,4},{12,8},{16,12},{20,16},{24,20},{28,24},{32,28}... | collective-permute-start | bytes 786440 | tf_op jit(solution)/shard_map/ppermute | solution.py:15
Sparse Core Ops, SparseCore 0:
  40.5 60.1 reduce-scatter.4
  103.7 67.5 reduce-scatter.2
where the time goes:
time: 240 us; the launch traced here: 239 us
  waiting for transfers between devices  177 us (74%)
  starting transfers between devices  31.6 us (13%)
  between operations  13.5 us (6%)
  local copies, waits for them, and re-layouts  7.88 us (3%)
  matrix products  5.79 us (2%)
  other arithmetic  3.62 us (2%)
    reduce_scatter x2, waiting for transfers between devices, body(): lax.psum_scatter((product * scale_factor).astype(jnp.bfloat16), 'own', sc...  109 us
    ppermute x4, waiting for transfers between devices, passed_along(): return lax.ppermute(value, axis, pairs)  41.4 us
    all_to_all x2, waiting for transfers between devices, body(): lax.all_to_all(split_view, 'own', split_axis=0, concat_axis=0, tiled=True)  26.6 us
    ppermute x4, starting transfers between devices, passed_along(): return lax.ppermute(value, axis, pairs)  17.6 us
    all_to_all x2, starting transfers between devices, body(): lax.all_to_all(split_view, 'own', split_axis=0, concat_axis=0, tiled=True)  13.9 us
    dot_general x2, matrix products, body(): lax.dot_general(ordered, right_side, (((1,), (1,)), ((), ())), preferred_...  5.79 us
  transfers between devices with their start and end apart: 8, of which 8 were waited for; matrix products, arithmetic and copies ran while one was open for 2% of the time, Pallas kernels for 0%

commit v1 on v0

v1 whole, which is shorter than its diff:
```python
import math

import jax
import jax.numpy as jnp
import numpy as np
from jax import lax
from jax.sharding import PartitionSpec as P

BLOCK = 32


def natural_order(owners, block_count):
    rows = np.arange(owners * block_count * BLOCK)
    owner, block, place = rows // (block_count * BLOCK), rows // BLOCK % block_count, rows % BLOCK
    return (block * owners + owner) * BLOCK + place


def body(pair_density, coulomb):
    points, transitions, _, g_local = pair_density.shape
    row_total = points * transitions
    owners = lax.axis_size("own")
    groups = lax.axis_size("kp")
    own_rows = row_total // owners
    half = own_rows // 2
    block_count = own_rows // BLOCK
    scale = 1.0 / math.sqrt(g_local * owners)
    me = lax.axis_index("own")
    odd = lax.axis_index("kp") % 2 == 1

    near_raw = lax.ppermute(pair_density, "kp", [(i, (i + 1) % groups) for i in range(groups)])
    ahead_raw = lax.ppermute(pair_density, "kp", [(i, (i - 2) % groups) for i in range(0, groups, 2)])
    behind_raw = lax.ppermute(near_raw, "kp", [(i, i + 1) for i in range(0, groups, 2)])

    def planes(raw):
        return raw.reshape(row_total, 2 * g_local)

    weighted = (pair_density.astype(jnp.float32) * coulomb).astype(jnp.bfloat16)
    weighted = weighted.reshape(block_count, owners, BLOCK, 2, g_local)
    weighted = jnp.roll(weighted, -me, axis=1)
    weighted = weighted.transpose(1, 3, 0, 2, 4).reshape(owners, 2, own_rows, g_local)
    real_part, imag_part = weighted[:, 0], weighted[:, 1]
    left = jnp.stack(
        [
            jnp.concatenate([real_part, imag_part], axis=-1),
            jnp.concatenate([-imag_part, real_part], axis=-1),
        ],
        axis=1,
    )

    def product(rows, right):
        out = lax.dot_general(
            rows, right, (((2,), (1,)), ((), ())), preferred_element_type=jnp.float32
        )
        return out * scale

    up = [(o, (o + 1) % owners) for o in range(owners)]
    down = [(o, (o - 1) % owners) for o in range(owners)]

    def first(right):
        to_up = jnp.concatenate([left[2, :, :half], left[1, :, half:]], axis=1)
        to_down = jnp.concatenate([left[3, :, :half], left[2, :, half:]], axis=1)
        return (
            lax.ppermute(product(to_up, right).astype(jnp.bfloat16), "own", up),
            lax.ppermute(product(to_down, right).astype(jnp.bfloat16), "own", down),
        )

    def second(right, from_down, from_up):
        to_up = product(left[1, :, :half], right) + from_down[:, :half].astype(jnp.float32)
        to_down = product(left[3, :, half:], right) + from_up[:, half:].astype(jnp.float32)
        return (
            lax.ppermute(to_up.astype(jnp.bfloat16), "own", up),
            lax.ppermute(to_down.astype(jnp.bfloat16), "own", down),
        )

    def third(right, from_down, from_up, late_down, late_up):
        low = product(left[0, :, :half], right) + from_up[:, :half].astype(jnp.float32) + late_down.astype(jnp.float32)
        high = product(left[0, :, half:], right) + from_down[:, half:].astype(jnp.float32) + late_up.astype(jnp.float32)
        return jnp.concatenate([low, high], axis=1).astype(jnp.bfloat16)

    order = natural_order(owners, block_count)
    pick = jnp.asarray(np.eye(row_total, dtype=np.float32)[order], jnp.bfloat16)

    def turned(block):
        sign = jnp.array([1.0, -1.0], jnp.bfloat16).reshape(2, 1, 1)
        out = lax.dot_general(
            pick, block * sign, (((1,), (2,)), ((), ())), preferred_element_type=jnp.float32
        )
        return out.astype(jnp.bfloat16)

    def gathered(pieces):
        swapped = lax.all_to_all(
            pieces.reshape(owners, own_rows, 2, own_rows), "own", split_axis=0, concat_axis=0, tiled=True
        )
        swapped = swapped.transpose(1, 2, 0, 3).reshape(own_rows, 2, row_total)
        out = lax.dot_general(swapped, pick, (((2,), (0,)), ((), ())), preferred_element_type=jnp.float32)
        return out.astype(jnp.bfloat16)

    right_1 = planes(near_raw)
    got_1 = first(right_1)
    right_2 = planes(jnp.where(odd, behind_raw, ahead_raw))
    got_2 = first(right_2)
    late_1 = second(right_1, *got_1)
    late_2 = second(right_2, *got_2)
    block_1 = third(right_1, *got_1, *late_1)
    back_1 = lax.ppermute(turned(block_1), "kp", [(i, (i - 1) % groups) for i in range(groups)])
    block_2 = third(right_2, *got_2, *late_2)
    back_2 = lax.ppermute(
        turned(block_2), "kp", [(i, (i - 2 if i % 2 else i + 2) % groups) for i in range(groups)]
    )
    back_1 = gathered(back_1)
    back_2 = gathered(back_2)
    block_1 = block_1.transpose(1, 0, 2)
    block_2 = block_2.transpose(1, 0, 2)
    return jnp.stack(
        [block_1, jnp.where(odd, block_2, back_2), back_1, jnp.where(odd, back_2, block_2)], axis=0
    )


def solution(mesh):
    placed = (P("kp", None, None, "own"), P("own"))
    return jax.shard_map(
        body,
        mesh=mesh,
        in_specs=placed,
        out_specs=P(None, ("kp", "own"), None, None),
        check_vma=False,
    )
```

time: 240 us -> 207 us (0.86)
  the two profiles are of different devices: /device:TPU:7 before, /device:TPU:40 now
where the time goes in v1:
time: 207 us; the launch traced here: 206 us
  waiting for transfers between devices  92.6 us (45%)
  starting transfers between devices  79.4 us (38%)
  matrix products  17 us (8%)
  local copies, waits for them, and re-layouts  10 us (5%)
  other arithmetic  6.26 us (3%)
    ppermute x2, waiting for transfers between devices, first(): lax.ppermute(product(to_up, right).astype(jnp.bfloat16), 'own', up)  26.5 us
    all_to_all x2, starting transfers between devices, gathered(): lax.all_to_all(pieces.reshape(owners, own_rows, 2, own_rows), 'own', spli...  19.9 us
    ppermute x2, starting transfers between devices, first(): lax.ppermute(product(to_down, right).astype(jnp.bfloat16), 'own', down)  15.9 us
    ppermute x2, waiting for transfers between devices, second(): lax.ppermute(to_up.astype(jnp.bfloat16), 'own', up)  15.3 us
    dot_general x12, matrix products, product(): lax.dot_general(rows, right, (((2,), (1,)), ((), ())), preferred_element_...  15 us
    ppermute x2, starting transfers between devices, second(): lax.ppermute(to_down.astype(jnp.bfloat16), 'own', down)  12.6 us
    ppermute x1, waiting for transfers between devices, body(): lax.ppermute(pair_density, 'kp', [(i, (i + 1) % groups) for i in range(gr...  12.4 us
    all_to_all x2, waiting for transfers between devices, gathered(): lax.all_to_all(pieces.reshape(owners, own_rows, 2, own_rows), 'own', spli...  12.3 us
  transfers between devices with their start and end apart: 15, of which 9 were waited for; matrix products, arithmetic and copies ran while one was open for 13% of the time, Pallas kernels for 0%

profile of v1, /device:TPU:40, one launch (start us, length us, event | category | flops | bytes accessed | tf_op | source)
XLA Modules:
  0.0 205.8 jit_solution(9308173397808600100)
XLA Ops:
  0.0 1.9 collective-permute-start
  1.9 2.0 multiply_convert_fusion
  4.2 0.4 fusion.27
  5.1 1.0 fusion.47
  6.1 12.4 %collective-permute-done = bf16[2,256,2,512]{3,2,1,0:T(2,128)(2,1)} collective-permute-done((bf16[2,256,2,512]{3,2,1,0:T(2,128)(2,1)}, bf16[2,256,2,512]{3,2,1,0:T(2,128)(2,1)}, u32[]{:S(2)}, u32[]{:S(2)}) %collective-permute-start) | collective-permute-done | bytes 1048608 | tf_op jit(solution)/shard_map/ppermute | solution.py:30
  18.5 1.8 reshape.37
  20.3 2.2 %fusion = bf16[2,128,512]{2,1,0:T(8,128)(2,1)} fusion(bf16[512,1024,1]{1,0,2:T(8,128)(2,1)S(1)} %reshape.37, bf16[2,64,1024]{2,1,0:T(8,128)(2,1)} %get-tuple-element.7, bf16[2,64,1024]{2,1,0:T(8,128)(2,1)} %get-tuple-element.6), kind=kOutput, calls=%fused_computation.22 | convolution fusion | flops 269746176 | bytes 1835008 | tf_op jit(solution)/shard_map/dot_general | solution.py:51
  22.5 11.8 %collective-permute-start.1 = (bf16[2,128,512]{2,1,0:T(8,128)(2,1)}, bf16[2,128,512]{2,1,0:T(8,128)(2,1)}, u32[]{:S(2)}, u32[]{:S(2)}) collective-permute-start(bf16[2,128,512]{2,1,0:T(8,128)(2,1)} %fusion), channel_id=1, source_target_pairs={{0,3},{1,0},{2,1},{3,2},{4,7},{5,4},{6,5},{7,6},{8,11},{9,8},{10,9... | collective-permute-start | bytes 786440 | tf_op jit(solution)/shard_map/ppermute | solution.py:64
  34.4 3.0 %collective-permute-start.6 = (bf16[2,256,2,512]{3,2,1,0:T(2,128)(2,1)}, bf16[2,256,2,512]{3,2,1,0:T(2,128)(2,1)}, u32[]{:S(2)}, u32[]{:S(2)}) collective-permute-start(bf16[2,256,2,512]{3,2,1,0:T(2,128)(2,1)} %param.5), channel_id=1, source_target_pairs={{0,504},{8,0},{16,8},{24,16},{32,24},{40,32},{48,40},{56,48},{64,5... | collective-permute-start | bytes 3145736 | tf_op jit(solution)/shard_map/ppermute | solution.py:31
  37.4 1.5 fusion.1
  38.9 1.9 collective-permute-start.2
  40.8 1.4 collective-permute-start.5
  42.2 12.1 %collective-permute-done.1 = bf16[2,128,512]{2,1,0:T(8,128)(2,1)} collective-permute-done((bf16[2,128,512]{2,1,0:T(8,128)(2,1)}, bf16[2,128,512]{2,1,0:T(8,128)(2,1)}, u32[]{:S(2)}, u32[]{:S(2)}) %collective-permute-start.1) | collective-permute-done | bytes 262176 | tf_op jit(solution)/shard_map/ppermute | solution.py:64
  54.3 1.4 fusion.22
  55.7 8.5 %collective-permute-start.4 = (bf16[2,64,512]{2,1,0:T(8,128)(2,1)S(1)}, bf16[2,64,512]{2,1,0:T(8,128)(2,1)S(1)}, u32[]{:S(2)}, u32[]{:S(2)}) collective-permute-start(bf16[2,64,512]{2,1,0:T(8,128)(2,1)S(1)} %fusion.22), channel_id=1, source_target_pairs={{0,3},{1,0},{2,1},{3,2},{4,7},{5,4},{6,5},{7,6},{8,11},{9,8},{10,9... | collective-permute-start | bytes 393224 | tf_op jit(solution)/shard_map/ppermute | solution.py:72
  64.3 4.5 %collective-permute-done.2 = bf16[2,128,512]{2,1,0:T(8,128)(2,1)S(1)} collective-permute-done((bf16[2,128,512]{2,1,0:T(8,128)(2,1)S(1)}, bf16[2,128,512]{2,1,0:T(8,128)(2,1)S(1)}, u32[]{:S(2)}, u32[]{:S(2)}) %collective-permute-start.2) | collective-permute-done | bytes 262176 | tf_op jit(solution)/shard_map/ppermute | solution.py:63
  68.8 0.5 fusion.20
  69.3 1.9 collective-permute-start.3
  71.2 4.1 %collective-permute-done.4 = bf16[2,64,512]{2,1,0:T(8,128)(2,1)S(1)} collective-permute-done((bf16[2,64,512]{2,1,0:T(8,128)(2,1)S(1)}, bf16[2,64,512]{2,1,0:T(8,128)(2,1)S(1)}, u32[]{:S(2)}, u32[]{:S(2)}) %collective-permute-start.4) | collective-permute-done | bytes 131104 | tf_op jit(solution)/shard_map/ppermute | solution.py:72
  75.3 0.5 fusion.21
  75.8 8.3 %collective-permute-done.3 = bf16[2,64,512]{2,1,0:T(8,128)(2,1)S(1)} collective-permute-done((bf16[2,64,512]{2,1,0:T(8,128)(2,1)S(1)}, bf16[2,64,512]{2,1,0:T(8,128)(2,1)S(1)}, u32[]{:S(2)}, u32[]{:S(2)}) %collective-permute-start.3) | collective-permute-done | bytes 131104 | tf_op jit(solution)/shard_map/ppermute | solution.py:71
  84.1 1.4 fusion.19
  85.5 1.1 fusion.5
  86.6 1.9 collective-permute-start.12
  88.6 2.3 %broadcast_select_fusion = bf16[2,64,8,512]{3,2,1,0:T(8,128)(2,1)} fusion(bf16[2,64,8,512]{3,2,1,0:T(8,128)(2,1)S(1)} %bitcast.106, bf16[2,64,8,512]{3,2,1,0:T(8,128)(2,1)} %bitcast.100, pred[]{:T(512)S(6)} %eq.8), kind=kLoop, calls=%fused_computation.17 | loop fusion | flops 524288 | bytes 3145729 | tf_op jit(solution)/shard_map/jit(_where)/select_n | solution.py:100
  90.9 1.8 reshape.38
  92.7 2.2 %fusion.2 = bf16[2,128,512]{2,1,0:T(8,128)(2,1)} fusion(bf16[512,1024,1]{1,0,2:T(8,128)(2,1)S(1)} %reshape.38, bf16[2,64,1024]{2,1,0:T(8,128)(2,1)} %get-tuple-element.7, bf16[2,64,1024]{2,1,0:T(8,128)(2,1)} %get-tuple-element.6), kind=kOutput, calls=%fused_computation.24 | convolution fusion | flops 269746176 | bytes 1835008 | tf_op jit(solution)/shard_map/dot_general | solution.py:51
  94.9 4.0 %collective-permute-start.7 = (bf16[2,128,512]{2,1,0:T(8,128)(2,1)}, bf16[2,128,512]{2,1,0:T(8,128)(2,1)}, u32[]{:S(2)}, u32[]{:S(2)}) collective-permute-start(bf16[2,128,512]{2,1,0:T(8,128)(2,1)} %fusion.2), channel_id=1, source_target_pairs={{0,3},{1,0},{2,1},{3,2},{4,7},{5,4},{6,5},{7,6},{8,11},{9,8},{10,9... | collective-permute-start | bytes 786440 | tf_op jit(solution)/shard_map/ppermute | solution.py:64
  99.0 1.7 copy_bitcast_fusion
  100.7 5.1 %all-to-all-start.1 = ((bf16[4,128,2,128]{1,3,2,0:T(8,128)(2,1)}), bf16[4,128,2,128]{1,3,2,0:T(8,128)(2,1)}, u32[]{:S(2)}, u32[]{:S(2)}) async-start(bf16[4,128,2,128]{1,3,2,0:T(8,128)(2,1)} %copy_bitcast_fusion), calls=%async_computation.1 | async-start | bytes 524288 | tf_op jit(solution)/shard_map/all_to_all | solution.py:91
  105.8 1.5 fusion.3
  107.3 7.8 %collective-permute-start.8 = (bf16[2,128,512]{2,1,0:T(8,128)(2,1)S(1)}, bf16[2,128,512]{2,1,0:T(8,128)(2,1)S(1)}, u32[]{:S(2)}, u32[]{:S(2)}) collective-permute-start(bf16[2,128,512]{2,1,0:T(8,128)(2,1)S(1)} %fusion.3), channel_id=1, source_target_pairs={{0,1},{1,2},{2,3},{3,0},{4,5},{5,6},{6,7},{7,4},{8,9},{9,10},{10,1... | collective-permute-start | bytes 786440 | tf_op jit(solution)/shard_map/ppermute | solution.py:63
  115.1 1.4 fusion.26
  116.5 4.0 %collective-permute-start.10 = (bf16[2,64,512]{2,1,0:T(8,128)(2,1)S(1)}, bf16[2,64,512]{2,1,0:T(8,128)(2,1)S(1)}, u32[]{:S(2)}, u32[]{:S(2)}) collective-permute-start(bf16[2,64,512]{2,1,0:T(8,128)(2,1)S(1)} %fusion.26), channel_id=1, source_target_pairs={{0,3},{1,0},{2,1},{3,2},{4,7},{5,4},{6,5},{7,6},{8,11},{9,8},{10,9... | collective-permute-start | bytes 393224 | tf_op jit(solution)/shard_map/ppermute | solution.py:72
  120.6 22.0 %collective-permute-done.8 = bf16[2,128,512]{2,1,0:T(8,128)(2,1)S(1)} collective-permute-done((bf16[2,128,512]{2,1,0:T(8,128)(2,1)S(1)}, bf16[2,128,512]{2,1,0:T(8,128)(2,1)S(1)}, u32[]{:S(2)}, u32[]{:S(2)}) %collective-permute-start.8) | collective-permute-done | bytes 262176 | tf_op jit(solution)/shard_map/ppermute | solution.py:63
  142.6 0.5 fusion.24
  143.1 9.3 %collective-permute-start.9 = (bf16[2,64,512]{2,1,0:T(8,128)(2,1)S(1)}, bf16[2,64,512]{2,1,0:T(8,128)(2,1)S(1)}, u32[]{:S(2)}, u32[]{:S(2)}) collective-permute-start(bf16[2,64,512]{2,1,0:T(8,128)(2,1)S(1)} %fusion.24), channel_id=1, source_target_pairs={{0,1},{1,2},{2,3},{3,0},{4,5},{5,6},{6,7},{7,4},{8,9},{9,10},{10,1... | collective-permute-start | bytes 393224 | tf_op jit(solution)/shard_map/ppermute | solution.py:71
  152.4 0.5 fusion.25
  152.9 7.0 %collective-permute-done.9 = bf16[2,64,512]{2,1,0:T(8,128)(2,1)S(1)} collective-permute-done((bf16[2,64,512]{2,1,0:T(8,128)(2,1)S(1)}, bf16[2,64,512]{2,1,0:T(8,128)(2,1)S(1)}, u32[]{:S(2)}, u32[]{:S(2)}) %collective-permute-start.9) | collective-permute-done | bytes 131104 | tf_op jit(solution)/shard_map/ppermute | solution.py:71
  159.9 1.4 fusion.23
  161.4 0.3 fusion.4
  161.7 1.9 collective-permute-start.11
  163.6 9.9 %collective-permute-done.11 = bf16[512,2,128]{0,2,1:T(8,128)(2,1)S(1)} collective-permute-done((bf16[512,2,128]{0,2,1:T(8,128)(2,1)S(1)}, bf16[512,2,128]{0,2,1:T(8,128)(2,1)S(1)}, u32[]{:S(2)}, u32[]{:S(2)}) %collective-permute-start.11) | collective-permute-done | bytes 262176 | tf_op jit(solution)/shard_map/ppermute | solution.py:107
  173.5 0.8 copy_bitcast_fusion.1
  174.3 14.8 %all-to-all-start = ((bf16[4,128,2,128]{1,3,2,0:T(8,128)(2,1)}), bf16[4,128,2,128]{1,3,2,0:T(8,128)(2,1)S(1)}, u32[]{:S(2)}, u32[]{:S(2)}) async-start(bf16[4,128,2,128]{1,3,2,0:T(8,128)(2,1)} %copy_bitcast_fusion.1), calls=%async_computation | async-start | bytes 524288 | tf_op jit(solution)/shard_map/all_to_all | solution.py:91
  189.1 1.1 copy.18
  190.7 12.3 %all-to-all-done = bf16[4,128,2,128]{1,3,2,0:T(8,128)(2,1)S(1)} async-done(((bf16[4,128,2,128]{1,3,2,0:T(8,128)(2,1)}), bf16[4,128,2,128]{1,3,2,0:T(8,128)(2,1)S(1)}, u32[]{:S(2)}, u32[]{:S(2)}) %all-to-all-start) | async-done | bytes 262176 | tf_op jit(solution)/shard_map/all_to_all | solution.py:91
  203.7 2.0 copy.19
  (37 shorter events, 1.9 us)
Async XLA Ops:
  0.0 18.5 %collective-permute-start = (bf16[2,256,2,512]{3,2,1,0:T(2,128)(2,1)}, bf16[2,256,2,512]{3,2,1,0:T(2,128)(2,1)}, u32[]{:S(2)}, u32[]{:S(2)}) collective-permute-start(bf16[2,256,2,512]{3,2,1,0:T(2,128)(2,1)} %param.5), channel_id=1, source_target_pairs={{0,4},{4,8},{8,12},{12,16},{16,20},{20,24},{24,28},{28,32},{32,36}... | collective-permute-start | bytes 3145736 | tf_op jit(solution)/shard_map/ppermute | solution.py:30
  22.5 31.8 %collective-permute-start.1 = (bf16[2,128,512]{2,1,0:T(8,128)(2,1)}, bf16[2,128,512]{2,1,0:T(8,128)(2,1)}, u32[]{:S(2)}, u32[]{:S(2)}) collective-permute-start(bf16[2,128,512]{2,1,0:T(8,128)(2,1)} %fusion), channel_id=1, source_target_pairs={{0,3},{1,0},{2,1},{3,2},{4,7},{5,4},{6,5},{7,6},{8,11},{9,8},{10,9... | collective-permute-start | bytes 786440 | tf_op jit(solution)/shard_map/ppermute | solution.py:64
  34.4 54.2 %collective-permute-start.6 = (bf16[2,256,2,512]{3,2,1,0:T(2,128)(2,1)}, bf16[2,256,2,512]{3,2,1,0:T(2,128)(2,1)}, u32[]{:S(2)}, u32[]{:S(2)}) collective-permute-start(bf16[2,256,2,512]{3,2,1,0:T(2,128)(2,1)} %param.5), channel_id=1, source_target_pairs={{0,504},{8,0},{16,8},{24,16},{32,24},{40,32},{48,40},{56,48},{64,5... | collective-permute-start | bytes 3145736 | tf_op jit(solution)/shard_map/ppermute | solution.py:31
  38.9 29.9 %collective-permute-start.2 = (bf16[2,128,512]{2,1,0:T(8,128)(2,1)S(1)}, bf16[2,128,512]{2,1,0:T(8,128)(2,1)S(1)}, u32[]{:S(2)}, u32[]{:S(2)}) collective-permute-start(bf16[2,128,512]{2,1,0:T(8,128)(2,1)S(1)} %fusion.1), channel_id=1, source_target_pairs={{0,1},{1,2},{2,3},{3,0},{4,5},{5,6},{6,7},{7,4},{8,9},{9,10},{10,1... | collective-permute-start | bytes 786440 | tf_op jit(solution)/shard_map/ppermute | solution.py:63
  40.8 47.7 %collective-permute-start.5 = (bf16[2,256,2,512]{3,2,1,0:T(2,128)(2,1)}, bf16[2,256,2,512]{3,2,1,0:T(2,128)(2,1)S(1)}, u32[]{:S(2)}, u32[]{:S(2)}) collective-permute-start(bf16[2,256,2,512]{3,2,1,0:T(2,128)(2,1)} %collective-permute-done), channel_id=1, source_target_pairs={{0,4},{8,12},{16,20},{24,28},{32,36},{40,44},{48,52},{56,60},{64,6... | collective-permute-start | bytes 3145736 | tf_op jit(solution)/shard_map/ppermute | solution.py:32
  55.7 19.6 %collective-permute-start.4 = (bf16[2,64,512]{2,1,0:T(8,128)(2,1)S(1)}, bf16[2,64,512]{2,1,0:T(8,128)(2,1)S(1)}, u32[]{:S(2)}, u32[]{:S(2)}) collective-permute-start(bf16[2,64,512]{2,1,0:T(8,128)(2,1)S(1)} %fusion.22), channel_id=1, source_target_pairs={{0,3},{1,0},{2,1},{3,2},{4,7},{5,4},{6,5},{7,6},{8,11},{9,8},{10,9... | collective-permute-start | bytes 393224 | tf_op jit(solution)/shard_map/ppermute | solution.py:72
  69.3 14.8 %collective-permute-start.3 = (bf16[2,64,512]{2,1,0:T(8,128)(2,1)S(1)}, bf16[2,64,512]{2,1,0:T(8,128)(2,1)S(1)}, u32[]{:S(2)}, u32[]{:S(2)}) collective-permute-start(bf16[2,64,512]{2,1,0:T(8,128)(2,1)S(1)} %fusion.20), channel_id=1, source_target_pairs={{0,1},{1,2},{2,3},{3,0},{4,5},{5,6},{6,7},{7,4},{8,9},{9,10},{10,1... | collective-permute-start | bytes 393224 | tf_op jit(solution)/shard_map/ppermute | solution.py:71
  75.8 9.7 %copy-start.2 = (bf16[512,512,1]{1,0,2:T(8,128)(2,1)S(1)}, bf16[512,512,1]{1,0,2:T(8,128)(2,1)}, u32[]{:S(2)}) copy-start(bf16[512,512,1]{1,0,2:T(8,128)(2,1)} %constant.54) | copy-start | bytes 1572868
  75.8 9.7 %copy-start.9 = (bf16[2]{0:T(256)(128)(2,1)S(1)}, bf16[2]{0:T(256)(128)(2,1)}, u32[]{:S(2)}) copy-start(bf16[2]{0:T(256)(128)(2,1)} %constant.52.clone) | copy-start | bytes 16
  85.5 3.0 %copy-start = (bf16[2,64,512]{2,1,0:T(8,128)(2,1)}, bf16[2,64,512]{2,1,0:T(8,128)(2,1)S(1)}, u32[]{:S(2)}) copy-start(bf16[2,64,512]{2,1,0:T(8,128)(2,1)S(1)} %fusion.19) | copy-start | bytes 393220
  86.6 12.3 %collective-permute-start.12 = (bf16[512,2,128]{0,2,1:T(8,128)(2,1)}, bf16[512,2,128]{0,2,1:T(8,128)(2,1)}, u32[]{:S(2)}, u32[]{:S(2)}) collective-permute-start(bf16[512,2,128]{0,2,1:T(8,128)(2,1)} %fusion.5), channel_id=1, source_target_pairs={{0,508},{4,0},{8,4},{12,8},{16,12},{20,16},{24,20},{28,24},{32,28}... | collective-permute-start | bytes 786440 | tf_op jit(solution)/shard_map/ppermute | solution.py:105
  94.9 20.2 %collective-permute-start.7 = (bf16[2,128,512]{2,1,0:T(8,128)(2,1)}, bf16[2,128,512]{2,1,0:T(8,128)(2,1)}, u32[]{:S(2)}, u32[]{:S(2)}) collective-permute-start(bf16[2,128,512]{2,1,0:T(8,128)(2,1)} %fusion.2), channel_id=1, source_target_pairs={{0,3},{1,0},{2,1},{3,2},{4,7},{5,4},{6,5},{7,6},{8,11},{9,8},{10,9... | collective-permute-start | bytes 786440 | tf_op jit(solution)/shard_map/ppermute | solution.py:64
  100.7 73.6 %all-to-all-start.1 = ((bf16[4,128,2,128]{1,3,2,0:T(8,128)(2,1)}), bf16[4,128,2,128]{1,3,2,0:T(8,128)(2,1)}, u32[]{:S(2)}, u32[]{:S(2)}) async-start(bf16[4,128,2,128]{1,3,2,0:T(8,128)(2,1)} %copy_bitcast_fusion), calls=%async_computation.1 | async-start | bytes 524288 | tf_op jit(solution)/shard_map/all_to_all | solution.py:91
  107.3 35.3 %collective-permute-start.8 = (bf16[2,128,512]{2,1,0:T(8,128)(2,1)S(1)}, bf16[2,128,512]{2,1,0:T(8,128)(2,1)S(1)}, u32[]{:S(2)}, u32[]{:S(2)}) collective-permute-start(bf16[2,128,512]{2,1,0:T(8,128)(2,1)S(1)} %fusion.3), channel_id=1, source_target_pairs={{0,1},{1,2},{2,3},{3,0},{4,5},{5,6},{6,7},{7,4},{8,9},{9,10},{10,1... | collective-permute-start | bytes 786440 | tf_op jit(solution)/shard_map/ppermute | solution.py:63
  116.5 35.9 %collective-permute-start.10 = (bf16[2,64,512]{2,1,0:T(8,128)(2,1)S(1)}, bf16[2,64,512]{2,1,0:T(8,128)(2,1)S(1)}, u32[]{:S(2)}, u32[]{:S(2)}) collective-permute-start(bf16[2,64,512]{2,1,0:T(8,128)(2,1)S(1)} %fusion.26), channel_id=1, source_target_pairs={{0,3},{1,0},{2,1},{3,2},{4,7},{5,4},{6,5},{7,6},{8,11},{9,8},{10,9... | collective-permute-start | bytes 393224 | tf_op jit(solution)/shard_map/ppermute | solution.py:72
  143.1 16.9 %collective-permute-start.9 = (bf16[2,64,512]{2,1,0:T(8,128)(2,1)S(1)}, bf16[2,64,512]{2,1,0:T(8,128)(2,1)S(1)}, u32[]{:S(2)}, u32[]{:S(2)}) collective-permute-start(bf16[2,64,512]{2,1,0:T(8,128)(2,1)S(1)} %fusion.24), channel_id=1, source_target_pairs={{0,1},{1,2},{2,3},{3,0},{4,5},{5,6},{6,7},{7,4},{8,9},{9,10},{10,1... | collective-permute-start | bytes 393224 | tf_op jit(solution)/shard_map/ppermute | solution.py:71
  152.9 8.4 %copy-start.5 = (bf16[2,64,512]{2,1,0:T(8,128)(2,1)}, bf16[2,64,512]{2,1,0:T(8,128)(2,1)S(1)}, u32[]{:S(2)}) copy-start(bf16[2,64,512]{2,1,0:T(8,128)(2,1)S(1)} %fusion.25) | copy-start | bytes 393220
  152.9 8.4 %copy-start.3 = (bf16[512,512,1]{1,0,2:T(8,128)(2,1)S(1)}, bf16[512,512,1]{1,0,2:T(8,128)(2,1)}, u32[]{:S(2)}) copy-start(bf16[512,512,1]{1,0,2:T(8,128)(2,1)} %constant.54) | copy-start | bytes 1572868
  161.4 12.1 %copy-start.7 = (bf16[2,64,512]{2,1,0:T(8,128)(2,1)}, bf16[2,64,512]{2,1,0:T(8,128)(2,1)S(1)}, u32[]{:S(2)}) copy-start(bf16[2,64,512]{2,1,0:T(8,128)(2,1)S(1)} %fusion.23) | copy-start | bytes 393220
  161.4 27.7 %copy-start.1 = (bf16[2,64,512]{2,1,0:T(8,128)(2,1)S(1)}, bf16[2,64,512]{2,1,0:T(8,128)(2,1)}, u32[]{:S(2)}) copy-start(bf16[2,64,512]{2,1,0:T(8,128)(2,1)} %copy-done) | copy-start | bytes 393220
  161.7 11.8 %collective-permute-start.11 = (bf16[512,2,128]{0,2,1:T(8,128)(2,1)S(1)}, bf16[512,2,128]{0,2,1:T(8,128)(2,1)S(1)}, u32[]{:S(2)}, u32[]{:S(2)}) collective-permute-start(bf16[512,2,128]{0,2,1:T(8,128)(2,1)S(1)} %fusion.4), channel_id=1, source_target_pairs={{0,8},{4,508},{8,16},{12,4},{16,24},{20,12},{24,32},{28,20},{32,40... | collective-permute-start | bytes 786440 | tf_op jit(solution)/shard_map/ppermute | solution.py:107
  174.3 16.1 %copy-start.4 = (bf16[512,512,1]{1,0,2:T(8,128)(2,1)S(1)}, bf16[512,512,1]{1,0,2:T(8,128)(2,1)}, u32[]{:S(2)}) copy-start(bf16[512,512,1]{1,0,2:T(8,128)(2,1)} %constant.54) | copy-start | bytes 1572868
  174.3 28.7 %all-to-all-start = ((bf16[4,128,2,128]{1,3,2,0:T(8,128)(2,1)}), bf16[4,128,2,128]{1,3,2,0:T(8,128)(2,1)S(1)}, u32[]{:S(2)}, u32[]{:S(2)}) async-start(bf16[4,128,2,128]{1,3,2,0:T(8,128)(2,1)} %copy_bitcast_fusion.1), calls=%async_computation | async-start | bytes 524288 | tf_op jit(solution)/shard_map/all_to_all | solution.py:91
  190.4 12.9 %copy-start.6 = (bf16[2,64,512]{2,1,0:T(8,128)(2,1)S(1)}, bf16[2,64,512]{2,1,0:T(8,128)(2,1)}, u32[]{:S(2)}) copy-start(bf16[2,64,512]{2,1,0:T(8,128)(2,1)} %copy-done.5) | copy-start | bytes 393220
  190.4 12.9 %copy-start.8 = (bf16[2,64,512]{2,1,0:T(8,128)(2,1)S(1)}, bf16[2,64,512]{2,1,0:T(8,128)(2,1)}, u32[]{:S(2)}) copy-start(bf16[2,64,512]{2,1,0:T(8,128)(2,1)} %copy-done.7) | copy-start | bytes 393220

commit v2 on v1

--- a/solution.py
+++ b/solution.py
@@ -29,7 +29,6 @@
 
     near_raw = lax.ppermute(pair_density, "kp", [(i, (i + 1) % groups) for i in range(groups)])
     ahead_raw = lax.ppermute(pair_density, "kp", [(i, (i - 2) % groups) for i in range(0, groups, 2)])
-    behind_raw = lax.ppermute(near_raw, "kp", [(i, i + 1) for i in range(0, groups, 2)])
 
     def planes(raw):
         return raw.reshape(row_total, 2 * g_local)
@@ -56,21 +55,10 @@
     up = [(o, (o + 1) % owners) for o in range(owners)]
     down = [(o, (o - 1) % owners) for o in range(owners)]
 
-    def first(right):
-        to_up = jnp.concatenate([left[2, :, :half], left[1, :, half:]], axis=1)
-        to_down = jnp.concatenate([left[3, :, :half], left[2, :, half:]], axis=1)
-        return (
-            lax.ppermute(product(to_up, right).astype(jnp.bfloat16), "own", up),
-            lax.ppermute(product(to_down, right).astype(jnp.bfloat16), "own", down),
-        )
-
-    def second(right, from_down, from_up):
+    def second_products(right, from_down, from_up):
         to_up = product(left[1, :, :half], right) + from_down[:, :half].astype(jnp.float32)
         to_down = product(left[3, :, half:], right) + from_up[:, half:].astype(jnp.float32)
-        return (
-            lax.ppermute(to_up.astype(jnp.bfloat16), "own", up),
-            lax.ppermute(to_down.astype(jnp.bfloat16), "own", down),
-        )
+        return to_up.astype(jnp.bfloat16), to_down.astype(jnp.bfloat16)
 
     def third(right, from_down, from_up, late_down, late_up):
         low = product(left[0, :, :half], right) + from_up[:, :half].astype(jnp.float32) + late_down.astype(jnp.float32)
@@ -95,12 +83,27 @@
         out = lax.dot_general(swapped, pick, (((2,), (0,)), ((), ())), preferred_element_type=jnp.float32)
         return out.astype(jnp.bfloat16)
 
+    def first_products(right):
+        to_up = jnp.concatenate([left[2, :, :half], left[1, :, half:]], axis=1)
+        to_down = jnp.concatenate([left[3, :, :half], left[2, :, half:]], axis=1)
+        return (product(to_up, right).astype(jnp.bfloat16), product(to_down, right).astype(jnp.bfloat16))
+
+    def sends(pieces):
+        return lax.ppermute(pieces[0], "own", up), lax.ppermute(pieces[1], "own", down)
+
+    near_raw, ahead_raw, left = lax.optimization_barrier((near_raw, ahead_raw, left))
+    behind_raw = lax.ppermute(near_raw, "kp", [(i, i + 1) for i in range(0, groups, 2)])
     right_1 = planes(near_raw)
-    got_1 = first(right_1)
+    pieces_1 = first_products(right_1)
+    got_1 = sends(pieces_1)
     right_2 = planes(jnp.where(odd, behind_raw, ahead_raw))
-    got_2 = first(right_2)
-    late_1 = second(right_1, *got_1)
-    late_2 = second(right_2, *got_2)
+    pieces_2 = first_products(right_2)
+    got_2 = sends(pieces_2)
+    got_1, _ = lax.optimization_barrier((got_1, pieces_2))
+    late_1 = sends(second_products(right_1, *got_1))
+    pieces_2 = second_products(right_2, *got_2)
+    late_2 = sends(pieces_2)
+    late_1, _ = lax.optimization_barrier((late_1, pieces_2))
     block_1 = third(right_1, *got_1, *late_1)
     back_1 = lax.ppermute(turned(block_1), "kp", [(i, (i - 1) % groups) for i in range(groups)])
     block_2 = third(right_2, *got_2, *late_2)

time: 207 us -> 186 us (0.90)
  the two profiles are of different devices: /device:TPU:40 before, /device:TPU:24 now
where the time goes in v2:
time: 186 us; the launch traced here: 185 us
  waiting for transfers between devices  82.8 us (45%)
  starting transfers between devices  77 us (41%)
  matrix products  13.5 us (7%)
  local copies, waits for them, and re-layouts  7.12 us (4%)
  other arithmetic  4.35 us (2%)
    ppermute x4, waiting for transfers between devices, sends(): lax.ppermute(pieces[1], 'own', down)  31.5 us
    ppermute x4, starting transfers between devices, sends(): lax.ppermute(pieces[0], 'own', up)  24 us
    all_to_all x2, starting transfers between devices, gathered(): lax.all_to_all(pieces.reshape(owners, own_rows, 2, own_rows), 'own', spli...  18.2 us
    ppermute x4, starting transfers between devices, sends(): lax.ppermute(pieces[1], 'own', down)  17.8 us
    ppermute x1, waiting for transfers between devices, body(): lax.ppermute(turned(block_2), 'kp', [(i, (i - 2 if i % 2 else i + 2) % gr...  16.1 us
    all_to_all x2, waiting for transfers between devices, gathered(): lax.all_to_all(pieces.reshape(owners, own_rows, 2, own_rows), 'own', spli...  13.2 us
    dot_general x12, matrix products, product(): lax.dot_general(rows, right, (((2,), (1,)), ((), ())), preferred_element_...  12.2 us
    ppermute x1, starting transfers between devices, body(): lax.ppermute(pair_density, 'kp', [(i, (i - 2) % groups) for i in range(0,...  8.91 us
  transfers between devices with their start and end apart: 15, of which 7 were waited for; matrix products, arithmetic and copies ran while one was open for 12% of the time, Pallas kernels for 0%

profile of v2, /device:TPU:24, one launch (start us, length us, event | category | flops | bytes accessed | tf_op | source)
XLA Modules:
  0.0 185.3 jit_solution(12085971469340760751)
XLA Ops:
  0.0 1.9 %collective-permute-start = (bf16[2,256,2,512]{3,2,1,0:T(2,128)(2,1)}, bf16[2,256,2,512]{3,2,1,0:T(2,128)(2,1)}, u32[]{:S(2)}, u32[]{:S(2)}) collective-permute-start(bf16[2,256,2,512]{3,2,1,0:T(2,128)(2,1)} %param.5), channel_id=1, source_target_pairs={{0,4},{4,8},{8,12},{12,16},{16,20},{20,24},{24,28},{28,32},{32,36}... | collective-permute-start | bytes 3145736 | tf_op jit(solution)/shard_map/ppermute | solution.py:30
  1.9 8.9 %collective-permute-start.1 = (bf16[2,256,2,512]{3,2,1,0:T(2,128)(2,1)}, bf16[2,256,2,512]{3,2,1,0:T(2,128)(2,1)}, u32[]{:S(2)}, u32[]{:S(2)}) collective-permute-start(bf16[2,256,2,512]{3,2,1,0:T(2,128)(2,1)} %param.5), channel_id=1, source_target_pairs={{0,504},{8,0},{16,8},{24,16},{32,24},{40,32},{48,40},{56,48},{64,5... | collective-permute-start | bytes 3145736 | tf_op jit(solution)/shard_map/ppermute | solution.py:31
  10.8 2.0 %multiply_convert_fusion = bf16[2,256,2,512]{3,2,1,0:T(2,128)(2,1)S(1)} fusion(bf16[2,256,2,512]{3,2,1,0:T(2,128)(2,1)} %param.5, f32[512]{0:T(512)} %param.6), kind=kLoop, calls=%fused_computation.3 | loop fusion | flops 1572864 | bytes 2099200 | tf_op jit(solution)/shard_map/convert_element_type | solution.py:36
  12.9 0.2 copy.12
  13.1 0.4 fusion.27
  13.9 0.2 pad_maximum_fusion
  14.1 7.1 %collective-permute-done = bf16[2,256,2,512]{3,2,1,0:T(2,128)(2,1)} collective-permute-done((bf16[2,256,2,512]{3,2,1,0:T(2,128)(2,1)}, bf16[2,256,2,512]{3,2,1,0:T(2,128)(2,1)}, u32[]{:S(2)}, u32[]{:S(2)}) %collective-permute-start) | collective-permute-done | bytes 1048608 | tf_op jit(solution)/shard_map/ppermute | solution.py:30
  21.2 2.2 %collective-permute-done.1 = bf16[2,256,2,512]{3,2,1,0:T(2,128)(2,1)} collective-permute-done((bf16[2,256,2,512]{3,2,1,0:T(2,128)(2,1)}, bf16[2,256,2,512]{3,2,1,0:T(2,128)(2,1)}, u32[]{:S(2)}, u32[]{:S(2)}) %collective-permute-start.1) | collective-permute-done | bytes 1048608 | tf_op jit(solution)/shard_map/ppermute | solution.py:31
  23.4 2.3 %collective-permute-start.4 = (bf16[2,256,2,512]{3,2,1,0:T(2,128)(2,1)}, bf16[2,256,2,512]{3,2,1,0:T(2,128)(2,1)}, u32[]{:S(2)}, u32[]{:S(2)}) collective-permute-start(bf16[2,256,2,512]{3,2,1,0:T(2,128)(2,1)} %collective-permute-done), channel_id=1, source_target_pairs={{0,4},{8,12},{16,20},{24,28},{32,36},{40,44},{48,52},{56,60},{64,6... | collective-permute-start | bytes 3145736 | tf_op jit(solution)/shard_map/ppermute | solution.py:95
  25.7 1.8 reshape.37
  27.7 1.2 fusion
  28.9 9.1 %collective-permute-start.2 = (bf16[2,128,512]{2,1,0:T(8,128)(2,1)}, bf16[2,128,512]{2,1,0:T(8,128)(2,1)S(1)}, u32[]{:S(2)}, u32[]{:S(2)}) collective-permute-start(bf16[2,128,512]{2,1,0:T(8,128)(2,1)} %fusion), channel_id=1, source_target_pairs={{0,1},{1,2},{2,3},{3,0},{4,5},{5,6},{6,7},{7,4},{8,9},{9,10},{10,1... | collective-permute-start | bytes 786440 | tf_op jit(solution)/shard_map/ppermute | solution.py:92
  38.0 1.2 fusion.1
  39.1 3.3 %collective-permute-start.3 = (bf16[2,128,512]{2,1,0:T(8,128)(2,1)}, bf16[2,128,512]{2,1,0:T(8,128)(2,1)}, u32[]{:S(2)}, u32[]{:S(2)}) collective-permute-start(bf16[2,128,512]{2,1,0:T(8,128)(2,1)} %fusion.1), channel_id=1, source_target_pairs={{0,3},{1,0},{2,1},{3,2},{4,7},{5,4},{6,5},{7,6},{8,11},{9,8},{10,9... | collective-permute-start | bytes 786440 | tf_op jit(solution)/shard_map/ppermute | solution.py:92
  42.5 1.4 broadcast_select_fusion
  43.9 0.8 reshape.38
  44.7 1.7 fusion.3
  46.3 7.8 %collective-permute-start.8 = (bf16[2,128,512]{2,1,0:T(8,128)(2,1)S(1)}, bf16[2,128,512]{2,1,0:T(8,128)(2,1)S(1)}, u32[]{:S(2)}, u32[]{:S(2)}) collective-permute-start(bf16[2,128,512]{2,1,0:T(8,128)(2,1)S(1)} %fusion.3), channel_id=1, source_target_pairs={{0,3},{1,0},{2,1},{3,2},{4,7},{5,4},{6,5},{7,6},{8,11},{9,8},{10,9... | collective-permute-start | bytes 786440 | tf_op jit(solution)/shard_map/ppermute | solution.py:92
  54.2 1.4 fusion.2
  55.6 1.9 %collective-permute-start.7 = (bf16[2,128,512]{2,1,0:T(8,128)(2,1)S(1)}, bf16[2,128,512]{2,1,0:T(8,128)(2,1)S(1)}, u32[]{:S(2)}, u32[]{:S(2)}) collective-permute-start(bf16[2,128,512]{2,1,0:T(8,128)(2,1)S(1)} %fusion.2), channel_id=1, source_target_pairs={{0,1},{1,2},{2,3},{3,0},{4,5},{5,6},{6,7},{7,4},{8,9},{9,10},{10,1... | collective-permute-start | bytes 786440 | tf_op jit(solution)/shard_map/ppermute | solution.py:92
  57.6 5.0 %collective-permute-done.2 = bf16[2,128,512]{2,1,0:T(8,128)(2,1)S(1)} collective-permute-done((bf16[2,128,512]{2,1,0:T(8,128)(2,1)}, bf16[2,128,512]{2,1,0:T(8,128)(2,1)S(1)}, u32[]{:S(2)}, u32[]{:S(2)}) %collective-permute-start.2) | collective-permute-done | bytes 262176 | tf_op jit(solution)/shard_map/ppermute | solution.py:92
  62.6 31.4 %collective-permute-done.3 = bf16[2,128,512]{2,1,0:T(8,128)(2,1)} collective-permute-done((bf16[2,128,512]{2,1,0:T(8,128)(2,1)}, bf16[2,128,512]{2,1,0:T(8,128)(2,1)}, u32[]{:S(2)}, u32[]{:S(2)}) %collective-permute-start.3) | collective-permute-done | bytes 262176 | tf_op jit(solution)/shard_map/ppermute | solution.py:92
  94.0 0.5 fusion.20
  94.5 7.4 %collective-permute-start.5 = (bf16[2,64,512]{2,1,0:T(8,128)(2,1)S(1)}, bf16[2,64,512]{2,1,0:T(8,128)(2,1)S(1)}, u32[]{:S(2)}, u32[]{:S(2)}) collective-permute-start(bf16[2,64,512]{2,1,0:T(8,128)(2,1)S(1)} %fusion.20), channel_id=1, source_target_pairs={{0,1},{1,2},{2,3},{3,0},{4,5},{5,6},{6,7},{7,4},{8,9},{9,10},{10,1... | collective-permute-start | bytes 393224 | tf_op jit(solution)/shard_map/ppermute | solution.py:92
  101.9 1.4 fusion.21
  103.3 2.4 %collective-permute-start.6 = (bf16[2,64,512]{2,1,0:T(8,128)(2,1)S(1)}, bf16[2,64,512]{2,1,0:T(8,128)(2,1)S(1)}, u32[]{:S(2)}, u32[]{:S(2)}) collective-permute-start(bf16[2,64,512]{2,1,0:T(8,128)(2,1)S(1)} %fusion.21), channel_id=1, source_target_pairs={{0,3},{1,0},{2,1},{3,2},{4,7},{5,4},{6,5},{7,6},{8,11},{9,8},{10,9... | collective-permute-start | bytes 393224 | tf_op jit(solution)/shard_map/ppermute | solution.py:92
  105.7 0.5 fusion.23
  106.2 4.3 %collective-permute-start.10 = (bf16[2,64,512]{2,1,0:T(8,128)(2,1)S(1)}, bf16[2,64,512]{2,1,0:T(8,128)(2,1)S(1)}, u32[]{:S(2)}, u32[]{:S(2)}) collective-permute-start(bf16[2,64,512]{2,1,0:T(8,128)(2,1)S(1)} %fusion.23), channel_id=1, source_target_pairs={{0,3},{1,0},{2,1},{3,2},{4,7},{5,4},{6,5},{7,6},{8,11},{9,8},{10,9... | collective-permute-start | bytes 393224 | tf_op jit(solution)/shard_map/ppermute | solution.py:92
  110.5 0.5 fusion.22
  111.0 5.6 %collective-permute-start.9 = (bf16[2,64,512]{2,1,0:T(8,128)(2,1)S(1)}, bf16[2,64,512]{2,1,0:T(8,128)(2,1)}, u32[]{:S(2)}, u32[]{:S(2)}) collective-permute-start(bf16[2,64,512]{2,1,0:T(8,128)(2,1)S(1)} %fusion.22), channel_id=1, source_target_pairs={{0,1},{1,2},{2,3},{3,0},{4,5},{5,6},{6,7},{7,4},{8,9},{9,10},{10,1... | collective-permute-start | bytes 393224 | tf_op jit(solution)/shard_map/ppermute | solution.py:92
  116.7 0.5 fusion.24
  117.2 1.4 fusion.19
  118.6 0.3 fusion.5
  118.9 1.9 %collective-permute-start.12 = (bf16[512,2,128]{0,2,1:T(8,128)(2,1)S(1)}, bf16[512,2,128]{0,2,1:T(8,128)(2,1)S(1)}, u32[]{:S(2)}, u32[]{:S(2)}) collective-permute-start(bf16[512,2,128]{0,2,1:T(8,128)(2,1)S(1)} %fusion.5), channel_id=1, source_target_pairs={{0,508},{4,0},{8,4},{12,8},{16,12},{20,16},{24,20},{28,24},{32,28}... | collective-permute-start | bytes 786440 | tf_op jit(solution)/shard_map/ppermute | solution.py:108
  120.9 0.5 fusion.26
  121.4 7.6 %collective-permute-done.12 = bf16[512,2,128]{0,2,1:T(8,128)(2,1)S(1)} collective-permute-done((bf16[512,2,128]{0,2,1:T(8,128)(2,1)S(1)}, bf16[512,2,128]{0,2,1:T(8,128)(2,1)S(1)}, u32[]{:S(2)}, u32[]{:S(2)}) %collective-permute-start.12) | collective-permute-done | bytes 262176 | tf_op jit(solution)/shard_map/ppermute | solution.py:108
  129.0 0.7 copy_bitcast_fusion
  129.8 7.3 %all-to-all-start.1 = ((bf16[4,128,2,128]{1,3,2,0:T(8,128)(2,1)}), bf16[4,128,2,128]{1,3,2,0:T(8,128)(2,1)S(1)}, u32[]{:S(2)}, u32[]{:S(2)}) async-start(bf16[4,128,2,128]{1,3,2,0:T(8,128)(2,1)} %copy_bitcast_fusion), calls=%async_computation.1 | async-start | bytes 524288 | tf_op jit(solution)/shard_map/all_to_all | solution.py:79
  137.1 1.5 fusion.25
  138.6 0.3 fusion.4
  138.9 1.9 %collective-permute-start.11 = (bf16[512,2,128]{0,2,1:T(8,128)(2,1)S(1)}, bf16[512,2,128]{0,2,1:T(8,128)(2,1)S(1)}, u32[]{:S(2)}, u32[]{:S(2)}) collective-permute-start(bf16[512,2,128]{0,2,1:T(8,128)(2,1)S(1)} %fusion.4), channel_id=1, source_target_pairs={{0,8},{4,508},{8,16},{12,4},{16,24},{20,12},{24,32},{28,20},{32,40... | collective-permute-start | bytes 786440 | tf_op jit(solution)/shard_map/ppermute | solution.py:110
  140.9 16.1 %collective-permute-done.11 = bf16[512,2,128]{0,2,1:T(8,128)(2,1)S(1)} collective-permute-done((bf16[512,2,128]{0,2,1:T(8,128)(2,1)S(1)}, bf16[512,2,128]{0,2,1:T(8,128)(2,1)S(1)}, u32[]{:S(2)}, u32[]{:S(2)}) %collective-permute-start.11) | collective-permute-done | bytes 262176 | tf_op jit(solution)/shard_map/ppermute | solution.py:110
  156.9 0.8 copy_bitcast_fusion.1
  157.7 10.9 %all-to-all-start = ((bf16[4,128,2,128]{1,3,2,0:T(8,128)(2,1)}), bf16[4,128,2,128]{1,3,2,0:T(8,128)(2,1)S(1)}, u32[]{:S(2)}, u32[]{:S(2)}) async-start(bf16[4,128,2,128]{1,3,2,0:T(8,128)(2,1)} %copy_bitcast_fusion.1), calls=%async_computation | async-start | bytes 524288 | tf_op jit(solution)/shard_map/all_to_all | solution.py:79
  168.9 0.3 fusion.6
  169.2 13.2 %all-to-all-done = bf16[4,128,2,128]{1,3,2,0:T(8,128)(2,1)S(1)} async-done(((bf16[4,128,2,128]{1,3,2,0:T(8,128)(2,1)}), bf16[4,128,2,128]{1,3,2,0:T(8,128)(2,1)S(1)}, u32[]{:S(2)}, u32[]{:S(2)}) %all-to-all-start) | async-done | bytes 262176 | tf_op jit(solution)/shard_map/all_to_all | solution.py:79
  182.8 0.3 fusion.28
  183.2 2.0 %copy.19 = bf16[4,128,2,512]{3,2,1,0:T(2,128)(2,1)} copy(bf16[4,128,2,512]{3,1,2,0:T(8,128)(2,1)S(1)} %pad_maximum_fusion.1) | data formatting | bytes 2097152 | tf_op jit(solution)/shard_map/stack | solution.py:117
  (36 shorter events, 1.2 us)
Async XLA Ops:
  0.0 21.2 %collective-permute-start = (bf16[2,256,2,512]{3,2,1,0:T(2,128)(2,1)}, bf16[2,256,2,512]{3,2,1,0:T(2,128)(2,1)}, u32[]{:S(2)}, u32[]{:S(2)}) collective-permute-start(bf16[2,256,2,512]{3,2,1,0:T(2,128)(2,1)} %param.5), channel_id=1, source_target_pairs={{0,4},{4,8},{8,12},{12,16},{16,20},{20,24},{24,28},{28,32},{32,36}... | collective-permute-start | bytes 3145736 | tf_op jit(solution)/shard_map/ppermute | solution.py:30
  1.9 21.5 %collective-permute-start.1 = (bf16[2,256,2,512]{3,2,1,0:T(2,128)(2,1)}, bf16[2,256,2,512]{3,2,1,0:T(2,128)(2,1)}, u32[]{:S(2)}, u32[]{:S(2)}) collective-permute-start(bf16[2,256,2,512]{3,2,1,0:T(2,128)(2,1)} %param.5), channel_id=1, source_target_pairs={{0,504},{8,0},{16,8},{24,16},{32,24},{40,32},{48,40},{56,48},{64,5... | collective-permute-start | bytes 3145736 | tf_op jit(solution)/shard_map/ppermute | solution.py:31
  14.1 13.5 %copy-start = (bf16[4,2,128,1024]{3,2,1,0:T(8,128)(2,1)}, bf16[4,2,128,1024]{3,2,1,0:T(8,128)(2,1)S(1)}, u32[]{:S(2)}) copy-start(bf16[4,2,128,1024]{3,2,1,0:T(8,128)(2,1)S(1)} %pad_maximum_fusion) | copy-start | bytes 6291460
  23.4 19.0 %collective-permute-start.4 = (bf16[2,256,2,512]{3,2,1,0:T(2,128)(2,1)}, bf16[2,256,2,512]{3,2,1,0:T(2,128)(2,1)}, u32[]{:S(2)}, u32[]{:S(2)}) collective-permute-start(bf16[2,256,2,512]{3,2,1,0:T(2,128)(2,1)} %collective-permute-done), channel_id=1, source_target_pairs={{0,4},{8,12},{16,20},{24,28},{32,36},{40,44},{48,52},{56,60},{64,6... | collective-permute-start | bytes 3145736 | tf_op jit(solution)/shard_map/ppermute | solution.py:95
  27.6 11.5 %copy-start.3 = (bf16[2,64,1024]{2,1,0:T(8,128)(2,1)}, bf16[2,64,1024]{2,1,0:T(8,128)(2,1)S(1)}, u32[]{:S(2)}) copy-start(bf16[2,64,1024]{2,1,0:T(8,128)(2,1)S(1)} %get-tuple-element.19) | copy-start | bytes 786436
  27.6 14.9 %copy-start.5 = (bf16[2,64,1024]{2,1,0:T(8,128)(2,1)}, bf16[2,64,1024]{2,1,0:T(8,128)(2,1)S(1)}, u32[]{:S(2)}) copy-start(bf16[2,64,1024]{2,1,0:T(8,128)(2,1)S(1)} %get-tuple-element.22) | copy-start | bytes 786436
  27.6 14.9 %copy-start.6 = (bf16[2,64,1024]{2,1,0:T(8,128)(2,1)}, bf16[2,64,1024]{2,1,0:T(8,128)(2,1)S(1)}, u32[]{:S(2)}) copy-start(bf16[2,64,1024]{2,1,0:T(8,128)(2,1)S(1)} %get-tuple-element.20) | copy-start | bytes 786436
  27.7 14.9 %copy-start.7 = (bf16[2,64,1024]{2,1,0:T(8,128)(2,1)}, bf16[2,64,1024]{2,1,0:T(8,128)(2,1)S(1)}, u32[]{:S(2)}) copy-start(bf16[2,64,1024]{2,1,0:T(8,128)(2,1)S(1)} %get-tuple-element.21) | copy-start | bytes 786436
  28.9 33.7 %collective-permute-start.2 = (bf16[2,128,512]{2,1,0:T(8,128)(2,1)}, bf16[2,128,512]{2,1,0:T(8,128)(2,1)S(1)}, u32[]{:S(2)}, u32[]{:S(2)}) collective-permute-start(bf16[2,128,512]{2,1,0:T(8,128)(2,1)} %fusion), channel_id=1, source_target_pairs={{0,1},{1,2},{2,3},{3,0},{4,5},{5,6},{6,7},{7,4},{8,9},{9,10},{10,1... | collective-permute-start | bytes 786440 | tf_op jit(solution)/shard_map/ppermute | solution.py:92
  39.1 54.9 %collective-permute-start.3 = (bf16[2,128,512]{2,1,0:T(8,128)(2,1)}, bf16[2,128,512]{2,1,0:T(8,128)(2,1)}, u32[]{:S(2)}, u32[]{:S(2)}) collective-permute-start(bf16[2,128,512]{2,1,0:T(8,128)(2,1)} %fusion.1), channel_id=1, source_target_pairs={{0,3},{1,0},{2,1},{3,2},{4,7},{5,4},{6,5},{7,6},{8,11},{9,8},{10,9... | collective-permute-start | bytes 786440 | tf_op jit(solution)/shard_map/ppermute | solution.py:92
  44.6 9.5 %copy-start.4 = (bf16[2,64,1024]{2,1,0:T(8,128)(2,1)S(1)}, bf16[2,64,1024]{2,1,0:T(8,128)(2,1)}, u32[]{:S(2)}) copy-start(bf16[2,64,1024]{2,1,0:T(8,128)(2,1)} %copy-done.3) | copy-start | bytes 786436
  44.7 49.4 %copy-start.1 = (bf16[4,2,128,1024]{3,2,1,0:T(8,128)(2,1)S(1)}, bf16[4,2,128,1024]{3,2,1,0:T(8,128)(2,1)}, u32[]{:S(2)}) copy-start(bf16[4,2,128,1024]{3,2,1,0:T(8,128)(2,1)} %copy-done) | copy-start | bytes 6291460
  46.3 59.4 %collective-permute-start.8 = (bf16[2,128,512]{2,1,0:T(8,128)(2,1)S(1)}, bf16[2,128,512]{2,1,0:T(8,128)(2,1)S(1)}, u32[]{:S(2)}, u32[]{:S(2)}) collective-permute-start(bf16[2,128,512]{2,1,0:T(8,128)(2,1)S(1)} %fusion.3), channel_id=1, source_target_pairs={{0,3},{1,0},{2,1},{3,2},{4,7},{5,4},{6,5},{7,6},{8,11},{9,8},{10,9... | collective-permute-start | bytes 786440 | tf_op jit(solution)/shard_map/ppermute | solution.py:92
  55.6 54.9 %collective-permute-start.7 = (bf16[2,128,512]{2,1,0:T(8,128)(2,1)S(1)}, bf16[2,128,512]{2,1,0:T(8,128)(2,1)S(1)}, u32[]{:S(2)}, u32[]{:S(2)}) collective-permute-start(bf16[2,128,512]{2,1,0:T(8,128)(2,1)S(1)} %fusion.2), channel_id=1, source_target_pairs={{0,1},{1,2},{2,3},{3,0},{4,5},{5,6},{6,7},{7,4},{8,9},{9,10},{10,1... | collective-permute-start | bytes 786440 | tf_op jit(solution)/shard_map/ppermute | solution.py:92
  94.5 22.1 %collective-permute-start.5 = (bf16[2,64,512]{2,1,0:T(8,128)(2,1)S(1)}, bf16[2,64,512]{2,1,0:T(8,128)(2,1)S(1)}, u32[]{:S(2)}, u32[]{:S(2)}) collective-permute-start(bf16[2,64,512]{2,1,0:T(8,128)(2,1)S(1)} %fusion.20), channel_id=1, source_target_pairs={{0,1},{1,2},{2,3},{3,0},{4,5},{5,6},{6,7},{7,4},{8,9},{9,10},{10,1... | collective-permute-start | bytes 393224 | tf_op jit(solution)/shard_map/ppermute | solution.py:92
  103.3 13.3 %collective-permute-start.6 = (bf16[2,64,512]{2,1,0:T(8,128)(2,1)S(1)}, bf16[2,64,512]{2,1,0:T(8,128)(2,1)S(1)}, u32[]{:S(2)}, u32[]{:S(2)}) collective-permute-start(bf16[2,64,512]{2,1,0:T(8,128)(2,1)S(1)} %fusion.21), channel_id=1, source_target_pairs={{0,3},{1,0},{2,1},{3,2},{4,7},{5,4},{6,5},{7,6},{8,11},{9,8},{10,9... | collective-permute-start | bytes 393224 | tf_op jit(solution)/shard_map/ppermute | solution.py:92
  106.2 14.7 %collective-permute-start.10 = (bf16[2,64,512]{2,1,0:T(8,128)(2,1)S(1)}, bf16[2,64,512]{2,1,0:T(8,128)(2,1)S(1)}, u32[]{:S(2)}, u32[]{:S(2)}) collective-permute-start(bf16[2,64,512]{2,1,0:T(8,128)(2,1)S(1)} %fusion.23), channel_id=1, source_target_pairs={{0,3},{1,0},{2,1},{3,2},{4,7},{5,4},{6,5},{7,6},{8,11},{9,8},{10,9... | collective-permute-start | bytes 393224 | tf_op jit(solution)/shard_map/ppermute | solution.py:92
  111.0 7.6 %copy-start.2 = (bf16[512,512,1]{1,0,2:T(8,128)(2,1)S(1)}, bf16[512,512,1]{1,0,2:T(8,128)(2,1)}, u32[]{:S(2)}) copy-start(bf16[512,512,1]{1,0,2:T(8,128)(2,1)} %constant.54) | copy-start | bytes 1572868
  111.0 7.6 %copy-start.8 = (bf16[2]{0:T(256)(128)(2,1)S(1)}, bf16[2]{0:T(256)(128)(2,1)}, u32[]{:S(2)}) copy-start(bf16[2]{0:T(256)(128)(2,1)} %constant.52.clone) | copy-start | bytes 16
  111.0 26.0 %collective-permute-start.9 = (bf16[2,64,512]{2,1,0:T(8,128)(2,1)S(1)}, bf16[2,64,512]{2,1,0:T(8,128)(2,1)}, u32[]{:S(2)}, u32[]{:S(2)}) collective-permute-start(bf16[2,64,512]{2,1,0:T(8,128)(2,1)S(1)} %fusion.22), channel_id=1, source_target_pairs={{0,1},{1,2},{2,3},{3,0},{4,5},{5,6},{6,7},{7,4},{8,9},{9,10},{10,1... | collective-permute-start | bytes 393224 | tf_op jit(solution)/shard_map/ppermute | solution.py:92
  118.9 10.1 %collective-permute-start.12 = (bf16[512,2,128]{0,2,1:T(8,128)(2,1)S(1)}, bf16[512,2,128]{0,2,1:T(8,128)(2,1)S(1)}, u32[]{:S(2)}, u32[]{:S(2)}) collective-permute-start(bf16[512,2,128]{0,2,1:T(8,128)(2,1)S(1)} %fusion.5), channel_id=1, source_target_pairs={{0,508},{4,0},{8,4},{12,8},{16,12},{20,16},{24,20},{28,24},{32,28}... | collective-permute-start | bytes 786440 | tf_op jit(solution)/shard_map/ppermute | solution.py:108
  129.8 27.9 %all-to-all-start.1 = ((bf16[4,128,2,128]{1,3,2,0:T(8,128)(2,1)}), bf16[4,128,2,128]{1,3,2,0:T(8,128)(2,1)S(1)}, u32[]{:S(2)}, u32[]{:S(2)}) async-start(bf16[4,128,2,128]{1,3,2,0:T(8,128)(2,1)} %copy_bitcast_fusion), calls=%async_computation.1 | async-start | bytes 524288 | tf_op jit(solution)/shard_map/all_to_all | solution.py:79
  138.9 18.0 %collective-permute-start.11 = (bf16[512,2,128]{0,2,1:T(8,128)(2,1)S(1)}, bf16[512,2,128]{0,2,1:T(8,128)(2,1)S(1)}, u32[]{:S(2)}, u32[]{:S(2)}) collective-permute-start(bf16[512,2,128]{0,2,1:T(8,128)(2,1)S(1)} %fusion.4), channel_id=1, source_target_pairs={{0,8},{4,508},{8,16},{12,4},{16,24},{20,12},{24,32},{28,20},{32,40... | collective-permute-start | bytes 786440 | tf_op jit(solution)/shard_map/ppermute | solution.py:110
  157.7 24.8 %all-to-all-start = ((bf16[4,128,2,128]{1,3,2,0:T(8,128)(2,1)}), bf16[4,128,2,128]{1,3,2,0:T(8,128)(2,1)S(1)}, u32[]{:S(2)}, u32[]{:S(2)}) async-start(bf16[4,128,2,128]{1,3,2,0:T(8,128)(2,1)} %copy_bitcast_fusion.1), calls=%async_computation | async-start | bytes 524288 | tf_op jit(solution)/shard_map/all_to_all | solution.py:79

commit v3 on v2

--- a/solution.py
+++ b/solution.py
@@ -56,14 +56,15 @@
     down = [(o, (o - 1) % owners) for o in range(owners)]
 
     def second_products(right, from_down, from_up):
-        to_up = product(left[1, :, :half], right) + from_down[:, :half].astype(jnp.float32)
-        to_down = product(left[3, :, half:], right) + from_up[:, half:].astype(jnp.float32)
+        low = jnp.pad(from_down, ((0, 0), (0, half), (0, 0))).astype(jnp.float32)
+        high = jnp.pad(from_up, ((0, 0), (half, 0), (0, 0))).astype(jnp.float32)
+        to_up = product(left[1], right) + low
+        to_down = product(left[3], right) + high
         return to_up.astype(jnp.bfloat16), to_down.astype(jnp.bfloat16)
 
-    def third(right, from_down, from_up, late_down, late_up):
-        low = product(left[0, :, :half], right) + from_up[:, :half].astype(jnp.float32) + late_down.astype(jnp.float32)
-        high = product(left[0, :, half:], right) + from_down[:, half:].astype(jnp.float32) + late_up.astype(jnp.float32)
-        return jnp.concatenate([low, high], axis=1).astype(jnp.bfloat16)
+    def third(right, from_down, from_up):
+        out = product(left[0], right) + from_down.astype(jnp.float32) + from_up.astype(jnp.float32)
+        return out.astype(jnp.bfloat16)
 
     order = natural_order(owners, block_count)
     pick = jnp.asarray(np.eye(row_total, dtype=np.float32)[order], jnp.bfloat16)
@@ -84,9 +85,10 @@
         return out.astype(jnp.bfloat16)
 
     def first_products(right):
-        to_up = jnp.concatenate([left[2, :, :half], left[1, :, half:]], axis=1)
-        to_down = jnp.concatenate([left[3, :, :half], left[2, :, half:]], axis=1)
-        return (product(to_up, right).astype(jnp.bfloat16), product(to_down, right).astype(jnp.bfloat16))
+        return (
+            product(left[2, :, :half], right).astype(jnp.bfloat16),
+            product(left[2, :, half:], right).astype(jnp.bfloat16),
+        )
 
     def sends(pieces):
         return lax.ppermute(pieces[0], "own", up), lax.ppermute(pieces[1], "own", down)
@@ -104,9 +106,9 @@
     pieces_2 = second_products(right_2, *got_2)
     late_2 = sends(pieces_2)
     late_1, _ = lax.optimization_barrier((late_1, pieces_2))
-    block_1 = third(right_1, *got_1, *late_1)
+    block_1 = third(right_1, *late_1)
     back_1 = lax.ppermute(turned(block_1), "kp", [(i, (i - 1) % groups) for i in range(groups)])
-    block_2 = third(right_2, *got_2, *late_2)
+    block_2 = third(right_2, *late_2)
     back_2 = lax.ppermute(
         turned(block_2), "kp", [(i, (i - 2 if i % 2 else i + 2) % groups) for i in range(groups)]
     )

time: 186 us -> 177 us (0.952)
  waiting for transfers between devices: 82.8 us -> 74.3 us
  matrix products: 13.5 us -> 11.2 us
    ppermute x4, waiting for transfers between devices: 31.5 us -> 4.01 us  [sends(): lax.ppermute(pieces[1], 'own', down)]
    ppermute x4, waiting for transfers between devices: 5.05 us -> 31.1 us  [sends(): lax.ppermute(pieces[0], 'own', up)]
    ppermute x1, waiting for transfers between devices: 7.65 us -> 0.01 us  [body(): lax.ppermute(turned(block_1), 'kp', [(i, (i - 1) % groups) for i in range...]
    all_to_all x2, starting transfers between devices: 18.2 us -> 15.6 us  [gathered(): lax.all_to_all(pieces.reshape(owners, own_rows, 2, own_rows), 'own', spli...]
    dot_general x12 -> x10, matrix products: 12.2 us -> 9.88 us  [product(): lax.dot_general(rows, right, (((2,), (1,)), ((), ())), preferred_element_...]
  transfers between devices with their start and end apart: 15 -> 15, of which waited for: 7 -> 8; matrix products, arithmetic and copies ran while one was open for 12% -> 12% of each run, Pallas kernels for 0% -> 0%
where the time goes in v3:
time: 177 us; the launch traced here: 176 us
  starting transfers between devices  76.1 us (43%)
  waiting for transfers between devices  74.3 us (42%)
  matrix products  11.2 us (6%)
  local copies, waits for them, and re-layouts  8.12 us (5%)
  other arithmetic  5.5 us (3%)
    ppermute x4, waiting for transfers between devices, sends(): lax.ppermute(pieces[0], 'own', up)  31.1 us
    ppermute x4, starting transfers between devices, sends(): lax.ppermute(pieces[0], 'own', up)  22.2 us
    ppermute x4, starting transfers between devices, sends(): lax.ppermute(pieces[1], 'own', down)  19.5 us
    ppermute x1, waiting for transfers between devices, body(): lax.ppermute(turned(block_2), 'kp', [(i, (i - 2 if i % 2 else i + 2) % gr...  17 us
    all_to_all x2, starting transfers between devices, gathered(): lax.all_to_all(pieces.reshape(owners, own_rows, 2, own_rows), 'own', spli...  15.6 us
    all_to_all x2, waiting for transfers between devices, gathered(): lax.all_to_all(pieces.reshape(owners, own_rows, 2, own_rows), 'own', spli...  14.1 us
    dot_general x10, matrix products, product(): lax.dot_general(rows, right, (((2,), (1,)), ((), ())), preferred_element_...  9.88 us
    ppermute x1, starting transfers between devices, body(): lax.ppermute(pair_density, 'kp', [(i, (i - 2) % groups) for i in range(0,...  8.91 us
  transfers between devices with their start and end apart: 15, of which 8 were waited for; matrix products, arithmetic and copies ran while one was open for 12% of the time, Pallas kernels for 0%

profile of v3, /device:TPU:24, one launch (start us, length us, event | category | flops | bytes accessed | tf_op | source)
XLA Modules:
  0.0 175.5 jit_solution(5956085939478227260)
XLA Ops:
  0.0 1.9 %collective-permute-start = (bf16[2,256,2,512]{3,2,1,0:T(2,128)(2,1)}, bf16[2,256,2,512]{3,2,1,0:T(2,128)(2,1)}, u32[]{:S(2)}, u32[]{:S(2)}) collective-permute-start(bf16[2,256,2,512]{3,2,1,0:T(2,128)(2,1)} %param.5), channel_id=1, source_target_pairs={{0,4},{4,8},{8,12},{12,16},{16,20},{20,24},{24,28},{28,32},{32,36}... | collective-permute-start | bytes 3145736 | tf_op jit(solution)/shard_map/ppermute | solution.py:30
  1.9 8.9 %collective-permute-start.1 = (bf16[2,256,2,512]{3,2,1,0:T(2,128)(2,1)}, bf16[2,256,2,512]{3,2,1,0:T(2,128)(2,1)S(1)}, u32[]{:S(2)}, u32[]{:S(2)}) collective-permute-start(bf16[2,256,2,512]{3,2,1,0:T(2,128)(2,1)} %param.5), channel_id=1, source_target_pairs={{0,504},{8,0},{16,8},{24,16},{32,24},{40,32},{48,40},{56,48},{64,5... | collective-permute-start | bytes 3145736 | tf_op jit(solution)/shard_map/ppermute | solution.py:31
  10.8 2.0 %multiply_convert_fusion = bf16[2,256,2,512]{3,2,1,0:T(2,128)(2,1)S(1)} fusion(bf16[2,256,2,512]{3,2,1,0:T(2,128)(2,1)} %param.5, f32[512]{0:T(512)} %param.6), kind=kLoop, calls=%fused_computation.3 | loop fusion | flops 1572864 | bytes 2099200 | tf_op jit(solution)/shard_map/convert_element_type | solution.py:36
  12.9 0.2 copy.12
  13.1 0.4 fusion.21
  13.7 0.3 maximum_bitcast_fusion
  13.9 1.5 pad_maximum_fusion
  15.5 5.8 %collective-permute-done = bf16[2,256,2,512]{3,2,1,0:T(2,128)(2,1)} collective-permute-done((bf16[2,256,2,512]{3,2,1,0:T(2,128)(2,1)}, bf16[2,256,2,512]{3,2,1,0:T(2,128)(2,1)}, u32[]{:S(2)}, u32[]{:S(2)}) %collective-permute-start) | collective-permute-done | bytes 1048608 | tf_op jit(solution)/shard_map/ppermute | solution.py:30
  21.2 2.2 %collective-permute-done.1 = bf16[2,256,2,512]{3,2,1,0:T(2,128)(2,1)S(1)} collective-permute-done((bf16[2,256,2,512]{3,2,1,0:T(2,128)(2,1)}, bf16[2,256,2,512]{3,2,1,0:T(2,128)(2,1)S(1)}, u32[]{:S(2)}, u32[]{:S(2)}) %collective-permute-start.1) | collective-permute-done | bytes 1048608 | tf_op jit(solution)/shard_map/ppermute | solution.py:31
  23.4 2.3 %collective-permute-start.4 = (bf16[2,256,2,512]{3,2,1,0:T(2,128)(2,1)}, bf16[2,256,2,512]{3,2,1,0:T(2,128)(2,1)}, u32[]{:S(2)}, u32[]{:S(2)}) collective-permute-start(bf16[2,256,2,512]{3,2,1,0:T(2,128)(2,1)} %collective-permute-done), channel_id=1, source_target_pairs={{0,4},{8,12},{16,20},{24,28},{32,36},{40,44},{48,52},{56,60},{64,6... | collective-permute-start | bytes 3145736 | tf_op jit(solution)/shard_map/ppermute | solution.py:97
  25.7 1.9 %reshape.37 = bf16[512,1024,1]{1,0,2:T(8,128)(2,1)S(1)} reshape(bf16[2,256,2,512]{3,2,1,0:T(2,128)(2,1)} %collective-permute-done) | data formatting | bytes 2097152 | tf_op jit(solution)/shard_map/reshape | solution.py:34
  27.6 1.4 fusion.17
  29.0 9.1 %collective-permute-start.2 = (bf16[2,64,512]{2,1,0:T(8,128)(2,1)S(1)}, bf16[2,64,512]{2,1,0:T(8,128)(2,1)S(1)}, u32[]{:S(2)}, u32[]{:S(2)}) collective-permute-start(bf16[2,64,512]{2,1,0:T(8,128)(2,1)S(1)} %fusion.17), channel_id=1, source_target_pairs={{0,1},{1,2},{2,3},{3,0},{4,5},{5,6},{6,7},{7,4},{8,9},{9,10},{10,1... | collective-permute-start | bytes 393224 | tf_op jit(solution)/shard_map/ppermute | solution.py:94
  38.1 1.4 fusion.18
  39.6 3.3 %collective-permute-start.3 = (bf16[2,64,512]{2,1,0:T(8,128)(2,1)S(1)}, bf16[2,64,512]{2,1,0:T(8,128)(2,1)S(1)}, u32[]{:S(2)}, u32[]{:S(2)}) collective-permute-start(bf16[2,64,512]{2,1,0:T(8,128)(2,1)S(1)} %fusion.18), channel_id=1, source_target_pairs={{0,3},{1,0},{2,1},{3,2},{4,7},{5,4},{6,5},{7,6},{8,11},{9,8},{10,9... | collective-permute-start | bytes 393224 | tf_op jit(solution)/shard_map/ppermute | solution.py:94
  43.0 1.1 broadcast_select_fusion
  44.1 1.8 %reshape.38 = bf16[512,1024,1]{1,0,2:T(8,128)(2,1)S(1)} reshape(bf16[2,256,2,512]{3,2,1,0:T(2,128)(2,1)} %bitcast.100) | data formatting | bytes 2097152 | tf_op jit(solution)/shard_map/reshape | solution.py:34
  45.9 1.6 fusion.20
  47.5 7.8 %collective-permute-start.8 = (bf16[2,64,512]{2,1,0:T(8,128)(2,1)S(1)}, bf16[2,64,512]{2,1,0:T(8,128)(2,1)S(1)}, u32[]{:S(2)}, u32[]{:S(2)}) collective-permute-start(bf16[2,64,512]{2,1,0:T(8,128)(2,1)S(1)} %fusion.20), channel_id=1, source_target_pairs={{0,3},{1,0},{2,1},{3,2},{4,7},{5,4},{6,5},{7,6},{8,11},{9,8},{10,9... | collective-permute-start | bytes 393224 | tf_op jit(solution)/shard_map/ppermute | solution.py:94
  55.3 1.4 fusion.19
  56.7 1.9 %collective-permute-start.7 = (bf16[2,64,512]{2,1,0:T(8,128)(2,1)S(1)}, bf16[2,64,512]{2,1,0:T(8,128)(2,1)S(1)}, u32[]{:S(2)}, u32[]{:S(2)}) collective-permute-start(bf16[2,64,512]{2,1,0:T(8,128)(2,1)S(1)} %fusion.19), channel_id=1, source_target_pairs={{0,1},{1,2},{2,3},{3,0},{4,5},{5,6},{6,7},{7,4},{8,9},{9,10},{10,1... | collective-permute-start | bytes 393224 | tf_op jit(solution)/shard_map/ppermute | solution.py:94
  58.7 4.0 %collective-permute-done.3 = bf16[2,64,512]{2,1,0:T(8,128)(2,1)S(1)} collective-permute-done((bf16[2,64,512]{2,1,0:T(8,128)(2,1)S(1)}, bf16[2,64,512]{2,1,0:T(8,128)(2,1)S(1)}, u32[]{:S(2)}, u32[]{:S(2)}) %collective-permute-start.3) | collective-permute-done | bytes 131104 | tf_op jit(solution)/shard_map/ppermute | solution.py:94
  62.7 0.5 fusion.13
  63.2 6.8 %collective-permute-start.5 = (bf16[2,128,512]{2,1,0:T(8,128)(2,1)S(1)}, bf16[2,128,512]{2,1,0:T(8,128)(2,1)S(1)}, u32[]{:S(2)}, u32[]{:S(2)}) collective-permute-start(bf16[2,128,512]{2,1,0:T(8,128)(2,1)S(1)} %fusion.13), channel_id=1, source_target_pairs={{0,1},{1,2},{2,3},{3,0},{4,5},{5,6},{6,7},{7,4},{8,9},{9,10},{10,1... | collective-permute-start | bytes 786440 | tf_op jit(solution)/shard_map/ppermute | solution.py:94
  70.0 0.5 fusion.12
  70.5 2.9 %collective-permute-start.6 = (bf16[2,128,512]{2,1,0:T(8,128)(2,1)S(1)}, bf16[2,128,512]{2,1,0:T(8,128)(2,1)S(1)}, u32[]{:S(2)}, u32[]{:S(2)}) collective-permute-start(bf16[2,128,512]{2,1,0:T(8,128)(2,1)S(1)} %fusion.12), channel_id=1, source_target_pairs={{0,3},{1,0},{2,1},{3,2},{4,7},{5,4},{6,5},{7,6},{8,11},{9,8},{10,9... | collective-permute-start | bytes 786440 | tf_op jit(solution)/shard_map/ppermute | solution.py:94
  73.4 0.5 fusion.10
  74.0 6.5 %collective-permute-done.7 = bf16[2,64,512]{2,1,0:T(8,128)(2,1)S(1)} collective-permute-done((bf16[2,64,512]{2,1,0:T(8,128)(2,1)S(1)}, bf16[2,64,512]{2,1,0:T(8,128)(2,1)S(1)}, u32[]{:S(2)}, u32[]{:S(2)}) %collective-permute-start.7) | collective-permute-done | bytes 131104 | tf_op jit(solution)/shard_map/ppermute | solution.py:94
  80.5 0.5 fusion.11
  81.0 11.8 %collective-permute-done.5 = bf16[2,128,512]{2,1,0:T(8,128)(2,1)S(1)} collective-permute-done((bf16[2,128,512]{2,1,0:T(8,128)(2,1)S(1)}, bf16[2,128,512]{2,1,0:T(8,128)(2,1)S(1)}, u32[]{:S(2)}, u32[]{:S(2)}) %collective-permute-start.5) | collective-permute-done | bytes 262176 | tf_op jit(solution)/shard_map/ppermute | solution.py:94
  92.8 0.5 fusion.8
  93.3 0.3 fusion.15
  93.7 3.8 %collective-permute-start.12 = (bf16[512,2,128]{0,2,1:T(8,128)(2,1)S(1)}, bf16[512,2,128]{0,2,1:T(8,128)(2,1)S(1)}, u32[]{:S(2)}, u32[]{:S(2)}) collective-permute-start(bf16[512,2,128]{0,2,1:T(8,128)(2,1)S(1)} %fusion.15), channel_id=1, source_target_pairs={{0,508},{4,0},{8,4},{12,8},{16,12},{20,16},{24,20},{28,24},{32,28}... | collective-permute-start | bytes 786440 | tf_op jit(solution)/shard_map/ppermute | solution.py:110
  97.5 5.4 %collective-permute-start.10 = (bf16[2,128,512]{2,1,0:T(8,128)(2,1)S(1)}, bf16[2,128,512]{2,1,0:T(8,128)(2,1)S(1)}, u32[]{:S(2)}, u32[]{:S(2)}) collective-permute-start(bf16[2,128,512]{2,1,0:T(8,128)(2,1)S(1)} %fusion.10), channel_id=1, source_target_pairs={{0,3},{1,0},{2,1},{3,2},{4,7},{5,4},{6,5},{7,6},{8,11},{9,8},{10,9... | collective-permute-start | bytes 786440 | tf_op jit(solution)/shard_map/ppermute | solution.py:94
  102.9 4.3 %collective-permute-start.9 = (bf16[2,128,512]{2,1,0:T(8,128)(2,1)S(1)}, bf16[2,128,512]{2,1,0:T(8,128)(2,1)S(1)}, u32[]{:S(2)}, u32[]{:S(2)}) collective-permute-start(bf16[2,128,512]{2,1,0:T(8,128)(2,1)S(1)} %fusion.11), channel_id=1, source_target_pairs={{0,1},{1,2},{2,3},{3,0},{4,5},{5,6},{6,7},{7,4},{8,9},{9,10},{10,1... | collective-permute-start | bytes 786440 | tf_op jit(solution)/shard_map/ppermute | solution.py:94
  107.2 0.7 copy_bitcast_fusion
  108.0 6.9 %all-to-all-start.1 = ((bf16[4,128,2,128]{1,3,2,0:T(8,128)(2,1)}), bf16[4,128,2,128]{1,3,2,0:T(8,128)(2,1)S(1)}, u32[]{:S(2)}, u32[]{:S(2)}) async-start(bf16[4,128,2,128]{1,3,2,0:T(8,128)(2,1)} %copy_bitcast_fusion), calls=%async_computation.1 | async-start | bytes 524288 | tf_op jit(solution)/shard_map/all_to_all | solution.py:80
  114.9 12.8 %collective-permute-done.9 = bf16[2,128,512]{2,1,0:T(8,128)(2,1)S(1)} collective-permute-done((bf16[2,128,512]{2,1,0:T(8,128)(2,1)S(1)}, bf16[2,128,512]{2,1,0:T(8,128)(2,1)S(1)}, u32[]{:S(2)}, u32[]{:S(2)}) %collective-permute-start.9) | collective-permute-done | bytes 262176 | tf_op jit(solution)/shard_map/ppermute | solution.py:94
  127.7 1.6 fusion.9
  129.2 0.3 fusion.14
  129.6 1.9 %collective-permute-start.11 = (bf16[512,2,128]{0,2,1:T(8,128)(2,1)S(1)}, bf16[512,2,128]{0,2,1:T(8,128)(2,1)S(1)}, u32[]{:S(2)}, u32[]{:S(2)}) collective-permute-start(bf16[512,2,128]{0,2,1:T(8,128)(2,1)S(1)} %fusion.14), channel_id=1, source_target_pairs={{0,8},{4,508},{8,16},{12,4},{16,24},{20,12},{24,32},{28,20},{32,40... | collective-permute-start | bytes 786440 | tf_op jit(solution)/shard_map/ppermute | solution.py:112
  131.5 17.0 %collective-permute-done.11 = bf16[512,2,128]{0,2,1:T(8,128)(2,1)S(1)} collective-permute-done((bf16[512,2,128]{0,2,1:T(8,128)(2,1)S(1)}, bf16[512,2,128]{0,2,1:T(8,128)(2,1)S(1)}, u32[]{:S(2)}, u32[]{:S(2)}) %collective-permute-start.11) | collective-permute-done | bytes 262176 | tf_op jit(solution)/shard_map/ppermute | solution.py:112
  148.5 0.8 copy_bitcast_fusion.1
  149.3 8.7 %all-to-all-start = ((bf16[4,128,2,128]{1,3,2,0:T(8,128)(2,1)}), bf16[4,128,2,128]{1,3,2,0:T(8,128)(2,1)S(1)}, u32[]{:S(2)}, u32[]{:S(2)}) async-start(bf16[4,128,2,128]{1,3,2,0:T(8,128)(2,1)} %copy_bitcast_fusion.1), calls=%async_computation | async-start | bytes 524288 | tf_op jit(solution)/shard_map/all_to_all | solution.py:80
  158.3 0.3 fusion.16
  158.6 14.1 %all-to-all-done = bf16[4,128,2,128]{1,3,2,0:T(8,128)(2,1)S(1)} async-done(((bf16[4,128,2,128]{1,3,2,0:T(8,128)(2,1)}), bf16[4,128,2,128]{1,3,2,0:T(8,128)(2,1)S(1)}, u32[]{:S(2)}, u32[]{:S(2)}) %all-to-all-start) | async-done | bytes 262176 | tf_op jit(solution)/shard_map/all_to_all | solution.py:80
  173.0 0.3 fusion.34
  173.5 2.0 %copy.19 = bf16[4,128,2,512]{3,2,1,0:T(2,128)(2,1)} copy(bf16[4,128,2,512]{3,1,2,0:T(8,128)(2,1)S(1)} %pad_maximum_fusion.1) | data formatting | bytes 2097152 | tf_op jit(solution)/shard_map/stack | solution.py:119
  (24 shorter events, 0.9 us)
Async XLA Ops:
  0.0 21.2 %collective-permute-start = (bf16[2,256,2,512]{3,2,1,0:T(2,128)(2,1)}, bf16[2,256,2,512]{3,2,1,0:T(2,128)(2,1)}, u32[]{:S(2)}, u32[]{:S(2)}) collective-permute-start(bf16[2,256,2,512]{3,2,1,0:T(2,128)(2,1)} %param.5), channel_id=1, source_target_pairs={{0,4},{4,8},{8,12},{12,16},{16,20},{20,24},{24,28},{28,32},{32,36}... | collective-permute-start | bytes 3145736 | tf_op jit(solution)/shard_map/ppermute | solution.py:30
  1.9 21.5 %collective-permute-start.1 = (bf16[2,256,2,512]{3,2,1,0:T(2,128)(2,1)}, bf16[2,256,2,512]{3,2,1,0:T(2,128)(2,1)S(1)}, u32[]{:S(2)}, u32[]{:S(2)}) collective-permute-start(bf16[2,256,2,512]{3,2,1,0:T(2,128)(2,1)} %param.5), channel_id=1, source_target_pairs={{0,504},{8,0},{16,8},{24,16},{32,24},{40,32},{48,40},{56,48},{64,5... | collective-permute-start | bytes 3145736 | tf_op jit(solution)/shard_map/ppermute | solution.py:31
  23.4 2.3 %copy-start.2 = (bf16[2,256,2,512]{3,2,1,0:T(2,128)(2,1)}, bf16[2,256,2,512]{3,2,1,0:T(2,128)(2,1)S(1)}, u32[]{:S(2)}) copy-start(bf16[2,256,2,512]{3,2,1,0:T(2,128)(2,1)S(1)} %collective-permute-done.1) | copy-start | bytes 3145732
  23.4 19.5 %collective-permute-start.4 = (bf16[2,256,2,512]{3,2,1,0:T(2,128)(2,1)}, bf16[2,256,2,512]{3,2,1,0:T(2,128)(2,1)}, u32[]{:S(2)}, u32[]{:S(2)}) collective-permute-start(bf16[2,256,2,512]{3,2,1,0:T(2,128)(2,1)} %collective-permute-done), channel_id=1, source_target_pairs={{0,4},{8,12},{16,20},{24,28},{32,36},{40,44},{48,52},{56,60},{64,6... | collective-permute-start | bytes 3145736 | tf_op jit(solution)/shard_map/ppermute | solution.py:97
  25.7 17.3 %copy-start.3 = (bf16[2,256,2,512]{3,2,1,0:T(2,128)(2,1)S(1)}, bf16[2,256,2,512]{3,2,1,0:T(2,128)(2,1)}, u32[]{:S(2)}) copy-start(bf16[2,256,2,512]{3,2,1,0:T(2,128)(2,1)} %copy-done.2) | copy-start | bytes 3145732
  29.0 29.6 %collective-permute-start.2 = (bf16[2,64,512]{2,1,0:T(8,128)(2,1)S(1)}, bf16[2,64,512]{2,1,0:T(8,128)(2,1)S(1)}, u32[]{:S(2)}, u32[]{:S(2)}) collective-permute-start(bf16[2,64,512]{2,1,0:T(8,128)(2,1)S(1)} %fusion.17), channel_id=1, source_target_pairs={{0,1},{1,2},{2,3},{3,0},{4,5},{5,6},{6,7},{7,4},{8,9},{9,10},{10,1... | collective-permute-start | bytes 393224 | tf_op jit(solution)/shard_map/ppermute | solution.py:94
  39.6 23.1 %collective-permute-start.3 = (bf16[2,64,512]{2,1,0:T(8,128)(2,1)S(1)}, bf16[2,64,512]{2,1,0:T(8,128)(2,1)S(1)}, u32[]{:S(2)}, u32[]{:S(2)}) collective-permute-start(bf16[2,64,512]{2,1,0:T(8,128)(2,1)S(1)} %fusion.18), channel_id=1, source_target_pairs={{0,3},{1,0},{2,1},{3,2},{4,7},{5,4},{6,5},{7,6},{8,11},{9,8},{10,9... | collective-permute-start | bytes 393224 | tf_op jit(solution)/shard_map/ppermute | solution.py:94
  45.9 16.8 %copy-start.1 = (bf16[4,2,128,1024]{3,2,1,0:T(8,128)(2,1)S(1)}, bf16[4,2,128,1024]{3,2,1,0:T(8,128)(2,1)}, u32[]{:S(2)}) copy-start(bf16[4,2,128,1024]{3,2,1,0:T(8,128)(2,1)} %pad_maximum_fusion) | copy-start | bytes 6291460
  47.5 26.0 %collective-permute-start.8 = (bf16[2,64,512]{2,1,0:T(8,128)(2,1)S(1)}, bf16[2,64,512]{2,1,0:T(8,128)(2,1)S(1)}, u32[]{:S(2)}, u32[]{:S(2)}) collective-permute-start(bf16[2,64,512]{2,1,0:T(8,128)(2,1)S(1)} %fusion.20), channel_id=1, source_target_pairs={{0,3},{1,0},{2,1},{3,2},{4,7},{5,4},{6,5},{7,6},{8,11},{9,8},{10,9... | collective-permute-start | bytes 393224 | tf_op jit(solution)/shard_map/ppermute | solution.py:94
  56.7 23.8 %collective-permute-start.7 = (bf16[2,64,512]{2,1,0:T(8,128)(2,1)S(1)}, bf16[2,64,512]{2,1,0:T(8,128)(2,1)S(1)}, u32[]{:S(2)}, u32[]{:S(2)}) collective-permute-start(bf16[2,64,512]{2,1,0:T(8,128)(2,1)S(1)} %fusion.19), channel_id=1, source_target_pairs={{0,1},{1,2},{2,3},{3,0},{4,5},{5,6},{6,7},{7,4},{8,9},{9,10},{10,1... | collective-permute-start | bytes 393224 | tf_op jit(solution)/shard_map/ppermute | solution.py:94
  63.2 29.6 %collective-permute-start.5 = (bf16[2,128,512]{2,1,0:T(8,128)(2,1)S(1)}, bf16[2,128,512]{2,1,0:T(8,128)(2,1)S(1)}, u32[]{:S(2)}, u32[]{:S(2)}) collective-permute-start(bf16[2,128,512]{2,1,0:T(8,128)(2,1)S(1)} %fusion.13), channel_id=1, source_target_pairs={{0,1},{1,2},{2,3},{3,0},{4,5},{5,6},{6,7},{7,4},{8,9},{9,10},{10,1... | collective-permute-start | bytes 786440 | tf_op jit(solution)/shard_map/ppermute | solution.py:94
  70.5 22.3 %collective-permute-start.6 = (bf16[2,128,512]{2,1,0:T(8,128)(2,1)S(1)}, bf16[2,128,512]{2,1,0:T(8,128)(2,1)S(1)}, u32[]{:S(2)}, u32[]{:S(2)}) collective-permute-start(bf16[2,128,512]{2,1,0:T(8,128)(2,1)S(1)} %fusion.12), channel_id=1, source_target_pairs={{0,3},{1,0},{2,1},{3,2},{4,7},{5,4},{6,5},{7,6},{8,11},{9,8},{10,9... | collective-permute-start | bytes 786440 | tf_op jit(solution)/shard_map/ppermute | solution.py:94
  73.9 19.4 %copy-start = (bf16[512,512,1]{1,0,2:T(8,128)(2,1)S(1)}, bf16[512,512,1]{1,0,2:T(8,128)(2,1)}, u32[]{:S(2)}) copy-start(bf16[512,512,1]{1,0,2:T(8,128)(2,1)} %constant.65) | copy-start | bytes 1572868
  73.9 19.4 %copy-start.4 = (bf16[2]{0:T(256)(128)(2,1)S(1)}, bf16[2]{0:T(256)(128)(2,1)}, u32[]{:S(2)}) copy-start(bf16[2]{0:T(256)(128)(2,1)} %constant.55.clone) | copy-start | bytes 16
  93.7 13.5 %collective-permute-start.12 = (bf16[512,2,128]{0,2,1:T(8,128)(2,1)S(1)}, bf16[512,2,128]{0,2,1:T(8,128)(2,1)S(1)}, u32[]{:S(2)}, u32[]{:S(2)}) collective-permute-start(bf16[512,2,128]{0,2,1:T(8,128)(2,1)S(1)} %fusion.15), channel_id=1, source_target_pairs={{0,508},{4,0},{8,4},{12,8},{16,12},{20,16},{24,20},{28,24},{32,28}... | collective-permute-start | bytes 786440 | tf_op jit(solution)/shard_map/ppermute | solution.py:110
  97.5 17.5 %collective-permute-start.10 = (bf16[2,128,512]{2,1,0:T(8,128)(2,1)S(1)}, bf16[2,128,512]{2,1,0:T(8,128)(2,1)S(1)}, u32[]{:S(2)}, u32[]{:S(2)}) collective-permute-start(bf16[2,128,512]{2,1,0:T(8,128)(2,1)S(1)} %fusion.10), channel_id=1, source_target_pairs={{0,3},{1,0},{2,1},{3,2},{4,7},{5,4},{6,5},{7,6},{8,11},{9,8},{10,9... | collective-permute-start | bytes 786440 | tf_op jit(solution)/shard_map/ppermute | solution.py:94
  102.9 24.8 %collective-permute-start.9 = (bf16[2,128,512]{2,1,0:T(8,128)(2,1)S(1)}, bf16[2,128,512]{2,1,0:T(8,128)(2,1)S(1)}, u32[]{:S(2)}, u32[]{:S(2)}) collective-permute-start(bf16[2,128,512]{2,1,0:T(8,128)(2,1)S(1)} %fusion.11), channel_id=1, source_target_pairs={{0,1},{1,2},{2,3},{3,0},{4,5},{5,6},{6,7},{7,4},{8,9},{9,10},{10,1... | collective-permute-start | bytes 786440 | tf_op jit(solution)/shard_map/ppermute | solution.py:94
  108.0 41.3 %all-to-all-start.1 = ((bf16[4,128,2,128]{1,3,2,0:T(8,128)(2,1)}), bf16[4,128,2,128]{1,3,2,0:T(8,128)(2,1)S(1)}, u32[]{:S(2)}, u32[]{:S(2)}) async-start(bf16[4,128,2,128]{1,3,2,0:T(8,128)(2,1)} %copy_bitcast_fusion), calls=%async_computation.1 | async-start | bytes 524288 | tf_op jit(solution)/shard_map/all_to_all | solution.py:80
  129.6 19.0 %collective-permute-start.11 = (bf16[512,2,128]{0,2,1:T(8,128)(2,1)S(1)}, bf16[512,2,128]{0,2,1:T(8,128)(2,1)S(1)}, u32[]{:S(2)}, u32[]{:S(2)}) collective-permute-start(bf16[512,2,128]{0,2,1:T(8,128)(2,1)S(1)} %fusion.14), channel_id=1, source_target_pairs={{0,8},{4,508},{8,16},{12,4},{16,24},{20,12},{24,32},{28,20},{32,40... | collective-permute-start | bytes 786440 | tf_op jit(solution)/shard_map/ppermute | solution.py:112
  149.3 23.4 %all-to-all-start = ((bf16[4,128,2,128]{1,3,2,0:T(8,128)(2,1)}), bf16[4,128,2,128]{1,3,2,0:T(8,128)(2,1)S(1)}, u32[]{:S(2)}, u32[]{:S(2)}) async-start(bf16[4,128,2,128]{1,3,2,0:T(8,128)(2,1)} %copy_bitcast_fusion.1), calls=%async_computation | async-start | bytes 524288 | tf_op jit(solution)/shard_map/all_to_all | solution.py:80

commit v4 on v3

--- a/solution.py
+++ b/solution.py
@@ -68,20 +68,29 @@
 
     order = natural_order(owners, block_count)
     pick = jnp.asarray(np.eye(row_total, dtype=np.float32)[order], jnp.bfloat16)
+    pick = jnp.roll(pick.reshape(owners, own_rows, row_total), -me, axis=0)
 
-    def turned(block):
+    def turned_sends(block, partner):
         sign = jnp.array([1.0, -1.0], jnp.bfloat16).reshape(2, 1, 1)
+        block = block * sign
+        got = []
+        for ahead in range(owners):
+            piece = lax.dot_general(
+                pick[ahead], block, (((1,), (2,)), ((), ())), preferred_element_type=jnp.float32
+            ).astype(jnp.bfloat16)
+            pairs = [
+                (i * owners + o, partner(i) % groups * owners + (o + ahead) % owners)
+                for i in range(groups)
+                for o in range(owners)
+            ]
+            got.append(lax.ppermute(piece, ("kp", "own"), pairs))
+        return got
+
+    def natural(got):
+        pieces = jnp.concatenate([got[-ahead % owners] for ahead in range(owners)], axis=2)
         out = lax.dot_general(
-            pick, block * sign, (((1,), (2,)), ((), ())), preferred_element_type=jnp.float32
+            pieces, pick.reshape(row_total, row_total), (((2,), (0,)), ((), ())), preferred_element_type=jnp.float32
         )
-        return out.astype(jnp.bfloat16)
-
-    def gathered(pieces):
-        swapped = lax.all_to_all(
-            pieces.reshape(owners, own_rows, 2, own_rows), "own", split_axis=0, concat_axis=0, tiled=True
-        )
-        swapped = swapped.transpose(1, 2, 0, 3).reshape(own_rows, 2, row_total)
-        out = lax.dot_general(swapped, pick, (((2,), (0,)), ((), ())), preferred_element_type=jnp.float32)
         return out.astype(jnp.bfloat16)
 
     def first_products(right):
@@ -107,13 +116,11 @@
     late_2 = sends(pieces_2)
     late_1, _ = lax.optimization_barrier((late_1, pieces_2))
     block_1 = third(right_1, *late_1)
-    back_1 = lax.ppermute(turned(block_1), "kp", [(i, (i - 1) % groups) for i in range(groups)])
+    back_1 = turned_sends(block_1, lambda i: i - 1)
     block_2 = third(right_2, *late_2)
-    back_2 = lax.ppermute(
-        turned(block_2), "kp", [(i, (i - 2 if i % 2 else i + 2) % groups) for i in range(groups)]
-    )
-    back_1 = gathered(back_1)
-    back_2 = gathered(back_2)
+    back_2 = turned_sends(block_2, lambda i: i - 2 if i % 2 else i + 2)
+    back_1 = natural(back_1)
+    back_2 = natural(back_2)
     block_1 = block_1.transpose(1, 0, 2)
     block_2 = block_2.transpose(1, 0, 2)
     return jnp.stack(

time: 177 us -> 171 us (0.966)
  waiting for transfers between devices: 74.3 us -> 56.6 us
  starting transfers between devices: 76.1 us -> 90.1 us
  local copies, waits for them, and re-layouts: 8.12 us -> 5.78 us
    ppermute x2 -> x8, starting transfers between devices: 5.68 us -> 37.2 us  [turned_sends(): got.append(lax.ppermute(piece, ('kp', 'own'), pairs))]
    all_to_all x2 -> x0, starting transfers between devices: 15.6 us -> none  [gathered(): lax.all_to_all(pieces.reshape(owners, own_rows, 2, own_rows), 'own', spli...]
    all_to_all x2 -> x0, waiting for transfers between devices: 14.1 us -> none  [gathered(): lax.all_to_all(pieces.reshape(owners, own_rows, 2, own_rows), 'own', spli...]
    ppermute x2 -> x8, waiting for transfers between devices: 17 us -> 11.6 us  [turned_sends(): got.append(lax.ppermute(piece, ('kp', 'own'), pairs))]
    ppermute x4, starting transfers between devices: 22.2 us -> 17.7 us  [sends(): lax.ppermute(pieces[0], 'own', up)]
    ppermute x4, waiting for transfers between devices: 31.1 us -> 34.9 us  [sends(): lax.ppermute(pieces[0], 'own', up)]
    ppermute x4, starting transfers between devices: 19.5 us -> 22.1 us  [sends(): lax.ppermute(pieces[1], 'own', down)]
    ppermute x4, waiting for transfers between devices: 4.01 us -> 2.08 us  [sends(): lax.ppermute(pieces[1], 'own', down)]
  transfers between devices with their start and end apart: 15 -> 19, of which waited for: 8 -> 7; matrix products, arithmetic and copies ran while one was open for 12% -> 12% of each run, Pallas kernels for 0% -> 0%
where the time goes in v4:
time: 171 us; the launch traced here: 170 us
  starting transfers between devices  90.1 us (53%)
  waiting for transfers between devices  56.6 us (33%)
  matrix products  12.8 us (7%)
  local copies, waits for them, and re-layouts  5.78 us (3%)
  other arithmetic  4.53 us (3%)
    ppermute x8, starting transfers between devices, turned_sends(): got.append(lax.ppermute(piece, ('kp', 'own'), pairs))  37.2 us
    ppermute x4, waiting for transfers between devices, sends(): lax.ppermute(pieces[0], 'own', up)  34.9 us
    ppermute x4, starting transfers between devices, sends(): lax.ppermute(pieces[1], 'own', down)  22.1 us
    ppermute x4, starting transfers between devices, sends(): lax.ppermute(pieces[0], 'own', up)  17.7 us
    ppermute x8, waiting for transfers between devices, turned_sends(): got.append(lax.ppermute(piece, ('kp', 'own'), pairs))  11.6 us
    dot_general x10, matrix products, product(): lax.dot_general(rows, right, (((2,), (1,)), ((), ())), preferred_element_...  9.82 us
    ppermute x1, starting transfers between devices, body(): lax.ppermute(pair_density, 'kp', [(i, (i - 2) % groups) for i in range(0,...  8.91 us
    ppermute x1, waiting for transfers between devices, body(): lax.ppermute(pair_density, 'kp', [(i, (i + 1) % groups) for i in range(gr...  5.74 us
  transfers between devices with their start and end apart: 19, of which 7 were waited for; matrix products, arithmetic and copies ran while one was open for 12% of the time, Pallas kernels for 0%

profile of v4, /device:TPU:24, one launch (start us, length us, event | category | flops | bytes accessed | tf_op | source)
XLA Modules:
  0.0 170.3 jit_solution(3275038768939910639)
XLA Ops:
  0.0 1.9 %collective-permute-start = (bf16[2,256,2,512]{3,2,1,0:T(2,128)(2,1)}, bf16[2,256,2,512]{3,2,1,0:T(2,128)(2,1)}, u32[]{:S(2)}, u32[]{:S(2)}) collective-permute-start(bf16[2,256,2,512]{3,2,1,0:T(2,128)(2,1)} %param.5), channel_id=1, source_target_pairs={{0,4},{4,8},{8,12},{12,16},{16,20},{20,24},{24,28},{28,32},{32,36}... | collective-permute-start | bytes 3145736 | tf_op jit(solution)/shard_map/ppermute | solution.py:30
  1.9 8.9 %collective-permute-start.1 = (bf16[2,256,2,512]{3,2,1,0:T(2,128)(2,1)}, bf16[2,256,2,512]{3,2,1,0:T(2,128)(2,1)S(1)}, u32[]{:S(2)}, u32[]{:S(2)}) collective-permute-start(bf16[2,256,2,512]{3,2,1,0:T(2,128)(2,1)} %param.5), channel_id=1, source_target_pairs={{0,504},{8,0},{16,8},{24,16},{32,24},{40,32},{48,40},{56,48},{64,5... | collective-permute-start | bytes 3145736 | tf_op jit(solution)/shard_map/ppermute | solution.py:31
  10.8 2.0 %multiply_convert_fusion = bf16[2,256,2,512]{3,2,1,0:T(2,128)(2,1)S(1)} fusion(bf16[2,256,2,512]{3,2,1,0:T(2,128)(2,1)} %param.5, f32[512]{0:T(512)} %param.6), kind=kLoop, calls=%fused_computation.3 | loop fusion | flops 1572864 | bytes 2099200 | tf_op jit(solution)/shard_map/convert_element_type | solution.py:36
  13.1 0.4 fusion.19
  14.0 1.5 pad_maximum_fusion
  15.5 5.7 %collective-permute-done = bf16[2,256,2,512]{3,2,1,0:T(2,128)(2,1)} collective-permute-done((bf16[2,256,2,512]{3,2,1,0:T(2,128)(2,1)}, bf16[2,256,2,512]{3,2,1,0:T(2,128)(2,1)}, u32[]{:S(2)}, u32[]{:S(2)}) %collective-permute-start) | collective-permute-done | bytes 1048608 | tf_op jit(solution)/shard_map/ppermute | solution.py:30
  21.2 2.2 %collective-permute-done.1 = bf16[2,256,2,512]{3,2,1,0:T(2,128)(2,1)S(1)} collective-permute-done((bf16[2,256,2,512]{3,2,1,0:T(2,128)(2,1)}, bf16[2,256,2,512]{3,2,1,0:T(2,128)(2,1)S(1)}, u32[]{:S(2)}, u32[]{:S(2)}) %collective-permute-start.1) | collective-permute-done | bytes 1048608 | tf_op jit(solution)/shard_map/ppermute | solution.py:31
  23.4 2.2 %collective-permute-start.4 = (bf16[2,256,2,512]{3,2,1,0:T(2,128)(2,1)}, bf16[2,256,2,512]{3,2,1,0:T(2,128)(2,1)}, u32[]{:S(2)}, u32[]{:S(2)}) collective-permute-start(bf16[2,256,2,512]{3,2,1,0:T(2,128)(2,1)} %collective-permute-done), channel_id=1, source_target_pairs={{0,4},{8,12},{16,20},{24,28},{32,36},{40,44},{48,52},{56,60},{64,6... | collective-permute-start | bytes 3145736 | tf_op jit(solution)/shard_map/ppermute | solution.py:106
  25.7 0.8 constant_dynamic-slice_fusion
  26.5 1.8 %reshape.30 = bf16[512,1024,1]{1,0,2:T(8,128)(2,1)S(1)} reshape(bf16[2,256,2,512]{3,2,1,0:T(2,128)(2,1)} %collective-permute-done) | data formatting | bytes 2097152 | tf_op jit(solution)/shard_map/reshape | solution.py:34
  28.3 1.4 fusion.15
  29.8 9.1 %collective-permute-start.2 = (bf16[2,64,512]{2,1,0:T(8,128)(2,1)S(1)}, bf16[2,64,512]{2,1,0:T(8,128)(2,1)}, u32[]{:S(2)}, u32[]{:S(2)}) collective-permute-start(bf16[2,64,512]{2,1,0:T(8,128)(2,1)S(1)} %fusion.15), channel_id=1, source_target_pairs={{0,1},{1,2},{2,3},{3,0},{4,5},{5,6},{6,7},{7,4},{8,9},{9,10},{10,1... | collective-permute-start | bytes 393224 | tf_op jit(solution)/shard_map/ppermute | solution.py:103
  38.9 1.5 fusion.16
  40.5 3.3 %collective-permute-start.3 = (bf16[2,64,512]{2,1,0:T(8,128)(2,1)S(1)}, bf16[2,64,512]{2,1,0:T(8,128)(2,1)S(1)}, u32[]{:S(2)}, u32[]{:S(2)}) collective-permute-start(bf16[2,64,512]{2,1,0:T(8,128)(2,1)S(1)} %fusion.16), channel_id=1, source_target_pairs={{0,3},{1,0},{2,1},{3,2},{4,7},{5,4},{6,5},{7,6},{8,11},{9,8},{10,9... | collective-permute-start | bytes 393224 | tf_op jit(solution)/shard_map/ppermute | solution.py:103
  44.0 0.8 reshape.31
  44.7 1.6 fusion.18
  46.3 7.8 %collective-permute-start.8 = (bf16[2,64,512]{2,1,0:T(8,128)(2,1)S(1)}, bf16[2,64,512]{2,1,0:T(8,128)(2,1)S(1)}, u32[]{:S(2)}, u32[]{:S(2)}) collective-permute-start(bf16[2,64,512]{2,1,0:T(8,128)(2,1)S(1)} %fusion.18), channel_id=1, source_target_pairs={{0,3},{1,0},{2,1},{3,2},{4,7},{5,4},{6,5},{7,6},{8,11},{9,8},{10,9... | collective-permute-start | bytes 393224 | tf_op jit(solution)/shard_map/ppermute | solution.py:103
  54.2 1.4 fusion.17
  55.6 1.9 %collective-permute-start.7 = (bf16[2,64,512]{2,1,0:T(8,128)(2,1)S(1)}, bf16[2,64,512]{2,1,0:T(8,128)(2,1)S(1)}, u32[]{:S(2)}, u32[]{:S(2)}) collective-permute-start(bf16[2,64,512]{2,1,0:T(8,128)(2,1)S(1)} %fusion.17), channel_id=1, source_target_pairs={{0,1},{1,2},{2,3},{3,0},{4,5},{5,6},{6,7},{7,4},{8,9},{9,10},{10,1... | collective-permute-start | bytes 393224 | tf_op jit(solution)/shard_map/ppermute | solution.py:103
  57.6 2.1 %collective-permute-done.3 = bf16[2,64,512]{2,1,0:T(8,128)(2,1)S(1)} collective-permute-done((bf16[2,64,512]{2,1,0:T(8,128)(2,1)S(1)}, bf16[2,64,512]{2,1,0:T(8,128)(2,1)S(1)}, u32[]{:S(2)}, u32[]{:S(2)}) %collective-permute-start.3) | collective-permute-done | bytes 131104 | tf_op jit(solution)/shard_map/ppermute | solution.py:103
  59.6 1.4 fusion.13
  61.0 4.7 %collective-permute-start.5 = (bf16[2,128,512]{2,1,0:T(8,128)(2,1)S(1)}, bf16[2,128,512]{2,1,0:T(8,128)(2,1)S(1)}, u32[]{:S(2)}, u32[]{:S(2)}) collective-permute-start(bf16[2,128,512]{2,1,0:T(8,128)(2,1)S(1)} %fusion.13), channel_id=1, source_target_pairs={{0,1},{1,2},{2,3},{3,0},{4,5},{5,6},{6,7},{7,4},{8,9},{9,10},{10,1... | collective-permute-start | bytes 786440 | tf_op jit(solution)/shard_map/ppermute | solution.py:103
  65.7 0.5 fusion.12
  66.2 5.0 %collective-permute-start.6 = (bf16[2,128,512]{2,1,0:T(8,128)(2,1)S(1)}, bf16[2,128,512]{2,1,0:T(8,128)(2,1)S(1)}, u32[]{:S(2)}, u32[]{:S(2)}) collective-permute-start(bf16[2,128,512]{2,1,0:T(8,128)(2,1)S(1)} %fusion.12), channel_id=1, source_target_pairs={{0,3},{1,0},{2,1},{3,2},{4,7},{5,4},{6,5},{7,6},{8,11},{9,8},{10,9... | collective-permute-start | bytes 786440 | tf_op jit(solution)/shard_map/ppermute | solution.py:103
  71.3 0.5 fusion.10
  71.8 5.9 %collective-permute-start.10 = (bf16[2,128,512]{2,1,0:T(8,128)(2,1)S(1)}, bf16[2,128,512]{2,1,0:T(8,128)(2,1)S(1)}, u32[]{:S(2)}, u32[]{:S(2)}) collective-permute-start(bf16[2,128,512]{2,1,0:T(8,128)(2,1)S(1)} %fusion.10), channel_id=1, source_target_pairs={{0,3},{1,0},{2,1},{3,2},{4,7},{5,4},{6,5},{7,6},{8,11},{9,8},{10,9... | collective-permute-start | bytes 786440 | tf_op jit(solution)/shard_map/ppermute | solution.py:103
  77.7 13.7 %collective-permute-done.7 = bf16[2,64,512]{2,1,0:T(8,128)(2,1)S(1)} collective-permute-done((bf16[2,64,512]{2,1,0:T(8,128)(2,1)S(1)}, bf16[2,64,512]{2,1,0:T(8,128)(2,1)S(1)}, u32[]{:S(2)}, u32[]{:S(2)}) %collective-permute-start.7) | collective-permute-done | bytes 131104 | tf_op jit(solution)/shard_map/ppermute | solution.py:103
  91.4 0.5 fusion.11
  91.9 1.9 %collective-permute-start.9 = (bf16[2,128,512]{2,1,0:T(8,128)(2,1)S(1)}, bf16[2,128,512]{2,1,0:T(8,128)(2,1)S(1)}, u32[]{:S(2)}, u32[]{:S(2)}) collective-permute-start(bf16[2,128,512]{2,1,0:T(8,128)(2,1)S(1)} %fusion.11), channel_id=1, source_target_pairs={{0,1},{1,2},{2,3},{3,0},{4,5},{5,6},{6,7},{7,4},{8,9},{9,10},{10,1... | collective-permute-start | bytes 786440 | tf_op jit(solution)/shard_map/ppermute | solution.py:103
  93.8 21.2 %collective-permute-done.5 = bf16[2,128,512]{2,1,0:T(8,128)(2,1)S(1)} collective-permute-done((bf16[2,128,512]{2,1,0:T(8,128)(2,1)S(1)}, bf16[2,128,512]{2,1,0:T(8,128)(2,1)S(1)}, u32[]{:S(2)}, u32[]{:S(2)}) %collective-permute-start.5) | collective-permute-done | bytes 262176 | tf_op jit(solution)/shard_map/ppermute | solution.py:103
  115.1 0.5 fusion.8
  115.6 0.3 convolution_convert_fusion.2
  115.9 1.9 %collective-permute-start.18 = (bf16[128,2,128]{2,0,1:T(8,128)(2,1)S(1)}, bf16[128,2,128]{2,0,1:T(8,128)(2,1)S(1)}, u32[]{:S(2)}, u32[]{:S(2)}) collective-permute-start(bf16[128,2,128]{2,0,1:T(8,128)(2,1)S(1)} %convolution_convert_fusion.2), channel_id=1, source_target_pairs={{0,509},{1,510},{2,511},{3,508},{4,1},{5,2},{6,3},{7,0},{8,5},{9,6... | collective-permute-start | bytes 196616 | tf_op jit(solution)/shard_map/ppermute | solution.py:86
  117.8 0.3 convolution_convert_fusion.3
  118.1 7.9 %collective-permute-start.17 = (bf16[128,2,128]{2,0,1:T(8,128)(2,1)S(1)}, bf16[128,2,128]{2,0,1:T(8,128)(2,1)S(1)}, u32[]{:S(2)}, u32[]{:S(2)}) collective-permute-start(bf16[128,2,128]{2,0,1:T(8,128)(2,1)S(1)} %convolution_convert_fusion.3), channel_id=1, source_target_pairs={{0,510},{1,511},{2,508},{3,509},{4,2},{5,3},{6,0},{7,1},{8,6},{9,7... | collective-permute-start | bytes 196616 | tf_op jit(solution)/shard_map/ppermute | solution.py:86
  126.1 0.3 convolution_convert_fusion.4
  126.4 1.9 %collective-permute-start.16 = (bf16[128,2,128]{2,0,1:T(8,128)(2,1)S(1)}, bf16[128,2,128]{2,0,1:T(8,128)(2,1)S(1)}, u32[]{:S(2)}, u32[]{:S(2)}) collective-permute-start(bf16[128,2,128]{2,0,1:T(8,128)(2,1)S(1)} %convolution_convert_fusion.4), channel_id=1, source_target_pairs={{0,511},{1,508},{2,509},{3,510},{4,3},{5,0},{6,1},{7,2},{8,7},{9,4... | collective-permute-start | bytes 196616 | tf_op jit(solution)/shard_map/ppermute | solution.py:86
  128.6 2.1 %collective-permute-start.15 = (bf16[128,2,128]{2,0,1:T(8,128)(2,1)S(1)}, bf16[128,2,128]{2,0,1:T(8,128)(2,1)S(1)}, u32[]{:S(2)}, u32[]{:S(2)}) collective-permute-start(bf16[128,2,128]{2,0,1:T(8,128)(2,1)S(1)} %convolution_convert_fusion.5), channel_id=1, source_target_pairs={{0,508},{1,509},{2,510},{3,511},{4,0},{5,1},{6,2},{7,3},{8,4},{9,5... | collective-permute-start | bytes 196616 | tf_op jit(solution)/shard_map/ppermute | solution.py:86
  130.7 0.5 fusion.9
  132.4 9.0 %collective-permute-start.14 = (bf16[128,2,128]{2,0,1:T(8,128)(2,1)S(1)}, bf16[128,2,128]{2,0,1:T(8,128)(2,1)S(1)}, u32[]{:S(2)}, u32[]{:S(2)}) collective-permute-start(bf16[128,2,128]{2,0,1:T(8,128)(2,1)S(1)} %convolution_convert_fusion.6), channel_id=1, source_target_pairs={{0,9},{1,10},{2,11},{3,8},{4,509},{5,510},{6,511},{7,508},{8,17},{... | collective-permute-start | bytes 196616 | tf_op jit(solution)/shard_map/ppermute | solution.py:86
  141.4 10.6 %collective-permute-start.13 = (bf16[128,2,128]{2,0,1:T(8,128)(2,1)S(1)}, bf16[128,2,128]{2,0,1:T(8,128)(2,1)S(1)}, u32[]{:S(2)}, u32[]{:S(2)}) collective-permute-start(bf16[128,2,128]{2,0,1:T(8,128)(2,1)S(1)} %convolution_convert_fusion.7), channel_id=1, source_target_pairs={{0,10},{1,11},{2,8},{3,9},{4,510},{5,511},{6,508},{7,509},{8,18},{... | collective-permute-start | bytes 196616 | tf_op jit(solution)/shard_map/ppermute | solution.py:86
  152.0 1.9 %collective-permute-start.12 = (bf16[128,2,128]{2,0,1:T(8,128)(2,1)S(1)}, bf16[128,2,128]{2,0,1:T(8,128)(2,1)S(1)}, u32[]{:S(2)}, u32[]{:S(2)}) collective-permute-start(bf16[128,2,128]{2,0,1:T(8,128)(2,1)S(1)} %convolution_convert_fusion.8), channel_id=1, source_target_pairs={{0,11},{1,8},{2,9},{3,10},{4,511},{5,508},{6,509},{7,510},{8,19},{... | collective-permute-start | bytes 196616 | tf_op jit(solution)/shard_map/ppermute | solution.py:86
  154.0 1.9 %collective-permute-start.11 = (bf16[128,2,128]{2,0,1:T(8,128)(2,1)S(1)}, bf16[128,2,128]{2,0,1:T(8,128)(2,1)S(1)}, u32[]{:S(2)}, u32[]{:S(2)}) collective-permute-start(bf16[128,2,128]{2,0,1:T(8,128)(2,1)S(1)} %convolution_convert_fusion.9), channel_id=1, source_target_pairs={{0,8},{1,9},{2,10},{3,11},{4,508},{5,509},{6,510},{7,511},{8,16},{... | collective-permute-start | bytes 196616 | tf_op jit(solution)/shard_map/ppermute | solution.py:86
  155.9 0.3 fusion.14
  156.2 1.3 collective-permute-done.13
  157.5 10.3 %collective-permute-done.12 = bf16[128,2,128]{2,0,1:T(8,128)(2,1)S(1)} collective-permute-done((bf16[128,2,128]{2,0,1:T(8,128)(2,1)S(1)}, bf16[128,2,128]{2,0,1:T(8,128)(2,1)S(1)}, u32[]{:S(2)}, u32[]{:S(2)}) %collective-permute-start.12) | collective-permute-done | bytes 65568 | tf_op jit(solution)/shard_map/ppermute | solution.py:86
  167.8 0.3 fusion.46
  168.2 2.0 %copy.9 = bf16[4,128,2,512]{3,2,1,0:T(2,128)(2,1)} copy(bf16[4,128,2,512]{3,1,2,0:T(8,128)(2,1)S(1)} %pad_maximum_fusion.1) | data formatting | bytes 2097152 | tf_op jit(solution)/shard_map/stack | solution.py:126
  (37 shorter events, 2.4 us)
Async XLA Ops:
  0.0 21.2 %collective-permute-start = (bf16[2,256,2,512]{3,2,1,0:T(2,128)(2,1)}, bf16[2,256,2,512]{3,2,1,0:T(2,128)(2,1)}, u32[]{:S(2)}, u32[]{:S(2)}) collective-permute-start(bf16[2,256,2,512]{3,2,1,0:T(2,128)(2,1)} %param.5), channel_id=1, source_target_pairs={{0,4},{4,8},{8,12},{12,16},{16,20},{20,24},{24,28},{28,32},{32,36}... | collective-permute-start | bytes 3145736 | tf_op jit(solution)/shard_map/ppermute | solution.py:30
  1.9 21.5 %collective-permute-start.1 = (bf16[2,256,2,512]{3,2,1,0:T(2,128)(2,1)}, bf16[2,256,2,512]{3,2,1,0:T(2,128)(2,1)S(1)}, u32[]{:S(2)}, u32[]{:S(2)}) collective-permute-start(bf16[2,256,2,512]{3,2,1,0:T(2,128)(2,1)} %param.5), channel_id=1, source_target_pairs={{0,504},{8,0},{16,8},{24,16},{32,24},{40,32},{48,40},{56,48},{64,5... | collective-permute-start | bytes 3145736 | tf_op jit(solution)/shard_map/ppermute | solution.py:31
  13.9 11.8 %copy-start.1 = (bf16[8,128,512]{2,1,0:T(8,128)(2,1)S(1)}, bf16[8,128,512]{2,1,0:T(8,128)(2,1)}, u32[]{:S(2)}) copy-start(bf16[8,128,512]{2,1,0:T(8,128)(2,1)} %constant.76) | copy-start | bytes 3145732
  23.4 6.3 %copy-start.3 = (bf16[2,256,2,512]{3,2,1,0:T(2,128)(2,1)}, bf16[2,256,2,512]{3,2,1,0:T(2,128)(2,1)S(1)}, u32[]{:S(2)}) copy-start(bf16[2,256,2,512]{3,2,1,0:T(2,128)(2,1)S(1)} %collective-permute-done.1) | copy-start | bytes 3145732
  23.4 20.4 %collective-permute-start.4 = (bf16[2,256,2,512]{3,2,1,0:T(2,128)(2,1)}, bf16[2,256,2,512]{3,2,1,0:T(2,128)(2,1)}, u32[]{:S(2)}, u32[]{:S(2)}) collective-permute-start(bf16[2,256,2,512]{3,2,1,0:T(2,128)(2,1)} %collective-permute-done), channel_id=1, source_target_pairs={{0,4},{8,12},{16,20},{24,28},{32,36},{40,44},{48,52},{56,60},{64,6... | collective-permute-start | bytes 3145736 | tf_op jit(solution)/shard_map/ppermute | solution.py:106
  29.8 27.8 %collective-permute-start.2 = (bf16[2,64,512]{2,1,0:T(8,128)(2,1)S(1)}, bf16[2,64,512]{2,1,0:T(8,128)(2,1)}, u32[]{:S(2)}, u32[]{:S(2)}) collective-permute-start(bf16[2,64,512]{2,1,0:T(8,128)(2,1)S(1)} %fusion.15), channel_id=1, source_target_pairs={{0,1},{1,2},{2,3},{3,0},{4,5},{5,6},{6,7},{7,4},{8,9},{9,10},{10,1... | collective-permute-start | bytes 393224 | tf_op jit(solution)/shard_map/ppermute | solution.py:103
  38.9 4.9 %copy-start.4 = (bf16[2,256,2,512]{3,2,1,0:T(2,128)(2,1)S(1)}, bf16[2,256,2,512]{3,2,1,0:T(2,128)(2,1)}, u32[]{:S(2)}) copy-start(bf16[2,256,2,512]{3,2,1,0:T(2,128)(2,1)} %copy-done.3) | copy-start | bytes 3145732
  40.5 19.2 %collective-permute-start.3 = (bf16[2,64,512]{2,1,0:T(8,128)(2,1)S(1)}, bf16[2,64,512]{2,1,0:T(8,128)(2,1)S(1)}, u32[]{:S(2)}, u32[]{:S(2)}) collective-permute-start(bf16[2,64,512]{2,1,0:T(8,128)(2,1)S(1)} %fusion.16), channel_id=1, source_target_pairs={{0,3},{1,0},{2,1},{3,2},{4,7},{5,4},{6,5},{7,6},{8,11},{9,8},{10,9... | collective-permute-start | bytes 393224 | tf_op jit(solution)/shard_map/ppermute | solution.py:103
  44.7 14.9 %copy-start = (bf16[4,2,128,1024]{3,2,1,0:T(8,128)(2,1)S(1)}, bf16[4,2,128,1024]{3,2,1,0:T(8,128)(2,1)}, u32[]{:S(2)}) copy-start(bf16[4,2,128,1024]{3,2,1,0:T(8,128)(2,1)} %pad_maximum_fusion) | copy-start | bytes 6291460
  46.3 24.9 %collective-permute-start.8 = (bf16[2,64,512]{2,1,0:T(8,128)(2,1)S(1)}, bf16[2,64,512]{2,1,0:T(8,128)(2,1)S(1)}, u32[]{:S(2)}, u32[]{:S(2)}) collective-permute-start(bf16[2,64,512]{2,1,0:T(8,128)(2,1)S(1)} %fusion.18), channel_id=1, source_target_pairs={{0,3},{1,0},{2,1},{3,2},{4,7},{5,4},{6,5},{7,6},{8,11},{9,8},{10,9... | collective-permute-start | bytes 393224 | tf_op jit(solution)/shard_map/ppermute | solution.py:103
  55.6 35.8 %collective-permute-start.7 = (bf16[2,64,512]{2,1,0:T(8,128)(2,1)S(1)}, bf16[2,64,512]{2,1,0:T(8,128)(2,1)S(1)}, u32[]{:S(2)}, u32[]{:S(2)}) collective-permute-start(bf16[2,64,512]{2,1,0:T(8,128)(2,1)S(1)} %fusion.17), channel_id=1, source_target_pairs={{0,1},{1,2},{2,3},{3,0},{4,5},{5,6},{6,7},{7,4},{8,9},{9,10},{10,1... | collective-permute-start | bytes 393224 | tf_op jit(solution)/shard_map/ppermute | solution.py:103
  61.0 54.0 %collective-permute-start.5 = (bf16[2,128,512]{2,1,0:T(8,128)(2,1)S(1)}, bf16[2,128,512]{2,1,0:T(8,128)(2,1)S(1)}, u32[]{:S(2)}, u32[]{:S(2)}) collective-permute-start(bf16[2,128,512]{2,1,0:T(8,128)(2,1)S(1)} %fusion.13), channel_id=1, source_target_pairs={{0,1},{1,2},{2,3},{3,0},{4,5},{5,6},{6,7},{7,4},{8,9},{9,10},{10,1... | collective-permute-start | bytes 786440 | tf_op jit(solution)/shard_map/ppermute | solution.py:103
  66.2 48.8 %collective-permute-start.6 = (bf16[2,128,512]{2,1,0:T(8,128)(2,1)S(1)}, bf16[2,128,512]{2,1,0:T(8,128)(2,1)S(1)}, u32[]{:S(2)}, u32[]{:S(2)}) collective-permute-start(bf16[2,128,512]{2,1,0:T(8,128)(2,1)S(1)} %fusion.12), channel_id=1, source_target_pairs={{0,3},{1,0},{2,1},{3,2},{4,7},{5,4},{6,5},{7,6},{8,11},{9,8},{10,9... | collective-permute-start | bytes 786440 | tf_op jit(solution)/shard_map/ppermute | solution.py:103
  71.8 43.8 %copy-start.2 = (bf16[8,128,512]{2,1,0:T(8,128)(2,1)S(1)}, bf16[8,128,512]{2,1,0:T(8,128)(2,1)}, u32[]{:S(2)}) copy-start(bf16[8,128,512]{2,1,0:T(8,128)(2,1)} %constant.76) | copy-start | bytes 3145732
  71.8 43.8 %copy-start.6 = (bf16[2]{0:T(256)(128)(2,1)S(1)}, bf16[2]{0:T(256)(128)(2,1)}, u32[]{:S(2)}) copy-start(bf16[2]{0:T(256)(128)(2,1)} %constant.65.clone) | copy-start | bytes 16
  71.8 56.8 %collective-permute-start.10 = (bf16[2,128,512]{2,1,0:T(8,128)(2,1)S(1)}, bf16[2,128,512]{2,1,0:T(8,128)(2,1)S(1)}, u32[]{:S(2)}, u32[]{:S(2)}) collective-permute-start(bf16[2,128,512]{2,1,0:T(8,128)(2,1)S(1)} %fusion.10), channel_id=1, source_target_pairs={{0,3},{1,0},{2,1},{3,2},{4,7},{5,4},{6,5},{7,6},{8,11},{9,8},{10,9... | collective-permute-start | bytes 786440 | tf_op jit(solution)/shard_map/ppermute | solution.py:103
  91.9 38.8 %collective-permute-start.9 = (bf16[2,128,512]{2,1,0:T(8,128)(2,1)S(1)}, bf16[2,128,512]{2,1,0:T(8,128)(2,1)S(1)}, u32[]{:S(2)}, u32[]{:S(2)}) collective-permute-start(bf16[2,128,512]{2,1,0:T(8,128)(2,1)S(1)} %fusion.11), channel_id=1, source_target_pairs={{0,1},{1,2},{2,3},{3,0},{4,5},{5,6},{6,7},{7,4},{8,9},{9,10},{10,1... | collective-permute-start | bytes 786440 | tf_op jit(solution)/shard_map/ppermute | solution.py:103
  115.9 25.5 %collective-permute-start.18 = (bf16[128,2,128]{2,0,1:T(8,128)(2,1)S(1)}, bf16[128,2,128]{2,0,1:T(8,128)(2,1)S(1)}, u32[]{:S(2)}, u32[]{:S(2)}) collective-permute-start(bf16[128,2,128]{2,0,1:T(8,128)(2,1)S(1)} %convolution_convert_fusion.2), channel_id=1, source_target_pairs={{0,509},{1,510},{2,511},{3,508},{4,1},{5,2},{6,3},{7,0},{8,5},{9,6... | collective-permute-start | bytes 196616 | tf_op jit(solution)/shard_map/ppermute | solution.py:86
  118.1 33.9 %collective-permute-start.17 = (bf16[128,2,128]{2,0,1:T(8,128)(2,1)S(1)}, bf16[128,2,128]{2,0,1:T(8,128)(2,1)S(1)}, u32[]{:S(2)}, u32[]{:S(2)}) collective-permute-start(bf16[128,2,128]{2,0,1:T(8,128)(2,1)S(1)} %convolution_convert_fusion.3), channel_id=1, source_target_pairs={{0,510},{1,511},{2,508},{3,509},{4,2},{5,3},{6,0},{7,1},{8,6},{9,7... | collective-permute-start | bytes 196616 | tf_op jit(solution)/shard_map/ppermute | solution.py:86
  126.4 27.6 %collective-permute-start.16 = (bf16[128,2,128]{2,0,1:T(8,128)(2,1)S(1)}, bf16[128,2,128]{2,0,1:T(8,128)(2,1)S(1)}, u32[]{:S(2)}, u32[]{:S(2)}) collective-permute-start(bf16[128,2,128]{2,0,1:T(8,128)(2,1)S(1)} %convolution_convert_fusion.4), channel_id=1, source_target_pairs={{0,511},{1,508},{2,509},{3,510},{4,3},{5,0},{6,1},{7,2},{8,7},{9,4... | collective-permute-start | bytes 196616 | tf_op jit(solution)/shard_map/ppermute | solution.py:86
  128.6 27.3 %copy-start.5 = (bf16[4,128,512]{2,1,0:T(8,128)(2,1)S(1)}, bf16[4,128,512]{2,1,0:T(8,128)(2,1)}, u32[]{:S(2)}) copy-start(bf16[4,128,512]{2,1,0:T(8,128)(2,1)} %constant_dynamic-slice_fusion) | copy-start | bytes 1572868
  128.6 27.3 %collective-permute-start.15 = (bf16[128,2,128]{2,0,1:T(8,128)(2,1)S(1)}, bf16[128,2,128]{2,0,1:T(8,128)(2,1)S(1)}, u32[]{:S(2)}, u32[]{:S(2)}) collective-permute-start(bf16[128,2,128]{2,0,1:T(8,128)(2,1)S(1)} %convolution_convert_fusion.5), channel_id=1, source_target_pairs={{0,508},{1,509},{2,510},{3,511},{4,0},{5,1},{6,2},{7,3},{8,4},{9,5... | collective-permute-start | bytes 196616 | tf_op jit(solution)/shard_map/ppermute | solution.py:86
  132.4 23.8 %collective-permute-start.14 = (bf16[128,2,128]{2,0,1:T(8,128)(2,1)S(1)}, bf16[128,2,128]{2,0,1:T(8,128)(2,1)S(1)}, u32[]{:S(2)}, u32[]{:S(2)}) collective-permute-start(bf16[128,2,128]{2,0,1:T(8,128)(2,1)S(1)} %convolution_convert_fusion.6), channel_id=1, source_target_pairs={{0,9},{1,10},{2,11},{3,8},{4,509},{5,510},{6,511},{7,508},{8,17},{... | collective-permute-start | bytes 196616 | tf_op jit(solution)/shard_map/ppermute | solution.py:86
  141.4 16.1 %collective-permute-start.13 = (bf16[128,2,128]{2,0,1:T(8,128)(2,1)S(1)}, bf16[128,2,128]{2,0,1:T(8,128)(2,1)S(1)}, u32[]{:S(2)}, u32[]{:S(2)}) collective-permute-start(bf16[128,2,128]{2,0,1:T(8,128)(2,1)S(1)} %convolution_convert_fusion.7), channel_id=1, source_target_pairs={{0,10},{1,11},{2,8},{3,9},{4,510},{5,511},{6,508},{7,509},{8,18},{... | collective-permute-start | bytes 196616 | tf_op jit(solution)/shard_map/ppermute | solution.py:86
  152.0 15.8 %collective-permute-start.12 = (bf16[128,2,128]{2,0,1:T(8,128)(2,1)S(1)}, bf16[128,2,128]{2,0,1:T(8,128)(2,1)S(1)}, u32[]{:S(2)}, u32[]{:S(2)}) collective-permute-start(bf16[128,2,128]{2,0,1:T(8,128)(2,1)S(1)} %convolution_convert_fusion.8), channel_id=1, source_target_pairs={{0,11},{1,8},{2,9},{3,10},{4,511},{5,508},{6,509},{7,510},{8,19},{... | collective-permute-start | bytes 196616 | tf_op jit(solution)/shard_map/ppermute | solution.py:86
  154.0 13.8 %collective-permute-start.11 = (bf16[128,2,128]{2,0,1:T(8,128)(2,1)S(1)}, bf16[128,2,128]{2,0,1:T(8,128)(2,1)S(1)}, u32[]{:S(2)}, u32[]{:S(2)}) collective-permute-start(bf16[128,2,128]{2,0,1:T(8,128)(2,1)S(1)} %convolution_convert_fusion.9), channel_id=1, source_target_pairs={{0,8},{1,9},{2,10},{3,11},{4,508},{5,509},{6,510},{7,511},{8,16},{... | collective-permute-start | bytes 196616 | tf_op jit(solution)/shard_map/ppermute | solution.py:86

commit v5 on v0

v5 whole, which is shorter than its diff:
```python
import math

import jax
import jax.numpy as jnp
import numpy as np
from jax import lax
from jax.sharding import PartitionSpec as P

BLOCK = 32


def owner_order(owners, blocks):
    count = owners * blocks * BLOCK
    rows = np.arange(count)
    owner, block, place = rows // (blocks * BLOCK), rows // BLOCK % blocks, rows % BLOCK
    column = (block * owners + owner) * BLOCK + place
    return np.eye(count, dtype=np.float32)[column].reshape(owners, blocks * BLOCK, count)


def body(pair_density, coulomb):
    points, transitions, _, g_local = pair_density.shape
    owners = lax.axis_size("own")
    groups = lax.axis_size("kp")
    blocks = transitions // (owners * BLOCK)
    rows = blocks * BLOCK
    depth = 2 * g_local
    scale = 1.0 / math.sqrt(g_local * owners)
    me = lax.axis_index("own")
    odd = lax.axis_index("kp") % 2 == 1
    parity = odd.astype(jnp.int32)

    def exchange_kp(value, partner):
        return lax.ppermute(value, "kp", [(i, partner(i) % groups) for i in range(groups)])

    def exchange_own(value, first):
        pairs = []
        for i in range(groups):
            flip = 1 if (i % 2 == 0) == first else 3
            pairs += [(i * owners + o, i * owners + (o ^ flip)) for o in range(owners)]
        return lax.ppermute(value, ("kp", "own"), pairs)

    def mate(i):
        return i + 1 if i % 2 == 0 else i - 1

    def across(i):
        return i - 1 if i % 2 == 0 else i + 1

    def second_next(i):
        return i + 2 if i % 2 == 0 else i - 2

    near_flip, far_flip = 1 + 2 * parity, 3 - 2 * parity
    relative = [me ^ near_flip, me ^ 2, me ^ far_flip, me]
    swapped = [me ^ far_flip, me ^ 2, me ^ near_flip, me]

    def by_owner(value, order, axis):
        return [lax.dynamic_index_in_dim(value, o, axis, keepdims=False) for o in order]

    plain = pair_density.reshape(points, transitions, depth)
    sent = jnp.stack([lax.dynamic_index_in_dim(plain, parity, 0, False), lax.dynamic_index_in_dim(plain, 1 - parity, 0, False)])
    mate_right = exchange_kp(sent, mate)
    next_right = exchange_kp(sent, across)

    weights = jnp.concatenate([coulomb, coulomb]) * scale
    weighted = (plain.astype(jnp.float32) * weights).astype(jnp.bfloat16)
    turned_weighted = jnp.concatenate([-weighted[..., g_local:], weighted[..., :g_local]], axis=-1)
    left = jnp.stack([weighted, turned_weighted], axis=1)
    left = left.reshape(points, 2, blocks, owners, BLOCK, depth)
    pieces = [x.reshape(points, 2 * rows, depth) for x in by_owner(left, relative, 3)]
    left_away = jnp.concatenate(pieces[:2], axis=1)
    left_second, left_own = pieces[2], pieces[3]

    def product(left_rows, right):
        return lax.dot_general(
            left_rows, right, (((2,), (2,)), ((0,), (0,))), preferred_element_type=jnp.float32
        )

    def whole(left_rows, right):
        out = lax.dot_general(
            left_rows.reshape(-1, depth),
            right.reshape(-1, depth),
            (((1,), (1,)), ((), ())),
            preferred_element_type=jnp.float32,
        )
        return out.reshape(points, -1, points * transitions)

    def wide(value):
        return value.astype(jnp.float32)

    def low(value):
        return value.astype(jnp.bfloat16)

    left_away, left_second, left_own, mate_right = lax.optimization_barrier(
        (left_away, left_second, left_own, mate_right)
    )
    away_mate = low(product(left_away, mate_right))
    next_right, _ = lax.optimization_barrier((next_right, away_mate))
    got_mate = exchange_own(away_mate, True)
    far_right = exchange_kp(next_right, mate)
    away_next = low(product(left_away, next_right))
    far_right, _ = lax.optimization_barrier((far_right, away_next))
    got_next = exchange_own(away_next, True)
    away_far = low(whole(left_away, far_right))
    got_mate, got_next, _ = lax.optimization_barrier((got_mate, got_next, away_far))
    got_far = exchange_own(away_far, True)

    def kept(got, slot):
        return wide(got[:, slot * 2 * rows : (slot + 1) * 2 * rows])

    second_pair = jnp.concatenate(
        [
            low(product(left_second, mate_right) + kept(got_mate, 1)),
            low(product(left_second, next_right) + kept(got_next, 1)),
        ],
        axis=2,
    )
    late_pair = exchange_own(second_pair, False)
    second_far = low(whole(left_second, far_right) + kept(got_far, 1))
    late_pair, _ = lax.optimization_barrier((late_pair, second_far))
    late_far = exchange_own(second_far, False)

    def finished(total):
        total = low(total).reshape(points, 2, rows, -1)
        return total.transpose(1, 0, 2, 3).reshape(2, points * rows, -1)

    block_mate = finished(product(left_own, mate_right) + kept(got_mate, 0) + wide(late_pair[..., :transitions]))
    block_next = finished(product(left_own, next_right) + kept(got_next, 0) + wide(late_pair[..., transitions:]))
    block_far = finished(whole(left_own, far_right) + kept(got_far, 0) + wide(late_far))

    pick_columns = jnp.asarray(owner_order(owners, blocks), jnp.bfloat16)
    pick_same = jnp.concatenate(by_owner(pick_columns, relative, 0), axis=0)
    pick_other = jnp.concatenate(by_owner(pick_columns, swapped, 0), axis=0)
    pick_rows = jnp.asarray(owner_order(owners, points * blocks), jnp.bfloat16)
    pick_rows = jnp.concatenate(by_owner(pick_rows, relative, 0), axis=0)
    sign = jnp.array([1.0, -1.0], jnp.bfloat16).reshape(2, 1, 1)

    def turned(block, pick):
        out = lax.dot_general(
            pick, block * sign, (((1,), (2,)), ((), ())), preferred_element_type=jnp.float32
        )
        return low(out).reshape(owners, rows, 2, points * rows)

    back_mate = exchange_kp(turned(block_mate, pick_other), mate)
    back_next = exchange_kp(turned(block_next, pick_other), across)
    back_far = exchange_kp(
        jnp.concatenate([turned(block_far[..., :transitions], pick_same), turned(block_far[..., transitions:], pick_same)], axis=1),
        second_next,
    )

    def natural(tiles, first, second):
        joined = jnp.concatenate([first[0], second[1], second[0], tiles[3]], axis=-1)
        out = lax.dot_general(joined, pick_rows, (((2,), (0,)), ((), ())), preferred_element_type=jnp.float32)
        return low(out)

    back_pair = jnp.concatenate([back_mate, back_next], axis=1)
    first_pair = exchange_own(back_pair[:2], True)
    first_far = exchange_own(back_far[:2], True)
    then_pair = exchange_own(jnp.stack([back_pair[2], first_pair[1]]), False)
    then_far = exchange_own(jnp.stack([back_far[2], first_far[1]]), False)
    back_pair = natural(back_pair, first_pair, then_pair)
    back_far = natural(back_far, first_far, then_far)

    def mixed(block, back):
        block = block.reshape(2, points, rows, transitions).transpose(1, 2, 0, 3)
        back = back.reshape(rows, 2, points, transitions)
        out = []
        for row_point in range(points):
            line = []
            for column_point in range(points):
                here = odd if row_point == column_point else ~odd
                line.append(jnp.where(here, block[row_point], back[:, :, column_point]))
            out.append(jnp.concatenate(line, axis=-1))
        return jnp.concatenate(out, axis=0)

    with_mate = mixed(block_mate, back_pair[:rows])
    with_next = mixed(block_next, back_pair[rows:])
    here_far = block_far.transpose(1, 0, 2)
    here_far = jnp.where(odd, jnp.roll(here_far, transitions, axis=2), here_far)
    back_far = jnp.where(odd, jnp.roll(back_far, rows, axis=0), back_far)
    return jnp.stack(
        [
            jnp.where(odd, with_mate, with_next),
            jnp.where(odd, here_far, back_far),
            jnp.where(odd, with_next, with_mate),
            jnp.where(odd, back_far, here_far),
        ],
        axis=0,
    )


def solution(mesh):
    placed = (P("kp", None, None, "own"), P("own"))
    return jax.shard_map(
        body,
        mesh=mesh,
        in_specs=placed,
        out_specs=P(None, ("kp", "own"), None, None),
        check_vma=False,
    )
```

time: 240 us -> 185 us (0.77)
  the two profiles are of different devices: /device:TPU:7 before, /device:TPU:30 now
where the time goes in v5:
time: 185 us; the launch traced here: 184 us
  starting transfers between devices  107 us (58%)
  waiting for transfers between devices  51.8 us (28%)
  matrix products  14.3 us (8%)
  local copies, waits for them, and re-layouts  5.42 us (3%)
  other arithmetic  4.86 us (3%)
    ppermute x9, starting transfers between devices, exchange_own(): return lax.ppermute(value, ('kp', 'own'), pairs)  75.3 us
    ppermute x9, waiting for transfers between devices, exchange_own(): return lax.ppermute(value, ('kp', 'own'), pairs)  43.9 us
    ppermute x6, starting transfers between devices, exchange_kp(): lax.ppermute(value, 'kp', [(i, partner(i) % groups) for i in range(groups)])  31.6 us
    dot_general x6, matrix products, product(): lax.dot_general(left_rows, right, (((2,), (2,)), ((0,), (0,))), preferred...  10.3 us
    ppermute x6, waiting for transfers between devices, exchange_kp(): lax.ppermute(value, 'kp', [(i, partner(i) % groups) for i in range(groups)])  7.91 us
  transfers between devices with their start and end apart: 15, of which 7 were waited for; matrix products, arithmetic and copies ran while one was open for 8% of the time, Pallas kernels for 0%

profile of v5, /device:TPU:30, one launch (start us, length us, event | category | flops | bytes accessed | tf_op | source)
XLA Modules:
  0.0 184.1 jit_solution(1927383272550174379)
XLA Ops:
  0.0 1.8 reshape.222
  1.9 1.1 pad_maximum_fusion.2
  3.0 1.9 %collective-permute-start = (bf16[2,256,1024]{2,1,0:T(8,128)(2,1)}, bf16[2,256,1024]{2,1,0:T(8,128)(2,1)}, u32[]{:S(2)}, u32[]{:S(2)}) collective-permute-start(bf16[2,256,1024]{2,1,0:T(8,128)(2,1)} %pad_maximum_fusion.2), channel_id=1, source_target_pairs={{0,4},{4,0},{8,12},{12,8},{16,20},{20,16},{24,28},{28,24},{32,36},... | collective-permute-start | bytes 3145736 | tf_op jit(solution)/shard_map/ppermute | solution.py:33
  4.9 2.8 %collective-permute-start.2 = (bf16[2,256,1024]{2,1,0:T(8,128)(2,1)}, bf16[2,256,1024]{2,1,0:T(8,128)(2,1)}, u32[]{:S(2)}, u32[]{:S(2)}) collective-permute-start(bf16[2,256,1024]{2,1,0:T(8,128)(2,1)} %pad_maximum_fusion.2), channel_id=1, source_target_pairs={{0,508},{4,8},{8,4},{12,16},{16,12},{20,24},{24,20},{28,32},{32,28... | collective-permute-start | bytes 3145736 | tf_op jit(solution)/shard_map/ppermute | solution.py:33
  7.8 0.2 multiply_convert_fusion
  8.0 1.1 slice_negate_fusion
  9.1 0.6 reshape.240
  9.6 1.3 pad_maximum_fusion
  10.9 0.3 multiply_convert_fusion.1
  11.2 0.2 fusion.9
  11.7 1.7 convolution_convert_fusion.2
  13.4 7.9 %collective-permute-done.2 = bf16[2,256,1024]{2,1,0:T(8,128)(2,1)} collective-permute-done((bf16[2,256,1024]{2,1,0:T(8,128)(2,1)}, bf16[2,256,1024]{2,1,0:T(8,128)(2,1)}, u32[]{:S(2)}, u32[]{:S(2)}) %collective-permute-start.2) | collective-permute-done | bytes 1048608 | tf_op jit(solution)/shard_map/ppermute | solution.py:33
  21.3 4.5 %collective-permute-start.4 = (bf16[2,256,1024]{2,1,0:T(8,128)(2,1)}, bf16[2,256,1024]{2,1,0:T(8,128)(2,1)S(1)}, u32[]{:S(2)}, u32[]{:S(2)}) collective-permute-start(bf16[2,256,1024]{2,1,0:T(8,128)(2,1)} %collective-permute-done.2), channel_id=1, source_target_pairs={{0,4},{4,0},{8,12},{12,8},{16,20},{20,16},{24,28},{28,24},{32,36},... | collective-permute-start | bytes 3145736 | tf_op jit(solution)/shard_map/ppermute | solution.py:33
  25.9 9.1 %collective-permute-start.1 = (bf16[2,256,256]{2,1,0:T(8,128)(2,1)S(1)}, bf16[2,256,256]{2,1,0:T(8,128)(2,1)S(1)}, u32[]{:S(2)}, u32[]{:S(2)}) collective-permute-start(bf16[2,256,256]{2,1,0:T(8,128)(2,1)S(1)} %convolution_convert_fusion.2), channel_id=1, source_target_pairs={{0,1},{1,0},{2,3},{3,2},{4,7},{5,6},{6,5},{7,4},{8,9},{9,8},{10,11... | collective-permute-start | bytes 786440 | tf_op jit(solution)/shard_map/ppermute | solution.py:40
  35.0 1.7 convolution_convert_fusion.1
  36.7 1.9 %collective-permute-start.3 = (bf16[2,256,256]{2,1,0:T(8,128)(2,1)S(1)}, bf16[2,256,256]{2,1,0:T(8,128)(2,1)S(1)}, u32[]{:S(2)}, u32[]{:S(2)}) collective-permute-start(bf16[2,256,256]{2,1,0:T(8,128)(2,1)S(1)} %convolution_convert_fusion.1), channel_id=1, source_target_pairs={{0,1},{1,0},{2,3},{3,2},{4,7},{5,6},{6,5},{7,4},{8,9},{9,8},{10,11... | collective-permute-start | bytes 786440 | tf_op jit(solution)/shard_map/ppermute | solution.py:40
  38.6 0.7 convolution_convert_fusion
  39.4 7.8 %collective-permute-start.6 = (bf16[2,256,512]{2,1,0:T(8,128)(2,1)S(1)}, bf16[2,256,512]{2,1,0:T(8,128)(2,1)S(1)}, u32[]{:S(2)}, u32[]{:S(2)}) collective-permute-start(bf16[2,256,512]{2,1,0:T(8,128)(2,1)S(1)} %convolution_convert_fusion), channel_id=1, source_target_pairs={{0,1},{1,0},{2,3},{3,2},{4,7},{5,6},{6,5},{7,4},{8,9},{9,8},{10,11... | collective-permute-start | bytes 1572872 | tf_op jit(solution)/shard_map/ppermute | solution.py:40
  47.2 3.4 %collective-permute-done.3 = bf16[2,256,256]{2,1,0:T(8,128)(2,1)S(1)} collective-permute-done((bf16[2,256,256]{2,1,0:T(8,128)(2,1)S(1)}, bf16[2,256,256]{2,1,0:T(8,128)(2,1)S(1)}, u32[]{:S(2)}, u32[]{:S(2)}) %collective-permute-start.3) | collective-permute-done | bytes 262176 | tf_op jit(solution)/shard_map/ppermute | solution.py:40
  50.6 1.7 fusion.6
  52.3 1.7 fusion.7
  54.0 32.1 %collective-permute-start.5 = (bf16[2,128,512]{2,1,0:T(8,128)(2,1)S(1)}, bf16[2,128,512]{2,1,0:T(8,128)(2,1)S(1)}, u32[]{:S(2)}, u32[]{:S(2)}) collective-permute-start(bf16[2,128,512]{2,1,0:T(8,128)(2,1)S(1)} %pad_maximum_fusion.4), channel_id=1, source_target_pairs={{0,3},{1,2},{2,1},{3,0},{4,5},{5,4},{6,7},{7,6},{8,11},{9,10},{10,... | collective-permute-start | bytes 786440 | tf_op jit(solution)/shard_map/ppermute | solution.py:40
  86.1 1.2 fusion.1
  87.3 5.3 %collective-permute-done.5 = bf16[2,128,512]{2,1,0:T(8,128)(2,1)S(1)} collective-permute-done((bf16[2,128,512]{2,1,0:T(8,128)(2,1)S(1)}, bf16[2,128,512]{2,1,0:T(8,128)(2,1)S(1)}, u32[]{:S(2)}, u32[]{:S(2)}) %collective-permute-start.5) | collective-permute-done | bytes 262176 | tf_op jit(solution)/shard_map/ppermute | solution.py:40
  92.6 1.7 fusion.5
  94.3 1.8 fusion.8
  96.3 0.2 convolution_convert_fusion.8
  96.5 1.9 %collective-permute-start.7 = (bf16[4,64,2,128]{3,1,2,0:T(8,128)(2,1)S(1)}, bf16[4,64,2,128]{3,1,2,0:T(8,128)(2,1)S(1)}, u32[]{:S(2)}, u32[]{:S(2)}) collective-permute-start(bf16[4,64,2,128]{3,1,2,0:T(8,128)(2,1)S(1)} %copy.25), channel_id=1, source_target_pairs={{0,4},{4,0},{8,12},{12,8},{16,20},{20,16},{24,28},{28,24},{32,36},... | collective-permute-start | bytes 393224 | tf_op jit(solution)/shard_map/ppermute | solution.py:33
  98.4 0.2 convolution_convert_fusion.7
  98.7 5.2 %collective-permute-start.8 = (bf16[4,64,2,128]{3,1,2,0:T(8,128)(2,1)S(1)}, bf16[4,64,2,128]{3,1,2,0:T(8,128)(2,1)S(1)}, u32[]{:S(2)}, u32[]{:S(2)}) collective-permute-start(bf16[4,64,2,128]{3,1,2,0:T(8,128)(2,1)S(1)} %copy.27), channel_id=1, source_target_pairs={{0,508},{4,8},{8,4},{12,16},{16,12},{20,24},{24,20},{28,32},{32,28... | collective-permute-start | bytes 393224 | tf_op jit(solution)/shard_map/ppermute | solution.py:33
  104.0 8.9 %collective-permute-start.11 = (bf16[2,128,512]{2,1,0:T(8,128)(2,1)}, bf16[2,128,512]{2,1,0:T(8,128)(2,1)S(1)}, u32[]{:S(2)}, u32[]{:S(2)}) collective-permute-start(bf16[2,128,512]{2,1,0:T(8,128)(2,1)} %fusion.1), channel_id=1, source_target_pairs={{0,3},{1,2},{2,1},{3,0},{4,5},{5,4},{6,7},{7,6},{8,11},{9,10},{10,... | collective-permute-start | bytes 786440 | tf_op jit(solution)/shard_map/ppermute | solution.py:40
  113.0 3.3 %collective-permute-start.9 = (bf16[2,128,2,128]{3,1,2,0:T(8,128)(2,1)S(1)}, bf16[2,128,2,128]{3,1,2,0:T(8,128)(2,1)S(1)}, u32[]{:S(2)}, u32[]{:S(2)}) collective-permute-start(bf16[2,128,2,128]{3,1,2,0:T(8,128)(2,1)S(1)} %slice.176), channel_id=1, source_target_pairs={{0,1},{1,0},{2,3},{3,2},{4,7},{5,6},{6,5},{7,4},{8,9},{9,8},{10,11... | collective-permute-start | bytes 393224 | tf_op jit(solution)/shard_map/ppermute | solution.py:40
  116.3 5.6 %collective-permute-done.11 = bf16[2,128,512]{2,1,0:T(8,128)(2,1)S(1)} collective-permute-done((bf16[2,128,512]{2,1,0:T(8,128)(2,1)}, bf16[2,128,512]{2,1,0:T(8,128)(2,1)S(1)}, u32[]{:S(2)}, u32[]{:S(2)}) %collective-permute-start.11) | collective-permute-done | bytes 262176 | tf_op jit(solution)/shard_map/ppermute | solution.py:40
  121.9 0.5 fusion.2
  122.4 0.3 convolution_convert_fusion.6
  122.7 0.3 convolution_convert_fusion.5
  123.1 15.3 %collective-permute-start.12 = (bf16[4,128,2,128]{3,1,2,0:T(8,128)(2,1)S(1)}, bf16[4,128,2,128]{3,1,2,0:T(8,128)(2,1)S(1)}, u32[]{:S(2)}, u32[]{:S(2)}) collective-permute-start(bf16[4,128,2,128]{3,1,2,0:T(8,128)(2,1)S(1)} %copy.36), channel_id=1, source_target_pairs={{0,8},{4,508},{8,16},{12,4},{16,24},{20,12},{24,32},{28,20},{32,40... | collective-permute-start | bytes 786440 | tf_op jit(solution)/shard_map/ppermute | solution.py:33
  138.4 8.3 %collective-permute-start.10 = (bf16[2,128,2,128]{3,1,2,0:T(8,128)(2,1)S(1)}, bf16[2,128,2,128]{3,1,2,0:T(8,128)(2,1)S(1)}, u32[]{:S(2)}, u32[]{:S(2)}) collective-permute-start(bf16[2,128,2,128]{3,1,2,0:T(8,128)(2,1)S(1)} %pad_maximum_fusion.12), channel_id=1, source_target_pairs={{0,3},{1,2},{2,1},{3,0},{4,5},{5,4},{6,7},{7,6},{8,11},{9,10},{10,... | collective-permute-start | bytes 393224 | tf_op jit(solution)/shard_map/ppermute | solution.py:40
  146.7 9.1 %collective-permute-done.10 = bf16[2,128,2,128]{3,1,2,0:T(8,128)(2,1)S(1)} collective-permute-done((bf16[2,128,2,128]{3,1,2,0:T(8,128)(2,1)S(1)}, bf16[2,128,2,128]{3,1,2,0:T(8,128)(2,1)S(1)}, u32[]{:S(2)}, u32[]{:S(2)}) %collective-permute-start.10) | collective-permute-done | bytes 131104 | tf_op jit(solution)/shard_map/ppermute | solution.py:40
  155.8 0.3 convolution_convert_fusion.4
  156.2 0.2 fusion.48
  156.4 0.2 fusion.49
  156.8 1.9 %collective-permute-start.13 = (bf16[2,128,2,128]{3,1,2,0:T(8,128)(2,1)S(1)}, bf16[2,128,2,128]{3,1,2,0:T(8,128)(2,1)S(1)}, u32[]{:S(2)}, u32[]{:S(2)}) collective-permute-start(bf16[2,128,2,128]{3,1,2,0:T(8,128)(2,1)S(1)} %slice.197), channel_id=1, source_target_pairs={{0,1},{1,0},{2,3},{3,2},{4,7},{5,6},{6,5},{7,4},{8,9},{9,8},{10,11... | collective-permute-start | bytes 393224 | tf_op jit(solution)/shard_map/ppermute | solution.py:40
  158.7 11.9 %collective-permute-done.13 = bf16[2,128,2,128]{3,1,2,0:T(8,128)(2,1)S(1)} collective-permute-done((bf16[2,128,2,128]{3,1,2,0:T(8,128)(2,1)S(1)}, bf16[2,128,2,128]{3,1,2,0:T(8,128)(2,1)S(1)}, u32[]{:S(2)}, u32[]{:S(2)}) %collective-permute-start.13) | collective-permute-done | bytes 131104 | tf_op jit(solution)/shard_map/ppermute | solution.py:40
  170.6 1.9 %collective-permute-start.14 = (bf16[2,128,2,128]{3,1,2,0:T(8,128)(2,1)S(1)}, bf16[2,128,2,128]{3,1,2,0:T(8,128)(2,1)S(1)}, u32[]{:S(2)}, u32[]{:S(2)}) collective-permute-start(bf16[2,128,2,128]{3,1,2,0:T(8,128)(2,1)S(1)} %pad_maximum_fusion.13), channel_id=1, source_target_pairs={{0,3},{1,2},{2,1},{3,0},{4,5},{5,4},{6,7},{7,6},{8,11},{9,10},{10,... | collective-permute-start | bytes 393224 | tf_op jit(solution)/shard_map/ppermute | solution.py:40
  172.7 8.7 %collective-permute-done.14 = bf16[2,128,2,128]{3,1,2,0:T(8,128)(2,1)S(1)} collective-permute-done((bf16[2,128,2,128]{3,1,2,0:T(8,128)(2,1)S(1)}, bf16[2,128,2,128]{3,1,2,0:T(8,128)(2,1)S(1)}, u32[]{:S(2)}, u32[]{:S(2)}) %collective-permute-start.14) | collective-permute-done | bytes 131104 | tf_op jit(solution)/shard_map/ppermute | solution.py:40
  181.4 0.3 convolution_convert_fusion.3
  182.1 2.0 %copy.35 = bf16[4,128,2,512]{3,2,1,0:T(2,128)(2,1)} copy(bf16[4,128,2,512]{3,1,2,0:T(8,128)(2,1)S(1)} %pad_maximum_fusion.3) | data formatting | bytes 2097152 | tf_op jit(solution)/shard_map/stack | solution.py:179
  (61 shorter events, 1.4 us)
Async XLA Ops:
  1.8 5.9 %copy-start.3 = (f32[512]{0:T(512)S(1)}, f32[512]{0:T(512)}, u32[]{:S(2)}) copy-start(f32[512]{0:T(512)} %param.6) | copy-start | bytes 6148
  3.0 8.7 %collective-permute-start = (bf16[2,256,1024]{2,1,0:T(8,128)(2,1)}, bf16[2,256,1024]{2,1,0:T(8,128)(2,1)}, u32[]{:S(2)}, u32[]{:S(2)}) collective-permute-start(bf16[2,256,1024]{2,1,0:T(8,128)(2,1)} %pad_maximum_fusion.2), channel_id=1, source_target_pairs={{0,4},{4,0},{8,12},{12,8},{16,20},{20,16},{24,28},{28,24},{32,36},... | collective-permute-start | bytes 3145736 | tf_op jit(solution)/shard_map/ppermute | solution.py:33
  4.9 16.4 %collective-permute-start.2 = (bf16[2,256,1024]{2,1,0:T(8,128)(2,1)}, bf16[2,256,1024]{2,1,0:T(8,128)(2,1)}, u32[]{:S(2)}, u32[]{:S(2)}) collective-permute-start(bf16[2,256,1024]{2,1,0:T(8,128)(2,1)} %pad_maximum_fusion.2), channel_id=1, source_target_pairs={{0,508},{4,8},{8,4},{12,16},{16,12},{20,24},{24,20},{28,32},{32,28... | collective-permute-start | bytes 3145736 | tf_op jit(solution)/shard_map/ppermute | solution.py:33
  7.7 1.3 copy-start
  11.6 14.2 %copy-start.2 = (bf16[4,64,256]{2,1,0:T(8,128)(2,1)S(1)}, bf16[4,64,256]{2,1,0:T(8,128)(2,1)}, u32[]{:S(2)}) copy-start(bf16[4,64,256]{2,1,0:T(8,128)(2,1)} %constant.80.clone) | copy-start | bytes 393220
  21.3 17.3 %collective-permute-start.4 = (bf16[2,256,1024]{2,1,0:T(8,128)(2,1)}, bf16[2,256,1024]{2,1,0:T(8,128)(2,1)S(1)}, u32[]{:S(2)}, u32[]{:S(2)}) collective-permute-start(bf16[2,256,1024]{2,1,0:T(8,128)(2,1)} %collective-permute-done.2), channel_id=1, source_target_pairs={{0,4},{4,0},{8,12},{12,8},{16,20},{20,16},{24,28},{28,24},{32,36},... | collective-permute-start | bytes 3145736 | tf_op jit(solution)/shard_map/ppermute | solution.py:33
  25.9 24.7 %collective-permute-start.1 = (bf16[2,256,256]{2,1,0:T(8,128)(2,1)S(1)}, bf16[2,256,256]{2,1,0:T(8,128)(2,1)S(1)}, u32[]{:S(2)}, u32[]{:S(2)}) collective-permute-start(bf16[2,256,256]{2,1,0:T(8,128)(2,1)S(1)} %convolution_convert_fusion.2), channel_id=1, source_target_pairs={{0,1},{1,0},{2,3},{3,2},{4,7},{5,6},{6,5},{7,4},{8,9},{9,8},{10,11... | collective-permute-start | bytes 786440 | tf_op jit(solution)/shard_map/ppermute | solution.py:40
  36.7 13.9 %collective-permute-start.3 = (bf16[2,256,256]{2,1,0:T(8,128)(2,1)S(1)}, bf16[2,256,256]{2,1,0:T(8,128)(2,1)S(1)}, u32[]{:S(2)}, u32[]{:S(2)}) collective-permute-start(bf16[2,256,256]{2,1,0:T(8,128)(2,1)S(1)} %convolution_convert_fusion.1), channel_id=1, source_target_pairs={{0,1},{1,0},{2,3},{3,2},{4,7},{5,6},{6,5},{7,4},{8,9},{9,8},{10,11... | collective-permute-start | bytes 786440 | tf_op jit(solution)/shard_map/ppermute | solution.py:40
  39.4 46.8 %collective-permute-start.6 = (bf16[2,256,512]{2,1,0:T(8,128)(2,1)S(1)}, bf16[2,256,512]{2,1,0:T(8,128)(2,1)S(1)}, u32[]{:S(2)}, u32[]{:S(2)}) collective-permute-start(bf16[2,256,512]{2,1,0:T(8,128)(2,1)S(1)} %convolution_convert_fusion), channel_id=1, source_target_pairs={{0,1},{1,0},{2,3},{3,2},{4,7},{5,6},{6,5},{7,4},{8,9},{9,8},{10,11... | collective-permute-start | bytes 1572872 | tf_op jit(solution)/shard_map/ppermute | solution.py:40
  54.0 38.6 %collective-permute-start.5 = (bf16[2,128,512]{2,1,0:T(8,128)(2,1)S(1)}, bf16[2,128,512]{2,1,0:T(8,128)(2,1)S(1)}, u32[]{:S(2)}, u32[]{:S(2)}) collective-permute-start(bf16[2,128,512]{2,1,0:T(8,128)(2,1)S(1)} %pad_maximum_fusion.4), channel_id=1, source_target_pairs={{0,3},{1,2},{2,1},{3,0},{4,5},{5,4},{6,7},{7,6},{8,11},{9,10},{10,... | collective-permute-start | bytes 786440 | tf_op jit(solution)/shard_map/ppermute | solution.py:40
  87.3 8.8 %copy-start.4 = (bf16[2]{0:T(256)(128)(2,1)S(1)}, bf16[2]{0:T(256)(128)(2,1)}, u32[]{:S(2)}) copy-start(bf16[2]{0:T(256)(128)(2,1)} %constant.82.clone) | copy-start | bytes 16
  94.3 9.5 %copy-start.1 = (bf16[4,128,512]{2,1,0:T(8,128)(2,1)S(1)}, bf16[4,128,512]{2,1,0:T(8,128)(2,1)}, u32[]{:S(2)}) copy-start(bf16[4,128,512]{2,1,0:T(8,128)(2,1)} %constant.81.clone) | copy-start | bytes 1572868
  96.5 16.4 %collective-permute-start.7 = (bf16[4,64,2,128]{3,1,2,0:T(8,128)(2,1)S(1)}, bf16[4,64,2,128]{3,1,2,0:T(8,128)(2,1)S(1)}, u32[]{:S(2)}, u32[]{:S(2)}) collective-permute-start(bf16[4,64,2,128]{3,1,2,0:T(8,128)(2,1)S(1)} %copy.25), channel_id=1, source_target_pairs={{0,4},{4,0},{8,12},{12,8},{16,20},{20,16},{24,28},{28,24},{32,36},... | collective-permute-start | bytes 393224 | tf_op jit(solution)/shard_map/ppermute | solution.py:33
  98.7 14.2 %collective-permute-start.8 = (bf16[4,64,2,128]{3,1,2,0:T(8,128)(2,1)S(1)}, bf16[4,64,2,128]{3,1,2,0:T(8,128)(2,1)S(1)}, u32[]{:S(2)}, u32[]{:S(2)}) collective-permute-start(bf16[4,64,2,128]{3,1,2,0:T(8,128)(2,1)S(1)} %copy.27), channel_id=1, source_target_pairs={{0,508},{4,8},{8,4},{12,16},{16,12},{20,24},{24,20},{28,32},{32,28... | collective-permute-start | bytes 393224 | tf_op jit(solution)/shard_map/ppermute | solution.py:33
  104.0 18.0 %collective-permute-start.11 = (bf16[2,128,512]{2,1,0:T(8,128)(2,1)}, bf16[2,128,512]{2,1,0:T(8,128)(2,1)S(1)}, u32[]{:S(2)}, u32[]{:S(2)}) collective-permute-start(bf16[2,128,512]{2,1,0:T(8,128)(2,1)} %fusion.1), channel_id=1, source_target_pairs={{0,3},{1,2},{2,1},{3,0},{4,5},{5,4},{6,7},{7,6},{8,11},{9,10},{10,... | collective-permute-start | bytes 786440 | tf_op jit(solution)/shard_map/ppermute | solution.py:40
  113.0 25.4 %collective-permute-start.9 = (bf16[2,128,2,128]{3,1,2,0:T(8,128)(2,1)S(1)}, bf16[2,128,2,128]{3,1,2,0:T(8,128)(2,1)S(1)}, u32[]{:S(2)}, u32[]{:S(2)}) collective-permute-start(bf16[2,128,2,128]{3,1,2,0:T(8,128)(2,1)S(1)} %slice.176), channel_id=1, source_target_pairs={{0,1},{1,0},{2,3},{3,2},{4,7},{5,6},{6,5},{7,4},{8,9},{9,8},{10,11... | collective-permute-start | bytes 393224 | tf_op jit(solution)/shard_map/ppermute | solution.py:40
  123.1 33.6 %collective-permute-start.12 = (bf16[4,128,2,128]{3,1,2,0:T(8,128)(2,1)S(1)}, bf16[4,128,2,128]{3,1,2,0:T(8,128)(2,1)S(1)}, u32[]{:S(2)}, u32[]{:S(2)}) collective-permute-start(bf16[4,128,2,128]{3,1,2,0:T(8,128)(2,1)S(1)} %copy.36), channel_id=1, source_target_pairs={{0,8},{4,508},{8,16},{12,4},{16,24},{20,12},{24,32},{28,20},{32,40... | collective-permute-start | bytes 786440 | tf_op jit(solution)/shard_map/ppermute | solution.py:33
  138.4 17.4 %collective-permute-start.10 = (bf16[2,128,2,128]{3,1,2,0:T(8,128)(2,1)S(1)}, bf16[2,128,2,128]{3,1,2,0:T(8,128)(2,1)S(1)}, u32[]{:S(2)}, u32[]{:S(2)}) collective-permute-start(bf16[2,128,2,128]{3,1,2,0:T(8,128)(2,1)S(1)} %pad_maximum_fusion.12), channel_id=1, source_target_pairs={{0,3},{1,2},{2,1},{3,0},{4,5},{5,4},{6,7},{7,6},{8,11},{9,10},{10,... | collective-permute-start | bytes 393224 | tf_op jit(solution)/shard_map/ppermute | solution.py:40
  156.8 13.8 %collective-permute-start.13 = (bf16[2,128,2,128]{3,1,2,0:T(8,128)(2,1)S(1)}, bf16[2,128,2,128]{3,1,2,0:T(8,128)(2,1)S(1)}, u32[]{:S(2)}, u32[]{:S(2)}) collective-permute-start(bf16[2,128,2,128]{3,1,2,0:T(8,128)(2,1)S(1)} %slice.197), channel_id=1, source_target_pairs={{0,1},{1,0},{2,3},{3,2},{4,7},{5,6},{6,5},{7,4},{8,9},{9,8},{10,11... | collective-permute-start | bytes 393224 | tf_op jit(solution)/shard_map/ppermute | solution.py:40
  170.6 10.8 %collective-permute-start.14 = (bf16[2,128,2,128]{3,1,2,0:T(8,128)(2,1)S(1)}, bf16[2,128,2,128]{3,1,2,0:T(8,128)(2,1)S(1)}, u32[]{:S(2)}, u32[]{:S(2)}) collective-permute-start(bf16[2,128,2,128]{3,1,2,0:T(8,128)(2,1)S(1)} %pad_maximum_fusion.13), channel_id=1, source_target_pairs={{0,3},{1,2},{2,1},{3,0},{4,5},{5,4},{6,7},{7,6},{8,11},{9,10},{10,... | collective-permute-start | bytes 393224 | tf_op jit(solution)/shard_map/ppermute | solution.py:40

commit v6 on v5

v6 whole, which is shorter than its diff:
```python
import math

import jax
import jax.numpy as jnp
import numpy as np
from jax import lax
from jax.experimental import pallas as pl
from jax.experimental.pallas import tpu as pltpu
from jax.sharding import PartitionSpec as P

BLOCK = 32


def owner_order(owners, blocks):
    count = owners * blocks * BLOCK
    rows = np.arange(count)
    owner, block, place = rows // (blocks * BLOCK), rows // BLOCK % blocks, rows % BLOCK
    column = (block * owners + owner) * BLOCK + place
    return np.eye(count, dtype=np.float32)[column].reshape(owners, blocks * BLOCK, count)


def local(kernel, shapes, *operands, scalars=0):
    vmem = pl.BlockSpec(memory_space=pltpu.VMEM)
    smem = pl.BlockSpec(memory_space=pltpu.SMEM)
    several = len(shapes) > 1
    out_shape = [jax.ShapeDtypeStruct(s, jnp.bfloat16) for s in shapes]
    return pl.pallas_call(
        kernel,
        out_shape=out_shape if several else out_shape[0],
        in_specs=[smem] * scalars + [vmem] * (len(operands) - scalars),
        out_specs=[vmem] * len(shapes) if several else vmem,
        compiler_params=pltpu.CompilerParams(vmem_limit_bytes=40 * 1024 * 1024),
        cost_estimate=pl.CostEstimate(flops=0, transcendentals=0, bytes_accessed=0),
    )(*operands)


def dots(left, right):
    return lax.dot_general(left, right, (((1,), (1,)), ((), ())), preferred_element_type=jnp.float32)


def low(value):
    return value.astype(jnp.bfloat16)


def wide(value):
    return value.astype(jnp.float32)


def left_kernel(order_ref, plain_ref, weight_ref, left_ref):
    points, transitions, depth = plain_ref.shape
    owners = order_ref.shape[0]
    blocks = transitions // (owners * BLOCK)
    weight = weight_ref[...]
    for point in range(points):
        for slot in range(owners):
            for block in range(blocks):
                start = pl.multiple_of((block * owners + order_ref[slot]) * BLOCK, BLOCK)
                rows = wide(plain_ref[point, pl.ds(start, BLOCK), :]) * weight
                place = pl.ds(block * BLOCK, BLOCK)
                left_ref[point, slot, 0, place, :] = low(rows)
                left_ref[point, slot, 1, place, : depth // 2] = low(-rows[:, depth // 2 :])
                left_ref[point, slot, 1, place, depth // 2 :] = low(rows[:, : depth // 2])


def away_kernel(left_ref, right_ref, out_ref):
    for point in range(out_ref.shape[0]):
        out_ref[point] = low(dots(left_ref[point], right_ref[point]))


def away_whole_kernel(left_ref, right_ref, out_ref):
    points, _, columns = out_ref.shape
    count = columns // points
    for point in range(points):
        for part in range(points):
            out_ref[point, :, part * count : (part + 1) * count] = low(dots(left_ref[point], right_ref[part]))


def second_pair_kernel(left_ref, mate_ref, next_ref, got_mate_ref, got_next_ref, out_ref):
    points, count, columns = out_ref.shape
    half = columns // 2
    for point in range(points):
        for part, (right_ref, got_ref) in enumerate(((mate_ref, got_mate_ref), (next_ref, got_next_ref))):
            total = dots(left_ref[point], right_ref[point]) + wide(got_ref[point, count:, :])
            out_ref[point, :, part * half : (part + 1) * half] = low(total)


def second_whole_kernel(left_ref, right_ref, got_ref, out_ref):
    points, count, columns = out_ref.shape
    half = columns // points
    for point in range(points):
        for part in range(points):
            span = pl.ds(part * half, half)
            total = dots(left_ref[point], right_ref[part]) + wide(got_ref[point, count:, span])
            out_ref[point, :, span] = low(total)


def picked(order_ref, slot, rows, owners, transitions):
    n = lax.broadcasted_iota(jnp.int32, (rows, transitions), 0)
    column = lax.broadcasted_iota(jnp.int32, (rows, transitions), 1)
    target = (n // BLOCK * owners + order_ref[slot]) * BLOCK + n % BLOCK
    return low(jnp.where(column == target, 1.0, 0.0))


def turn(order_ref, block_ref, span, back_ref, index):
    points, count, _ = block_ref.shape
    rows = count // 2
    owners = order_ref.shape[0]
    stacked = jnp.concatenate(
        [block_ref[point, p * rows : (p + 1) * rows, span] for p in range(2) for point in range(points)], axis=0
    )
    for slot in range(owners):
        pick = picked(order_ref, slot, rows, owners, stacked.shape[1])
        out = dots(pick, stacked)
        back_ref[slot, *index, 0] = low(out[:, : points * rows])
        back_ref[slot, *index, 1] = low(-out[:, points * rows :])


def finish_pair_kernel(
    order_ref, left_ref, mate_ref, next_ref, got_mate_ref, got_next_ref, late_ref,
    mate_block_ref, next_block_ref, mate_back_ref, next_back_ref,
):
    points, count, half = mate_block_ref.shape
    for part, (right_ref, got_ref, block_ref, back_ref) in enumerate(
        (
            (mate_ref, got_mate_ref, mate_block_ref, mate_back_ref),
            (next_ref, got_next_ref, next_block_ref, next_back_ref),
        )
    ):
        for point in range(points):
            total = dots(left_ref[point], right_ref[point]) + wide(got_ref[point, :count, :])
            block_ref[point] = low(total + wide(late_ref[point, :, part * half : (part + 1) * half]))
        turn(order_ref, block_ref, pl.ds(0, half), back_ref, ())


def finish_whole_kernel(order_ref, left_ref, right_ref, got_ref, late_ref, block_ref, back_ref):
    points, count, columns = block_ref.shape
    half = columns // points
    for part in range(points):
        span = pl.ds(part * half, half)
        for point in range(points):
            total = dots(left_ref[point], right_ref[part]) + wide(got_ref[point, :count, span])
            block_ref[point, :, span] = low(total + wide(late_ref[point, :, span]))
        turn(order_ref, block_ref, span, back_ref, (part,))


def body(pair_density, coulomb):
    points, transitions, _, g_local = pair_density.shape
    owners = lax.axis_size("own")
    groups = lax.axis_size("kp")
    blocks = transitions // (owners * BLOCK)
    rows = blocks * BLOCK
    depth = 2 * g_local
    scale = 1.0 / math.sqrt(g_local * owners)
    me = lax.axis_index("own")
    odd = lax.axis_index("kp") % 2 == 1
    parity = odd.astype(jnp.int32)

    def exchange_kp(value, partner):
        return lax.ppermute(value, "kp", [(i, partner(i) % groups) for i in range(groups)])

    def flips(i):
        return [1, 2, 3, 0] if i % 2 == 0 else [3, 2, 1, 0]

    def exchange(value, slot, partner):
        pairs = [
            (i * owners + o, partner(i) % groups * owners + (o ^ flips(i)[slot]))
            for i in range(groups)
            for o in range(owners)
        ]
        return lax.ppermute(value, ("kp", "own"), pairs)

    def exchange_own(value, first):
        return exchange(value, 0 if first else 2, lambda i: i)

    def mate(i):
        return i + 1 if i % 2 == 0 else i - 1

    def across(i):
        return i - 1 if i % 2 == 0 else i + 1

    def second_next(i):
        return i + 2 if i % 2 == 0 else i - 2

    near_flip, far_flip = 1 + 2 * parity, 3 - 2 * parity
    relative = jnp.stack([me ^ near_flip, me ^ 2, me ^ far_flip, me])
    swapped = jnp.stack([me ^ far_flip, me ^ 2, me ^ near_flip, me])

    plain = pair_density.reshape(points, transitions, depth)
    sent = jnp.stack([lax.dynamic_index_in_dim(plain, parity, 0, False), lax.dynamic_index_in_dim(plain, 1 - parity, 0, False)])
    mate_right = exchange_kp(sent, mate)
    next_right = exchange_kp(sent, across)

    weights = (jnp.concatenate([coulomb, coulomb]) * scale).reshape(1, depth)
    left = local(left_kernel, [(points, owners, 2, rows, depth)], relative, plain, weights, scalars=1)
    left_away = left[:, :2].reshape(points, 4 * rows, depth)
    left_second = left[:, 2].reshape(points, 2 * rows, depth)
    left_own = left[:, 3].reshape(points, 2 * rows, depth)

    left_away, left_second, left_own, mate_right = lax.optimization_barrier(
        (left_away, left_second, left_own, mate_right)
    )
    half_shape = (points, 4 * rows, transitions)
    whole_shape = (points, 4 * rows, points * transitions)
    late_shape = (points, 2 * rows, points * transitions)
    away_mate = local(away_kernel, [half_shape], left_away, mate_right)
    next_right, _ = lax.optimization_barrier((next_right, away_mate))
    got_mate = exchange_own(away_mate, True)
    far_right = exchange_kp(next_right, mate)
    away_next = local(away_kernel, [half_shape], left_away, next_right)
    far_right, _ = lax.optimization_barrier((far_right, away_next))
    got_next = exchange_own(away_next, True)
    away_far = local(away_whole_kernel, [whole_shape], left_away, far_right)
    got_mate, got_next, _ = lax.optimization_barrier((got_mate, got_next, away_far))
    got_far = exchange_own(away_far, True)

    second_pair = local(second_pair_kernel, [late_shape], left_second, mate_right, next_right, got_mate, got_next)
    late_pair = exchange_own(second_pair, False)
    second_far = local(second_whole_kernel, [late_shape], left_second, far_right, got_far)
    late_pair, _ = lax.optimization_barrier((late_pair, second_far))
    late_far = exchange_own(second_far, False)

    half_block = (points, 2 * rows, transitions)
    half_back = (owners, 2, rows, points * rows)
    block_mate, block_next, back_mate, back_next = local(
        finish_pair_kernel, [half_block, half_block, half_back, half_back],
        swapped, left_own, mate_right, next_right, got_mate, got_next, late_pair, scalars=1,
    )
    back_mate = exchange_kp(back_mate, mate)
    back_next = exchange_kp(back_next, across)
    block_far, back_far = local(
        finish_whole_kernel, [late_shape, (owners, points, 2, rows, points * rows)],
        relative, left_own, far_right, got_far, late_far, scalars=1,
    )
    back_far = [exchange(back_far[slot], slot, second_next) for slot in range(owners)]

    pick_rows = jnp.asarray(owner_order(owners, points * blocks), jnp.bfloat16)
    pick_rows = jnp.concatenate([lax.dynamic_index_in_dim(pick_rows, relative[slot], 0, False) for slot in range(owners)], axis=0)

    def natural(tiles):
        joined = jnp.concatenate(tiles, axis=-1)
        out = lax.dot_general(joined, pick_rows, (((3,), (0,)), ((), ())), preferred_element_type=jnp.float32)
        return low(out)

    back_pair = jnp.stack([back_mate, back_next], axis=1)
    first = exchange_own(back_pair[:2], True)
    then = exchange_own(jnp.stack([back_pair[2], first[1]]), False)
    back_pair = natural([first[0], then[1], then[0], back_pair[3]])
    back_far = natural(back_far)

    def mixed(block, back):
        block = block.reshape(points, 2, rows, transitions)
        back = back.reshape(2, rows, points, transitions)
        out = []
        for row_point in range(points):
            line = []
            for column_point in range(points):
                here = odd if row_point == column_point else ~odd
                line.append(jnp.where(here, block[row_point], back[:, :, column_point]))
            out.append(jnp.concatenate(line, axis=-1))
        return jnp.stack(out)

    with_mate = mixed(block_mate, back_pair[0])
    with_next = mixed(block_next, back_pair[1])
    here_far = block_far.reshape(points, 2, rows, points * transitions)
    here_far = jnp.where(odd, jnp.roll(here_far, transitions, axis=3), here_far)
    back_far = jnp.where(odd, back_far[::-1], back_far)
    out = jnp.stack(
        [
            jnp.where(odd, with_mate, with_next),
            jnp.where(odd, here_far, back_far),
            jnp.where(odd, with_next, with_mate),
            jnp.where(odd, back_far, here_far),
        ],
        axis=0,
    )
    return out.transpose(0, 1, 3, 2, 4).reshape(4, points * rows, 2, points * transitions)


def solution(mesh):
    placed = (P("kp", None, None, "own"), P("own"))
    return jax.shard_map(
        body,
        mesh=mesh,
        in_specs=placed,
        out_specs=P(None, ("kp", "own"), None, None),
        check_vma=False,
    )
```

time: 185 us -> 169 us (0.914)
  the two profiles are of different devices: /device:TPU:30 before, /device:TPU:120 now
where the time goes in v6:
time: 169 us; the launch traced here: 168 us
  starting transfers between devices  78.9 us (47%)
  waiting for transfers between devices  67.5 us (40%)
  Pallas kernels  11.4 us (7%)
  local copies, waits for them, and re-layouts  7.79 us (5%)
    ppermute x11, starting transfers between devices, exchange(): return lax.ppermute(value, ('kp', 'own'), pairs)  62.8 us
    ppermute x11, waiting for transfers between devices, exchange(): return lax.ppermute(value, ('kp', 'own'), pairs)  49.5 us
    ppermute x5, waiting for transfers between devices, exchange_kp(): lax.ppermute(value, 'kp', [(i, partner(i) % groups) for i in range(groups)])  18 us
    ppermute x5, starting transfers between devices, exchange_kp(): lax.ppermute(value, 'kp', [(i, partner(i) % groups) for i in range(groups)])  16.1 us
    pallas_call x8, Pallas kernels, local(): pl.pallas_call(kernel, out_shape=out_shape if several else out_shape[0],...  11.4 us
  transfers between devices with their start and end apart: 16, of which 5 were waited for; matrix products, arithmetic and copies ran while one was open for 2% of the time, Pallas kernels for 7%

profile of v6, /device:TPU:120, one launch (start us, length us, event | category | flops | bytes accessed | tf_op | source)
XLA Modules:
  0.0 168.3 jit_solution(1405942576020830760)
XLA Ops:
  0.0 1.8 %reshape.170.plain_ref = bf16[2,256,1024]{2,1,0:T(8,128)(2,1)S(1)} reshape(bf16[2,256,2,512]{3,2,1,0:T(2,128)(2,1)} %param.3) | data formatting | bytes 2097152 | tf_op jit(solution)/shard_map/reshape | solution.py:188
  1.8 0.0 copy-start.5
  1.8 0.1 constant_dynamic-slice_fusion.1
  1.9 1.1 pad_maximum_fusion
  3.0 1.9 %collective-permute-start = (bf16[2,256,1024]{2,1,0:T(8,128)(2,1)}, bf16[2,256,1024]{2,1,0:T(8,128)(2,1)S(1)}, u32[]{:S(2)}, u32[]{:S(2)}) collective-permute-start(bf16[2,256,1024]{2,1,0:T(8,128)(2,1)} %pad_maximum_fusion), channel_id=1, source_target_pairs={{0,4},{4,0},{8,12},{12,8},{16,20},{20,16},{24,28},{28,24},{32,36},... | collective-permute-start | bytes 3145736 | tf_op jit(solution)/shard_map/ppermute | solution.py:159
  4.9 4.3 %collective-permute-start.1 = (bf16[2,256,1024]{2,1,0:T(8,128)(2,1)}, bf16[2,256,1024]{2,1,0:T(8,128)(2,1)S(1)}, u32[]{:S(2)}, u32[]{:S(2)}) collective-permute-start(bf16[2,256,1024]{2,1,0:T(8,128)(2,1)} %pad_maximum_fusion), channel_id=1, source_target_pairs={{0,508},{4,8},{8,4},{12,16},{16,12},{20,24},{24,20},{28,32},{32,28... | collective-permute-start | bytes 3145736 | tf_op jit(solution)/shard_map/ppermute | solution.py:159
  9.2 0.1 add_add_fusion
  9.3 0.8 shard_map.37
  10.1 0.1 slice.118
  10.2 0.9 fusion.20
  11.1 0.5 shard_map.38
  11.5 11.8 %collective-permute-done.1.right_ref.next_ref = bf16[2,256,1024]{2,1,0:T(8,128)(2,1)S(1)} collective-permute-done((bf16[2,256,1024]{2,1,0:T(8,128)(2,1)}, bf16[2,256,1024]{2,1,0:T(8,128)(2,1)S(1)}, u32[]{:S(2)}, u32[]{:S(2)}) %collective-permute-start.1) | collective-permute-done | bytes 1048608 | tf_op jit(solution)/shard_map/ppermute | solution.py:159
  23.3 1.9 %collective-permute-start.4 = (bf16[2,256,1024]{2,1,0:T(8,128)(2,1)S(1)}, bf16[2,256,1024]{2,1,0:T(8,128)(2,1)S(1)}, u32[]{:S(2)}, u32[]{:S(2)}) collective-permute-start(bf16[2,256,1024]{2,1,0:T(8,128)(2,1)S(1)} %collective-permute-done.1.right_ref.next_ref), channel_id=1, source_target_pairs={{0,4},{4,0},{8,12},{12,8},{16,20},{20,16},{24,28},{28,24},{32,36},... | collective-permute-start | bytes 3145736 | tf_op jit(solution)/shard_map/ppermute | solution.py:159
  25.2 0.5 shard_map.39
  25.7 9.1 %collective-permute-start.2 = (bf16[2,256,256]{2,1,0:T(8,128)(2,1)S(1)}, bf16[2,256,256]{2,1,0:T(8,128)(2,1)S(1)}, u32[]{:S(2)}, u32[]{:S(2)}) collective-permute-start(bf16[2,256,256]{2,1,0:T(8,128)(2,1)S(1)} %shard_map.38), channel_id=1, source_target_pairs={{0,1},{1,0},{2,3},{3,2},{4,7},{5,6},{6,5},{7,4},{8,9},{9,8},{10,11... | collective-permute-start | bytes 786440 | tf_op jit(solution)/shard_map/ppermute | solution.py:170
  34.8 1.9 %collective-permute-start.3 = (bf16[2,256,256]{2,1,0:T(8,128)(2,1)S(1)}, bf16[2,256,256]{2,1,0:T(8,128)(2,1)S(1)}, u32[]{:S(2)}, u32[]{:S(2)}) collective-permute-start(bf16[2,256,256]{2,1,0:T(8,128)(2,1)S(1)} %shard_map.39), channel_id=1, source_target_pairs={{0,1},{1,0},{2,3},{3,2},{4,7},{5,6},{6,5},{7,4},{8,9},{9,8},{10,11... | collective-permute-start | bytes 786440 | tf_op jit(solution)/shard_map/ppermute | solution.py:170
  36.7 1.5 shard_map.40
  38.3 7.8 %collective-permute-start.6 = (bf16[2,256,512]{2,1,0:T(8,128)(2,1)}, bf16[2,256,512]{2,1,0:T(8,128)(2,1)}, u32[]{:S(2)}, u32[]{:S(2)}) collective-permute-start(bf16[2,256,512]{2,1,0:T(8,128)(2,1)} %shard_map.40), channel_id=1, source_target_pairs={{0,1},{1,0},{2,3},{3,2},{4,7},{5,6},{6,5},{7,4},{8,9},{9,8},{10,11... | collective-permute-start | bytes 1572872 | tf_op jit(solution)/shard_map/ppermute | solution.py:170
  46.1 28.4 %collective-permute-done.3.got_next_ref = bf16[2,256,256]{2,1,0:T(8,128)(2,1)S(1)} collective-permute-done((bf16[2,256,256]{2,1,0:T(8,128)(2,1)S(1)}, bf16[2,256,256]{2,1,0:T(8,128)(2,1)S(1)}, u32[]{:S(2)}, u32[]{:S(2)}) %collective-permute-start.3) | collective-permute-done | bytes 262176 | tf_op jit(solution)/shard_map/ppermute | solution.py:170
  74.5 1.5 shard_map.41
  76.1 5.0 %collective-permute-start.5 = (bf16[2,128,512]{2,1,0:T(8,128)(2,1)}, bf16[2,128,512]{2,1,0:T(8,128)(2,1)}, u32[]{:S(2)}, u32[]{:S(2)}) collective-permute-start(bf16[2,128,512]{2,1,0:T(8,128)(2,1)} %shard_map.41), channel_id=1, source_target_pairs={{0,3},{1,2},{2,1},{3,0},{4,5},{5,4},{6,7},{7,6},{8,11},{9,10},{10,... | collective-permute-start | bytes 786440 | tf_op jit(solution)/shard_map/ppermute | solution.py:170
  81.1 1.2 dynamic-slice_bitcast_fusion.3
  82.3 12.7 %collective-permute-done.6.got_ref = bf16[2,256,512]{2,1,0:T(8,128)(2,1)} collective-permute-done((bf16[2,256,512]{2,1,0:T(8,128)(2,1)}, bf16[2,256,512]{2,1,0:T(8,128)(2,1)}, u32[]{:S(2)}, u32[]{:S(2)}) %collective-permute-start.6) | collective-permute-done | bytes 524320 | tf_op jit(solution)/shard_map/ppermute | solution.py:170
  95.1 1.0 copy-done.2
  96.1 1.9 %shard_map.42 = bf16[2,128,512]{2,1,0:T(8,128)(2,1)S(1)} custom-call(bf16[2,128,1024]{2,1,0:T(8,128)(2,1)S(1)} %bitcast.96, bf16[2,256,1024]{2,1,0:T(8,128)(2,1)S(1)} %collective-permute-done.4.right_ref, bf16[2,256,512]{2,1,0:T(8,128)(2,1)} %collective-permute-done.6.got_ref), custom_call_target="tpu_custom_call" | custom-call | tf_op jit(solution)/shard_map/pallas_call | solution.py:27
  98.0 1.9 %collective-permute-start.11 = (bf16[2,128,512]{2,1,0:T(8,128)(2,1)S(1)}, bf16[2,128,512]{2,1,0:T(8,128)(2,1)S(1)}, u32[]{:S(2)}, u32[]{:S(2)}) collective-permute-start(bf16[2,128,512]{2,1,0:T(8,128)(2,1)S(1)} %shard_map.42), channel_id=1, source_target_pairs={{0,3},{1,2},{2,1},{3,0},{4,5},{5,4},{6,7},{7,6},{8,11},{9,10},{10,... | collective-permute-start | bytes 786440 | tf_op jit(solution)/shard_map/ppermute | solution.py:170
  99.9 2.3 %shard_map.43 = (bf16[2,128,256]{2,1,0:T(8,128)(2,1)S(1)}, bf16[2,128,256]{2,1,0:T(8,128)(2,1)S(1)}, bf16[4,2,64,128]{3,2,1,0:T(8,128)(2,1)S(1)}, bf16[4,2,64,128]{3,2,1,0:T(8,128)(2,1)S(1)}) custom-call(s32[4]{0:T(128)S(1)} %get-tuple-element.81.order_ref, bf16[2,128,1024]{2,1,0:T(8,128)(2,1)S(1)} %bitcast.93, ...), custom_call_target="tpu_custom_call" | custom-call | tf_op jit(solution)/shard_map/pallas_call | solution.py:27
  102.2 6.0 %collective-permute-start.8 = (bf16[4,2,64,128]{3,2,1,0:T(8,128)(2,1)S(1)}, bf16[4,2,64,128]{3,2,1,0:T(8,128)(2,1)S(1)}, u32[]{:S(2)}, u32[]{:S(2)}) collective-permute-start(bf16[4,2,64,128]{3,2,1,0:T(8,128)(2,1)S(1)} %get-tuple-element.31), channel_id=1, source_target_pairs={{0,508},{4,8},{8,4},{12,16},{16,12},{20,24},{24,20},{28,32},{32,28... | collective-permute-start | bytes 393224 | tf_op jit(solution)/shard_map/ppermute | solution.py:159
  108.3 1.9 %collective-permute-start.7 = (bf16[4,2,64,128]{3,2,1,0:T(8,128)(2,1)S(1)}, bf16[4,2,64,128]{3,2,1,0:T(8,128)(2,1)S(1)}, u32[]{:S(2)}, u32[]{:S(2)}) collective-permute-start(bf16[4,2,64,128]{3,2,1,0:T(8,128)(2,1)S(1)} %get-tuple-element.30), channel_id=1, source_target_pairs={{0,4},{4,0},{8,12},{12,8},{16,20},{20,16},{24,28},{28,24},{32,36},... | collective-permute-start | bytes 393224 | tf_op jit(solution)/shard_map/ppermute | solution.py:159
  110.2 6.2 %collective-permute-done.8 = bf16[4,2,64,128]{3,2,1,0:T(8,128)(2,1)S(1)} collective-permute-done((bf16[4,2,64,128]{3,2,1,0:T(8,128)(2,1)S(1)}, bf16[4,2,64,128]{3,2,1,0:T(8,128)(2,1)S(1)}, u32[]{:S(2)}, u32[]{:S(2)}) %collective-permute-start.8) | collective-permute-done | bytes 131104 | tf_op jit(solution)/shard_map/ppermute | solution.py:159
  116.5 1.9 %collective-permute-start.9 = (bf16[2,2,2,64,128]{4,3,2,1,0:T(8,128)(2,1)S(1)}, bf16[2,2,2,64,128]{4,3,2,1,0:T(8,128)(2,1)S(1)}, u32[]{:S(2)}, u32[]{:S(2)}) collective-permute-start(bf16[2,2,2,64,128]{4,3,2,1,0:T(8,128)(2,1)S(1)} %copy.19), channel_id=1, source_target_pairs={{0,1},{1,0},{2,3},{3,2},{4,7},{5,6},{6,5},{7,4},{8,9},{9,8},{10,11... | collective-permute-start | bytes 393224 | tf_op jit(solution)/shard_map/ppermute | solution.py:170
  118.4 0.0 collective-permute-done.11.late_ref
  118.4 2.4 %shard_map.44 = (bf16[2,128,512]{2,1,0:T(8,128)(2,1)S(1)}, bf16[4,2,2,64,128]{4,3,2,1,0:T(8,128)(2,1)S(1)}) custom-call(s32[4]{0:T(128)S(1)} %get-tuple-element.82.order_ref, bf16[2,128,1024]{2,1,0:T(8,128)(2,1)S(1)} %bitcast.94, bf16[2,256,1024]{2,1,0:T(8,128)(2,1)S(1)} %collective-permute-done.4.right_ref, ...), custom_call_target="tpu_custom_call" | custom-call | tf_op jit(solution)/shard_map/pallas_call | solution.py:27
  120.9 1.9 %collective-permute-start.12 = (bf16[2,2,64,128]{3,2,1,0:T(8,128)(2,1)S(1)}, bf16[2,2,64,128]{3,2,1,0:T(8,128)(2,1)S(1)}, u32[]{:S(2)}, u32[]{:S(2)}) collective-permute-start(bf16[2,2,64,128]{3,2,1,0:T(8,128)(2,1)S(1)} %get-tuple-element.53), channel_id=1, source_target_pairs={{0,9},{1,8},{2,11},{3,10},{4,511},{5,510},{6,509},{7,508},{8,17},{... | collective-permute-start | bytes 196616 | tf_op jit(solution)/shard_map/ppermute | solution.py:170
  122.8 12.1 %collective-permute-start.13 = (bf16[2,2,64,128]{3,2,1,0:T(8,128)(2,1)S(1)}, bf16[2,2,64,128]{3,2,1,0:T(8,128)(2,1)S(1)}, u32[]{:S(2)}, u32[]{:S(2)}) collective-permute-start(bf16[2,2,64,128]{3,2,1,0:T(8,128)(2,1)S(1)} %get-tuple-element.56), channel_id=1, source_target_pairs={{0,10},{1,11},{2,8},{3,9},{4,510},{5,511},{6,508},{7,509},{8,18},{... | collective-permute-start | bytes 196616 | tf_op jit(solution)/shard_map/ppermute | solution.py:170
  134.9 9.2 %collective-permute-start.14 = (bf16[2,2,64,128]{3,2,1,0:T(8,128)(2,1)S(1)}, bf16[2,2,64,128]{3,2,1,0:T(8,128)(2,1)S(1)}, u32[]{:S(2)}, u32[]{:S(2)}) collective-permute-start(bf16[2,2,64,128]{3,2,1,0:T(8,128)(2,1)S(1)} %get-tuple-element.55), channel_id=1, source_target_pairs={{0,11},{1,10},{2,9},{3,8},{4,509},{5,508},{6,511},{7,510},{8,19},{... | collective-permute-start | bytes 196616 | tf_op jit(solution)/shard_map/ppermute | solution.py:170
  144.1 9.9 %collective-permute-start.15 = (bf16[2,2,64,128]{3,2,1,0:T(8,128)(2,1)S(1)}, bf16[2,2,64,128]{3,2,1,0:T(8,128)(2,1)S(1)}, u32[]{:S(2)}, u32[]{:S(2)}) collective-permute-start(bf16[2,2,64,128]{3,2,1,0:T(8,128)(2,1)S(1)} %get-tuple-element.54), channel_id=1, source_target_pairs={{0,8},{1,9},{2,10},{3,11},{4,508},{5,509},{6,510},{7,511},{8,16},{... | collective-permute-start | bytes 196616 | tf_op jit(solution)/shard_map/ppermute | solution.py:170
  154.2 1.9 %collective-permute-start.10 = (bf16[2,2,2,64,128]{4,3,2,1,0:T(8,128)(2,1)S(1)}, bf16[2,2,2,64,128]{4,3,2,1,0:T(8,128)(2,1)S(1)}, u32[]{:S(2)}, u32[]{:S(2)}) collective-permute-start(bf16[2,2,2,64,128]{4,3,2,1,0:T(8,128)(2,1)S(1)} %pad_maximum_fusion.3), channel_id=1, source_target_pairs={{0,3},{1,2},{2,1},{3,0},{4,5},{5,4},{6,7},{7,6},{8,11},{9,10},{10,... | collective-permute-start | bytes 393224 | tf_op jit(solution)/shard_map/ppermute | solution.py:170
  156.1 0.3 convolution_convert_fusion
  156.5 0.1 select_bitcast_fusion.1
  156.6 8.3 %collective-permute-done.10 = bf16[2,2,2,64,128]{4,3,2,1,0:T(8,128)(2,1)S(1)} collective-permute-done((bf16[2,2,2,64,128]{4,3,2,1,0:T(8,128)(2,1)S(1)}, bf16[2,2,2,64,128]{4,3,2,1,0:T(8,128)(2,1)S(1)}, u32[]{:S(2)}, u32[]{:S(2)}) %collective-permute-start.10) | collective-permute-done | bytes 131104 | tf_op jit(solution)/shard_map/ppermute | solution.py:170
  165.0 0.3 convolution_convert_fusion.1
  165.3 0.2 fusion.24
  165.6 0.2 fusion.26
  165.9 0.1 broadcast_select_fusion.1
  166.0 0.1 maximum_bitcast_fusion
  166.1 0.1 copy.16
  166.2 2.1 %copy.17 = bf16[4,128,2,512]{3,2,1,0:T(2,128)(2,1)} copy(bf16[4,128,2,512]{3,1,2,0:T(8,128)(2,1)S(1)} %bitcast.99) | data formatting | bytes 2097152 | tf_op jit(solution)/shard_map/reshape | solution.py:276
  (40 shorter events, 0.4 us)
Async XLA Ops:
  1.8 7.5 %copy-start.5 = (f32[512]{0:T(512)S(1)}, f32[512]{0:T(512)}, u32[]{:S(2)}) copy-start(f32[512]{0:T(512)} %param.4) | copy-start | bytes 6148
  3.0 8.1 %collective-permute-start = (bf16[2,256,1024]{2,1,0:T(8,128)(2,1)}, bf16[2,256,1024]{2,1,0:T(8,128)(2,1)S(1)}, u32[]{:S(2)}, u32[]{:S(2)}) collective-permute-start(bf16[2,256,1024]{2,1,0:T(8,128)(2,1)} %pad_maximum_fusion), channel_id=1, source_target_pairs={{0,4},{4,0},{8,12},{12,8},{16,20},{20,16},{24,28},{28,24},{32,36},... | collective-permute-start | bytes 3145736 | tf_op jit(solution)/shard_map/ppermute | solution.py:159
  4.9 18.4 %collective-permute-start.1 = (bf16[2,256,1024]{2,1,0:T(8,128)(2,1)}, bf16[2,256,1024]{2,1,0:T(8,128)(2,1)S(1)}, u32[]{:S(2)}, u32[]{:S(2)}) collective-permute-start(bf16[2,256,1024]{2,1,0:T(8,128)(2,1)} %pad_maximum_fusion), channel_id=1, source_target_pairs={{0,508},{4,8},{8,4},{12,16},{16,12},{20,24},{24,20},{28,32},{32,28... | collective-permute-start | bytes 3145736 | tf_op jit(solution)/shard_map/ppermute | solution.py:159
  11.0 63.5 %copy-start.1 = (bf16[2,1,2,64,1024]{4,3,2,1,0:T(8,128)(2,1)}, bf16[2,1,2,64,1024]{4,3,2,1,0:T(8,128)(2,1)S(1)}, u32[]{:S(2)}) copy-start(bf16[2,1,2,64,1024]{4,3,2,1,0:T(8,128)(2,1)S(1)} %get-tuple-element.36) | copy-start | bytes 1572868
  23.3 13.4 %collective-permute-start.4 = (bf16[2,256,1024]{2,1,0:T(8,128)(2,1)S(1)}, bf16[2,256,1024]{2,1,0:T(8,128)(2,1)S(1)}, u32[]{:S(2)}, u32[]{:S(2)}) collective-permute-start(bf16[2,256,1024]{2,1,0:T(8,128)(2,1)S(1)} %collective-permute-done.1.right_ref.next_ref), channel_id=1, source_target_pairs={{0,4},{4,0},{8,12},{12,8},{16,20},{20,16},{24,28},{28,24},{32,36},... | collective-permute-start | bytes 3145736 | tf_op jit(solution)/shard_map/ppermute | solution.py:159
  25.7 48.8 %collective-permute-start.2 = (bf16[2,256,256]{2,1,0:T(8,128)(2,1)S(1)}, bf16[2,256,256]{2,1,0:T(8,128)(2,1)S(1)}, u32[]{:S(2)}, u32[]{:S(2)}) collective-permute-start(bf16[2,256,256]{2,1,0:T(8,128)(2,1)S(1)} %shard_map.38), channel_id=1, source_target_pairs={{0,1},{1,0},{2,3},{3,2},{4,7},{5,6},{6,5},{7,4},{8,9},{9,8},{10,11... | collective-permute-start | bytes 786440 | tf_op jit(solution)/shard_map/ppermute | solution.py:170
  34.8 39.7 %collective-permute-start.3 = (bf16[2,256,256]{2,1,0:T(8,128)(2,1)S(1)}, bf16[2,256,256]{2,1,0:T(8,128)(2,1)S(1)}, u32[]{:S(2)}, u32[]{:S(2)}) collective-permute-start(bf16[2,256,256]{2,1,0:T(8,128)(2,1)S(1)} %shard_map.39), channel_id=1, source_target_pairs={{0,1},{1,0},{2,3},{3,2},{4,7},{5,6},{6,5},{7,4},{8,9},{9,8},{10,11... | collective-permute-start | bytes 786440 | tf_op jit(solution)/shard_map/ppermute | solution.py:170
  38.3 56.8 %collective-permute-start.6 = (bf16[2,256,512]{2,1,0:T(8,128)(2,1)}, bf16[2,256,512]{2,1,0:T(8,128)(2,1)}, u32[]{:S(2)}, u32[]{:S(2)}) collective-permute-start(bf16[2,256,512]{2,1,0:T(8,128)(2,1)} %shard_map.40), channel_id=1, source_target_pairs={{0,1},{1,0},{2,3},{3,2},{4,7},{5,6},{6,5},{7,4},{8,9},{9,8},{10,11... | collective-permute-start | bytes 1572872 | tf_op jit(solution)/shard_map/ppermute | solution.py:170
  74.5 1.6 copy-start.3
  76.1 23.8 %collective-permute-start.5 = (bf16[2,128,512]{2,1,0:T(8,128)(2,1)}, bf16[2,128,512]{2,1,0:T(8,128)(2,1)}, u32[]{:S(2)}, u32[]{:S(2)}) collective-permute-start(bf16[2,128,512]{2,1,0:T(8,128)(2,1)} %shard_map.41), channel_id=1, source_target_pairs={{0,3},{1,2},{2,1},{3,0},{4,5},{5,4},{6,7},{7,6},{8,11},{9,10},{10,... | collective-permute-start | bytes 786440 | tf_op jit(solution)/shard_map/ppermute | solution.py:170
  81.1 18.8 %copy-start = (bf16[2,1,2,64,1024]{4,3,2,1,0:T(8,128)(2,1)S(1)}, bf16[2,1,2,64,1024]{4,3,2,1,0:T(8,128)(2,1)}, u32[]{:S(2)}) copy-start(bf16[2,1,2,64,1024]{4,3,2,1,0:T(8,128)(2,1)} %get-tuple-element.35) | copy-start | bytes 1572868
  81.1 18.8 %copy-start.4 = (bf16[2,256,256]{2,1,0:T(8,128)(2,1)S(1)}, bf16[2,256,256]{2,1,0:T(8,128)(2,1)}, u32[]{:S(2)}) copy-start(bf16[2,256,256]{2,1,0:T(8,128)(2,1)} %copy-done.3) | copy-start | bytes 786436
  95.0 1.0 copy-start.2
  98.0 20.5 %collective-permute-start.11 = (bf16[2,128,512]{2,1,0:T(8,128)(2,1)S(1)}, bf16[2,128,512]{2,1,0:T(8,128)(2,1)S(1)}, u32[]{:S(2)}, u32[]{:S(2)}) collective-permute-start(bf16[2,128,512]{2,1,0:T(8,128)(2,1)S(1)} %shard_map.42), channel_id=1, source_target_pairs={{0,3},{1,2},{2,1},{3,0},{4,5},{5,4},{6,7},{7,6},{8,11},{9,10},{10,... | collective-permute-start | bytes 786440 | tf_op jit(solution)/shard_map/ppermute | solution.py:170
  102.2 14.2 %collective-permute-start.8 = (bf16[4,2,64,128]{3,2,1,0:T(8,128)(2,1)S(1)}, bf16[4,2,64,128]{3,2,1,0:T(8,128)(2,1)S(1)}, u32[]{:S(2)}, u32[]{:S(2)}) collective-permute-start(bf16[4,2,64,128]{3,2,1,0:T(8,128)(2,1)S(1)} %get-tuple-element.31), channel_id=1, source_target_pairs={{0,508},{4,8},{8,4},{12,16},{16,12},{20,24},{24,20},{28,32},{32,28... | collective-permute-start | bytes 393224 | tf_op jit(solution)/shard_map/ppermute | solution.py:159
  108.3 8.2 %collective-permute-start.7 = (bf16[4,2,64,128]{3,2,1,0:T(8,128)(2,1)S(1)}, bf16[4,2,64,128]{3,2,1,0:T(8,128)(2,1)S(1)}, u32[]{:S(2)}, u32[]{:S(2)}) collective-permute-start(bf16[4,2,64,128]{3,2,1,0:T(8,128)(2,1)S(1)} %get-tuple-element.30), channel_id=1, source_target_pairs={{0,4},{4,0},{8,12},{12,8},{16,20},{20,16},{24,28},{28,24},{32,36},... | collective-permute-start | bytes 393224 | tf_op jit(solution)/shard_map/ppermute | solution.py:159
  116.5 37.7 %collective-permute-start.9 = (bf16[2,2,2,64,128]{4,3,2,1,0:T(8,128)(2,1)S(1)}, bf16[2,2,2,64,128]{4,3,2,1,0:T(8,128)(2,1)S(1)}, u32[]{:S(2)}, u32[]{:S(2)}) collective-permute-start(bf16[2,2,2,64,128]{4,3,2,1,0:T(8,128)(2,1)S(1)} %copy.19), channel_id=1, source_target_pairs={{0,1},{1,0},{2,3},{3,2},{4,7},{5,6},{6,5},{7,4},{8,9},{9,8},{10,11... | collective-permute-start | bytes 393224 | tf_op jit(solution)/shard_map/ppermute | solution.py:170
  120.9 35.2 %collective-permute-start.12 = (bf16[2,2,64,128]{3,2,1,0:T(8,128)(2,1)S(1)}, bf16[2,2,64,128]{3,2,1,0:T(8,128)(2,1)S(1)}, u32[]{:S(2)}, u32[]{:S(2)}) collective-permute-start(bf16[2,2,64,128]{3,2,1,0:T(8,128)(2,1)S(1)} %get-tuple-element.53), channel_id=1, source_target_pairs={{0,9},{1,8},{2,11},{3,10},{4,511},{5,510},{6,509},{7,508},{8,17},{... | collective-permute-start | bytes 196616 | tf_op jit(solution)/shard_map/ppermute | solution.py:170
  122.8 33.3 %collective-permute-start.13 = (bf16[2,2,64,128]{3,2,1,0:T(8,128)(2,1)S(1)}, bf16[2,2,64,128]{3,2,1,0:T(8,128)(2,1)S(1)}, u32[]{:S(2)}, u32[]{:S(2)}) collective-permute-start(bf16[2,2,64,128]{3,2,1,0:T(8,128)(2,1)S(1)} %get-tuple-element.56), channel_id=1, source_target_pairs={{0,10},{1,11},{2,8},{3,9},{4,510},{5,511},{6,508},{7,509},{8,18},{... | collective-permute-start | bytes 196616 | tf_op jit(solution)/shard_map/ppermute | solution.py:170
  134.9 21.2 %collective-permute-start.14 = (bf16[2,2,64,128]{3,2,1,0:T(8,128)(2,1)S(1)}, bf16[2,2,64,128]{3,2,1,0:T(8,128)(2,1)S(1)}, u32[]{:S(2)}, u32[]{:S(2)}) collective-permute-start(bf16[2,2,64,128]{3,2,1,0:T(8,128)(2,1)S(1)} %get-tuple-element.55), channel_id=1, source_target_pairs={{0,11},{1,10},{2,9},{3,8},{4,509},{5,508},{6,511},{7,510},{8,19},{... | collective-permute-start | bytes 196616 | tf_op jit(solution)/shard_map/ppermute | solution.py:170
  144.1 12.0 %collective-permute-start.15 = (bf16[2,2,64,128]{3,2,1,0:T(8,128)(2,1)S(1)}, bf16[2,2,64,128]{3,2,1,0:T(8,128)(2,1)S(1)}, u32[]{:S(2)}, u32[]{:S(2)}) collective-permute-start(bf16[2,2,64,128]{3,2,1,0:T(8,128)(2,1)S(1)} %get-tuple-element.54), channel_id=1, source_target_pairs={{0,8},{1,9},{2,10},{3,11},{4,508},{5,509},{6,510},{7,511},{8,16},{... | collective-permute-start | bytes 196616 | tf_op jit(solution)/shard_map/ppermute | solution.py:170
  154.2 10.8 %collective-permute-start.10 = (bf16[2,2,2,64,128]{4,3,2,1,0:T(8,128)(2,1)S(1)}, bf16[2,2,2,64,128]{4,3,2,1,0:T(8,128)(2,1)S(1)}, u32[]{:S(2)}, u32[]{:S(2)}) collective-permute-start(bf16[2,2,2,64,128]{4,3,2,1,0:T(8,128)(2,1)S(1)} %pad_maximum_fusion.3), channel_id=1, source_target_pairs={{0,3},{1,2},{2,1},{3,0},{4,5},{5,4},{6,7},{7,6},{8,11},{9,10},{10,... | collective-permute-start | bytes 393224 | tf_op jit(solution)/shard_map/ppermute | solution.py:170

commit v7 on v6

--- a/solution.py
+++ b/solution.py
@@ -48,7 +48,7 @@
 
 def left_kernel(order_ref, plain_ref, weight_ref, left_ref):
     points, transitions, depth = plain_ref.shape
-    owners = order_ref.shape[0]
+    owners = order_ref.shape[0] - 1
     blocks = transitions // (owners * BLOCK)
     weight = weight_ref[...]
     for point in range(points):
@@ -62,9 +62,14 @@
                 left_ref[point, slot, 1, place, depth // 2 :] = low(rows[:, : depth // 2])
 
 
-def away_kernel(left_ref, right_ref, out_ref):
+def agreeing(order_ref, point):
+    even = order_ref[order_ref.shape[0] - 1]
+    return point + even - 2 * even * point
+
+
+def away_kernel(order_ref, left_ref, right_ref, out_ref):
     for point in range(out_ref.shape[0]):
-        out_ref[point] = low(dots(left_ref[point], right_ref[point]))
+        out_ref[point] = low(dots(left_ref[point], right_ref[agreeing(order_ref, point)]))
 
 
 def away_whole_kernel(left_ref, right_ref, out_ref):
@@ -75,13 +80,11 @@
             out_ref[point, :, part * count : (part + 1) * count] = low(dots(left_ref[point], right_ref[part]))
 
 
-def second_pair_kernel(left_ref, mate_ref, next_ref, got_mate_ref, got_next_ref, out_ref):
-    points, count, columns = out_ref.shape
-    half = columns // 2
-    for point in range(points):
-        for part, (right_ref, got_ref) in enumerate(((mate_ref, got_mate_ref), (next_ref, got_next_ref))):
-            total = dots(left_ref[point], right_ref[point]) + wide(got_ref[point, count:, :])
-            out_ref[point, :, part * half : (part + 1) * half] = low(total)
+def second_kernel(order_ref, left_ref, right_ref, got_ref, out_ref):
+    points, count, _ = out_ref.shape
+    for point in range(points):
+        total = dots(left_ref[point], right_ref[agreeing(order_ref, point)])
+        out_ref[point] = low(total + wide(got_ref[point, count:, :]))
 
 
 def second_whole_kernel(left_ref, right_ref, got_ref, out_ref):
@@ -104,7 +107,7 @@
 def turn(order_ref, block_ref, span, back_ref, index):
     points, count, _ = block_ref.shape
     rows = count // 2
-    owners = order_ref.shape[0]
+    owners = order_ref.shape[0] - 1
     stacked = jnp.concatenate(
         [block_ref[point, p * rows : (p + 1) * rows, span] for p in range(2) for point in range(points)], axis=0
     )
@@ -115,21 +118,12 @@
         back_ref[slot, *index, 1] = low(-out[:, points * rows :])
 
 
-def finish_pair_kernel(
-    order_ref, left_ref, mate_ref, next_ref, got_mate_ref, got_next_ref, late_ref,
-    mate_block_ref, next_block_ref, mate_back_ref, next_back_ref,
-):
-    points, count, half = mate_block_ref.shape
-    for part, (right_ref, got_ref, block_ref, back_ref) in enumerate(
-        (
-            (mate_ref, got_mate_ref, mate_block_ref, mate_back_ref),
-            (next_ref, got_next_ref, next_block_ref, next_back_ref),
-        )
-    ):
-        for point in range(points):
-            total = dots(left_ref[point], right_ref[point]) + wide(got_ref[point, :count, :])
-            block_ref[point] = low(total + wide(late_ref[point, :, part * half : (part + 1) * half]))
-        turn(order_ref, block_ref, pl.ds(0, half), back_ref, ())
+def finish_kernel(order_ref, left_ref, right_ref, got_ref, late_ref, block_ref, back_ref):
+    points, count, columns = block_ref.shape
+    for point in range(points):
+        total = dots(left_ref[point], right_ref[agreeing(order_ref, point)]) + wide(got_ref[point, :count, :])
+        block_ref[point] = low(total + wide(late_ref[point]))
+    turn(order_ref, block_ref, pl.ds(0, columns), back_ref, ())
 
 
 def finish_whole_kernel(order_ref, left_ref, right_ref, got_ref, late_ref, block_ref, back_ref):
@@ -182,13 +176,12 @@
         return i + 2 if i % 2 == 0 else i - 2
 
     near_flip, far_flip = 1 + 2 * parity, 3 - 2 * parity
-    relative = jnp.stack([me ^ near_flip, me ^ 2, me ^ far_flip, me])
-    swapped = jnp.stack([me ^ far_flip, me ^ 2, me ^ near_flip, me])
+    relative = jnp.stack([me ^ near_flip, me ^ 2, me ^ far_flip, me, 1 - parity])
+    swapped = jnp.stack([me ^ far_flip, me ^ 2, me ^ near_flip, me, 1 - parity])
 
     plain = pair_density.reshape(points, transitions, depth)
-    sent = jnp.stack([lax.dynamic_index_in_dim(plain, parity, 0, False), lax.dynamic_index_in_dim(plain, 1 - parity, 0, False)])
-    mate_right = exchange_kp(sent, mate)
-    next_right = exchange_kp(sent, across)
+    mate_right = exchange_kp(plain, mate)
+    next_right = exchange_kp(plain, across)
 
     weights = (jnp.concatenate([coulomb, coulomb]) * scale).reshape(1, depth)
     left = local(left_kernel, [(points, owners, 2, rows, depth)], relative, plain, weights, scalars=1)
@@ -199,37 +192,47 @@
     left_away, left_second, left_own, mate_right = lax.optimization_barrier(
         (left_away, left_second, left_own, mate_right)
     )
-    half_shape = (points, 4 * rows, transitions)
-    whole_shape = (points, 4 * rows, points * transitions)
-    late_shape = (points, 2 * rows, points * transitions)
-    away_mate = local(away_kernel, [half_shape], left_away, mate_right)
-    next_right, _ = lax.optimization_barrier((next_right, away_mate))
+    half_away = [(points, 4 * rows, transitions)]
+    whole_away = [(points, 4 * rows, points * transitions)]
+    half_block = (points, 2 * rows, transitions)
+    whole_block = (points, 2 * rows, points * transitions)
+    half_back = (owners, 2, rows, points * rows)
+    whole_back = (owners, points, 2, rows, points * rows)
+
+    away_mate = local(away_kernel, half_away, relative, left_away, mate_right, scalars=1)
     got_mate = exchange_own(away_mate, True)
+    second_mate = local(second_kernel, [half_block], relative, left_second, mate_right, got_mate, scalars=1)
+    late_mate = exchange_own(second_mate, False)
+    next_right, _ = lax.optimization_barrier((next_right, second_mate))
     far_right = exchange_kp(next_right, mate)
-    away_next = local(away_kernel, [half_shape], left_away, next_right)
+    away_next = local(away_kernel, half_away, relative, left_away, next_right, scalars=1)
+    got_next = exchange_own(away_next, True)
     far_right, _ = lax.optimization_barrier((far_right, away_next))
-    got_next = exchange_own(away_next, True)
-    away_far = local(away_whole_kernel, [whole_shape], left_away, far_right)
-    got_mate, got_next, _ = lax.optimization_barrier((got_mate, got_next, away_far))
+    away_far = local(away_whole_kernel, whole_away, left_away, far_right)
     got_far = exchange_own(away_far, True)
-
-    second_pair = local(second_pair_kernel, [late_shape], left_second, mate_right, next_right, got_mate, got_next)
-    late_pair = exchange_own(second_pair, False)
-    second_far = local(second_whole_kernel, [late_shape], left_second, far_right, got_far)
-    late_pair, _ = lax.optimization_barrier((late_pair, second_far))
+    late_mate, _ = lax.optimization_barrier((late_mate, away_far))
+    block_mate, back_mate = local(
+        finish_kernel, [half_block, half_back], swapped, left_own, mate_right, got_mate, late_mate, scalars=1
+    )
+    got_next, _ = lax.optimization_barrier((got_next, back_mate))
+    back_mate = exchange_kp(back_mate, mate)
+    second_next_part = local(second_kernel, [half_block], relative, left_second, next_right, got_next, scalars=1)
+    late_next = exchange_own(second_next_part, False)
+    block_next, back_next = local(
+        finish_kernel, [half_block, half_back], swapped, left_own, next_right, got_next, late_next, scalars=1
+    )
+    got_far, _ = lax.optimization_barrier((got_far, back_next))
+    back_next = exchange_kp(back_next, across)
+    second_far = local(second_whole_kernel, [whole_block], left_second, far_right, got_far)
     late_far = exchange_own(second_far, False)
-
-    half_block = (points, 2 * rows, transitions)
-    half_back = (owners, 2, rows, points * rows)
-    block_mate, block_next, back_mate, back_next = local(
-        finish_pair_kernel, [half_block, half_block, half_back, half_back],
-        swapped, left_own, mate_right, next_right, got_mate, got_next, late_pair, scalars=1,
-    )
-    back_mate = exchange_kp(back_mate, mate)
-    back_next = exchange_kp(back_next, across)
+    back_pair = jnp.stack([back_mate, back_next], axis=1)
+    back_pair, _ = lax.optimization_barrier((back_pair, second_far))
+    first = exchange_own(back_pair[:2], True)
+    then = jnp.stack([back_pair[2], first[1]])
+    late_far, _ = lax.optimization_barrier((late_far, then))
+    then = exchange_own(then, False)
     block_far, back_far = local(
-        finish_whole_kernel, [late_shape, (owners, points, 2, rows, points * rows)],
-        relative, left_own, far_right, got_far, late_far, scalars=1,
+        finish_whole_kernel, [whole_block, whole_back], relative, left_own, far_right, got_far, late_far, scalars=1
     )
     back_far = [exchange(back_far[slot], slot, second_next) for slot in range(owners)]
 
@@ -241,9 +244,6 @@
         out = lax.dot_general(joined, pick_rows, (((3,), (0,)), ((), ())), preferred_element_type=jnp.float32)
         return low(out)
 
-    back_pair = jnp.stack([back_mate, back_next], axis=1)
-    first = exchange_own(back_pair[:2], True)
-    then = exchange_own(jnp.stack([back_pair[2], first[1]]), False)
     back_pair = natural([first[0], then[1], then[0], back_pair[3]])
     back_far = natural(back_far)
 
@@ -262,8 +262,6 @@
     with_mate = mixed(block_mate, back_pair[0])
     with_next = mixed(block_next, back_pair[1])
     here_far = block_far.reshape(points, 2, rows, points * transitions)
-    here_far = jnp.where(odd, jnp.roll(here_far, transitions, axis=3), here_far)
-    back_far = jnp.where(odd, back_far[::-1], back_far)
     out = jnp.stack(
         [
             jnp.where(odd, with_mate, with_next),

time: 169 us -> 184 us (1.089)
  the two profiles are of different devices: /device:TPU:120 before, /device:TPU:122 now
where the time goes in v7:
time: 184 us; the launch traced here: 183 us
  starting transfers between devices  120 us (65%)
  waiting for transfers between devices  41.4 us (22%)
  Pallas kernels  12.7 us (7%)
  local copies, waits for them, and re-layouts  7.78 us (4%)
    ppermute x12, starting transfers between devices, exchange(): return lax.ppermute(value, ('kp', 'own'), pairs)  101 us
    ppermute x12, waiting for transfers between devices, exchange(): return lax.ppermute(value, ('kp', 'own'), pairs)  38.8 us
    ppermute x5, starting transfers between devices, exchange_kp(): lax.ppermute(value, 'kp', [(i, partner(i) % groups) for i in range(groups)])  19 us
    pallas_call x10, Pallas kernels, local(): pl.pallas_call(kernel, out_shape=out_shape if several else out_shape[0],...  12.7 us
  transfers between devices with their start and end apart: 17, of which 6 were waited for; matrix products, arithmetic and copies ran while one was open for 2% of the time, Pallas kernels for 6%

profile of v7, /device:TPU:122, one launch (start us, length us, event | category | flops | bytes accessed | tf_op | source)
XLA Modules:
  0.0 183.4 jit_solution(13332811610250065022)
XLA Ops:
  0.0 2.6 %reshape.170.plain_ref = bf16[2,256,1024]{2,1,0:T(8,128)(2,1)} reshape(bf16[2,256,2,512]{3,2,1,0:T(2,128)(2,1)} %param.3) | data formatting | bytes 2097152 | tf_op jit(solution)/shard_map/reshape | solution.py:182
  2.6 1.9 %collective-permute-start = (bf16[2,256,1024]{2,1,0:T(8,128)(2,1)}, bf16[2,256,1024]{2,1,0:T(8,128)(2,1)S(1)}, u32[]{:S(2)}, u32[]{:S(2)}) collective-permute-start(bf16[2,256,1024]{2,1,0:T(8,128)(2,1)} %reshape.170.plain_ref), channel_id=1, source_target_pairs={{0,4},{4,0},{8,12},{12,8},{16,20},{20,16},{24,28},{28,24},{32,36},... | collective-permute-start | bytes 3145736 | tf_op jit(solution)/shard_map/ppermute | solution.py:153
  4.5 2.5 %collective-permute-start.3 = (bf16[2,256,1024]{2,1,0:T(8,128)(2,1)}, bf16[2,256,1024]{2,1,0:T(8,128)(2,1)S(1)}, u32[]{:S(2)}, u32[]{:S(2)}) collective-permute-start(bf16[2,256,1024]{2,1,0:T(8,128)(2,1)} %reshape.170.plain_ref), channel_id=1, source_target_pairs={{0,508},{4,8},{8,4},{12,16},{16,12},{20,24},{24,20},{28,32},{32,28... | collective-permute-start | bytes 3145736 | tf_op jit(solution)/shard_map/ppermute | solution.py:153
  7.1 0.1 stack.73.order_ref
  7.2 1.5 shard_map.37
  8.6 0.1 slice.108
  8.8 0.9 fusion.16
  9.7 1.0 shard_map.38
  10.7 9.1 %collective-permute-start.1 = (bf16[2,256,256]{2,1,0:T(8,128)(2,1)S(1)}, bf16[2,256,256]{2,1,0:T(8,128)(2,1)S(1)}, u32[]{:S(2)}, u32[]{:S(2)}) collective-permute-start(bf16[2,256,256]{2,1,0:T(8,128)(2,1)S(1)} %shard_map.38), channel_id=1, source_target_pairs={{0,1},{1,0},{2,3},{3,2},{4,7},{5,6},{6,5},{7,4},{8,9},{9,8},{10,11... | collective-permute-start | bytes 786440 | tf_op jit(solution)/shard_map/ppermute | solution.py:164
  19.8 11.0 %collective-permute-done.1.got_ref = bf16[2,256,256]{2,1,0:T(8,128)(2,1)S(1)} collective-permute-done((bf16[2,256,256]{2,1,0:T(8,128)(2,1)S(1)}, bf16[2,256,256]{2,1,0:T(8,128)(2,1)S(1)}, u32[]{:S(2)}, u32[]{:S(2)}) %collective-permute-start.1) | collective-permute-done | bytes 262176 | tf_op jit(solution)/shard_map/ppermute | solution.py:164
  30.8 1.0 shard_map.39
  31.8 4.7 %collective-permute-start.4 = (bf16[2,256,1024]{2,1,0:T(8,128)(2,1)S(1)}, bf16[2,256,1024]{2,1,0:T(8,128)(2,1)S(1)}, u32[]{:S(2)}, u32[]{:S(2)}) collective-permute-start(bf16[2,256,1024]{2,1,0:T(8,128)(2,1)S(1)} %collective-permute-done.3.right_ref), channel_id=1, source_target_pairs={{0,4},{4,0},{8,12},{12,8},{16,20},{20,16},{24,28},{28,24},{32,36},... | collective-permute-start | bytes 3145736 | tf_op jit(solution)/shard_map/ppermute | solution.py:153
  36.6 1.7 shard_map.40
  38.3 5.5 %collective-permute-start.6 = (bf16[2,256,256]{2,1,0:T(8,128)(2,1)}, bf16[2,256,256]{2,1,0:T(8,128)(2,1)S(1)}, u32[]{:S(2)}, u32[]{:S(2)}) collective-permute-start(bf16[2,256,256]{2,1,0:T(8,128)(2,1)} %shard_map.40), channel_id=1, source_target_pairs={{0,1},{1,0},{2,3},{3,2},{4,7},{5,6},{6,5},{7,4},{8,9},{9,8},{10,11... | collective-permute-start | bytes 786440 | tf_op jit(solution)/shard_map/ppermute | solution.py:164
  43.8 6.0 %collective-permute-start.2 = (bf16[2,128,256]{2,1,0:T(8,128)(2,1)S(1)}, bf16[2,128,256]{2,1,0:T(8,128)(2,1)}, u32[]{:S(2)}, u32[]{:S(2)}) collective-permute-start(bf16[2,128,256]{2,1,0:T(8,128)(2,1)S(1)} %shard_map.39), channel_id=1, source_target_pairs={{0,3},{1,2},{2,1},{3,0},{4,5},{5,4},{6,7},{7,6},{8,11},{9,10},{10,... | collective-permute-start | bytes 393224 | tf_op jit(solution)/shard_map/ppermute | solution.py:164
  49.8 0.1 stack.72.order_ref
  49.9 1.3 dynamic-slice_bitcast_fusion.3
  51.3 0.7 shard_map.41
  52.0 6.0 %collective-permute-start.9 = (bf16[2,256,512]{2,1,0:T(8,128)(2,1)S(1)}, bf16[2,256,512]{2,1,0:T(8,128)(2,1)S(1)}, u32[]{:S(2)}, u32[]{:S(2)}) collective-permute-start(bf16[2,256,512]{2,1,0:T(8,128)(2,1)S(1)} %shard_map.41), channel_id=1, source_target_pairs={{0,1},{1,0},{2,3},{3,2},{4,7},{5,6},{6,5},{7,4},{8,9},{9,8},{10,11... | collective-permute-start | bytes 1572872 | tf_op jit(solution)/shard_map/ppermute | solution.py:164
  58.0 10.2 %collective-permute-done.2.late_ref = bf16[2,128,256]{2,1,0:T(8,128)(2,1)} collective-permute-done((bf16[2,128,256]{2,1,0:T(8,128)(2,1)S(1)}, bf16[2,128,256]{2,1,0:T(8,128)(2,1)}, u32[]{:S(2)}, u32[]{:S(2)}) %collective-permute-start.2) | collective-permute-done | bytes 131104 | tf_op jit(solution)/shard_map/ppermute | solution.py:164
  68.2 1.7 shard_map.42
  69.8 1.9 %collective-permute-start.5 = (bf16[4,2,64,128]{3,2,1,0:T(8,128)(2,1)S(1)}, bf16[4,2,64,128]{3,2,1,0:T(8,128)(2,1)S(1)}, u32[]{:S(2)}, u32[]{:S(2)}) collective-permute-start(bf16[4,2,64,128]{3,2,1,0:T(8,128)(2,1)S(1)} %get-tuple-element.30), channel_id=1, source_target_pairs={{0,4},{4,0},{8,12},{12,8},{16,20},{20,16},{24,28},{28,24},{32,36},... | collective-permute-start | bytes 393224 | tf_op jit(solution)/shard_map/ppermute | solution.py:153
  71.8 1.0 shard_map.43
  72.8 8.7 %collective-permute-start.7 = (bf16[2,128,256]{2,1,0:T(8,128)(2,1)S(1)}, bf16[2,128,256]{2,1,0:T(8,128)(2,1)S(1)}, u32[]{:S(2)}, u32[]{:S(2)}) collective-permute-start(bf16[2,128,256]{2,1,0:T(8,128)(2,1)S(1)} %shard_map.43), channel_id=1, source_target_pairs={{0,3},{1,2},{2,1},{3,0},{4,5},{5,4},{6,7},{7,6},{8,11},{9,10},{10,... | collective-permute-start | bytes 393224 | tf_op jit(solution)/shard_map/ppermute | solution.py:164
  81.5 5.5 %collective-permute-done.7.late_ref = bf16[2,128,256]{2,1,0:T(8,128)(2,1)S(1)} collective-permute-done((bf16[2,128,256]{2,1,0:T(8,128)(2,1)S(1)}, bf16[2,128,256]{2,1,0:T(8,128)(2,1)S(1)}, u32[]{:S(2)}, u32[]{:S(2)}) %collective-permute-start.7) | collective-permute-done | bytes 131104 | tf_op jit(solution)/shard_map/ppermute | solution.py:164
  87.0 1.3 shard_map.44
  88.2 7.9 %collective-permute-start.8 = (bf16[4,2,64,128]{3,2,1,0:T(8,128)(2,1)S(1)}, bf16[4,2,64,128]{3,2,1,0:T(8,128)(2,1)S(1)}, u32[]{:S(2)}, u32[]{:S(2)}) collective-permute-start(bf16[4,2,64,128]{3,2,1,0:T(8,128)(2,1)S(1)} %get-tuple-element.32), channel_id=1, source_target_pairs={{0,508},{4,8},{8,4},{12,16},{16,12},{20,24},{24,20},{28,32},{32,28... | collective-permute-start | bytes 393224 | tf_op jit(solution)/shard_map/ppermute | solution.py:153
  96.1 2.6 %collective-permute-done.8 = bf16[4,2,64,128]{3,2,1,0:T(8,128)(2,1)S(1)} collective-permute-done((bf16[4,2,64,128]{3,2,1,0:T(8,128)(2,1)S(1)}, bf16[4,2,64,128]{3,2,1,0:T(8,128)(2,1)S(1)}, u32[]{:S(2)}, u32[]{:S(2)}) %collective-permute-start.8) | collective-permute-done | bytes 131104 | tf_op jit(solution)/shard_map/ppermute | solution.py:153
  98.8 0.8 shard_map.45
  99.6 10.4 %collective-permute-start.12 = (bf16[2,128,512]{2,1,0:T(8,128)(2,1)S(1)}, bf16[2,128,512]{2,1,0:T(8,128)(2,1)S(1)}, u32[]{:S(2)}, u32[]{:S(2)}) collective-permute-start(bf16[2,128,512]{2,1,0:T(8,128)(2,1)S(1)} %shard_map.45), channel_id=1, source_target_pairs={{0,3},{1,2},{2,1},{3,0},{4,5},{5,4},{6,7},{7,6},{8,11},{9,10},{10,... | collective-permute-start | bytes 786440 | tf_op jit(solution)/shard_map/ppermute | solution.py:164
  110.1 8.0 %collective-permute-start.10 = (bf16[2,2,2,64,128]{4,3,2,1,0:T(8,128)(2,1)S(1)}, bf16[2,2,2,64,128]{4,3,2,1,0:T(8,128)(2,1)S(1)}, u32[]{:S(2)}, u32[]{:S(2)}) collective-permute-start(bf16[2,2,2,64,128]{4,3,2,1,0:T(8,128)(2,1)S(1)} %slice.111), channel_id=1, source_target_pairs={{0,1},{1,0},{2,3},{3,2},{4,7},{5,6},{6,5},{7,4},{8,9},{9,8},{10,11... | collective-permute-start | bytes 393224 | tf_op jit(solution)/shard_map/ppermute | solution.py:164
  118.1 4.5 %collective-permute-done.10 = bf16[2,2,2,64,128]{4,3,2,1,0:T(8,128)(2,1)S(1)} collective-permute-done((bf16[2,2,2,64,128]{4,3,2,1,0:T(8,128)(2,1)S(1)}, bf16[2,2,2,64,128]{4,3,2,1,0:T(8,128)(2,1)S(1)}, u32[]{:S(2)}, u32[]{:S(2)}) %collective-permute-start.10) | collective-permute-done | bytes 131104 | tf_op jit(solution)/shard_map/ppermute | solution.py:164
  122.6 2.8 %collective-permute-start.11 = (bf16[2,2,2,64,128]{4,3,2,1,0:T(8,128)(2,1)S(1)}, bf16[2,2,2,64,128]{4,3,2,1,0:T(8,128)(2,1)S(1)}, u32[]{:S(2)}, u32[]{:S(2)}) collective-permute-start(bf16[2,2,2,64,128]{4,3,2,1,0:T(8,128)(2,1)S(1)} %pad_maximum_fusion.3), channel_id=1, source_target_pairs={{0,3},{1,2},{2,1},{3,0},{4,5},{5,4},{6,7},{7,6},{8,11},{9,10},{10,... | collective-permute-start | bytes 393224 | tf_op jit(solution)/shard_map/ppermute | solution.py:164
  125.4 1.9 %shard_map.46 = (bf16[2,128,512]{2,1,0:T(8,128)(2,1)S(1)}, bf16[4,2,2,64,128]{4,3,2,1,0:T(8,128)(2,1)S(1)}) custom-call(s32[5]{0:T(128)S(1)} %stack.73.order_ref, bf16[2,128,1024]{2,1,0:T(8,128)(2,1)S(1)} %bitcast.96, bf16[2,256,1024]{2,1,0:T(8,128)(2,1)S(1)} %collective-permute-done.4.right_ref, bf16[2,256,512]{2,1,0:T(8,128)(2,1)S(1)} %collective-permute-done.9.got_ref, ...), custom_call_target="tpu_custom_call" | custom-call | tf_op jit(solution)/shard_map/pallas_call | solution.py:27
  127.3 7.5 %collective-permute-start.16 = (bf16[2,2,64,128]{3,2,1,0:T(8,128)(2,1)S(1)}, bf16[2,2,64,128]{3,2,1,0:T(8,128)(2,1)S(1)}, u32[]{:S(2)}, u32[]{:S(2)}) collective-permute-start(bf16[2,2,64,128]{3,2,1,0:T(8,128)(2,1)S(1)} %get-tuple-element.52), channel_id=1, source_target_pairs={{0,8},{1,9},{2,10},{3,11},{4,508},{5,509},{6,510},{7,511},{8,16},{... | collective-permute-start | bytes 196616 | tf_op jit(solution)/shard_map/ppermute | solution.py:164
  134.8 6.5 %collective-permute-start.15 = (bf16[2,2,64,128]{3,2,1,0:T(8,128)(2,1)S(1)}, bf16[2,2,64,128]{3,2,1,0:T(8,128)(2,1)S(1)}, u32[]{:S(2)}, u32[]{:S(2)}) collective-permute-start(bf16[2,2,64,128]{3,2,1,0:T(8,128)(2,1)S(1)} %get-tuple-element.53), channel_id=1, source_target_pairs={{0,11},{1,10},{2,9},{3,8},{4,509},{5,508},{6,511},{7,510},{8,19},{... | collective-permute-start | bytes 196616 | tf_op jit(solution)/shard_map/ppermute | solution.py:164
  141.3 28.5 %collective-permute-start.14 = (bf16[2,2,64,128]{3,2,1,0:T(8,128)(2,1)S(1)}, bf16[2,2,64,128]{3,2,1,0:T(8,128)(2,1)S(1)}, u32[]{:S(2)}, u32[]{:S(2)}) collective-permute-start(bf16[2,2,64,128]{3,2,1,0:T(8,128)(2,1)S(1)} %get-tuple-element.54), channel_id=1, source_target_pairs={{0,10},{1,11},{2,8},{3,9},{4,510},{5,511},{6,508},{7,509},{8,18},{... | collective-permute-start | bytes 196616 | tf_op jit(solution)/shard_map/ppermute | solution.py:164
  169.8 2.2 %collective-permute-start.13 = (bf16[2,2,64,128]{3,2,1,0:T(8,128)(2,1)S(1)}, bf16[2,2,64,128]{3,2,1,0:T(8,128)(2,1)S(1)}, u32[]{:S(2)}, u32[]{:S(2)}) collective-permute-start(bf16[2,2,64,128]{3,2,1,0:T(8,128)(2,1)S(1)} %get-tuple-element.51), channel_id=1, source_target_pairs={{0,9},{1,8},{2,11},{3,10},{4,511},{5,510},{6,509},{7,508},{8,17},{... | collective-permute-start | bytes 196616 | tf_op jit(solution)/shard_map/ppermute | solution.py:164
  172.0 0.3 convolution_convert_fusion.1
  172.4 0.2 fusion.21
  172.7 0.2 fusion.19
  172.9 0.1 broadcast_select_fusion.3
  173.0 0.1 broadcast_select_fusion.1
  173.1 7.7 %collective-permute-done.13 = bf16[2,2,64,128]{3,2,1,0:T(8,128)(2,1)S(1)} collective-permute-done((bf16[2,2,64,128]{3,2,1,0:T(8,128)(2,1)S(1)}, bf16[2,2,64,128]{3,2,1,0:T(8,128)(2,1)S(1)}, u32[]{:S(2)}, u32[]{:S(2)}) %collective-permute-start.13) | collective-permute-done | bytes 65568 | tf_op jit(solution)/shard_map/ppermute | solution.py:164
  180.8 0.3 select_bitcast_fusion.1
  181.1 0.1 maximum_bitcast_fusion
  181.2 0.1 copy.16
  181.3 2.1 %copy.17 = bf16[4,128,2,512]{3,2,1,0:T(2,128)(2,1)} copy(bf16[4,128,2,512]{3,1,2,0:T(8,128)(2,1)S(1)} %bitcast.101) | data formatting | bytes 2097152 | tf_op jit(solution)/shard_map/reshape | solution.py:274
  (62 shorter events, 0.4 us)
Async XLA Ops:
  0.0 7.2 %copy-start.15 = (f32[512]{0:T(512)S(1)}, f32[512]{0:T(512)}, u32[]{:S(2)}) copy-start(f32[512]{0:T(512)} %param.4) | copy-start | bytes 6148
  2.6 7.1 %collective-permute-start = (bf16[2,256,1024]{2,1,0:T(8,128)(2,1)}, bf16[2,256,1024]{2,1,0:T(8,128)(2,1)S(1)}, u32[]{:S(2)}, u32[]{:S(2)}) collective-permute-start(bf16[2,256,1024]{2,1,0:T(8,128)(2,1)} %reshape.170.plain_ref), channel_id=1, source_target_pairs={{0,4},{4,0},{8,12},{12,8},{16,20},{20,16},{24,28},{28,24},{32,36},... | collective-permute-start | bytes 3145736 | tf_op jit(solution)/shard_map/ppermute | solution.py:153
  4.5 27.3 %collective-permute-start.3 = (bf16[2,256,1024]{2,1,0:T(8,128)(2,1)}, bf16[2,256,1024]{2,1,0:T(8,128)(2,1)S(1)}, u32[]{:S(2)}, u32[]{:S(2)}) collective-permute-start(bf16[2,256,1024]{2,1,0:T(8,128)(2,1)} %reshape.170.plain_ref), channel_id=1, source_target_pairs={{0,508},{4,8},{8,4},{12,16},{16,12},{20,24},{24,20},{28,32},{32,28... | collective-permute-start | bytes 3145736 | tf_op jit(solution)/shard_map/ppermute | solution.py:153
  9.6 22.1 %copy-start.3 = (bf16[2,1,2,64,1024]{4,3,2,1,0:T(8,128)(2,1)}, bf16[2,1,2,64,1024]{4,3,2,1,0:T(8,128)(2,1)S(1)}, u32[]{:S(2)}) copy-start(bf16[2,1,2,64,1024]{4,3,2,1,0:T(8,128)(2,1)S(1)} %get-tuple-element.40) | copy-start | bytes 1572868
  9.6 22.2 %copy-start = (bf16[2,256,1024]{2,1,0:T(8,128)(2,1)}, bf16[2,256,1024]{2,1,0:T(8,128)(2,1)S(1)}, u32[]{:S(2)}) copy-start(bf16[2,256,1024]{2,1,0:T(8,128)(2,1)S(1)} %collective-permute-done.right_ref) | copy-start | bytes 3145732
  10.7 20.1 %collective-permute-start.1 = (bf16[2,256,256]{2,1,0:T(8,128)(2,1)S(1)}, bf16[2,256,256]{2,1,0:T(8,128)(2,1)S(1)}, u32[]{:S(2)}, u32[]{:S(2)}) collective-permute-start(bf16[2,256,256]{2,1,0:T(8,128)(2,1)S(1)} %shard_map.38), channel_id=1, source_target_pairs={{0,1},{1,0},{2,3},{3,2},{4,7},{5,6},{6,5},{7,4},{8,9},{9,8},{10,11... | collective-permute-start | bytes 786440 | tf_op jit(solution)/shard_map/ppermute | solution.py:164
  30.8 7.6 %copy-start.5 = (bf16[2,256,256]{2,1,0:T(8,128)(2,1)}, bf16[2,256,256]{2,1,0:T(8,128)(2,1)S(1)}, u32[]{:S(2)}) copy-start(bf16[2,256,256]{2,1,0:T(8,128)(2,1)S(1)} %collective-permute-done.1.got_ref) | copy-start | bytes 786436
  31.8 19.4 %collective-permute-start.4 = (bf16[2,256,1024]{2,1,0:T(8,128)(2,1)S(1)}, bf16[2,256,1024]{2,1,0:T(8,128)(2,1)S(1)}, u32[]{:S(2)}, u32[]{:S(2)}) collective-permute-start(bf16[2,256,1024]{2,1,0:T(8,128)(2,1)S(1)} %collective-permute-done.3.right_ref), channel_id=1, source_target_pairs={{0,4},{4,0},{8,12},{12,8},{16,20},{20,16},{24,28},{28,24},{32,36},... | collective-permute-start | bytes 3145736 | tf_op jit(solution)/shard_map/ppermute | solution.py:153
  38.3 33.5 %collective-permute-start.6 = (bf16[2,256,256]{2,1,0:T(8,128)(2,1)}, bf16[2,256,256]{2,1,0:T(8,128)(2,1)S(1)}, u32[]{:S(2)}, u32[]{:S(2)}) collective-permute-start(bf16[2,256,256]{2,1,0:T(8,128)(2,1)} %shard_map.40), channel_id=1, source_target_pairs={{0,1},{1,0},{2,3},{3,2},{4,7},{5,6},{6,5},{7,4},{8,9},{9,8},{10,11... | collective-permute-start | bytes 786440 | tf_op jit(solution)/shard_map/ppermute | solution.py:164
  43.8 24.3 %collective-permute-start.2 = (bf16[2,128,256]{2,1,0:T(8,128)(2,1)S(1)}, bf16[2,128,256]{2,1,0:T(8,128)(2,1)}, u32[]{:S(2)}, u32[]{:S(2)}) collective-permute-start(bf16[2,128,256]{2,1,0:T(8,128)(2,1)S(1)} %shard_map.39), channel_id=1, source_target_pairs={{0,3},{1,2},{2,1},{3,0},{4,5},{5,4},{6,7},{7,6},{8,11},{9,10},{10,... | collective-permute-start | bytes 393224 | tf_op jit(solution)/shard_map/ppermute | solution.py:164
  49.9 18.3 %copy-start.1 = (bf16[2,256,1024]{2,1,0:T(8,128)(2,1)S(1)}, bf16[2,256,1024]{2,1,0:T(8,128)(2,1)}, u32[]{:S(2)}) copy-start(bf16[2,256,1024]{2,1,0:T(8,128)(2,1)} %copy-done) | copy-start | bytes 3145732
  49.9 18.3 %copy-start.2 = (bf16[2,1,2,64,1024]{4,3,2,1,0:T(8,128)(2,1)S(1)}, bf16[2,1,2,64,1024]{4,3,2,1,0:T(8,128)(2,1)}, u32[]{:S(2)}) copy-start(bf16[2,1,2,64,1024]{4,3,2,1,0:T(8,128)(2,1)} %get-tuple-element.39) | copy-start | bytes 1572868
  49.9 18.3 %copy-start.6 = (bf16[2,256,256]{2,1,0:T(8,128)(2,1)S(1)}, bf16[2,256,256]{2,1,0:T(8,128)(2,1)}, u32[]{:S(2)}) copy-start(bf16[2,256,256]{2,1,0:T(8,128)(2,1)} %copy-done.5) | copy-start | bytes 786436
  51.2 120.8 %copy-start.7 = (bf16[128,512]{1,0:T(8,128)(2,1)}, bf16[128,512]{1,0:T(8,128)(2,1)S(1)}, u32[]{:S(2)}) copy-start(bf16[128,512]{1,0:T(8,128)(2,1)S(1)} %get-tuple-element.45) | copy-start | bytes 393220
  51.2 120.8 %copy-start.9 = (bf16[128,512]{1,0:T(8,128)(2,1)}, bf16[128,512]{1,0:T(8,128)(2,1)S(1)}, u32[]{:S(2)}) copy-start(bf16[128,512]{1,0:T(8,128)(2,1)S(1)} %get-tuple-element.46) | copy-start | bytes 393220
  51.2 120.8 %copy-start.11 = (bf16[128,512]{1,0:T(8,128)(2,1)}, bf16[128,512]{1,0:T(8,128)(2,1)S(1)}, u32[]{:S(2)}) copy-start(bf16[128,512]{1,0:T(8,128)(2,1)S(1)} %get-tuple-element.47) | copy-start | bytes 393220
  51.2 120.8 %copy-start.13 = (bf16[128,512]{1,0:T(8,128)(2,1)}, bf16[128,512]{1,0:T(8,128)(2,1)S(1)}, u32[]{:S(2)}) copy-start(bf16[128,512]{1,0:T(8,128)(2,1)S(1)} %get-tuple-element.48) | copy-start | bytes 393220
  51.2 20.5 %copy-start.4 = (bf16[2,1,2,64,1024]{4,3,2,1,0:T(8,128)(2,1)S(1)}, bf16[2,1,2,64,1024]{4,3,2,1,0:T(8,128)(2,1)}, u32[]{:S(2)}) copy-start(bf16[2,1,2,64,1024]{4,3,2,1,0:T(8,128)(2,1)} %copy-done.3) | copy-start | bytes 1572868
  52.0 46.8 %collective-permute-start.9 = (bf16[2,256,512]{2,1,0:T(8,128)(2,1)S(1)}, bf16[2,256,512]{2,1,0:T(8,128)(2,1)S(1)}, u32[]{:S(2)}, u32[]{:S(2)}) collective-permute-start(bf16[2,256,512]{2,1,0:T(8,128)(2,1)S(1)} %shard_map.41), channel_id=1, source_target_pairs={{0,1},{1,0},{2,3},{3,2},{4,7},{5,6},{6,5},{7,4},{8,9},{9,8},{10,11... | collective-permute-start | bytes 1572872 | tf_op jit(solution)/shard_map/ppermute | solution.py:164
  69.8 26.3 %collective-permute-start.5 = (bf16[4,2,64,128]{3,2,1,0:T(8,128)(2,1)S(1)}, bf16[4,2,64,128]{3,2,1,0:T(8,128)(2,1)S(1)}, u32[]{:S(2)}, u32[]{:S(2)}) collective-permute-start(bf16[4,2,64,128]{3,2,1,0:T(8,128)(2,1)S(1)} %get-tuple-element.30), channel_id=1, source_target_pairs={{0,4},{4,0},{8,12},{12,8},{16,20},{20,16},{24,28},{28,24},{32,36},... | collective-permute-start | bytes 393224 | tf_op jit(solution)/shard_map/ppermute | solution.py:153
  72.8 14.1 %collective-permute-start.7 = (bf16[2,128,256]{2,1,0:T(8,128)(2,1)S(1)}, bf16[2,128,256]{2,1,0:T(8,128)(2,1)S(1)}, u32[]{:S(2)}, u32[]{:S(2)}) collective-permute-start(bf16[2,128,256]{2,1,0:T(8,128)(2,1)S(1)} %shard_map.43), channel_id=1, source_target_pairs={{0,3},{1,2},{2,1},{3,0},{4,5},{5,4},{6,7},{7,6},{8,11},{9,10},{10,... | collective-permute-start | bytes 393224 | tf_op jit(solution)/shard_map/ppermute | solution.py:164
  88.2 10.5 %collective-permute-start.8 = (bf16[4,2,64,128]{3,2,1,0:T(8,128)(2,1)S(1)}, bf16[4,2,64,128]{3,2,1,0:T(8,128)(2,1)S(1)}, u32[]{:S(2)}, u32[]{:S(2)}) collective-permute-start(bf16[4,2,64,128]{3,2,1,0:T(8,128)(2,1)S(1)} %get-tuple-element.32), channel_id=1, source_target_pairs={{0,508},{4,8},{8,4},{12,16},{16,12},{20,24},{24,20},{28,32},{32,28... | collective-permute-start | bytes 393224 | tf_op jit(solution)/shard_map/ppermute | solution.py:153
  99.6 25.8 %collective-permute-start.12 = (bf16[2,128,512]{2,1,0:T(8,128)(2,1)S(1)}, bf16[2,128,512]{2,1,0:T(8,128)(2,1)S(1)}, u32[]{:S(2)}, u32[]{:S(2)}) collective-permute-start(bf16[2,128,512]{2,1,0:T(8,128)(2,1)S(1)} %shard_map.45), channel_id=1, source_target_pairs={{0,3},{1,2},{2,1},{3,0},{4,5},{5,4},{6,7},{7,6},{8,11},{9,10},{10,... | collective-permute-start | bytes 786440 | tf_op jit(solution)/shard_map/ppermute | solution.py:164
  110.1 12.5 %collective-permute-start.10 = (bf16[2,2,2,64,128]{4,3,2,1,0:T(8,128)(2,1)S(1)}, bf16[2,2,2,64,128]{4,3,2,1,0:T(8,128)(2,1)S(1)}, u32[]{:S(2)}, u32[]{:S(2)}) collective-permute-start(bf16[2,2,2,64,128]{4,3,2,1,0:T(8,128)(2,1)S(1)} %slice.111), channel_id=1, source_target_pairs={{0,1},{1,0},{2,3},{3,2},{4,7},{5,6},{6,5},{7,4},{8,9},{9,8},{10,11... | collective-permute-start | bytes 393224 | tf_op jit(solution)/shard_map/ppermute | solution.py:164
  122.6 49.3 %collective-permute-start.11 = (bf16[2,2,2,64,128]{4,3,2,1,0:T(8,128)(2,1)S(1)}, bf16[2,2,2,64,128]{4,3,2,1,0:T(8,128)(2,1)S(1)}, u32[]{:S(2)}, u32[]{:S(2)}) collective-permute-start(bf16[2,2,2,64,128]{4,3,2,1,0:T(8,128)(2,1)S(1)} %pad_maximum_fusion.3), channel_id=1, source_target_pairs={{0,3},{1,2},{2,1},{3,0},{4,5},{5,4},{6,7},{7,6},{8,11},{9,10},{10,... | collective-permute-start | bytes 393224 | tf_op jit(solution)/shard_map/ppermute | solution.py:164
  127.3 45.7 %collective-permute-start.16 = (bf16[2,2,64,128]{3,2,1,0:T(8,128)(2,1)S(1)}, bf16[2,2,64,128]{3,2,1,0:T(8,128)(2,1)S(1)}, u32[]{:S(2)}, u32[]{:S(2)}) collective-permute-start(bf16[2,2,64,128]{3,2,1,0:T(8,128)(2,1)S(1)} %get-tuple-element.52), channel_id=1, source_target_pairs={{0,8},{1,9},{2,10},{3,11},{4,508},{5,509},{6,510},{7,511},{8,16},{... | collective-permute-start | bytes 196616 | tf_op jit(solution)/shard_map/ppermute | solution.py:164
  134.8 38.3 %collective-permute-start.15 = (bf16[2,2,64,128]{3,2,1,0:T(8,128)(2,1)S(1)}, bf16[2,2,64,128]{3,2,1,0:T(8,128)(2,1)S(1)}, u32[]{:S(2)}, u32[]{:S(2)}) collective-permute-start(bf16[2,2,64,128]{3,2,1,0:T(8,128)(2,1)S(1)} %get-tuple-element.53), channel_id=1, source_target_pairs={{0,11},{1,10},{2,9},{3,8},{4,509},{5,508},{6,511},{7,510},{8,19},{... | collective-permute-start | bytes 196616 | tf_op jit(solution)/shard_map/ppermute | solution.py:164
  141.3 31.8 %collective-permute-start.14 = (bf16[2,2,64,128]{3,2,1,0:T(8,128)(2,1)S(1)}, bf16[2,2,64,128]{3,2,1,0:T(8,128)(2,1)S(1)}, u32[]{:S(2)}, u32[]{:S(2)}) collective-permute-start(bf16[2,2,64,128]{3,2,1,0:T(8,128)(2,1)S(1)} %get-tuple-element.54), channel_id=1, source_target_pairs={{0,10},{1,11},{2,8},{3,9},{4,510},{5,511},{6,508},{7,509},{8,18},{... | collective-permute-start | bytes 196616 | tf_op jit(solution)/shard_map/ppermute | solution.py:164
  169.8 11.0 %collective-permute-start.13 = (bf16[2,2,64,128]{3,2,1,0:T(8,128)(2,1)S(1)}, bf16[2,2,64,128]{3,2,1,0:T(8,128)(2,1)S(1)}, u32[]{:S(2)}, u32[]{:S(2)}) collective-permute-start(bf16[2,2,64,128]{3,2,1,0:T(8,128)(2,1)S(1)} %get-tuple-element.51), channel_id=1, source_target_pairs={{0,9},{1,8},{2,11},{3,10},{4,511},{5,510},{6,509},{7,508},{8,17},{... | collective-permute-start | bytes 196616 | tf_op jit(solution)/shard_map/ppermute | solution.py:164
  172.6 8.2 %copy-start.8 = (bf16[128,512]{1,0:T(8,128)(2,1)S(1)}, bf16[128,512]{1,0:T(8,128)(2,1)}, u32[]{:S(2)}) copy-start(bf16[128,512]{1,0:T(8,128)(2,1)} %copy-done.7) | copy-start | bytes 393220
  172.6 8.2 %copy-start.10 = (bf16[128,512]{1,0:T(8,128)(2,1)S(1)}, bf16[128,512]{1,0:T(8,128)(2,1)}, u32[]{:S(2)}) copy-start(bf16[128,512]{1,0:T(8,128)(2,1)} %copy-done.9) | copy-start | bytes 393220
  172.6 8.1 %copy-start.12 = (bf16[128,512]{1,0:T(8,128)(2,1)S(1)}, bf16[128,512]{1,0:T(8,128)(2,1)}, u32[]{:S(2)}) copy-start(bf16[128,512]{1,0:T(8,128)(2,1)} %copy-done.11) | copy-start | bytes 393220
  172.6 8.1 %copy-start.14 = (bf16[128,512]{1,0:T(8,128)(2,1)S(1)}, bf16[128,512]{1,0:T(8,128)(2,1)}, u32[]{:S(2)}) copy-start(bf16[128,512]{1,0:T(8,128)(2,1)} %copy-done.13) | copy-start | bytes 393220

commit v8 on v7

--- a/solution.py
+++ b/solution.py
@@ -67,34 +67,33 @@
     return point + even - 2 * even * point
 
 
-def away_kernel(order_ref, left_ref, right_ref, out_ref):
-    for point in range(out_ref.shape[0]):
-        out_ref[point] = low(dots(left_ref[point], right_ref[agreeing(order_ref, point)]))
-
-
-def away_whole_kernel(left_ref, right_ref, out_ref):
+def pair_kernel(order_ref, left_ref, mate_ref, next_ref, out_ref):
+    _, points, count, columns = out_ref.shape
+    half = columns // 2
+    for slot in range(order_ref.shape[0] - 1):
+        for point in range(points):
+            rows = left_ref[point, slot].reshape(count, -1)
+            for part, right_ref in enumerate((mate_ref, next_ref)):
+                out_ref[order_ref[slot], point, :, part * half : (part + 1) * half] = low(
+                    dots(rows, right_ref[agreeing(order_ref, point)])
+                )
+
+
+def away_kernel(left_ref, right_ref, out_ref):
     points, _, columns = out_ref.shape
-    count = columns // points
+    half = columns // points
     for point in range(points):
         for part in range(points):
-            out_ref[point, :, part * count : (part + 1) * count] = low(dots(left_ref[point], right_ref[part]))
-
-
-def second_kernel(order_ref, left_ref, right_ref, got_ref, out_ref):
-    points, count, _ = out_ref.shape
-    for point in range(points):
-        total = dots(left_ref[point], right_ref[agreeing(order_ref, point)])
-        out_ref[point] = low(total + wide(got_ref[point, count:, :]))
-
-
-def second_whole_kernel(left_ref, right_ref, got_ref, out_ref):
+            out_ref[point, :, part * half : (part + 1) * half] = low(dots(left_ref[point], right_ref[part]))
+
+
+def second_kernel(left_ref, right_ref, got_ref, out_ref):
     points, count, columns = out_ref.shape
     half = columns // points
     for point in range(points):
         for part in range(points):
             span = pl.ds(part * half, half)
-            total = dots(left_ref[point], right_ref[part]) + wide(got_ref[point, count:, span])
-            out_ref[point, :, span] = low(total)
+            out_ref[point, :, span] = low(dots(left_ref[point], right_ref[part]) + wide(got_ref[point, count:, span]))
 
 
 def picked(order_ref, slot, rows, owners, transitions):
@@ -119,14 +118,6 @@
 
 
 def finish_kernel(order_ref, left_ref, right_ref, got_ref, late_ref, block_ref, back_ref):
-    points, count, columns = block_ref.shape
-    for point in range(points):
-        total = dots(left_ref[point], right_ref[agreeing(order_ref, point)]) + wide(got_ref[point, :count, :])
-        block_ref[point] = low(total + wide(late_ref[point]))
-    turn(order_ref, block_ref, pl.ds(0, columns), back_ref, ())
-
-
-def finish_whole_kernel(order_ref, left_ref, right_ref, got_ref, late_ref, block_ref, back_ref):
     points, count, columns = block_ref.shape
     half = columns // points
     for part in range(points):
@@ -135,6 +126,12 @@
             total = dots(left_ref[point], right_ref[part]) + wide(got_ref[point, :count, span])
             block_ref[point, :, span] = low(total + wide(late_ref[point, :, span]))
         turn(order_ref, block_ref, span, back_ref, (part,))
+
+
+def turn_kernel(order_ref, block_ref, mate_back_ref, next_back_ref):
+    half = block_ref.shape[2] // 2
+    turn(order_ref, block_ref, pl.ds(0, half), mate_back_ref, ())
+    turn(order_ref, block_ref, pl.ds(half, half), next_back_ref, ())
 
 
 def body(pair_density, coulomb):
@@ -192,49 +189,31 @@
     left_away, left_second, left_own, mate_right = lax.optimization_barrier(
         (left_away, left_second, left_own, mate_right)
     )
-    half_away = [(points, 4 * rows, transitions)]
-    whole_away = [(points, 4 * rows, points * transitions)]
-    half_block = (points, 2 * rows, transitions)
-    whole_block = (points, 2 * rows, points * transitions)
+    columns = points * transitions
     half_back = (owners, 2, rows, points * rows)
-    whole_back = (owners, points, 2, rows, points * rows)
-
-    away_mate = local(away_kernel, half_away, relative, left_away, mate_right, scalars=1)
-    got_mate = exchange_own(away_mate, True)
-    second_mate = local(second_kernel, [half_block], relative, left_second, mate_right, got_mate, scalars=1)
-    late_mate = exchange_own(second_mate, False)
-    next_right, _ = lax.optimization_barrier((next_right, second_mate))
+    pair = local(
+        pair_kernel, [(owners, points, 2 * rows, columns)], relative, left, mate_right, next_right, scalars=1
+    )
+    block_pair = lax.psum_scatter(pair.reshape(-1, columns), "own", scatter_dimension=0, tiled=True)
+    block_pair = block_pair.reshape(points, 2 * rows, columns)
     far_right = exchange_kp(next_right, mate)
-    away_next = local(away_kernel, half_away, relative, left_away, next_right, scalars=1)
-    got_next = exchange_own(away_next, True)
-    far_right, _ = lax.optimization_barrier((far_right, away_next))
-    away_far = local(away_whole_kernel, whole_away, left_away, far_right)
-    got_far = exchange_own(away_far, True)
-    late_mate, _ = lax.optimization_barrier((late_mate, away_far))
-    block_mate, back_mate = local(
-        finish_kernel, [half_block, half_back], swapped, left_own, mate_right, got_mate, late_mate, scalars=1
-    )
-    got_next, _ = lax.optimization_barrier((got_next, back_mate))
+    far_right, _ = lax.optimization_barrier((far_right, pair))
+    away = local(away_kernel, [(points, 4 * rows, columns)], left_away, far_right)
+    got = exchange_own(away, True)
+    second = local(second_kernel, [(points, 2 * rows, columns)], left_second, far_right, got)
+    late = exchange_own(second, False)
+    back_mate, back_next = local(turn_kernel, [half_back, half_back], swapped, block_pair, scalars=1)
     back_mate = exchange_kp(back_mate, mate)
-    second_next_part = local(second_kernel, [half_block], relative, left_second, next_right, got_next, scalars=1)
-    late_next = exchange_own(second_next_part, False)
-    block_next, back_next = local(
-        finish_kernel, [half_block, half_back], swapped, left_own, next_right, got_next, late_next, scalars=1
-    )
-    got_far, _ = lax.optimization_barrier((got_far, back_next))
     back_next = exchange_kp(back_next, across)
-    second_far = local(second_whole_kernel, [whole_block], left_second, far_right, got_far)
-    late_far = exchange_own(second_far, False)
     back_pair = jnp.stack([back_mate, back_next], axis=1)
-    back_pair, _ = lax.optimization_barrier((back_pair, second_far))
     first = exchange_own(back_pair[:2], True)
-    then = jnp.stack([back_pair[2], first[1]])
-    late_far, _ = lax.optimization_barrier((late_far, then))
-    then = exchange_own(then, False)
+    then = exchange_own(jnp.stack([back_pair[2], first[1]]), False)
     block_far, back_far = local(
-        finish_whole_kernel, [whole_block, whole_back], relative, left_own, far_right, got_far, late_far, scalars=1
+        finish_kernel, [(points, 2 * rows, columns), (owners, points, 2, rows, points * rows)],
+        relative, left_own, far_right, got, late, scalars=1,
     )
     back_far = [exchange(back_far[slot], slot, second_next) for slot in range(owners)]
+    block_mate, block_next = block_pair[..., :transitions], block_pair[..., transitions:]
 
     pick_rows = jnp.asarray(owner_order(owners, points * blocks), jnp.bfloat16)
     pick_rows = jnp.concatenate([lax.dynamic_index_in_dim(pick_rows, relative[slot], 0, False) for slot in range(owners)], axis=0)

time: 184 us -> 201 us (1.092)
  the two profiles are of different devices: /device:TPU:122 before, /device:TPU:24 now
where the time goes in v8:
time: 201 us; the launch traced here: 200 us
  starting transfers between devices  86.8 us (43%)
  waiting for transfers between devices  80.9 us (40%)
  between operations  13.8 us (7%)
  Pallas kernels  10.7 us (5%)
  local copies, waits for them, and re-layouts  6.85 us (3%)
    ppermute x8, waiting for transfers between devices, exchange(): return lax.ppermute(value, ('kp', 'own'), pairs)  67.9 us
    ppermute x8, starting transfers between devices, exchange(): return lax.ppermute(value, ('kp', 'own'), pairs)  66.6 us
    ppermute x5, starting transfers between devices, exchange_kp(): lax.ppermute(value, 'kp', [(i, partner(i) % groups) for i in range(groups)])  20.2 us
    ppermute x5, waiting for transfers between devices, exchange_kp(): lax.ppermute(value, 'kp', [(i, partner(i) % groups) for i in range(groups)])  13 us
    pallas_call x6, Pallas kernels, local(): pl.pallas_call(kernel, out_shape=out_shape if several else out_shape[0],...  10.7 us
  transfers between devices with their start and end apart: 14, of which 7 were waited for; matrix products, arithmetic and copies ran while one was open for 1% of the time, Pallas kernels for 5%

profile of v8, /device:TPU:24, one launch (start us, length us, event | category | flops | bytes accessed | tf_op | source)
XLA Modules:
  0.0 200.1 jit_solution(11060185220538072573)
XLA Ops:
  6.5 1.8 reshape.176.plain_ref
  8.3 8.3 %collective-permute-start.1 = (bf16[2,256,1024]{2,1,0:T(8,128)(2,1)S(1)}, bf16[2,256,1024]{2,1,0:T(8,128)(2,1)}, u32[]{:S(2)}, u32[]{:S(2)}) collective-permute-start(bf16[2,256,1024]{2,1,0:T(8,128)(2,1)S(1)} %reshape.176.plain_ref), channel_id=1, source_target_pairs={{0,508},{4,8},{8,4},{12,16},{16,12},{20,24},{24,20},{28,32},{32,28... | collective-permute-start | bytes 3145736 | tf_op jit(solution)/shard_map/ppermute | solution.py:150
  16.7 1.9 collective-permute-start
  18.7 0.1 stack.72.order_ref
  18.8 0.8 shard_map.37.left_ref
  19.5 9.8 %collective-permute-done.1.next_ref = bf16[2,256,1024]{2,1,0:T(8,128)(2,1)} collective-permute-done((bf16[2,256,1024]{2,1,0:T(8,128)(2,1)S(1)}, bf16[2,256,1024]{2,1,0:T(8,128)(2,1)}, u32[]{:S(2)}, u32[]{:S(2)}) %collective-permute-start.1) | collective-permute-done | bytes 1048608 | tf_op jit(solution)/shard_map/ppermute | solution.py:150
  29.4 1.9 collective-permute-start.6
  31.3 1.1 fusion.20
  32.4 0.1 slice.114
  32.5 5.5 %shard_map.38 = bf16[4,2,128,512]{3,2,1,0:T(8,128)(2,1)} custom-call(s32[5]{0:T(128)S(1)} %stack.72.order_ref, bf16[2,4,2,64,1024]{4,3,2,1,0:T(8,128)(2,1)S(1)} %shard_map.37.left_ref, bf16[2,256,1024]{2,1,0:T(8,128)(2,1)} %collective-permute-done.mate_ref, bf16[2,256,1024]{2,1,0:T(8,128)(2,1)} %collective-permute-done.1.next_ref), custom_call_target="tpu_custom_call" | custom-call | tf_op jit(solution)/shard_map/pallas_call | solution.py:27
  38.0 0.0 reduce-scatter.2.cloned.1.call-update
  38.0 0.0 collective-permute-done.6.right_ref
  38.0 0.7 shard_map.40
  38.8 9.1 %collective-permute-start.7 = (bf16[2,256,512]{2,1,0:T(8,128)(2,1)S(1)}, bf16[2,256,512]{2,1,0:T(8,128)(2,1)S(1)}, u32[]{:S(2)}, u32[]{:S(2)}) collective-permute-start(bf16[2,256,512]{2,1,0:T(8,128)(2,1)S(1)} %shard_map.40), channel_id=1, source_target_pairs={{0,1},{1,0},{2,3},{3,2},{4,7},{5,6},{6,5},{7,4},{8,9},{9,8},{10,11... | collective-permute-start | bytes 1572872 | tf_op jit(solution)/shard_map/ppermute | solution.py:161
  47.9 36.6 %collective-permute-done.7.got_ref = bf16[2,256,512]{2,1,0:T(8,128)(2,1)S(1)} collective-permute-done((bf16[2,256,512]{2,1,0:T(8,128)(2,1)S(1)}, bf16[2,256,512]{2,1,0:T(8,128)(2,1)S(1)}, u32[]{:S(2)}, u32[]{:S(2)}) %collective-permute-start.7) | collective-permute-done | bytes 524320 | tf_op jit(solution)/shard_map/ppermute | solution.py:161
  84.5 0.8 shard_map.41
  85.4 0.0 copy-start.4
  85.4 20.6 %collective-permute-start.8 = (bf16[2,128,512]{2,1,0:T(8,128)(2,1)S(1)}, bf16[2,128,512]{2,1,0:T(8,128)(2,1)S(1)}, u32[]{:S(2)}, u32[]{:S(2)}) collective-permute-start(bf16[2,128,512]{2,1,0:T(8,128)(2,1)S(1)} %shard_map.41), channel_id=1, source_target_pairs={{0,3},{1,2},{2,1},{3,0},{4,5},{5,4},{6,7},{7,6},{8,11},{9,10},{10,... | collective-permute-start | bytes 786440 | tf_op jit(solution)/shard_map/ppermute | solution.py:161
  106.0 13.8 %collective-permute-done.8.late_ref = bf16[2,128,512]{2,1,0:T(8,128)(2,1)S(1)} collective-permute-done((bf16[2,128,512]{2,1,0:T(8,128)(2,1)S(1)}, bf16[2,128,512]{2,1,0:T(8,128)(2,1)S(1)}, u32[]{:S(2)}, u32[]{:S(2)}) %collective-permute-start.8) | collective-permute-done | bytes 262176 | tf_op jit(solution)/shard_map/ppermute | solution.py:161
  119.7 1.9 shard_map.42
  121.7 7.7 %collective-permute-start.10 = (bf16[2,2,64,128]{3,2,1,0:T(8,128)(2,1)S(1)}, bf16[2,2,64,128]{3,2,1,0:T(8,128)(2,1)S(1)}, u32[]{:S(2)}, u32[]{:S(2)}) collective-permute-start(bf16[2,2,64,128]{3,2,1,0:T(8,128)(2,1)S(1)} %get-tuple-element.44), channel_id=1, source_target_pairs={{0,10},{1,11},{2,8},{3,9},{4,510},{5,511},{6,508},{7,509},{8,18},{... | collective-permute-start | bytes 196616 | tf_op jit(solution)/shard_map/ppermute | solution.py:161
  129.4 0.1 stack.73.order_ref
  129.5 7.7 %collective-permute-start.11 = (bf16[2,2,64,128]{3,2,1,0:T(8,128)(2,1)S(1)}, bf16[2,2,64,128]{3,2,1,0:T(8,128)(2,1)S(1)}, u32[]{:S(2)}, u32[]{:S(2)}) collective-permute-start(bf16[2,2,64,128]{3,2,1,0:T(8,128)(2,1)S(1)} %get-tuple-element.43), channel_id=1, source_target_pairs={{0,11},{1,10},{2,9},{3,8},{4,509},{5,508},{6,511},{7,510},{8,19},{... | collective-permute-start | bytes 196616 | tf_op jit(solution)/shard_map/ppermute | solution.py:161
  137.2 6.2 %collective-permute-start.12 = (bf16[2,2,64,128]{3,2,1,0:T(8,128)(2,1)S(1)}, bf16[2,2,64,128]{3,2,1,0:T(8,128)(2,1)S(1)}, u32[]{:S(2)}, u32[]{:S(2)}) collective-permute-start(bf16[2,2,64,128]{3,2,1,0:T(8,128)(2,1)S(1)} %get-tuple-element.42), channel_id=1, source_target_pairs={{0,8},{1,9},{2,10},{3,11},{4,508},{5,509},{6,510},{7,511},{8,16},{... | collective-permute-start | bytes 196616 | tf_op jit(solution)/shard_map/ppermute | solution.py:161
  143.4 4.2 %collective-permute-start.9 = (bf16[2,2,64,128]{3,2,1,0:T(8,128)(2,1)S(1)}, bf16[2,2,64,128]{3,2,1,0:T(8,128)(2,1)S(1)}, u32[]{:S(2)}, u32[]{:S(2)}) collective-permute-start(bf16[2,2,64,128]{3,2,1,0:T(8,128)(2,1)S(1)} %get-tuple-element.41), channel_id=1, source_target_pairs={{0,9},{1,8},{2,11},{3,10},{4,511},{5,510},{6,509},{7,508},{8,17},{... | collective-permute-start | bytes 196616 | tf_op jit(solution)/shard_map/ppermute | solution.py:161
  147.6 0.0 reduce-scatter.2.cloned.1.call-done
  147.7 0.9 copy-done.2
  148.6 1.0 shard_map.39
  149.6 1.9 collective-permute-start.2
  151.5 0.0 collective-permute-done.10
  151.5 6.1 %collective-permute-start.3 = (bf16[4,2,64,128]{3,2,1,0:T(8,128)(2,1)S(1)}, bf16[4,2,64,128]{3,2,1,0:T(8,128)(2,1)S(1)}, u32[]{:S(2)}, u32[]{:S(2)}) collective-permute-start(bf16[4,2,64,128]{3,2,1,0:T(8,128)(2,1)S(1)} %get-tuple-element.16), channel_id=1, source_target_pairs={{0,508},{4,8},{8,4},{12,16},{16,12},{20,24},{24,20},{28,32},{32,28... | collective-permute-start | bytes 393224 | tf_op jit(solution)/shard_map/ppermute | solution.py:150
  157.8 0.0 collective-permute-done.11
  157.8 1.4 collective-permute-done.9
  159.2 0.3 convolution_convert_fusion
  159.5 3.1 %collective-permute-done.3 = bf16[4,2,64,128]{3,2,1,0:T(8,128)(2,1)S(1)} collective-permute-done((bf16[4,2,64,128]{3,2,1,0:T(8,128)(2,1)S(1)}, bf16[4,2,64,128]{3,2,1,0:T(8,128)(2,1)S(1)}, u32[]{:S(2)}, u32[]{:S(2)}) %collective-permute-start.3) | collective-permute-done | bytes 131104 | tf_op jit(solution)/shard_map/ppermute | solution.py:150
  162.7 9.1 %collective-permute-start.4 = (bf16[2,2,2,64,128]{4,3,2,1,0:T(8,128)(2,1)S(1)}, bf16[2,2,2,64,128]{4,3,2,1,0:T(8,128)(2,1)S(1)}, u32[]{:S(2)}, u32[]{:S(2)}) collective-permute-start(bf16[2,2,2,64,128]{4,3,2,1,0:T(8,128)(2,1)S(1)} %copy.19), channel_id=1, source_target_pairs={{0,1},{1,0},{2,3},{3,2},{4,7},{5,6},{6,5},{7,4},{8,9},{9,8},{10,11... | collective-permute-start | bytes 393224 | tf_op jit(solution)/shard_map/ppermute | solution.py:161
  171.8 0.1 select_bitcast_fusion.1
  171.9 7.2 %collective-permute-done.4 = bf16[2,2,2,64,128]{4,3,2,1,0:T(8,128)(2,1)S(1)} collective-permute-done((bf16[2,2,2,64,128]{4,3,2,1,0:T(8,128)(2,1)S(1)}, bf16[2,2,2,64,128]{4,3,2,1,0:T(8,128)(2,1)S(1)}, u32[]{:S(2)}, u32[]{:S(2)}) %collective-permute-start.4) | collective-permute-done | bytes 131104 | tf_op jit(solution)/shard_map/ppermute | solution.py:161
  179.2 1.9 collective-permute-start.5
  181.1 8.8 %collective-permute-done.5 = bf16[2,2,2,64,128]{4,3,2,1,0:T(8,128)(2,1)S(1)} collective-permute-done((bf16[2,2,2,64,128]{4,3,2,1,0:T(8,128)(2,1)S(1)}, bf16[2,2,2,64,128]{4,3,2,1,0:T(8,128)(2,1)S(1)}, u32[]{:S(2)}, u32[]{:S(2)}) %collective-permute-start.5) | collective-permute-done | bytes 131104 | tf_op jit(solution)/shard_map/ppermute | solution.py:161
  189.9 0.3 convolution_convert_fusion.1
  190.3 0.2 fusion.23
  190.6 0.2 fusion.24
  190.7 0.1 broadcast_select_fusion.3
  190.9 0.1 broadcast_select_fusion.1
  191.0 0.1 maximum_bitcast_fusion
  191.1 0.1 copy.16
  191.2 2.1 %copy.17 = bf16[4,128,2,512]{3,2,1,0:T(2,128)(2,1)} copy(bf16[4,128,2,512]{3,1,2,0:T(8,128)(2,1)S(1)} %bitcast.99) | data formatting | bytes 2097152 | tf_op jit(solution)/shard_map/reshape | solution.py:253
  (31 shorter events, 0.3 us)
Async XLA Ops:
  6.5 12.2 %copy-start.5 = (f32[512]{0:T(512)S(1)}, f32[512]{0:T(512)}, u32[]{:S(2)}) copy-start(f32[512]{0:T(512)} %param.4) | copy-start | bytes 6148
  6.5 141.1 %reduce-scatter.2.cloned.1.call-start = ((), (), s32[]{:S(2)}) async-start(), calls=%async_computation.1 | async-start | bytes 1310720 | tf_op jit(solution)/shard_map/reduce_scatter | solution.py:197
  8.3 21.0 %collective-permute-start.1 = (bf16[2,256,1024]{2,1,0:T(8,128)(2,1)S(1)}, bf16[2,256,1024]{2,1,0:T(8,128)(2,1)}, u32[]{:S(2)}, u32[]{:S(2)}) collective-permute-start(bf16[2,256,1024]{2,1,0:T(8,128)(2,1)S(1)} %reshape.176.plain_ref), channel_id=1, source_target_pairs={{0,508},{4,8},{8,4},{12,16},{16,12},{20,24},{24,20},{28,32},{32,28... | collective-permute-start | bytes 3145736 | tf_op jit(solution)/shard_map/ppermute | solution.py:150
  16.7 15.8 %collective-permute-start = (bf16[2,256,1024]{2,1,0:T(8,128)(2,1)S(1)}, bf16[2,256,1024]{2,1,0:T(8,128)(2,1)}, u32[]{:S(2)}, u32[]{:S(2)}) collective-permute-start(bf16[2,256,1024]{2,1,0:T(8,128)(2,1)S(1)} %reshape.176.plain_ref), channel_id=1, source_target_pairs={{0,4},{4,0},{8,12},{12,8},{16,20},{20,16},{24,28},{28,24},{32,36},... | collective-permute-start | bytes 3145736 | tf_op jit(solution)/shard_map/ppermute | solution.py:150
  29.4 8.7 %collective-permute-start.6 = (bf16[2,256,1024]{2,1,0:T(8,128)(2,1)}, bf16[2,256,1024]{2,1,0:T(8,128)(2,1)S(1)}, u32[]{:S(2)}, u32[]{:S(2)}) collective-permute-start(bf16[2,256,1024]{2,1,0:T(8,128)(2,1)} %collective-permute-done.1.next_ref), channel_id=1, source_target_pairs={{0,4},{4,0},{8,12},{12,8},{16,20},{20,16},{24,28},{28,24},{32,36},... | collective-permute-start | bytes 3145736 | tf_op jit(solution)/shard_map/ppermute | solution.py:150
  38.0 46.5 %copy-start.1 = (bf16[2,1,2,64,1024]{4,3,2,1,0:T(8,128)(2,1)S(1)}, bf16[2,1,2,64,1024]{4,3,2,1,0:T(8,128)(2,1)}, u32[]{:S(2)}) copy-start(bf16[2,1,2,64,1024]{4,3,2,1,0:T(8,128)(2,1)} %get-tuple-element.24) | copy-start | bytes 1572868
  38.0 81.7 %copy-start = (bf16[2,1,2,64,1024]{4,3,2,1,0:T(8,128)(2,1)S(1)}, bf16[2,1,2,64,1024]{4,3,2,1,0:T(8,128)(2,1)}, u32[]{:S(2)}) copy-start(bf16[2,1,2,64,1024]{4,3,2,1,0:T(8,128)(2,1)} %get-tuple-element.23) | copy-start | bytes 1572868
  38.8 45.7 %collective-permute-start.7 = (bf16[2,256,512]{2,1,0:T(8,128)(2,1)S(1)}, bf16[2,256,512]{2,1,0:T(8,128)(2,1)S(1)}, u32[]{:S(2)}, u32[]{:S(2)}) collective-permute-start(bf16[2,256,512]{2,1,0:T(8,128)(2,1)S(1)} %shard_map.40), channel_id=1, source_target_pairs={{0,1},{1,0},{2,3},{3,2},{4,7},{5,6},{6,5},{7,4},{8,9},{9,8},{10,11... | collective-permute-start | bytes 1572872 | tf_op jit(solution)/shard_map/ppermute | solution.py:161
  85.4 72.3 %copy-start.4 = (bf16[4,128,512]{2,1,0:T(8,128)(2,1)S(1)}, bf16[4,128,512]{2,1,0:T(8,128)(2,1)}, u32[]{:S(2)}) copy-start(bf16[4,128,512]{2,1,0:T(8,128)(2,1)} %constant.41.clone) | copy-start | bytes 1572868
  85.4 34.4 %collective-permute-start.8 = (bf16[2,128,512]{2,1,0:T(8,128)(2,1)S(1)}, bf16[2,128,512]{2,1,0:T(8,128)(2,1)S(1)}, u32[]{:S(2)}, u32[]{:S(2)}) collective-permute-start(bf16[2,128,512]{2,1,0:T(8,128)(2,1)S(1)} %shard_map.41), channel_id=1, source_target_pairs={{0,3},{1,2},{2,1},{3,0},{4,5},{5,4},{6,7},{7,6},{8,11},{9,10},{10,... | collective-permute-start | bytes 786440 | tf_op jit(solution)/shard_map/ppermute | solution.py:161
  121.7 29.9 %collective-permute-start.10 = (bf16[2,2,64,128]{3,2,1,0:T(8,128)(2,1)S(1)}, bf16[2,2,64,128]{3,2,1,0:T(8,128)(2,1)S(1)}, u32[]{:S(2)}, u32[]{:S(2)}) collective-permute-start(bf16[2,2,64,128]{3,2,1,0:T(8,128)(2,1)S(1)} %get-tuple-element.44), channel_id=1, source_target_pairs={{0,10},{1,11},{2,8},{3,9},{4,510},{5,511},{6,508},{7,509},{8,18},{... | collective-permute-start | bytes 196616 | tf_op jit(solution)/shard_map/ppermute | solution.py:161
  129.5 28.3 %collective-permute-start.11 = (bf16[2,2,64,128]{3,2,1,0:T(8,128)(2,1)S(1)}, bf16[2,2,64,128]{3,2,1,0:T(8,128)(2,1)S(1)}, u32[]{:S(2)}, u32[]{:S(2)}) collective-permute-start(bf16[2,2,64,128]{3,2,1,0:T(8,128)(2,1)S(1)} %get-tuple-element.43), channel_id=1, source_target_pairs={{0,11},{1,10},{2,9},{3,8},{4,509},{5,508},{6,511},{7,510},{8,19},{... | collective-permute-start | bytes 196616 | tf_op jit(solution)/shard_map/ppermute | solution.py:161
  137.2 20.5 %collective-permute-start.12 = (bf16[2,2,64,128]{3,2,1,0:T(8,128)(2,1)S(1)}, bf16[2,2,64,128]{3,2,1,0:T(8,128)(2,1)S(1)}, u32[]{:S(2)}, u32[]{:S(2)}) collective-permute-start(bf16[2,2,64,128]{3,2,1,0:T(8,128)(2,1)S(1)} %get-tuple-element.42), channel_id=1, source_target_pairs={{0,8},{1,9},{2,10},{3,11},{4,508},{5,509},{6,510},{7,511},{8,16},{... | collective-permute-start | bytes 196616 | tf_op jit(solution)/shard_map/ppermute | solution.py:161
  143.4 15.8 %collective-permute-start.9 = (bf16[2,2,64,128]{3,2,1,0:T(8,128)(2,1)S(1)}, bf16[2,2,64,128]{3,2,1,0:T(8,128)(2,1)S(1)}, u32[]{:S(2)}, u32[]{:S(2)}) collective-permute-start(bf16[2,2,64,128]{3,2,1,0:T(8,128)(2,1)S(1)} %get-tuple-element.41), channel_id=1, source_target_pairs={{0,9},{1,8},{2,11},{3,10},{4,511},{5,510},{6,509},{7,508},{8,17},{... | collective-permute-start | bytes 196616 | tf_op jit(solution)/shard_map/ppermute | solution.py:161
  147.7 1.0 copy-start.2
  149.6 9.9 %collective-permute-start.2 = (bf16[4,2,64,128]{3,2,1,0:T(8,128)(2,1)S(1)}, bf16[4,2,64,128]{3,2,1,0:T(8,128)(2,1)S(1)}, u32[]{:S(2)}, u32[]{:S(2)}) collective-permute-start(bf16[4,2,64,128]{3,2,1,0:T(8,128)(2,1)S(1)} %get-tuple-element.15), channel_id=1, source_target_pairs={{0,4},{4,0},{8,12},{12,8},{16,20},{20,16},{24,28},{28,24},{32,36},... | collective-permute-start | bytes 393224 | tf_op jit(solution)/shard_map/ppermute | solution.py:150
  151.5 11.1 %collective-permute-start.3 = (bf16[4,2,64,128]{3,2,1,0:T(8,128)(2,1)S(1)}, bf16[4,2,64,128]{3,2,1,0:T(8,128)(2,1)S(1)}, u32[]{:S(2)}, u32[]{:S(2)}) collective-permute-start(bf16[4,2,64,128]{3,2,1,0:T(8,128)(2,1)S(1)} %get-tuple-element.16), channel_id=1, source_target_pairs={{0,508},{4,8},{8,4},{12,16},{16,12},{20,24},{24,20},{28,32},{32,28... | collective-permute-start | bytes 393224 | tf_op jit(solution)/shard_map/ppermute | solution.py:150
  159.2 21.9 %copy-start.3 = (bf16[256,512]{1,0:T(8,128)(2,1)S(1)}, bf16[256,512]{1,0:T(8,128)(2,1)}, u32[]{:S(2)}) copy-start(bf16[256,512]{1,0:T(8,128)(2,1)} %reduce-scatter.2.cloned.1.call-done) | copy-start | bytes 786436
  162.7 16.5 %collective-permute-start.4 = (bf16[2,2,2,64,128]{4,3,2,1,0:T(8,128)(2,1)S(1)}, bf16[2,2,2,64,128]{4,3,2,1,0:T(8,128)(2,1)S(1)}, u32[]{:S(2)}, u32[]{:S(2)}) collective-permute-start(bf16[2,2,2,64,128]{4,3,2,1,0:T(8,128)(2,1)S(1)} %copy.19), channel_id=1, source_target_pairs={{0,1},{1,0},{2,3},{3,2},{4,7},{5,6},{6,5},{7,4},{8,9},{9,8},{10,11... | collective-permute-start | bytes 393224 | tf_op jit(solution)/shard_map/ppermute | solution.py:161
  179.2 10.8 %collective-permute-start.5 = (bf16[2,2,2,64,128]{4,3,2,1,0:T(8,128)(2,1)S(1)}, bf16[2,2,2,64,128]{4,3,2,1,0:T(8,128)(2,1)S(1)}, u32[]{:S(2)}, u32[]{:S(2)}) collective-permute-start(bf16[2,2,2,64,128]{4,3,2,1,0:T(8,128)(2,1)S(1)} %pad_maximum_fusion.2), channel_id=1, source_target_pairs={{0,3},{1,2},{2,1},{3,0},{4,5},{5,4},{6,7},{7,6},{8,11},{9,10},{10,... | collective-permute-start | bytes 393224 | tf_op jit(solution)/shard_map/ppermute | solution.py:161
Sparse Core Ops, SparseCore 0:
  38.1 79.7 reduce-scatter.1

commit v9 on v8

--- a/solution.py
+++ b/solution.py
@@ -67,19 +67,17 @@
     return point + even - 2 * even * point
 
 
-def pair_kernel(order_ref, left_ref, mate_ref, next_ref, out_ref):
-    _, points, count, columns = out_ref.shape
+def away_pair_kernel(order_ref, left_ref, mate_ref, next_ref, out_ref):
+    points, _, columns = out_ref.shape
     half = columns // 2
-    for slot in range(order_ref.shape[0] - 1):
-        for point in range(points):
-            rows = left_ref[point, slot].reshape(count, -1)
-            for part, right_ref in enumerate((mate_ref, next_ref)):
-                out_ref[order_ref[slot], point, :, part * half : (part + 1) * half] = low(
-                    dots(rows, right_ref[agreeing(order_ref, point)])
-                )
-
-
-def away_kernel(left_ref, right_ref, out_ref):
+    for point in range(points):
+        for part, right_ref in enumerate((mate_ref, next_ref)):
+            out_ref[point, :, part * half : (part + 1) * half] = low(
+                dots(left_ref[point], right_ref[agreeing(order_ref, point)])
+            )
+
+
+def away_far_kernel(left_ref, right_ref, out_ref):
     points, _, columns = out_ref.shape
     half = columns // points
     for point in range(points):
@@ -87,51 +85,96 @@
             out_ref[point, :, part * half : (part + 1) * half] = low(dots(left_ref[point], right_ref[part]))
 
 
-def second_kernel(left_ref, right_ref, got_ref, out_ref):
-    points, count, columns = out_ref.shape
-    half = columns // points
-    for point in range(points):
-        for part in range(points):
-            span = pl.ds(part * half, half)
-            out_ref[point, :, span] = low(dots(left_ref[point], right_ref[part]) + wide(got_ref[point, count:, span]))
-
-
-def picked(order_ref, slot, rows, owners, transitions):
+def picked(order_ref, slots, rows, owners, transitions):
     n = lax.broadcasted_iota(jnp.int32, (rows, transitions), 0)
     column = lax.broadcasted_iota(jnp.int32, (rows, transitions), 1)
-    target = (n // BLOCK * owners + order_ref[slot]) * BLOCK + n % BLOCK
-    return low(jnp.where(column == target, 1.0, 0.0))
-
-
-def turn(order_ref, block_ref, span, back_ref, index):
-    points, count, _ = block_ref.shape
+    target = (n // BLOCK * owners) * BLOCK + n % BLOCK
+    return jnp.concatenate(
+        [low(jnp.where(column == target + order_ref[slot] * BLOCK, 1.0, 0.0)) for slot in slots], axis=0
+    )
+
+
+def second_part(order_ref, second_left, own_left, right, got_ref, point, part, out_ref):
+    count = out_ref.shape[1]
+    half = right.shape[0]
+    owners = order_ref.shape[0] - 1
+    span = pl.ds(part * half, half)
+    out_ref[point, :, span] = low(dots(second_left, right) + wide(got_ref[point, count:, span]))
+    own = low(dots(own_left, right) + wide(got_ref[point, :count, span]))
+    pick = picked(order_ref, (2, 1), count // 2, owners, half)
+    out_ref[point, :, pl.ds(2 * half + part * count, count)] = low(dots(own, pick))
+
+
+def second_pair_kernel(order_ref, second_left_ref, own_left_ref, mate_ref, next_ref, got_ref, out_ref):
+    for point in range(out_ref.shape[0]):
+        for part, right_ref in enumerate((mate_ref, next_ref)):
+            right = right_ref[agreeing(order_ref, point)]
+            second_part(order_ref, second_left_ref[point], own_left_ref[point], right, got_ref, point, part, out_ref)
+
+
+def second_far_kernel(order_ref, second_left_ref, own_left_ref, right_ref, got_ref, out_ref):
+    for point in range(out_ref.shape[0]):
+        for part in range(out_ref.shape[0]):
+            second_part(
+                order_ref, second_left_ref[point], own_left_ref[point], right_ref[part], got_ref, point, part, out_ref
+            )
+
+
+def turned_part(order_ref, block_ref, second_ref, late_ref, part, same_ref, first_ref, index):
+    points, count, columns = block_ref.shape
+    half = columns // 2
     rows = count // 2
     owners = order_ref.shape[0] - 1
-    stacked = jnp.concatenate(
+    span = pl.ds(part * half, half)
+    own = jnp.concatenate(
         [block_ref[point, p * rows : (p + 1) * rows, span] for p in range(2) for point in range(points)], axis=0
     )
-    for slot in range(owners):
-        pick = picked(order_ref, slot, rows, owners, stacked.shape[1])
-        out = dots(pick, stacked)
-        back_ref[slot, *index, 0] = low(out[:, : points * rows])
-        back_ref[slot, *index, 1] = low(-out[:, points * rows :])
-
-
-def finish_kernel(order_ref, left_ref, right_ref, got_ref, late_ref, block_ref, back_ref):
+    pick = picked(order_ref, (3, 0), rows, owners, half)
+    others = []
+    for point in range(points):
+        other = dots(second_ref[point, :, span], pick) + wide(late_ref[point, :, pl.ds(columns + part * count, count)])
+        others.append(low(other))
+    other = jnp.concatenate(
+        [others[point][p * rows : (p + 1) * rows] for p in range(2) for point in range(points)], axis=0
+    )
+    n = lax.broadcasted_iota(jnp.int32, (count, count), 0)
+    same = low(jnp.where(n == lax.broadcasted_iota(jnp.int32, (count, count), 1), 1.0, 0.0))
+    for source, out in enumerate((dots(pick, own), dots(same, other))):
+        for to, ref in enumerate((same_ref, first_ref)):
+            piece = out[to * rows : (to + 1) * rows]
+            ref[source, *index, 0] = low(piece[:, : points * rows])
+            ref[source, *index, 1] = low(-piece[:, points * rows :])
+
+
+def finish_pair_kernel(
+    order_ref, left_ref, mate_ref, next_ref, got_ref, second_ref, late_ref,
+    block_ref, mate_same_ref, mate_first_ref, next_same_ref, next_first_ref,
+):
+    points, count, columns = block_ref.shape
+    half = columns // 2
+    for part, (right_ref, same_ref, first_ref) in enumerate(
+        ((mate_ref, mate_same_ref, mate_first_ref), (next_ref, next_same_ref, next_first_ref))
+    ):
+        span = pl.ds(part * half, half)
+        for point in range(points):
+            total = dots(left_ref[point], right_ref[agreeing(order_ref, point)])
+            total = total + wide(got_ref[point, :count, span]) + wide(late_ref[point, :, span])
+            block_ref[point, :, span] = low(total)
+        turned_part(order_ref, block_ref, second_ref, late_ref, part, same_ref, first_ref, ())
+
+
+def finish_far_kernel(
+    order_ref, left_ref, right_ref, got_ref, second_ref, late_ref, block_ref, same_ref, first_ref
+):
     points, count, columns = block_ref.shape
     half = columns // points
     for part in range(points):
         span = pl.ds(part * half, half)
         for point in range(points):
-            total = dots(left_ref[point], right_ref[part]) + wide(got_ref[point, :count, span])
-            block_ref[point, :, span] = low(total + wide(late_ref[point, :, span]))
-        turn(order_ref, block_ref, span, back_ref, (part,))
-
-
-def turn_kernel(order_ref, block_ref, mate_back_ref, next_back_ref):
-    half = block_ref.shape[2] // 2
-    turn(order_ref, block_ref, pl.ds(0, half), mate_back_ref, ())
-    turn(order_ref, block_ref, pl.ds(half, half), next_back_ref, ())
+            total = dots(left_ref[point], right_ref[part])
+            total = total + wide(got_ref[point, :count, span]) + wide(late_ref[point, :, span])
+            block_ref[point, :, span] = low(total)
+        turned_part(order_ref, block_ref, second_ref, late_ref, part, same_ref, first_ref, (part,))
 
 
 def body(pair_density, coulomb):
@@ -190,41 +233,55 @@
         (left_away, left_second, left_own, mate_right)
     )
     columns = points * transitions
-    half_back = (owners, 2, rows, points * rows)
-    pair = local(
-        pair_kernel, [(owners, points, 2 * rows, columns)], relative, left, mate_right, next_right, scalars=1
-    )
-    block_pair = lax.psum_scatter(pair.reshape(-1, columns), "own", scatter_dimension=0, tiled=True)
-    block_pair = block_pair.reshape(points, 2 * rows, columns)
+    away_shape = [(points, 4 * rows, columns)]
+    second_shape = [(points, 2 * rows, columns + 4 * rows)]
+    block_shape = (points, 2 * rows, columns)
+    pair_back = (2, 2, rows, points * rows)
+    far_back = (2, points, 2, rows, points * rows)
+
     far_right = exchange_kp(next_right, mate)
-    far_right, _ = lax.optimization_barrier((far_right, pair))
-    away = local(away_kernel, [(points, 4 * rows, columns)], left_away, far_right)
-    got = exchange_own(away, True)
-    second = local(second_kernel, [(points, 2 * rows, columns)], left_second, far_right, got)
-    late = exchange_own(second, False)
-    back_mate, back_next = local(turn_kernel, [half_back, half_back], swapped, block_pair, scalars=1)
-    back_mate = exchange_kp(back_mate, mate)
-    back_next = exchange_kp(back_next, across)
-    back_pair = jnp.stack([back_mate, back_next], axis=1)
-    first = exchange_own(back_pair[:2], True)
-    then = exchange_own(jnp.stack([back_pair[2], first[1]]), False)
-    block_far, back_far = local(
-        finish_kernel, [(points, 2 * rows, columns), (owners, points, 2, rows, points * rows)],
-        relative, left_own, far_right, got, late, scalars=1,
-    )
-    back_far = [exchange(back_far[slot], slot, second_next) for slot in range(owners)]
+    away_pair = local(away_pair_kernel, away_shape, relative, left_away, mate_right, next_right, scalars=1)
+    got_pair = exchange_own(away_pair, True)
+    far_right, _ = lax.optimization_barrier((far_right, away_pair))
+    away_far = local(away_far_kernel, away_shape, left_away, far_right)
+    got_far = exchange_own(away_far, True)
+    got_pair, _ = lax.optimization_barrier((got_pair, away_far))
+    second_pair = local(
+        second_pair_kernel, second_shape,
+        relative, left_second, left_own, mate_right, next_right, got_pair, scalars=1,
+    )
+    late_pair = exchange_own(second_pair, False)
+    second_far = local(
+        second_far_kernel, second_shape, relative, left_second, left_own, far_right, got_far, scalars=1
+    )
+    late_pair, _ = lax.optimization_barrier((late_pair, second_far))
+    late_far = exchange_own(second_far, False)
+    block_pair, mate_same, mate_first, next_same, next_first = local(
+        finish_pair_kernel, [block_shape] + [pair_back] * 4,
+        relative, left_own, mate_right, next_right, got_pair, second_pair, late_pair, scalars=1,
+    )
+    mate_back = exchange(mate_same, 3, mate), exchange(mate_first, 0, mate)
+    next_back = exchange(next_same, 3, across), exchange(next_first, 0, across)
+    block_far, far_same, far_first = local(
+        finish_far_kernel, [block_shape, far_back, far_back],
+        relative, left_own, far_right, got_far, second_far, late_far, scalars=1,
+    )
+    far_back = exchange(far_same, 3, second_next), exchange(far_first, 0, second_next)
+
+    pick_rows = jnp.asarray(owner_order(owners, points * blocks), jnp.bfloat16)
+
+    def natural(back, order):
+        same, first = back
+        pick = jnp.concatenate(
+            [lax.dynamic_index_in_dim(pick_rows, order[slot], 0, False) for slot in range(owners)], axis=0
+        )
+        joined = jnp.concatenate([first[0], first[1], same[1], same[0]], axis=-1)
+        joined = joined.reshape(-1, 2, rows, columns)
+        out = lax.dot_general(joined, pick, (((3,), (0,)), ((), ())), preferred_element_type=jnp.float32)
+        return low(out)
+
+    back_far = natural(far_back, relative)
     block_mate, block_next = block_pair[..., :transitions], block_pair[..., transitions:]
-
-    pick_rows = jnp.asarray(owner_order(owners, points * blocks), jnp.bfloat16)
-    pick_rows = jnp.concatenate([lax.dynamic_index_in_dim(pick_rows, relative[slot], 0, False) for slot in range(owners)], axis=0)
-
-    def natural(tiles):
-        joined = jnp.concatenate(tiles, axis=-1)
-        out = lax.dot_general(joined, pick_rows, (((3,), (0,)), ((), ())), preferred_element_type=jnp.float32)
-        return low(out)
-
-    back_pair = natural([first[0], then[1], then[0], back_pair[3]])
-    back_far = natural(back_far)
 
     def mixed(block, back):
         block = block.reshape(points, 2, rows, transitions)
@@ -238,8 +295,8 @@
             out.append(jnp.concatenate(line, axis=-1))
         return jnp.stack(out)
 
-    with_mate = mixed(block_mate, back_pair[0])
-    with_next = mixed(block_next, back_pair[1])
+    with_mate = mixed(block_mate, natural(mate_back, swapped)[0])
+    with_next = mixed(block_next, natural(next_back, swapped)[0])
     here_far = block_far.reshape(points, 2, rows, points * transitions)
     out = jnp.stack(
         [

time: 201 us -> 171 us (0.85)
  starting transfers between devices: 86.8 us -> 59.7 us
  between operations: 13.8 us -> 0.54 us
  Pallas kernels: 10.7 us -> 16.8 us
    ppermute x8 -> x10, starting transfers between devices: 66.6 us -> 47.5 us  [exchange(): return lax.ppermute(value, ('kp', 'own'), pairs)]
    ppermute x5 -> x3, starting transfers between devices: 20.2 us -> 12.2 us  [exchange_kp(): lax.ppermute(value, 'kp', [(i, partner(i) % groups) for i in range(groups)])]
    pallas_call x6 -> x7, Pallas kernels: 10.7 us -> 16.8 us  [local(): pl.pallas_call(kernel, out_shape=out_shape if several else out_shape[0],...]
    ppermute x5 -> x3, waiting for transfers between devices: 13 us -> 10.9 us  [exchange_kp(): lax.ppermute(value, 'kp', [(i, partner(i) % groups) for i in range(groups)])]
    ppermute x8 -> x10, waiting for transfers between devices: 67.9 us -> 69.9 us  [exchange(): return lax.ppermute(value, ('kp', 'own'), pairs)]
  transfers between devices with their start and end apart: 14 -> 13, of which waited for: 7 -> 6; matrix products, arithmetic and copies ran while one was open for 1% -> 3% of each run, Pallas kernels for 5% -> 9%
where the time goes in v9:
time: 171 us; the launch traced here: 169 us
  waiting for transfers between devices  80.7 us (47%)
  starting transfers between devices  59.7 us (35%)
  Pallas kernels  16.8 us (10%)
  local copies, waits for them, and re-layouts  8.14 us (5%)
  matrix products  1.86 us (1%)
    ppermute x10, waiting for transfers between devices, exchange(): return lax.ppermute(value, ('kp', 'own'), pairs)  69.9 us
    ppermute x10, starting transfers between devices, exchange(): return lax.ppermute(value, ('kp', 'own'), pairs)  47.5 us
    pallas_call x7, Pallas kernels, local(): pl.pallas_call(kernel, out_shape=out_shape if several else out_shape[0],...  16.8 us
    ppermute x3, starting transfers between devices, exchange_kp(): lax.ppermute(value, 'kp', [(i, partner(i) % groups) for i in range(groups)])  12.2 us
    ppermute x3, waiting for transfers between devices, exchange_kp(): lax.ppermute(value, 'kp', [(i, partner(i) % groups) for i in range(groups)])  10.9 us
  transfers between devices with their start and end apart: 13, of which 6 were waited for; matrix products, arithmetic and copies ran while one was open for 3% of the time, Pallas kernels for 9%

profile of v9, /device:TPU:24, one launch (start us, length us, event | category | flops | bytes accessed | tf_op | source)
XLA Modules:
  0.0 169.1 jit_solution(4075320942279499960)
XLA Ops:
  0.0 2.6 %reshape.182.plain_ref = bf16[2,256,1024]{2,1,0:T(8,128)(2,1)} reshape(bf16[2,256,2,512]{3,2,1,0:T(2,128)(2,1)} %param.3) | data formatting | bytes 2097152 | tf_op jit(solution)/shard_map/reshape | solution.py:222
  2.6 8.3 %collective-permute-start.1 = (bf16[2,256,1024]{2,1,0:T(8,128)(2,1)}, bf16[2,256,1024]{2,1,0:T(8,128)(2,1)S(1)}, u32[]{:S(2)}, u32[]{:S(2)}) collective-permute-start(bf16[2,256,1024]{2,1,0:T(8,128)(2,1)} %reshape.182.plain_ref), channel_id=1, source_target_pairs={{0,508},{4,8},{8,4},{12,16},{16,12},{20,24},{24,20},{28,32},{32,28... | collective-permute-start | bytes 3145736 | tf_op jit(solution)/shard_map/ppermute | solution.py:193
  10.9 1.9 %collective-permute-start = (bf16[2,256,1024]{2,1,0:T(8,128)(2,1)}, bf16[2,256,1024]{2,1,0:T(8,128)(2,1)}, u32[]{:S(2)}, u32[]{:S(2)}) collective-permute-start(bf16[2,256,1024]{2,1,0:T(8,128)(2,1)} %reshape.182.plain_ref), channel_id=1, source_target_pairs={{0,4},{4,0},{8,12},{12,8},{16,20},{20,16},{24,28},{28,24},{32,36},... | collective-permute-start | bytes 3145736 | tf_op jit(solution)/shard_map/ppermute | solution.py:193
  12.9 10.8 %collective-permute-done.1.next_ref = bf16[2,256,1024]{2,1,0:T(8,128)(2,1)S(1)} collective-permute-done((bf16[2,256,1024]{2,1,0:T(8,128)(2,1)}, bf16[2,256,1024]{2,1,0:T(8,128)(2,1)S(1)}, u32[]{:S(2)}, u32[]{:S(2)}) %collective-permute-start.1) | collective-permute-done | bytes 1048608 | tf_op jit(solution)/shard_map/ppermute | solution.py:193
  23.7 1.9 %collective-permute-start.3 = (bf16[2,256,1024]{2,1,0:T(8,128)(2,1)S(1)}, bf16[2,256,1024]{2,1,0:T(8,128)(2,1)S(1)}, u32[]{:S(2)}, u32[]{:S(2)}) collective-permute-start(bf16[2,256,1024]{2,1,0:T(8,128)(2,1)S(1)} %collective-permute-done.1.next_ref), channel_id=1, source_target_pairs={{0,4},{4,0},{8,12},{12,8},{16,20},{20,16},{24,28},{28,24},{32,36},... | collective-permute-start | bytes 3145736 | tf_op jit(solution)/shard_map/ppermute | solution.py:193
  25.6 0.1 stack.52.order_ref
  25.7 1.5 shard_map.37
  27.2 0.1 slice.110
  27.3 0.1 fusion.33
  27.4 0.0 collective-permute-done.mate_ref
  27.4 2.0 %shard_map.38 = bf16[2,256,512]{2,1,0:T(8,128)(2,1)S(1)} custom-call(s32[5]{0:T(128)S(1)} %stack.52.order_ref, bf16[2,256,1024]{2,1,0:T(8,128)(2,1)S(1)} %bitcast.98, bf16[2,256,1024]{2,1,0:T(8,128)(2,1)} %collective-permute-done.mate_ref, bf16[2,256,1024]{2,1,0:T(8,128)(2,1)S(1)} %collective-permute-done.1.next_ref), custom_call_target="tpu_custom_call" | custom-call | tf_op jit(solution)/shard_map/pallas_call | solution.py:27
  29.4 9.1 %collective-permute-start.2 = (bf16[2,256,512]{2,1,0:T(8,128)(2,1)S(1)}, bf16[2,256,512]{2,1,0:T(8,128)(2,1)S(1)}, u32[]{:S(2)}, u32[]{:S(2)}) collective-permute-start(bf16[2,256,512]{2,1,0:T(8,128)(2,1)S(1)} %shard_map.38), channel_id=1, source_target_pairs={{0,1},{1,0},{2,3},{3,2},{4,7},{5,6},{6,5},{7,4},{8,9},{9,8},{10,11... | collective-permute-start | bytes 1572872 | tf_op jit(solution)/shard_map/ppermute | solution.py:204
  38.5 0.0 collective-permute-done.3.right_ref
  38.5 1.5 shard_map.39
  40.0 1.9 %collective-permute-start.5 = (bf16[2,256,512]{2,1,0:T(8,128)(2,1)}, bf16[2,256,512]{2,1,0:T(8,128)(2,1)}, u32[]{:S(2)}, u32[]{:S(2)}) collective-permute-start(bf16[2,256,512]{2,1,0:T(8,128)(2,1)} %shard_map.39), channel_id=1, source_target_pairs={{0,1},{1,0},{2,3},{3,2},{4,7},{5,6},{6,5},{7,4},{8,9},{9,8},{10,11... | collective-permute-start | bytes 1572872 | tf_op jit(solution)/shard_map/ppermute | solution.py:204
  42.0 36.4 %collective-permute-done.2.got_ref = bf16[2,256,512]{2,1,0:T(8,128)(2,1)S(1)} collective-permute-done((bf16[2,256,512]{2,1,0:T(8,128)(2,1)S(1)}, bf16[2,256,512]{2,1,0:T(8,128)(2,1)S(1)}, u32[]{:S(2)}, u32[]{:S(2)}) %collective-permute-start.2) | collective-permute-done | bytes 524320 | tf_op jit(solution)/shard_map/ppermute | solution.py:204
  78.4 3.8 %shard_map.40.second_ref = bf16[2,128,768]{2,1,0:T(8,128)(2,1)} custom-call(s32[5]{0:T(128)S(1)} %stack.52.order_ref, bf16[2,128,1024]{2,1,0:T(8,128)(2,1)S(1)} %bitcast.100, bf16[2,128,1024]{2,1,0:T(8,128)(2,1)S(1)} %bitcast.94, bf16[2,256,1024]{2,1,0:T(8,128)(2,1)} %collective-permute-done.mate_ref, ...), custom_call_target="tpu_custom_call" | custom-call | tf_op jit(solution)/shard_map/pallas_call | solution.py:27
  82.2 0.8 copy-done
  83.0 11.0 %collective-permute-start.4 = (bf16[2,128,768]{2,1,0:T(8,128)(2,1)}, bf16[2,128,768]{2,1,0:T(8,128)(2,1)}, u32[]{:S(2)}, u32[]{:S(2)}) collective-permute-start(bf16[2,128,768]{2,1,0:T(8,128)(2,1)} %shard_map.40.second_ref), channel_id=1, source_target_pairs={{0,3},{1,2},{2,1},{3,0},{4,5},{5,4},{6,7},{7,6},{8,11},{9,10},{10,... | collective-permute-start | bytes 1179656 | tf_op jit(solution)/shard_map/ppermute | solution.py:204
  94.1 1.2 dynamic-slice_bitcast_fusion.1
  95.3 0.0 collective-permute-done.5.got_ref
  95.3 3.0 %shard_map.41.second_ref = bf16[2,128,768]{2,1,0:T(8,128)(2,1)S(1)} custom-call(s32[5]{0:T(128)S(1)} %stack.52.order_ref, bf16[2,128,1024]{2,1,0:T(8,128)(2,1)S(1)} %bitcast.101, bf16[2,128,1024]{2,1,0:T(8,128)(2,1)S(1)} %bitcast.95, bf16[2,256,1024]{2,1,0:T(8,128)(2,1)S(1)} %collective-permute-done.3.right_ref, ...), custom_call_target="tpu_custom_call" | custom-call | tf_op jit(solution)/shard_map/pallas_call | solution.py:27
  98.3 1.9 %collective-permute-start.10 = (bf16[2,128,768]{2,1,0:T(8,128)(2,1)S(1)}, bf16[2,128,768]{2,1,0:T(8,128)(2,1)S(1)}, u32[]{:S(2)}, u32[]{:S(2)}) collective-permute-start(bf16[2,128,768]{2,1,0:T(8,128)(2,1)S(1)} %shard_map.41.second_ref), channel_id=1, source_target_pairs={{0,3},{1,2},{2,1},{3,0},{4,5},{5,4},{6,7},{7,6},{8,11},{9,10},{10,... | collective-permute-start | bytes 1179656 | tf_op jit(solution)/shard_map/ppermute | solution.py:204
  100.3 19.8 %collective-permute-done.4.late_ref = bf16[2,128,768]{2,1,0:T(8,128)(2,1)} collective-permute-done((bf16[2,128,768]{2,1,0:T(8,128)(2,1)}, bf16[2,128,768]{2,1,0:T(8,128)(2,1)}, u32[]{:S(2)}, u32[]{:S(2)}) %collective-permute-start.4) | collective-permute-done | bytes 393248 | tf_op jit(solution)/shard_map/ppermute | solution.py:204
  120.1 2.7 %shard_map.42 = (bf16[2,128,512]{2,1,0:T(8,128)(2,1)S(1)}, bf16[2,2,64,128]{3,2,1,0:T(8,128)(2,1)S(1)}, bf16[2,2,64,128]{3,2,1,0:T(8,128)(2,1)S(1)}, bf16[2,2,64...) custom-call(s32[5]{0:T(128)S(1)} %stack.52.order_ref, bf16[2,128,1024]{2,1,0:T(8,128)(2,1)S(1)} %bitcast.96, ...), custom_call_target="tpu_custom_call" | custom-call | tf_op jit(solution)/shard_map/pallas_call | solution.py:27
  122.8 5.4 %collective-permute-start.6 = (bf16[2,2,64,128]{3,2,1,0:T(8,128)(2,1)S(1)}, bf16[2,2,64,128]{3,2,1,0:T(8,128)(2,1)S(1)}, u32[]{:S(2)}, u32[]{:S(2)}) collective-permute-start(bf16[2,2,64,128]{3,2,1,0:T(8,128)(2,1)S(1)} %get-tuple-element.28), channel_id=1, source_target_pairs={{0,5},{1,4},{2,7},{3,6},{4,3},{5,2},{6,1},{7,0},{8,13},{9,12},{10,... | collective-permute-start | bytes 196616 | tf_op jit(solution)/shard_map/ppermute | solution.py:204
  128.2 1.9 %collective-permute-start.7 = (bf16[2,2,64,128]{3,2,1,0:T(8,128)(2,1)S(1)}, bf16[2,2,64,128]{3,2,1,0:T(8,128)(2,1)S(1)}, u32[]{:S(2)}, u32[]{:S(2)}) collective-permute-start(bf16[2,2,64,128]{3,2,1,0:T(8,128)(2,1)S(1)} %get-tuple-element.29), channel_id=1, source_target_pairs={{0,4},{1,5},{2,6},{3,7},{4,0},{5,1},{6,2},{7,3},{8,12},{9,13},{10,... | collective-permute-start | bytes 196616 | tf_op jit(solution)/shard_map/ppermute | solution.py:204
  130.1 1.9 %collective-permute-start.8 = (bf16[2,2,64,128]{3,2,1,0:T(8,128)(2,1)S(1)}, bf16[2,2,64,128]{3,2,1,0:T(8,128)(2,1)S(1)}, u32[]{:S(2)}, u32[]{:S(2)}) collective-permute-start(bf16[2,2,64,128]{3,2,1,0:T(8,128)(2,1)S(1)} %get-tuple-element.30), channel_id=1, source_target_pairs={{0,509},{1,508},{2,511},{3,510},{4,11},{5,10},{6,9},{7,8},{8,5},{9... | collective-permute-start | bytes 196616 | tf_op jit(solution)/shard_map/ppermute | solution.py:204
  132.1 10.4 %collective-permute-start.9 = (bf16[2,2,64,128]{3,2,1,0:T(8,128)(2,1)S(1)}, bf16[2,2,64,128]{3,2,1,0:T(8,128)(2,1)S(1)}, u32[]{:S(2)}, u32[]{:S(2)}) collective-permute-start(bf16[2,2,64,128]{3,2,1,0:T(8,128)(2,1)S(1)} %get-tuple-element.31), channel_id=1, source_target_pairs={{0,508},{1,509},{2,510},{3,511},{4,8},{5,9},{6,10},{7,11},{8,4},{9... | collective-permute-start | bytes 196616 | tf_op jit(solution)/shard_map/ppermute | solution.py:204
  142.5 0.7 fusion.34
  143.1 0.0 collective-permute-done.6
  143.2 0.0 collective-permute-done.7
  143.2 0.2 convolution_convert_fusion.2
  143.5 0.2 fusion.35
  143.7 0.8 collective-permute-done.9
  144.5 1.3 convolution_convert_fusion.1
  145.9 0.2 fusion.36
  146.1 1.0 broadcast_select_fusion.3
  147.2 2.4 %shard_map.43 = (bf16[2,128,512]{2,1,0:T(8,128)(2,1)S(1)}, bf16[2,2,2,64,128]{4,3,2,1,0:T(8,128)(2,1)S(1)}, bf16[2,2,2,64,128]{4,3,2,1,0:T(8,128)(2,1)S(1)}) custom-call(s32[5]{0:T(128)S(1)} %stack.52.order_ref, bf16[2,128,1024]{2,1,0:T(8,128)(2,1)S(1)} %bitcast.97, bf16[2,256,1024]{2,1,0:T(8,128)(2,1)S(1)} %collective-permute-done.3.right_ref, ...), custom_call_target="tpu_custom_call" | custom-call | tf_op jit(solution)/shard_map/pallas_call | solution.py:27
  149.5 2.0 %collective-permute-start.11 = (bf16[2,2,2,64,128]{4,3,2,1,0:T(8,128)(2,1)S(1)}, bf16[2,2,2,64,128]{4,3,2,1,0:T(8,128)(2,1)S(1)}, u32[]{:S(2)}, u32[]{:S(2)}) collective-permute-start(bf16[2,2,2,64,128]{4,3,2,1,0:T(8,128)(2,1)S(1)} %get-tuple-element.33), channel_id=1, source_target_pairs={{0,9},{1,8},{2,11},{3,10},{4,511},{5,510},{6,509},{7,508},{8,17},{... | collective-permute-start | bytes 393224 | tf_op jit(solution)/shard_map/ppermute | solution.py:204
  151.5 0.1 broadcast_select_fusion.1
  151.6 1.9 %collective-permute-start.12 = (bf16[2,2,2,64,128]{4,3,2,1,0:T(8,128)(2,1)S(1)}, bf16[2,2,2,64,128]{4,3,2,1,0:T(8,128)(2,1)S(1)}, u32[]{:S(2)}, u32[]{:S(2)}) collective-permute-start(bf16[2,2,2,64,128]{4,3,2,1,0:T(8,128)(2,1)S(1)} %get-tuple-element.34), channel_id=1, source_target_pairs={{0,8},{1,9},{2,10},{3,11},{4,508},{5,509},{6,510},{7,511},{8,16},{... | collective-permute-start | bytes 393224 | tf_op jit(solution)/shard_map/ppermute | solution.py:204
  153.5 12.6 %collective-permute-done.11 = bf16[2,2,2,64,128]{4,3,2,1,0:T(8,128)(2,1)S(1)} collective-permute-done((bf16[2,2,2,64,128]{4,3,2,1,0:T(8,128)(2,1)S(1)}, bf16[2,2,2,64,128]{4,3,2,1,0:T(8,128)(2,1)S(1)}, u32[]{:S(2)}, u32[]{:S(2)}) %collective-permute-start.11) | collective-permute-done | bytes 131104 | tf_op jit(solution)/shard_map/ppermute | solution.py:204
  166.1 0.3 collective-permute-done.12
  166.5 0.3 convolution_convert_fusion
  166.9 0.1 maximum_bitcast_fusion
  167.0 0.1 copy.12
  167.1 2.0 %copy.13 = bf16[4,128,2,512]{3,2,1,0:T(2,128)(2,1)} copy(bf16[4,128,2,512]{3,1,2,0:T(8,128)(2,1)S(1)} %bitcast.103) | data formatting | bytes 2097152 | tf_op jit(solution)/shard_map/reshape | solution.py:310
  (37 shorter events, 0.3 us)
Async XLA Ops:
  0.0 25.7 %copy-start.10 = (f32[512]{0:T(512)S(1)}, f32[512]{0:T(512)}, u32[]{:S(2)}) copy-start(f32[512]{0:T(512)} %param.4) | copy-start | bytes 6148
  2.6 21.1 %collective-permute-start.1 = (bf16[2,256,1024]{2,1,0:T(8,128)(2,1)}, bf16[2,256,1024]{2,1,0:T(8,128)(2,1)S(1)}, u32[]{:S(2)}, u32[]{:S(2)}) collective-permute-start(bf16[2,256,1024]{2,1,0:T(8,128)(2,1)} %reshape.182.plain_ref), channel_id=1, source_target_pairs={{0,508},{4,8},{8,4},{12,16},{16,12},{20,24},{24,20},{28,32},{32,28... | collective-permute-start | bytes 3145736 | tf_op jit(solution)/shard_map/ppermute | solution.py:193
  10.9 16.5 %collective-permute-start = (bf16[2,256,1024]{2,1,0:T(8,128)(2,1)}, bf16[2,256,1024]{2,1,0:T(8,128)(2,1)}, u32[]{:S(2)}, u32[]{:S(2)}) collective-permute-start(bf16[2,256,1024]{2,1,0:T(8,128)(2,1)} %reshape.182.plain_ref), channel_id=1, source_target_pairs={{0,4},{4,0},{8,12},{12,8},{16,20},{20,16},{24,28},{28,24},{32,36},... | collective-permute-start | bytes 3145736 | tf_op jit(solution)/shard_map/ppermute | solution.py:193
  23.7 14.8 %collective-permute-start.3 = (bf16[2,256,1024]{2,1,0:T(8,128)(2,1)S(1)}, bf16[2,256,1024]{2,1,0:T(8,128)(2,1)S(1)}, u32[]{:S(2)}, u32[]{:S(2)}) collective-permute-start(bf16[2,256,1024]{2,1,0:T(8,128)(2,1)S(1)} %collective-permute-done.1.next_ref), channel_id=1, source_target_pairs={{0,4},{4,0},{8,12},{12,8},{16,20},{20,16},{24,28},{28,24},{32,36},... | collective-permute-start | bytes 3145736 | tf_op jit(solution)/shard_map/ppermute | solution.py:193
  29.4 49.0 %collective-permute-start.2 = (bf16[2,256,512]{2,1,0:T(8,128)(2,1)S(1)}, bf16[2,256,512]{2,1,0:T(8,128)(2,1)S(1)}, u32[]{:S(2)}, u32[]{:S(2)}) collective-permute-start(bf16[2,256,512]{2,1,0:T(8,128)(2,1)S(1)} %shard_map.38), channel_id=1, source_target_pairs={{0,1},{1,0},{2,3},{3,2},{4,7},{5,6},{6,5},{7,4},{8,9},{9,8},{10,11... | collective-permute-start | bytes 1572872 | tf_op jit(solution)/shard_map/ppermute | solution.py:204
  40.0 55.3 %collective-permute-start.5 = (bf16[2,256,512]{2,1,0:T(8,128)(2,1)}, bf16[2,256,512]{2,1,0:T(8,128)(2,1)}, u32[]{:S(2)}, u32[]{:S(2)}) collective-permute-start(bf16[2,256,512]{2,1,0:T(8,128)(2,1)} %shard_map.39), channel_id=1, source_target_pairs={{0,1},{1,0},{2,3},{3,2},{4,7},{5,6},{6,5},{7,4},{8,9},{9,8},{10,11... | collective-permute-start | bytes 1572872 | tf_op jit(solution)/shard_map/ppermute | solution.py:204
  82.2 0.8 copy-start
  83.0 37.1 %collective-permute-start.4 = (bf16[2,128,768]{2,1,0:T(8,128)(2,1)}, bf16[2,128,768]{2,1,0:T(8,128)(2,1)}, u32[]{:S(2)}, u32[]{:S(2)}) collective-permute-start(bf16[2,128,768]{2,1,0:T(8,128)(2,1)} %shard_map.40.second_ref), channel_id=1, source_target_pairs={{0,3},{1,2},{2,1},{3,0},{4,5},{5,4},{6,7},{7,6},{8,11},{9,10},{10,... | collective-permute-start | bytes 1179656 | tf_op jit(solution)/shard_map/ppermute | solution.py:204
  94.0 26.0 %copy-start.1 = (bf16[2,256,512]{2,1,0:T(8,128)(2,1)S(1)}, bf16[2,256,512]{2,1,0:T(8,128)(2,1)}, u32[]{:S(2)}) copy-start(bf16[2,256,512]{2,1,0:T(8,128)(2,1)} %copy-done) | copy-start | bytes 1572868
  95.3 47.9 %copy-start.2 = (bf16[128,512]{1,0:T(8,128)(2,1)}, bf16[128,512]{1,0:T(8,128)(2,1)S(1)}, u32[]{:S(2)}) copy-start(bf16[128,512]{1,0:T(8,128)(2,1)S(1)} %get-tuple-element.41) | copy-start | bytes 393220
  95.3 47.9 %copy-start.4 = (bf16[128,512]{1,0:T(8,128)(2,1)}, bf16[128,512]{1,0:T(8,128)(2,1)S(1)}, u32[]{:S(2)}) copy-start(bf16[128,512]{1,0:T(8,128)(2,1)S(1)} %get-tuple-element.42) | copy-start | bytes 393220
  95.3 47.9 %copy-start.6 = (bf16[128,512]{1,0:T(8,128)(2,1)}, bf16[128,512]{1,0:T(8,128)(2,1)S(1)}, u32[]{:S(2)}) copy-start(bf16[128,512]{1,0:T(8,128)(2,1)S(1)} %get-tuple-element.43) | copy-start | bytes 393220
  95.3 47.9 %copy-start.8 = (bf16[128,512]{1,0:T(8,128)(2,1)}, bf16[128,512]{1,0:T(8,128)(2,1)S(1)}, u32[]{:S(2)}) copy-start(bf16[128,512]{1,0:T(8,128)(2,1)S(1)} %get-tuple-element.44) | copy-start | bytes 393220
  98.3 48.8 %collective-permute-start.10 = (bf16[2,128,768]{2,1,0:T(8,128)(2,1)S(1)}, bf16[2,128,768]{2,1,0:T(8,128)(2,1)S(1)}, u32[]{:S(2)}, u32[]{:S(2)}) collective-permute-start(bf16[2,128,768]{2,1,0:T(8,128)(2,1)S(1)} %shard_map.41.second_ref), channel_id=1, source_target_pairs={{0,3},{1,2},{2,1},{3,0},{4,5},{5,4},{6,7},{7,6},{8,11},{9,10},{10,... | collective-permute-start | bytes 1179656 | tf_op jit(solution)/shard_map/ppermute | solution.py:204
  122.8 20.4 %collective-permute-start.6 = (bf16[2,2,64,128]{3,2,1,0:T(8,128)(2,1)S(1)}, bf16[2,2,64,128]{3,2,1,0:T(8,128)(2,1)S(1)}, u32[]{:S(2)}, u32[]{:S(2)}) collective-permute-start(bf16[2,2,64,128]{3,2,1,0:T(8,128)(2,1)S(1)} %get-tuple-element.28), channel_id=1, source_target_pairs={{0,5},{1,4},{2,7},{3,6},{4,3},{5,2},{6,1},{7,0},{8,13},{9,12},{10,... | collective-permute-start | bytes 196616 | tf_op jit(solution)/shard_map/ppermute | solution.py:204
  128.2 15.0 %collective-permute-start.7 = (bf16[2,2,64,128]{3,2,1,0:T(8,128)(2,1)S(1)}, bf16[2,2,64,128]{3,2,1,0:T(8,128)(2,1)S(1)}, u32[]{:S(2)}, u32[]{:S(2)}) collective-permute-start(bf16[2,2,64,128]{3,2,1,0:T(8,128)(2,1)S(1)} %get-tuple-element.29), channel_id=1, source_target_pairs={{0,4},{1,5},{2,6},{3,7},{4,0},{5,1},{6,2},{7,3},{8,12},{9,13},{10,... | collective-permute-start | bytes 196616 | tf_op jit(solution)/shard_map/ppermute | solution.py:204
  130.1 13.6 %collective-permute-start.8 = (bf16[2,2,64,128]{3,2,1,0:T(8,128)(2,1)S(1)}, bf16[2,2,64,128]{3,2,1,0:T(8,128)(2,1)S(1)}, u32[]{:S(2)}, u32[]{:S(2)}) collective-permute-start(bf16[2,2,64,128]{3,2,1,0:T(8,128)(2,1)S(1)} %get-tuple-element.30), channel_id=1, source_target_pairs={{0,509},{1,508},{2,511},{3,510},{4,11},{5,10},{6,9},{7,8},{8,5},{9... | collective-permute-start | bytes 196616 | tf_op jit(solution)/shard_map/ppermute | solution.py:204
  132.1 12.4 %collective-permute-start.9 = (bf16[2,2,64,128]{3,2,1,0:T(8,128)(2,1)S(1)}, bf16[2,2,64,128]{3,2,1,0:T(8,128)(2,1)S(1)}, u32[]{:S(2)}, u32[]{:S(2)}) collective-permute-start(bf16[2,2,64,128]{3,2,1,0:T(8,128)(2,1)S(1)} %get-tuple-element.31), channel_id=1, source_target_pairs={{0,508},{1,509},{2,510},{3,511},{4,8},{5,9},{6,10},{7,11},{8,4},{9... | collective-permute-start | bytes 196616 | tf_op jit(solution)/shard_map/ppermute | solution.py:204
  147.1 19.3 %copy-start.3 = (bf16[128,512]{1,0:T(8,128)(2,1)S(1)}, bf16[128,512]{1,0:T(8,128)(2,1)}, u32[]{:S(2)}) copy-start(bf16[128,512]{1,0:T(8,128)(2,1)} %copy-done.2) | copy-start | bytes 393220
  147.1 19.3 %copy-start.5 = (bf16[128,512]{1,0:T(8,128)(2,1)S(1)}, bf16[128,512]{1,0:T(8,128)(2,1)}, u32[]{:S(2)}) copy-start(bf16[128,512]{1,0:T(8,128)(2,1)} %copy-done.4) | copy-start | bytes 393220
  147.1 19.3 %copy-start.7 = (bf16[128,512]{1,0:T(8,128)(2,1)S(1)}, bf16[128,512]{1,0:T(8,128)(2,1)}, u32[]{:S(2)}) copy-start(bf16[128,512]{1,0:T(8,128)(2,1)} %copy-done.6) | copy-start | bytes 393220
  147.2 19.3 %copy-start.9 = (bf16[128,512]{1,0:T(8,128)(2,1)S(1)}, bf16[128,512]{1,0:T(8,128)(2,1)}, u32[]{:S(2)}) copy-start(bf16[128,512]{1,0:T(8,128)(2,1)} %copy-done.8) | copy-start | bytes 393220
  149.5 16.6 %collective-permute-start.11 = (bf16[2,2,2,64,128]{4,3,2,1,0:T(8,128)(2,1)S(1)}, bf16[2,2,2,64,128]{4,3,2,1,0:T(8,128)(2,1)S(1)}, u32[]{:S(2)}, u32[]{:S(2)}) collective-permute-start(bf16[2,2,2,64,128]{4,3,2,1,0:T(8,128)(2,1)S(1)} %get-tuple-element.33), channel_id=1, source_target_pairs={{0,9},{1,8},{2,11},{3,10},{4,511},{5,510},{6,509},{7,508},{8,17},{... | collective-permute-start | bytes 393224 | tf_op jit(solution)/shard_map/ppermute | solution.py:204
  151.6 14.8 %collective-permute-start.12 = (bf16[2,2,2,64,128]{4,3,2,1,0:T(8,128)(2,1)S(1)}, bf16[2,2,2,64,128]{4,3,2,1,0:T(8,128)(2,1)S(1)}, u32[]{:S(2)}, u32[]{:S(2)}) collective-permute-start(bf16[2,2,2,64,128]{4,3,2,1,0:T(8,128)(2,1)S(1)} %get-tuple-element.34), channel_id=1, source_target_pairs={{0,8},{1,9},{2,10},{3,11},{4,508},{5,509},{6,510},{7,511},{8,16},{... | collective-permute-start | bytes 393224 | tf_op jit(solution)/shard_map/ppermute | solution.py:204

commit v10 on v9

--- a/solution.py
+++ b/solution.py
@@ -19,7 +19,7 @@
     return np.eye(count, dtype=np.float32)[column].reshape(owners, blocks * BLOCK, count)
 
 
-def local(kernel, shapes, *operands, scalars=0):
+def local(kernel, shapes, *operands, scalars=0, moved=0):
     vmem = pl.BlockSpec(memory_space=pltpu.VMEM)
     smem = pl.BlockSpec(memory_space=pltpu.SMEM)
     several = len(shapes) > 1
@@ -30,7 +30,7 @@
         in_specs=[smem] * scalars + [vmem] * (len(operands) - scalars),
         out_specs=[vmem] * len(shapes) if several else vmem,
         compiler_params=pltpu.CompilerParams(vmem_limit_bytes=40 * 1024 * 1024),
-        cost_estimate=pl.CostEstimate(flops=0, transcendentals=0, bytes_accessed=0),
+        cost_estimate=pl.CostEstimate(flops=0, transcendentals=0, bytes_accessed=moved),
     )(*operands)
 
 
@@ -224,7 +224,7 @@
     next_right = exchange_kp(plain, across)
 
     weights = (jnp.concatenate([coulomb, coulomb]) * scale).reshape(1, depth)
-    left = local(left_kernel, [(points, owners, 2, rows, depth)], relative, plain, weights, scalars=1)
+    left = local(left_kernel, [(points, owners, 2, rows, depth)], relative, plain, weights, scalars=1, moved=4 << 20)
     left_away = left[:, :2].reshape(points, 4 * rows, depth)
     left_second = left[:, 2].reshape(points, 2 * rows, depth)
     left_own = left[:, 3].reshape(points, 2 * rows, depth)
@@ -239,29 +239,31 @@
     pair_back = (2, 2, rows, points * rows)
     far_back = (2, points, 2, rows, points * rows)
 
-    far_right = exchange_kp(next_right, mate)
     away_pair = local(away_pair_kernel, away_shape, relative, left_away, mate_right, next_right, scalars=1)
     got_pair = exchange_own(away_pair, True)
-    far_right, _ = lax.optimization_barrier((far_right, away_pair))
-    away_far = local(away_far_kernel, away_shape, left_away, far_right)
-    got_far = exchange_own(away_far, True)
-    got_pair, _ = lax.optimization_barrier((got_pair, away_far))
+    passed_on, _ = lax.optimization_barrier((next_right, away_pair))
+    far_right = exchange_kp(passed_on, mate)
     second_pair = local(
         second_pair_kernel, second_shape,
         relative, left_second, left_own, mate_right, next_right, got_pair, scalars=1,
     )
     late_pair = exchange_own(second_pair, False)
-    second_far = local(
-        second_far_kernel, second_shape, relative, left_second, left_own, far_right, got_far, scalars=1
-    )
-    late_pair, _ = lax.optimization_barrier((late_pair, second_far))
-    late_far = exchange_own(second_far, False)
+    far_right, _ = lax.optimization_barrier((far_right, second_pair))
+    away_far = local(away_far_kernel, away_shape, left_away, far_right)
+    got_far = exchange_own(away_far, True)
+    late_pair, _ = lax.optimization_barrier((late_pair, away_far))
     block_pair, mate_same, mate_first, next_same, next_first = local(
         finish_pair_kernel, [block_shape] + [pair_back] * 4,
         relative, left_own, mate_right, next_right, got_pair, second_pair, late_pair, scalars=1,
     )
     mate_back = exchange(mate_same, 3, mate), exchange(mate_first, 0, mate)
     next_back = exchange(next_same, 3, across), exchange(next_first, 0, across)
+    got_far, _ = lax.optimization_barrier((got_far, block_pair))
+    second_far = local(
+        second_far_kernel, second_shape, relative, left_second, left_own, far_right, got_far, scalars=1
+    )
+    late_far = exchange_own(second_far, False)
+    mate_back, next_back, _ = lax.optimization_barrier((mate_back, next_back, second_far))
     block_far, far_same, far_first = local(
         finish_far_kernel, [block_shape, far_back, far_back],
         relative, left_own, far_right, got_far, second_far, late_far, scalars=1,

time: 171 us -> 185 us (1.082)
  starting transfers between devices: 59.7 us -> 72.6 us
  waiting for transfers between devices: 80.7 us -> 83.7 us
  local copies, waits for them, and re-layouts: 8.14 us -> 11.1 us
  Pallas kernels: 16.8 us -> 14 us
    ppermute x10, starting transfers between devices: 47.5 us -> 59.8 us  [exchange(): return lax.ppermute(value, ('kp', 'own'), pairs)]
    unnamed x22 -> x28, local copies, waits for them, and re-layouts: 0.84 us -> 4.5 us
    ppermute x10, waiting for transfers between devices: 69.9 us -> 72.8 us  [exchange(): return lax.ppermute(value, ('kp', 'own'), pairs)]
    pallas_call x7, Pallas kernels: 16.8 us -> 14 us  [local(): pl.pallas_call(kernel, out_shape=out_shape if several else out_shape[0],...]
  transfers between devices with their start and end apart: 13 -> 13, of which waited for: 6 -> 6; matrix products, arithmetic and copies ran while one was open for 3% -> 2% of each run, Pallas kernels for 9% -> 6%
where the time goes in v10:
time: 185 us; the launch traced here: 184 us
  waiting for transfers between devices  83.7 us (45%)
  starting transfers between devices  72.6 us (39%)
  Pallas kernels  14 us (8%)
  local copies, waits for them, and re-layouts  11.1 us (6%)
  matrix products  1.86 us (1%)
    ppermute x10, waiting for transfers between devices, exchange(): return lax.ppermute(value, ('kp', 'own'), pairs)  72.8 us
    ppermute x10, starting transfers between devices, exchange(): return lax.ppermute(value, ('kp', 'own'), pairs)  59.8 us
    pallas_call x7, Pallas kernels, local(): pl.pallas_call(kernel, out_shape=out_shape if several else out_shape[0],...  14 us
    ppermute x3, starting transfers between devices, exchange_kp(): lax.ppermute(value, 'kp', [(i, partner(i) % groups) for i in range(groups)])  12.8 us
    ppermute x3, waiting for transfers between devices, exchange_kp(): lax.ppermute(value, 'kp', [(i, partner(i) % groups) for i in range(groups)])  10.9 us
    unnamed x28, local copies, waits for them, and re-layouts  4.5 us
  transfers between devices with their start and end apart: 13, of which 6 were waited for; matrix products, arithmetic and copies ran while one was open for 2% of the time, Pallas kernels for 6%

profile of v10, /device:TPU:24, one launch (start us, length us, event | category | flops | bytes accessed | tf_op | source)
XLA Modules:
  0.0 184.2 jit_solution(1894648742897937756)
XLA Ops:
  0.0 2.6 %reshape.182.plain_ref = bf16[2,256,1024]{2,1,0:T(8,128)(2,1)} reshape(bf16[2,256,2,512]{3,2,1,0:T(2,128)(2,1)} %param.3) | data formatting | bytes 2097152 | tf_op jit(solution)/shard_map/reshape | solution.py:222
  2.6 1.9 %collective-permute-start = (bf16[2,256,1024]{2,1,0:T(8,128)(2,1)}, bf16[2,256,1024]{2,1,0:T(8,128)(2,1)S(1)}, u32[]{:S(2)}, u32[]{:S(2)}) collective-permute-start(bf16[2,256,1024]{2,1,0:T(8,128)(2,1)} %reshape.182.plain_ref), channel_id=1, source_target_pairs={{0,4},{4,0},{8,12},{12,8},{16,20},{20,16},{24,28},{28,24},{32,36},... | collective-permute-start | bytes 3145736 | tf_op jit(solution)/shard_map/ppermute | solution.py:193
  4.5 9.0 %collective-permute-start.1 = (bf16[2,256,1024]{2,1,0:T(8,128)(2,1)}, bf16[2,256,1024]{2,1,0:T(8,128)(2,1)S(1)}, u32[]{:S(2)}, u32[]{:S(2)}) collective-permute-start(bf16[2,256,1024]{2,1,0:T(8,128)(2,1)} %reshape.182.plain_ref), channel_id=1, source_target_pairs={{0,508},{4,8},{8,4},{12,16},{16,12},{20,24},{24,20},{28,32},{32,28... | collective-permute-start | bytes 3145736 | tf_op jit(solution)/shard_map/ppermute | solution.py:193
  13.5 0.1 stack.52.order_ref
  13.6 1.5 shard_map.37
  15.1 0.1 slice.110
  15.2 0.1 fusion.33
  15.3 0.0 collective-permute-done.mate_ref
  15.3 10.9 %collective-permute-done.1.next_ref = bf16[2,256,1024]{2,1,0:T(8,128)(2,1)S(1)} collective-permute-done((bf16[2,256,1024]{2,1,0:T(8,128)(2,1)}, bf16[2,256,1024]{2,1,0:T(8,128)(2,1)S(1)}, u32[]{:S(2)}, u32[]{:S(2)}) %collective-permute-start.1) | collective-permute-done | bytes 1048608 | tf_op jit(solution)/shard_map/ppermute | solution.py:193
  26.2 1.3 shard_map.38
  27.5 0.0 copy-start
  27.5 1.0 copy-done
  28.5 1.9 %collective-permute-start.4 = (bf16[2,256,1024]{2,1,0:T(8,128)(2,1)}, bf16[2,256,1024]{2,1,0:T(8,128)(2,1)S(1)}, u32[]{:S(2)}, u32[]{:S(2)}) collective-permute-start(bf16[2,256,1024]{2,1,0:T(8,128)(2,1)} %copy-done), channel_id=1, source_target_pairs={{0,4},{4,0},{8,12},{12,8},{16,20},{20,16},{24,28},{28,24},{32,36},... | collective-permute-start | bytes 3145736 | tf_op jit(solution)/shard_map/ppermute | solution.py:193
  30.4 9.1 %collective-permute-start.2 = (bf16[2,256,512]{2,1,0:T(8,128)(2,1)S(1)}, bf16[2,256,512]{2,1,0:T(8,128)(2,1)S(1)}, u32[]{:S(2)}, u32[]{:S(2)}) collective-permute-start(bf16[2,256,512]{2,1,0:T(8,128)(2,1)S(1)} %shard_map.38), channel_id=1, source_target_pairs={{0,1},{1,0},{2,3},{3,2},{4,7},{5,6},{6,5},{7,4},{8,9},{9,8},{10,11... | collective-permute-start | bytes 1572872 | tf_op jit(solution)/shard_map/ppermute | solution.py:204
  39.5 22.4 %collective-permute-done.2.got_ref = bf16[2,256,512]{2,1,0:T(8,128)(2,1)S(1)} collective-permute-done((bf16[2,256,512]{2,1,0:T(8,128)(2,1)S(1)}, bf16[2,256,512]{2,1,0:T(8,128)(2,1)S(1)}, u32[]{:S(2)}, u32[]{:S(2)}) %collective-permute-start.2) | collective-permute-done | bytes 524320 | tf_op jit(solution)/shard_map/ppermute | solution.py:204
  61.9 1.2 copy-done.1
  63.1 2.4 %shard_map.39.second_ref = bf16[2,128,768]{2,1,0:T(8,128)(2,1)S(1)} custom-call(s32[5]{0:T(128)S(1)} %stack.52.order_ref, bf16[2,128,1024]{2,1,0:T(8,128)(2,1)S(1)} %bitcast.100, bf16[2,128,1024]{2,1,0:T(8,128)(2,1)S(1)} %bitcast.94, bf16[2,256,1024]{2,1,0:T(8,128)(2,1)S(1)} %collective-permute-done.mate_ref, bf16[2,256,1024]{2,1,0:T(8,128)(2,1)S(1)} %copy-done.1, ...), custom_call_target="tpu_custom_call" | custom-call | tf_op jit(solution)/shard_map/pallas_call | solution.py:27
  65.5 10.7 %collective-permute-start.3 = (bf16[2,128,768]{2,1,0:T(8,128)(2,1)S(1)}, bf16[2,128,768]{2,1,0:T(8,128)(2,1)}, u32[]{:S(2)}, u32[]{:S(2)}) collective-permute-start(bf16[2,128,768]{2,1,0:T(8,128)(2,1)S(1)} %shard_map.39.second_ref), channel_id=1, source_target_pairs={{0,3},{1,2},{2,1},{3,0},{4,5},{5,4},{6,7},{7,6},{8,11},{9,10},{10,... | collective-permute-start | bytes 1179656 | tf_op jit(solution)/shard_map/ppermute | solution.py:204
  76.3 1.5 shard_map.40
  77.8 4.1 %collective-permute-start.9 = (bf16[2,256,512]{2,1,0:T(8,128)(2,1)}, bf16[2,256,512]{2,1,0:T(8,128)(2,1)}, u32[]{:S(2)}, u32[]{:S(2)}) collective-permute-start(bf16[2,256,512]{2,1,0:T(8,128)(2,1)} %shard_map.40), channel_id=1, source_target_pairs={{0,1},{1,0},{2,3},{3,2},{4,7},{5,6},{6,5},{7,4},{8,9},{9,8},{10,11... | collective-permute-start | bytes 1572872 | tf_op jit(solution)/shard_map/ppermute | solution.py:204
  82.0 1.1 dynamic-slice_bitcast_fusion.1
  83.2 28.2 %collective-permute-done.3.late_ref = bf16[2,128,768]{2,1,0:T(8,128)(2,1)} collective-permute-done((bf16[2,128,768]{2,1,0:T(8,128)(2,1)S(1)}, bf16[2,128,768]{2,1,0:T(8,128)(2,1)}, u32[]{:S(2)}, u32[]{:S(2)}) %collective-permute-start.3) | collective-permute-done | bytes 393248 | tf_op jit(solution)/shard_map/ppermute | solution.py:204
  111.3 1.2 copy-done.2
  112.6 1.0 copy-done.4
  113.6 2.2 %shard_map.41 = (bf16[2,128,512]{2,1,0:T(8,128)(2,1)S(1)}, bf16[2,2,64,128]{3,2,1,0:T(8,128)(2,1)S(1)}, bf16[2,2,64,128]{3,2,1,0:T(8,128)(2,1)S(1)}, bf16[2,2,64...) custom-call(s32[5]{0:T(128)S(1)} %stack.52.order_ref, bf16[2,128,1024]{2,1,0:T(8,128)(2,1)S(1)} %bitcast.95, ...), custom_call_target="tpu_custom_call" | custom-call | tf_op jit(solution)/shard_map/pallas_call | solution.py:27
  115.9 3.1 %collective-permute-start.5 = (bf16[2,2,64,128]{3,2,1,0:T(8,128)(2,1)S(1)}, bf16[2,2,64,128]{3,2,1,0:T(8,128)(2,1)S(1)}, u32[]{:S(2)}, u32[]{:S(2)}) collective-permute-start(bf16[2,2,64,128]{3,2,1,0:T(8,128)(2,1)S(1)} %get-tuple-element.33), channel_id=1, source_target_pairs={{0,4},{1,5},{2,6},{3,7},{4,0},{5,1},{6,2},{7,3},{8,12},{9,13},{10,... | collective-permute-start | bytes 196616 | tf_op jit(solution)/shard_map/ppermute | solution.py:204
  119.0 7.9 %collective-permute-start.6 = (bf16[2,2,64,128]{3,2,1,0:T(8,128)(2,1)S(1)}, bf16[2,2,64,128]{3,2,1,0:T(8,128)(2,1)S(1)}, u32[]{:S(2)}, u32[]{:S(2)}) collective-permute-start(bf16[2,2,64,128]{3,2,1,0:T(8,128)(2,1)S(1)} %get-tuple-element.34), channel_id=1, source_target_pairs={{0,5},{1,4},{2,7},{3,6},{4,3},{5,2},{6,1},{7,0},{8,13},{9,12},{10,... | collective-permute-start | bytes 196616 | tf_op jit(solution)/shard_map/ppermute | solution.py:204
  126.9 1.9 %collective-permute-start.7 = (bf16[2,2,64,128]{3,2,1,0:T(8,128)(2,1)S(1)}, bf16[2,2,64,128]{3,2,1,0:T(8,128)(2,1)S(1)}, u32[]{:S(2)}, u32[]{:S(2)}) collective-permute-start(bf16[2,2,64,128]{3,2,1,0:T(8,128)(2,1)S(1)} %get-tuple-element.35), channel_id=1, source_target_pairs={{0,508},{1,509},{2,510},{3,511},{4,8},{5,9},{6,10},{7,11},{8,4},{9... | collective-permute-start | bytes 196616 | tf_op jit(solution)/shard_map/ppermute | solution.py:204
  128.8 7.8 %collective-permute-start.8 = (bf16[2,2,64,128]{3,2,1,0:T(8,128)(2,1)S(1)}, bf16[2,2,64,128]{3,2,1,0:T(8,128)(2,1)S(1)}, u32[]{:S(2)}, u32[]{:S(2)}) collective-permute-start(bf16[2,2,64,128]{3,2,1,0:T(8,128)(2,1)S(1)} %get-tuple-element.36), channel_id=1, source_target_pairs={{0,509},{1,508},{2,511},{3,510},{4,11},{5,10},{6,9},{7,8},{8,5},{9... | collective-permute-start | bytes 196616 | tf_op jit(solution)/shard_map/ppermute | solution.py:204
  136.7 2.9 %shard_map.42.second_ref = bf16[2,128,768]{2,1,0:T(8,128)(2,1)S(1)} custom-call(s32[5]{0:T(128)S(1)} %stack.52.order_ref, bf16[2,128,1024]{2,1,0:T(8,128)(2,1)S(1)} %bitcast.101, bf16[2,128,1024]{2,1,0:T(8,128)(2,1)S(1)} %bitcast.96, bf16[2,256,1024]{2,1,0:T(8,128)(2,1)S(1)} %collective-permute-done.4.right_ref, ...), custom_call_target="tpu_custom_call" | custom-call | tf_op jit(solution)/shard_map/pallas_call | solution.py:27
  139.6 4.7 %collective-permute-start.10 = (bf16[2,128,768]{2,1,0:T(8,128)(2,1)S(1)}, bf16[2,128,768]{2,1,0:T(8,128)(2,1)S(1)}, u32[]{:S(2)}, u32[]{:S(2)}) collective-permute-start(bf16[2,128,768]{2,1,0:T(8,128)(2,1)S(1)} %shard_map.42.second_ref), channel_id=1, source_target_pairs={{0,3},{1,2},{2,1},{3,0},{4,5},{5,4},{6,7},{7,6},{8,11},{9,10},{10,... | collective-permute-start | bytes 1179656 | tf_op jit(solution)/shard_map/ppermute | solution.py:204
  144.3 0.2 convolution_convert_fusion.2
  144.6 0.2 fusion.35
  144.9 1.3 convolution_convert_fusion.1
  146.2 0.2 fusion.36
  146.4 0.1 broadcast_select_fusion.3
  146.6 12.4 %collective-permute-done.10.late_ref = bf16[2,128,768]{2,1,0:T(8,128)(2,1)S(1)} collective-permute-done((bf16[2,128,768]{2,1,0:T(8,128)(2,1)S(1)}, bf16[2,128,768]{2,1,0:T(8,128)(2,1)S(1)}, u32[]{:S(2)}, u32[]{:S(2)}) %collective-permute-start.10) | collective-permute-done | bytes 393248 | tf_op jit(solution)/shard_map/ppermute | solution.py:204
  159.0 2.3 %shard_map.43 = (bf16[2,128,512]{2,1,0:T(8,128)(2,1)S(1)}, bf16[2,2,2,64,128]{4,3,2,1,0:T(8,128)(2,1)S(1)}, bf16[2,2,2,64,128]{4,3,2,1,0:T(8,128)(2,1)S(1)}) custom-call(s32[5]{0:T(128)S(1)} %stack.52.order_ref, bf16[2,128,1024]{2,1,0:T(8,128)(2,1)S(1)} %bitcast.97, bf16[2,256,1024]{2,1,0:T(8,128)(2,1)S(1)} %collective-permute-done.4.right_ref, ...), custom_call_target="tpu_custom_call" | custom-call | tf_op jit(solution)/shard_map/pallas_call | solution.py:27
  161.3 8.5 %collective-permute-start.11 = (bf16[2,2,2,64,128]{4,3,2,1,0:T(8,128)(2,1)S(1)}, bf16[2,2,2,64,128]{4,3,2,1,0:T(8,128)(2,1)S(1)}, u32[]{:S(2)}, u32[]{:S(2)}) collective-permute-start(bf16[2,2,2,64,128]{4,3,2,1,0:T(8,128)(2,1)S(1)} %get-tuple-element.43), channel_id=1, source_target_pairs={{0,9},{1,8},{2,11},{3,10},{4,511},{5,510},{6,509},{7,508},{8,17},{... | collective-permute-start | bytes 393224 | tf_op jit(solution)/shard_map/ppermute | solution.py:204
  169.8 0.1 broadcast_select_fusion.1
  169.9 1.9 %collective-permute-start.12 = (bf16[2,2,2,64,128]{4,3,2,1,0:T(8,128)(2,1)S(1)}, bf16[2,2,2,64,128]{4,3,2,1,0:T(8,128)(2,1)S(1)}, u32[]{:S(2)}, u32[]{:S(2)}) collective-permute-start(bf16[2,2,2,64,128]{4,3,2,1,0:T(8,128)(2,1)S(1)} %get-tuple-element.44), channel_id=1, source_target_pairs={{0,8},{1,9},{2,10},{3,11},{4,508},{5,509},{6,510},{7,511},{8,16},{... | collective-permute-start | bytes 393224 | tf_op jit(solution)/shard_map/ppermute | solution.py:204
  171.8 6.1 %collective-permute-done.11 = bf16[2,2,2,64,128]{4,3,2,1,0:T(8,128)(2,1)S(1)} collective-permute-done((bf16[2,2,2,64,128]{4,3,2,1,0:T(8,128)(2,1)S(1)}, bf16[2,2,2,64,128]{4,3,2,1,0:T(8,128)(2,1)S(1)}, u32[]{:S(2)}, u32[]{:S(2)}) %collective-permute-start.11) | collective-permute-done | bytes 131104 | tf_op jit(solution)/shard_map/ppermute | solution.py:204
  177.9 3.7 %collective-permute-done.12 = bf16[2,2,2,64,128]{4,3,2,1,0:T(8,128)(2,1)S(1)} collective-permute-done((bf16[2,2,2,64,128]{4,3,2,1,0:T(8,128)(2,1)S(1)}, bf16[2,2,2,64,128]{4,3,2,1,0:T(8,128)(2,1)S(1)}, u32[]{:S(2)}, u32[]{:S(2)}) %collective-permute-start.12) | collective-permute-done | bytes 131104 | tf_op jit(solution)/shard_map/ppermute | solution.py:204
  181.6 0.3 convolution_convert_fusion
  181.9 0.1 select_bitcast_fusion.1
  182.0 0.1 maximum_bitcast_fusion
  182.1 0.1 copy.12
  182.2 2.1 %copy.13 = bf16[4,128,2,512]{3,2,1,0:T(2,128)(2,1)} copy(bf16[4,128,2,512]{3,1,2,0:T(8,128)(2,1)S(1)} %bitcast.103) | data formatting | bytes 2097152 | tf_op jit(solution)/shard_map/reshape | solution.py:312
  (43 shorter events, 0.3 us)
Async XLA Ops:
  0.0 13.6 %copy-start.13 = (f32[512]{0:T(512)S(1)}, f32[512]{0:T(512)}, u32[]{:S(2)}) copy-start(f32[512]{0:T(512)} %param.4) | copy-start | bytes 6148
  2.6 12.7 %collective-permute-start = (bf16[2,256,1024]{2,1,0:T(8,128)(2,1)}, bf16[2,256,1024]{2,1,0:T(8,128)(2,1)S(1)}, u32[]{:S(2)}, u32[]{:S(2)}) collective-permute-start(bf16[2,256,1024]{2,1,0:T(8,128)(2,1)} %reshape.182.plain_ref), channel_id=1, source_target_pairs={{0,4},{4,0},{8,12},{12,8},{16,20},{20,16},{24,28},{28,24},{32,36},... | collective-permute-start | bytes 3145736 | tf_op jit(solution)/shard_map/ppermute | solution.py:193
  4.5 21.7 %collective-permute-start.1 = (bf16[2,256,1024]{2,1,0:T(8,128)(2,1)}, bf16[2,256,1024]{2,1,0:T(8,128)(2,1)S(1)}, u32[]{:S(2)}, u32[]{:S(2)}) collective-permute-start(bf16[2,256,1024]{2,1,0:T(8,128)(2,1)} %reshape.182.plain_ref), channel_id=1, source_target_pairs={{0,508},{4,8},{8,4},{12,16},{16,12},{20,24},{24,20},{28,32},{32,28... | collective-permute-start | bytes 3145736 | tf_op jit(solution)/shard_map/ppermute | solution.py:193
  27.5 1.0 copy-start
  28.5 47.8 %collective-permute-start.4 = (bf16[2,256,1024]{2,1,0:T(8,128)(2,1)}, bf16[2,256,1024]{2,1,0:T(8,128)(2,1)S(1)}, u32[]{:S(2)}, u32[]{:S(2)}) collective-permute-start(bf16[2,256,1024]{2,1,0:T(8,128)(2,1)} %copy-done), channel_id=1, source_target_pairs={{0,4},{4,0},{8,12},{12,8},{16,20},{20,16},{24,28},{28,24},{32,36},... | collective-permute-start | bytes 3145736 | tf_op jit(solution)/shard_map/ppermute | solution.py:193
  30.4 31.5 %collective-permute-start.2 = (bf16[2,256,512]{2,1,0:T(8,128)(2,1)S(1)}, bf16[2,256,512]{2,1,0:T(8,128)(2,1)S(1)}, u32[]{:S(2)}, u32[]{:S(2)}) collective-permute-start(bf16[2,256,512]{2,1,0:T(8,128)(2,1)S(1)} %shard_map.38), channel_id=1, source_target_pairs={{0,1},{1,0},{2,3},{3,2},{4,7},{5,6},{6,5},{7,4},{8,9},{9,8},{10,11... | collective-permute-start | bytes 1572872 | tf_op jit(solution)/shard_map/ppermute | solution.py:204
  61.9 1.2 copy-start.1
  63.1 14.7 %copy-start.3 = (bf16[2,256,512]{2,1,0:T(8,128)(2,1)}, bf16[2,256,512]{2,1,0:T(8,128)(2,1)S(1)}, u32[]{:S(2)}) copy-start(bf16[2,256,512]{2,1,0:T(8,128)(2,1)S(1)} %collective-permute-done.2.got_ref) | copy-start | bytes 1572868
  65.5 45.8 %collective-permute-start.3 = (bf16[2,128,768]{2,1,0:T(8,128)(2,1)S(1)}, bf16[2,128,768]{2,1,0:T(8,128)(2,1)}, u32[]{:S(2)}, u32[]{:S(2)}) collective-permute-start(bf16[2,128,768]{2,1,0:T(8,128)(2,1)S(1)} %shard_map.39.second_ref), channel_id=1, source_target_pairs={{0,3},{1,2},{2,1},{3,0},{4,5},{5,4},{6,7},{7,6},{8,11},{9,10},{10,... | collective-permute-start | bytes 1179656 | tf_op jit(solution)/shard_map/ppermute | solution.py:204
  77.8 58.9 %collective-permute-start.9 = (bf16[2,256,512]{2,1,0:T(8,128)(2,1)}, bf16[2,256,512]{2,1,0:T(8,128)(2,1)}, u32[]{:S(2)}, u32[]{:S(2)}) collective-permute-start(bf16[2,256,512]{2,1,0:T(8,128)(2,1)} %shard_map.40), channel_id=1, source_target_pairs={{0,1},{1,0},{2,3},{3,2},{4,7},{5,6},{6,5},{7,4},{8,9},{9,8},{10,11... | collective-permute-start | bytes 1572872 | tf_op jit(solution)/shard_map/ppermute | solution.py:204
  83.1 61.2 %copy-start.5 = (bf16[128,512]{1,0:T(8,128)(2,1)}, bf16[128,512]{1,0:T(8,128)(2,1)S(1)}, u32[]{:S(2)}) copy-start(bf16[128,512]{1,0:T(8,128)(2,1)S(1)} %get-tuple-element.51) | copy-start | bytes 393220
  83.1 61.2 %copy-start.7 = (bf16[128,512]{1,0:T(8,128)(2,1)}, bf16[128,512]{1,0:T(8,128)(2,1)S(1)}, u32[]{:S(2)}) copy-start(bf16[128,512]{1,0:T(8,128)(2,1)S(1)} %get-tuple-element.52) | copy-start | bytes 393220
  83.1 61.2 %copy-start.9 = (bf16[128,512]{1,0:T(8,128)(2,1)}, bf16[128,512]{1,0:T(8,128)(2,1)S(1)}, u32[]{:S(2)}) copy-start(bf16[128,512]{1,0:T(8,128)(2,1)S(1)} %get-tuple-element.53) | copy-start | bytes 393220
  83.1 61.2 %copy-start.11 = (bf16[128,512]{1,0:T(8,128)(2,1)}, bf16[128,512]{1,0:T(8,128)(2,1)S(1)}, u32[]{:S(2)}) copy-start(bf16[128,512]{1,0:T(8,128)(2,1)S(1)} %get-tuple-element.54) | copy-start | bytes 393220
  111.3 1.2 copy-start.2
  112.6 1.0 copy-start.4
  115.9 28.4 %collective-permute-start.5 = (bf16[2,2,64,128]{3,2,1,0:T(8,128)(2,1)S(1)}, bf16[2,2,64,128]{3,2,1,0:T(8,128)(2,1)S(1)}, u32[]{:S(2)}, u32[]{:S(2)}) collective-permute-start(bf16[2,2,64,128]{3,2,1,0:T(8,128)(2,1)S(1)} %get-tuple-element.33), channel_id=1, source_target_pairs={{0,4},{1,5},{2,6},{3,7},{4,0},{5,1},{6,2},{7,3},{8,12},{9,13},{10,... | collective-permute-start | bytes 196616 | tf_op jit(solution)/shard_map/ppermute | solution.py:204
  119.0 25.2 %collective-permute-start.6 = (bf16[2,2,64,128]{3,2,1,0:T(8,128)(2,1)S(1)}, bf16[2,2,64,128]{3,2,1,0:T(8,128)(2,1)S(1)}, u32[]{:S(2)}, u32[]{:S(2)}) collective-permute-start(bf16[2,2,64,128]{3,2,1,0:T(8,128)(2,1)S(1)} %get-tuple-element.34), channel_id=1, source_target_pairs={{0,5},{1,4},{2,7},{3,6},{4,3},{5,2},{6,1},{7,0},{8,13},{9,12},{10,... | collective-permute-start | bytes 196616 | tf_op jit(solution)/shard_map/ppermute | solution.py:204
  126.9 17.3 %collective-permute-start.7 = (bf16[2,2,64,128]{3,2,1,0:T(8,128)(2,1)S(1)}, bf16[2,2,64,128]{3,2,1,0:T(8,128)(2,1)S(1)}, u32[]{:S(2)}, u32[]{:S(2)}) collective-permute-start(bf16[2,2,64,128]{3,2,1,0:T(8,128)(2,1)S(1)} %get-tuple-element.35), channel_id=1, source_target_pairs={{0,508},{1,509},{2,510},{3,511},{4,8},{5,9},{6,10},{7,11},{8,4},{9... | collective-permute-start | bytes 196616 | tf_op jit(solution)/shard_map/ppermute | solution.py:204
  128.8 15.4 %collective-permute-start.8 = (bf16[2,2,64,128]{3,2,1,0:T(8,128)(2,1)S(1)}, bf16[2,2,64,128]{3,2,1,0:T(8,128)(2,1)S(1)}, u32[]{:S(2)}, u32[]{:S(2)}) collective-permute-start(bf16[2,2,64,128]{3,2,1,0:T(8,128)(2,1)S(1)} %get-tuple-element.36), channel_id=1, source_target_pairs={{0,509},{1,508},{2,511},{3,510},{4,11},{5,10},{6,9},{7,8},{8,5},{9... | collective-permute-start | bytes 196616 | tf_op jit(solution)/shard_map/ppermute | solution.py:204
  139.6 19.5 %collective-permute-start.10 = (bf16[2,128,768]{2,1,0:T(8,128)(2,1)S(1)}, bf16[2,128,768]{2,1,0:T(8,128)(2,1)S(1)}, u32[]{:S(2)}, u32[]{:S(2)}) collective-permute-start(bf16[2,128,768]{2,1,0:T(8,128)(2,1)S(1)} %shard_map.42.second_ref), channel_id=1, source_target_pairs={{0,3},{1,2},{2,1},{3,0},{4,5},{5,4},{6,7},{7,6},{8,11},{9,10},{10,... | collective-permute-start | bytes 1179656 | tf_op jit(solution)/shard_map/ppermute | solution.py:204
  146.6 35.0 %copy-start.6 = (bf16[128,512]{1,0:T(8,128)(2,1)S(1)}, bf16[128,512]{1,0:T(8,128)(2,1)}, u32[]{:S(2)}) copy-start(bf16[128,512]{1,0:T(8,128)(2,1)} %copy-done.5) | copy-start | bytes 393220
  146.6 35.0 %copy-start.8 = (bf16[128,512]{1,0:T(8,128)(2,1)S(1)}, bf16[128,512]{1,0:T(8,128)(2,1)}, u32[]{:S(2)}) copy-start(bf16[128,512]{1,0:T(8,128)(2,1)} %copy-done.7) | copy-start | bytes 393220
  146.6 35.0 %copy-start.10 = (bf16[128,512]{1,0:T(8,128)(2,1)S(1)}, bf16[128,512]{1,0:T(8,128)(2,1)}, u32[]{:S(2)}) copy-start(bf16[128,512]{1,0:T(8,128)(2,1)} %copy-done.9) | copy-start | bytes 393220
  146.6 35.0 %copy-start.12 = (bf16[128,512]{1,0:T(8,128)(2,1)S(1)}, bf16[128,512]{1,0:T(8,128)(2,1)}, u32[]{:S(2)}) copy-start(bf16[128,512]{1,0:T(8,128)(2,1)} %copy-done.11) | copy-start | bytes 393220
  161.3 16.6 %collective-permute-start.11 = (bf16[2,2,2,64,128]{4,3,2,1,0:T(8,128)(2,1)S(1)}, bf16[2,2,2,64,128]{4,3,2,1,0:T(8,128)(2,1)S(1)}, u32[]{:S(2)}, u32[]{:S(2)}) collective-permute-start(bf16[2,2,2,64,128]{4,3,2,1,0:T(8,128)(2,1)S(1)} %get-tuple-element.43), channel_id=1, source_target_pairs={{0,9},{1,8},{2,11},{3,10},{4,511},{5,510},{6,509},{7,508},{8,17},{... | collective-permute-start | bytes 393224 | tf_op jit(solution)/shard_map/ppermute | solution.py:204
  169.9 11.7 %collective-permute-start.12 = (bf16[2,2,2,64,128]{4,3,2,1,0:T(8,128)(2,1)S(1)}, bf16[2,2,2,64,128]{4,3,2,1,0:T(8,128)(2,1)S(1)}, u32[]{:S(2)}, u32[]{:S(2)}) collective-permute-start(bf16[2,2,2,64,128]{4,3,2,1,0:T(8,128)(2,1)S(1)} %get-tuple-element.44), channel_id=1, source_target_pairs={{0,8},{1,9},{2,10},{3,11},{4,508},{5,509},{6,510},{7,511},{8,16},{... | collective-permute-start | bytes 393224 | tf_op jit(solution)/shard_map/ppermute | solution.py:204

commit v11 on v9

v11 whole, which is shorter than its diff:
```python
import math

import jax
import jax.numpy as jnp
from jax import lax
from jax.experimental import pallas as pl
from jax.experimental.pallas import tpu as pltpu
from jax.sharding import PartitionSpec as P

BLOCK = 32


def local(kernel, shapes, *operands, scalars=0, moved=0):
    vmem = pl.BlockSpec(memory_space=pltpu.VMEM)
    smem = pl.BlockSpec(memory_space=pltpu.SMEM)
    several = len(shapes) > 1
    out_shape = [jax.ShapeDtypeStruct(s, jnp.bfloat16) for s in shapes]
    return pl.pallas_call(
        kernel,
        out_shape=out_shape if several else out_shape[0],
        in_specs=[smem] * scalars + [vmem] * (len(operands) - scalars),
        out_specs=[vmem] * len(shapes) if several else vmem,
        compiler_params=pltpu.CompilerParams(vmem_limit_bytes=40 * 1024 * 1024),
        cost_estimate=pl.CostEstimate(flops=0, transcendentals=0, bytes_accessed=moved),
    )(*operands)


def dots(left, right):
    return lax.dot_general(left, right, (((1,), (1,)), ((), ())), preferred_element_type=jnp.float32)


def low(value):
    return value.astype(jnp.bfloat16)


def wide(value):
    return value.astype(jnp.float32)


def left_kernel(order_ref, plain_ref, weight_ref, left_ref):
    points, transitions, depth = plain_ref.shape
    owners = order_ref.shape[0] - 1
    blocks = transitions // (owners * BLOCK)
    weight = weight_ref[...]
    for point in range(points):
        for slot in range(owners):
            for block in range(blocks):
                start = pl.multiple_of((block * owners + order_ref[slot]) * BLOCK, BLOCK)
                rows = wide(plain_ref[point, pl.ds(start, BLOCK), :]) * weight
                place = pl.ds(block * BLOCK, BLOCK)
                left_ref[point, slot, 0, place, :] = low(rows)
                left_ref[point, slot, 1, place, : depth // 2] = low(-rows[:, depth // 2 :])
                left_ref[point, slot, 1, place, depth // 2 :] = low(rows[:, : depth // 2])


def agreeing(order_ref, point):
    even = order_ref[order_ref.shape[0] - 1]
    return point + even - 2 * even * point


def away_pair_kernel(order_ref, left_ref, mate_ref, next_ref, out_ref):
    points, _, columns = out_ref.shape
    half = columns // 2
    for point in range(points):
        for part, right_ref in enumerate((mate_ref, next_ref)):
            out_ref[point, :, part * half : (part + 1) * half] = low(
                dots(left_ref[point], right_ref[agreeing(order_ref, point)])
            )


def away_far_kernel(left_ref, right_ref, out_ref):
    points, _, columns = out_ref.shape
    half = columns // points
    for point in range(points):
        for part in range(points):
            out_ref[point, :, part * half : (part + 1) * half] = low(dots(left_ref[point], right_ref[part]))


def rest_pair_kernel(order_ref, left_ref, mate_ref, next_ref, out_ref):
    _, points, count, columns = out_ref.shape
    half = columns // 2
    for point in range(points):
        rows = left_ref[point].reshape(2 * count, -1)
        for part, right_ref in enumerate((mate_ref, next_ref)):
            out = low(dots(rows, right_ref[agreeing(order_ref, point)]))
            out_ref[0, point, :, part * half : (part + 1) * half] = out[:count]
            out_ref[1, point, :, part * half : (part + 1) * half] = out[count:]


def rest_far_kernel(left_ref, right_ref, out_ref):
    _, points, count, columns = out_ref.shape
    half = columns // points
    for point in range(points):
        rows = left_ref[point].reshape(2 * count, -1)
        for part in range(points):
            out = low(dots(rows, right_ref[part]))
            out_ref[0, point, :, part * half : (part + 1) * half] = out[:count]
            out_ref[1, point, :, part * half : (part + 1) * half] = out[count:]


def picked(order_ref, slots, rows, owners, transitions):
    n = lax.broadcasted_iota(jnp.int32, (rows, transitions), 0)
    column = lax.broadcasted_iota(jnp.int32, (rows, transitions), 1)
    target = (n // BLOCK * owners) * BLOCK + n % BLOCK
    return jnp.concatenate(
        [low(jnp.where(column == target + order_ref[slot] * BLOCK, 1.0, 0.0)) for slot in slots], axis=0
    )


def second_kernel(order_ref, rest_ref, got_ref, out_ref):
    points, count, _ = out_ref.shape
    half = rest_ref.shape[3] // 2
    owners = order_ref.shape[0] - 1
    pick = picked(order_ref, (2, 1), count // 2, owners, half)
    for point in range(points):
        out_ref[point, :, : 2 * half] = low(wide(rest_ref[0, point]) + wide(got_ref[point, count:, :]))
        own = low(wide(rest_ref[1, point]) + wide(got_ref[point, :count, :]))
        for part in range(2):
            place = (2 * half + part * count, 2 * half + (part + 1) * count)
            out_ref[point, :, place[0] : place[1]] = low(dots(own[:, part * half : (part + 1) * half], pick))


def turned_part(order_ref, block_ref, second_ref, late_ref, part, same_ref, first_ref, index):
    points, count, columns = block_ref.shape
    half = columns // 2
    rows = count // 2
    owners = order_ref.shape[0] - 1
    span = pl.ds(part * half, half)
    own = jnp.concatenate(
        [block_ref[point, p * rows : (p + 1) * rows, span] for p in range(2) for point in range(points)], axis=0
    )
    pick = picked(order_ref, (3, 0), rows, owners, half)
    others = []
    for point in range(points):
        other = dots(second_ref[point, :, span], pick) + wide(late_ref[point, :, pl.ds(columns + part * count, count)])
        others.append(low(other))
    other = jnp.concatenate(
        [others[point][p * rows : (p + 1) * rows] for p in range(2) for point in range(points)], axis=0
    )
    n = lax.broadcasted_iota(jnp.int32, (count, count), 0)
    same = low(jnp.where(n == lax.broadcasted_iota(jnp.int32, (count, count), 1), 1.0, 0.0))
    for source, out in enumerate((dots(pick, own), dots(same, other))):
        for to, ref in enumerate((same_ref, first_ref)):
            piece = out[to * rows : (to + 1) * rows]
            ref[source, *index, 0] = low(piece[:, : points * rows])
            ref[source, *index, 1] = low(-piece[:, points * rows :])


def finish(order_ref, rest_ref, got_ref, second_ref, late_ref, block_ref):
    points, count, columns = block_ref.shape
    for point in range(points):
        total = wide(rest_ref[1, point]) + wide(got_ref[point, :count, :]) + wide(late_ref[point, :, :columns])
        block_ref[point] = low(total)


def finish_pair_kernel(
    order_ref, rest_ref, got_ref, second_ref, late_ref,
    block_ref, mate_same_ref, mate_first_ref, next_same_ref, next_first_ref,
):
    finish(order_ref, rest_ref, got_ref, second_ref, late_ref, block_ref)
    turned_part(order_ref, block_ref, second_ref, late_ref, 0, mate_same_ref, mate_first_ref, ())
    turned_part(order_ref, block_ref, second_ref, late_ref, 1, next_same_ref, next_first_ref, ())


def finish_far_kernel(order_ref, rest_ref, got_ref, second_ref, late_ref, block_ref, same_ref, first_ref):
    finish(order_ref, rest_ref, got_ref, second_ref, late_ref, block_ref)
    for part in range(block_ref.shape[0]):
        turned_part(order_ref, block_ref, second_ref, late_ref, part, same_ref, first_ref, (part,))


def merge_kernel(
    order_ref, pair_ref, far_ref, mate_same_ref, mate_first_ref, next_same_ref, next_first_ref,
    far_same_ref, far_first_ref, out_ref,
):
    points, count, columns = pair_ref.shape
    rows = count // 2
    half = columns // 2
    owners = order_ref.shape[0] - 1
    even = order_ref[owners]
    lanes = points * rows
    n = lax.broadcasted_iota(jnp.int32, (lanes, columns), 0)
    column = lax.broadcasted_iota(jnp.int32, (lanes, columns), 1)
    target = (n // BLOCK * owners) * BLOCK + n % BLOCK
    sources = [
        (mate_same_ref, 1, next_same_ref, 1, far_first_ref, 0),
        (mate_first_ref, 1, next_first_ref, 1, far_first_ref, 1),
        (mate_first_ref, 0, next_first_ref, 0, far_same_ref, 1),
        (mate_same_ref, 0, next_same_ref, 0, far_same_ref, 0),
    ]
    total = 0.0
    for slot, (mate_piece, i, next_piece, j, far_piece, k) in enumerate(sources):
        pick = low(jnp.where(column == target + order_ref[slot] * BLOCK, 1.0, 0.0))
        tiles = [mate_piece[i, p] for p in range(2)] + [next_piece[j, p] for p in range(2)]
        tiles += [far_piece[k, part, p] for part in range(points) for p in range(2)]
        total = total + lax.dot_general(
            jnp.concatenate(tiles, axis=0), pick, (((1,), (0,)), ((), ())), preferred_element_type=jnp.float32
        )
    back = low(total)
    for p in range(2):
        for part, place in ((0, 2 * even), (1, 2 - 2 * even)):
            natural = back[(2 * part + p) * rows : (2 * part + p + 1) * rows]
            for row_point in range(points):
                here = pair_ref[row_point, p * rows : (p + 1) * rows, part * half : (part + 1) * half]
                for column_point in range(points):
                    there = natural[:, column_point * half : (column_point + 1) * half]
                    mine = even == (0 if row_point == column_point else 1)
                    out_ref[
                        place, p, row_point * rows : (row_point + 1) * rows, column_point * half : (column_point + 1) * half
                    ] = jnp.where(mine, here, there)
        for point in range(points):
            span = slice(point * rows, (point + 1) * rows)
            out_ref[1 + 2 * even, p, span, :] = far_ref[point, p * rows : (p + 1) * rows, :]
            first = (4 + 2 * point + p) * rows
            out_ref[3 - 2 * even, p, span, :] = back[first : first + rows]


def body(pair_density, coulomb):
    points, transitions, _, g_local = pair_density.shape
    owners = lax.axis_size("own")
    groups = lax.axis_size("kp")
    blocks = transitions // (owners * BLOCK)
    rows = blocks * BLOCK
    depth = 2 * g_local
    scale = 1.0 / math.sqrt(g_local * owners)
    me = lax.axis_index("own")
    odd = lax.axis_index("kp") % 2 == 1
    parity = odd.astype(jnp.int32)

    def exchange_kp(value, partner):
        return lax.ppermute(value, "kp", [(i, partner(i) % groups) for i in range(groups)])

    def flips(i):
        return [1, 2, 3, 0] if i % 2 == 0 else [3, 2, 1, 0]

    def exchange(value, slot, partner):
        pairs = [
            (i * owners + o, partner(i) % groups * owners + (o ^ flips(i)[slot]))
            for i in range(groups)
            for o in range(owners)
        ]
        return lax.ppermute(value, ("kp", "own"), pairs)

    def exchange_own(value, first):
        return exchange(value, 0 if first else 2, lambda i: i)

    def mate(i):
        return i + 1 if i % 2 == 0 else i - 1

    def across(i):
        return i - 1 if i % 2 == 0 else i + 1

    def second_next(i):
        return i + 2 if i % 2 == 0 else i - 2

    near_flip, far_flip = 1 + 2 * parity, 3 - 2 * parity
    relative = jnp.stack([me ^ near_flip, me ^ 2, me ^ far_flip, me, 1 - parity])

    plain = pair_density.reshape(points, transitions, depth)
    mate_right = exchange_kp(plain, mate)
    next_right = exchange_kp(plain, across)

    weights = (jnp.concatenate([coulomb, coulomb]) * scale).reshape(1, depth)
    left = local(left_kernel, [(points, owners, 2, rows, depth)], relative, plain, weights, scalars=1, moved=4 << 20)
    left_away = left[:, :2].reshape(points, 4 * rows, depth)
    left_rest = left[:, 2:].reshape(points, 4 * rows, depth)

    left_away, left_rest, mate_right = lax.optimization_barrier((left_away, left_rest, mate_right))
    columns = points * transitions
    away_shape = [(points, 4 * rows, columns)]
    second_shape = [(points, 2 * rows, columns + 4 * rows)]
    block_shape = (points, 2 * rows, columns)
    pair_back = (2, 2, rows, points * rows)
    far_back = (2, points, 2, rows, points * rows)

    rest_shape = [(2, points, 2 * rows, columns)]

    far_right = exchange_kp(next_right, mate)
    away_pair = local(away_pair_kernel, away_shape, relative, left_away, mate_right, next_right, scalars=1)
    got_pair = exchange_own(away_pair, True)
    far_right, _ = lax.optimization_barrier((far_right, away_pair))
    away_far = local(away_far_kernel, away_shape, left_away, far_right)
    got_far = exchange_own(away_far, True)
    late_left, mate_right, next_right, far_right, _ = lax.optimization_barrier(
        (left_rest, mate_right, next_right, far_right, away_far)
    )
    rest_pair = local(
        rest_pair_kernel, rest_shape, relative, late_left, mate_right, next_right, scalars=1, moved=8 << 20
    )
    rest_far = local(rest_far_kernel, rest_shape, late_left, far_right, moved=8 << 20)
    got_pair, rest_pair, rest_far = lax.optimization_barrier((got_pair, rest_pair, rest_far))
    second_pair = local(second_kernel, second_shape, relative, rest_pair, got_pair, scalars=1)
    late_pair = exchange_own(second_pair, False)
    second_far = local(second_kernel, second_shape, relative, rest_far, got_far, scalars=1)
    late_pair, _ = lax.optimization_barrier((late_pair, second_far))
    late_far = exchange_own(second_far, False)
    block_pair, mate_same, mate_first, next_same, next_first = local(
        finish_pair_kernel, [block_shape] + [pair_back] * 4, relative, rest_pair, got_pair, second_pair, late_pair, scalars=1
    )
    block_far, far_same, far_first = local(
        finish_far_kernel, [block_shape, far_back, far_back], relative, rest_far, got_far, second_far, late_far, scalars=1
    )
    out = local(
        merge_kernel, [(4, 2, points * rows, columns)],
        relative, block_pair, block_far,
        exchange(mate_same, 3, mate), exchange(mate_first, 0, mate),
        exchange(next_same, 3, across), exchange(next_first, 0, across),
        exchange(far_same, 3, second_next), exchange(far_first, 0, second_next),
        scalars=1,
    )
    return out.transpose(0, 2, 1, 3)


def solution(mesh):
    placed = (P("kp", None, None, "own"), P("own"))
    return jax.shard_map(
        body,
        mesh=mesh,
        in_specs=placed,
        out_specs=P(None, ("kp", "own"), None, None),
        check_vma=False,
    )
```

time: 171 us -> 159 us (0.930)
  starting transfers between devices: 59.7 us -> 70.3 us
  waiting for transfers between devices: 80.7 us -> 72.5 us
  Pallas kernels: 16.8 us -> 11.4 us
  local copies, waits for them, and re-layouts: 8.14 us -> 4.14 us
  matrix products: 1.86 us -> 0 us
    ppermute x10, starting transfers between devices: 47.5 us -> 58.2 us  [exchange(): return lax.ppermute(value, ('kp', 'own'), pairs)]
    ppermute x10, waiting for transfers between devices: 69.9 us -> 61.9 us  [exchange(): return lax.ppermute(value, ('kp', 'own'), pairs)]
    pallas_call x7 -> x10, Pallas kernels: 16.8 us -> 11.4 us  [local(): pl.pallas_call(kernel, out_shape=out_shape if several else out_shape[0],...]
    reshape x1 -> x0, local copies, waits for them, and re-layouts: 2.05 us -> none  [body(): out.transpose(0, 1, 3, 2, 4)]
    transpose x1, local copies, waits for them, and re-layouts: 0.07 us -> 2.05 us  [body(): return out.transpose(0, 2, 1, 3)]
    dot_general x3 -> x0, matrix products: 1.86 us -> none  [natural(): lax.dot_general(joined, pick, (((3,), (0,)), ((), ())), preferred_element...]
  transfers between devices with their start and end apart: 13 -> 13, of which waited for: 6 -> 6; matrix products, arithmetic and copies ran while one was open for 3% -> 0% of each run, Pallas kernels for 9% -> 6%
where the time goes in v11:
time: 159 us
  waiting for transfers between devices  72.5 us (46%)
  starting transfers between devices  70.3 us (44%)
  Pallas kernels  11.4 us (7%)
  local copies, waits for them, and re-layouts  4.14 us (3%)
    ppermute x10, waiting for transfers between devices, exchange(): return lax.ppermute(value, ('kp', 'own'), pairs)  61.9 us
    ppermute x10, starting transfers between devices, exchange(): return lax.ppermute(value, ('kp', 'own'), pairs)  58.2 us
    ppermute x3, starting transfers between devices, exchange_kp(): lax.ppermute(value, 'kp', [(i, partner(i) % groups) for i in range(groups)])  12.2 us
    pallas_call x10, Pallas kernels, local(): pl.pallas_call(kernel, out_shape=out_shape if several else out_shape[0],...  11.4 us
    ppermute x3, waiting for transfers between devices, exchange_kp(): lax.ppermute(value, 'kp', [(i, partner(i) % groups) for i in range(groups)])  10.6 us
  transfers between devices with their start and end apart: 13, of which 6 were waited for; matrix products, arithmetic and copies ran while one was open for 0% of the time, Pallas kernels for 6%

profile of v11, /device:TPU:24, one launch (start us, length us, event | category | flops | bytes accessed | tf_op | source)
XLA Modules:
  0.0 158.7 jit_solution(15026795581078288784)
XLA Ops:
  0.0 0.0 copy-start
  0.0 1.8 %reshape.39.plain_ref = bf16[2,256,1024]{2,1,0:T(8,128)(2,1)S(1)} reshape(bf16[2,256,2,512]{3,2,1,0:T(2,128)(2,1)} %param.2) | data formatting | bytes 2097152 | tf_op jit(solution)/shard_map/reshape | solution.py:258
  1.8 8.3 %collective-permute-start.1 = (bf16[2,256,1024]{2,1,0:T(8,128)(2,1)S(1)}, bf16[2,256,1024]{2,1,0:T(8,128)(2,1)S(1)}, u32[]{:S(2)}, u32[]{:S(2)}) collective-permute-start(bf16[2,256,1024]{2,1,0:T(8,128)(2,1)S(1)} %reshape.39.plain_ref), channel_id=1, source_target_pairs={{0,508},{4,8},{8,4},{12,16},{16,12},{20,24},{24,20},{28,32},{32,28... | collective-permute-start | bytes 3145736 | tf_op jit(solution)/shard_map/ppermute | solution.py:230
  10.2 1.9 %collective-permute-start = (bf16[2,256,1024]{2,1,0:T(8,128)(2,1)S(1)}, bf16[2,256,1024]{2,1,0:T(8,128)(2,1)}, u32[]{:S(2)}, u32[]{:S(2)}) collective-permute-start(bf16[2,256,1024]{2,1,0:T(8,128)(2,1)S(1)} %reshape.39.plain_ref), channel_id=1, source_target_pairs={{0,4},{4,0},{8,12},{12,8},{16,20},{20,16},{24,28},{28,24},{32,36},... | collective-permute-start | bytes 3145736 | tf_op jit(solution)/shard_map/ppermute | solution.py:230
  12.1 10.6 %collective-permute-done.1.next_ref = bf16[2,256,1024]{2,1,0:T(8,128)(2,1)S(1)} collective-permute-done((bf16[2,256,1024]{2,1,0:T(8,128)(2,1)S(1)}, bf16[2,256,1024]{2,1,0:T(8,128)(2,1)S(1)}, u32[]{:S(2)}, u32[]{:S(2)}) %collective-permute-start.1) | collective-permute-done | bytes 1048608 | tf_op jit(solution)/shard_map/ppermute | solution.py:230
  22.7 1.9 %collective-permute-start.3 = (bf16[2,256,1024]{2,1,0:T(8,128)(2,1)S(1)}, bf16[2,256,1024]{2,1,0:T(8,128)(2,1)S(1)}, u32[]{:S(2)}, u32[]{:S(2)}) collective-permute-start(bf16[2,256,1024]{2,1,0:T(8,128)(2,1)S(1)} %collective-permute-done.1.next_ref), channel_id=1, source_target_pairs={{0,4},{4,0},{8,12},{12,8},{16,20},{20,16},{24,28},{28,24},{32,36},... | collective-permute-start | bytes 3145736 | tf_op jit(solution)/shard_map/ppermute | solution.py:230
  24.7 0.1 stack.23.order_ref
  24.8 0.0 copy-done
  24.8 0.8 shard_map.28
  25.5 0.2 fusion
  25.8 0.0 collective-permute-done.mate_ref
  25.8 2.0 %shard_map.29 = bf16[2,256,512]{2,1,0:T(8,128)(2,1)S(1)} custom-call(s32[5]{0:T(128)S(1)} %stack.23.order_ref, bf16[2,256,1024]{2,1,0:T(8,128)(2,1)S(1)} %bitcast.11, bf16[2,256,1024]{2,1,0:T(8,128)(2,1)} %collective-permute-done.mate_ref, bf16[2,256,1024]{2,1,0:T(8,128)(2,1)S(1)} %collective-permute-done.1.next_ref), custom_call_target="tpu_custom_call" | custom-call | tf_op jit(solution)/shard_map/pallas_call | solution.py:18
  27.8 9.1 %collective-permute-start.2 = (bf16[2,256,512]{2,1,0:T(8,128)(2,1)S(1)}, bf16[2,256,512]{2,1,0:T(8,128)(2,1)S(1)}, u32[]{:S(2)}, u32[]{:S(2)}) collective-permute-start(bf16[2,256,512]{2,1,0:T(8,128)(2,1)S(1)} %shard_map.29), channel_id=1, source_target_pairs={{0,1},{1,0},{2,3},{3,2},{4,7},{5,6},{6,5},{7,4},{8,9},{9,8},{10,11... | collective-permute-start | bytes 1572872 | tf_op jit(solution)/shard_map/ppermute | solution.py:241
  36.9 0.0 collective-permute-done.3.right_ref
  36.9 0.7 shard_map.30
  37.6 1.9 %collective-permute-start.5 = (bf16[2,256,512]{2,1,0:T(8,128)(2,1)S(1)}, bf16[2,256,512]{2,1,0:T(8,128)(2,1)S(1)}, u32[]{:S(2)}, u32[]{:S(2)}) collective-permute-start(bf16[2,256,512]{2,1,0:T(8,128)(2,1)S(1)} %shard_map.30), channel_id=1, source_target_pairs={{0,1},{1,0},{2,3},{3,2},{4,7},{5,6},{6,5},{7,4},{8,9},{9,8},{10,11... | collective-permute-start | bytes 1572872 | tf_op jit(solution)/shard_map/ppermute | solution.py:241
  39.6 0.8 shard_map.32.rest_ref
  40.3 2.0 %shard_map.31.rest_ref = bf16[2,2,128,512]{3,2,1,0:T(8,128)(2,1)S(1)} custom-call(s32[5]{0:T(128)S(1)} %stack.23.order_ref, bf16[2,256,1024]{2,1,0:T(8,128)(2,1)S(1)} %bitcast.10, bf16[2,256,1024]{2,1,0:T(8,128)(2,1)} %collective-permute-done.mate_ref, bf16[2,256,1024]{2,1,0:T(8,128)(2,1)S(1)} %collective-permute-done.1.next_ref), custom_call_target="tpu_custom_call" | custom-call | bytes 8388608 | tf_op jit(solution)/shard_map/pallas_call | solution.py:18
  42.3 38.8 %collective-permute-done.2.got_ref = bf16[2,256,512]{2,1,0:T(8,128)(2,1)S(1)} collective-permute-done((bf16[2,256,512]{2,1,0:T(8,128)(2,1)S(1)}, bf16[2,256,512]{2,1,0:T(8,128)(2,1)S(1)}, u32[]{:S(2)}, u32[]{:S(2)}) %collective-permute-start.2) | collective-permute-done | bytes 524320 | tf_op jit(solution)/shard_map/ppermute | solution.py:241
  81.1 0.8 shard_map.33.second_ref
  81.9 11.3 %collective-permute-start.4 = (bf16[2,128,768]{2,1,0:T(8,128)(2,1)S(1)}, bf16[2,128,768]{2,1,0:T(8,128)(2,1)S(1)}, u32[]{:S(2)}, u32[]{:S(2)}) collective-permute-start(bf16[2,128,768]{2,1,0:T(8,128)(2,1)S(1)} %shard_map.33.second_ref), channel_id=1, source_target_pairs={{0,3},{1,2},{2,1},{3,0},{4,5},{5,4},{6,7},{7,6},{8,11},{9,10},{10,... | collective-permute-start | bytes 1179656 | tf_op jit(solution)/shard_map/ppermute | solution.py:241
  93.3 0.0 collective-permute-done.5.got_ref
  93.3 0.8 shard_map.34.second_ref
  94.1 12.3 %collective-permute-start.6 = (bf16[2,128,768]{2,1,0:T(8,128)(2,1)S(1)}, bf16[2,128,768]{2,1,0:T(8,128)(2,1)S(1)}, u32[]{:S(2)}, u32[]{:S(2)}) collective-permute-start(bf16[2,128,768]{2,1,0:T(8,128)(2,1)S(1)} %shard_map.34.second_ref), channel_id=1, source_target_pairs={{0,3},{1,2},{2,1},{3,0},{4,5},{5,4},{6,7},{7,6},{8,11},{9,10},{10,... | collective-permute-start | bytes 1179656 | tf_op jit(solution)/shard_map/ppermute | solution.py:241
  106.4 9.9 %collective-permute-done.4.late_ref = bf16[2,128,768]{2,1,0:T(8,128)(2,1)S(1)} collective-permute-done((bf16[2,128,768]{2,1,0:T(8,128)(2,1)S(1)}, bf16[2,128,768]{2,1,0:T(8,128)(2,1)S(1)}, u32[]{:S(2)}, u32[]{:S(2)}) %collective-permute-start.4) | collective-permute-done | bytes 393248 | tf_op jit(solution)/shard_map/ppermute | solution.py:241
  116.4 1.1 shard_map.35
  117.5 3.9 %collective-permute-start.10 = (bf16[2,2,64,128]{3,2,1,0:T(8,128)(2,1)S(1)}, bf16[2,2,64,128]{3,2,1,0:T(8,128)(2,1)S(1)}, u32[]{:S(2)}, u32[]{:S(2)}) collective-permute-start(bf16[2,2,64,128]{3,2,1,0:T(8,128)(2,1)S(1)} %get-tuple-element.42), channel_id=1, source_target_pairs={{0,509},{1,508},{2,511},{3,510},{4,11},{5,10},{6,9},{7,8},{8,5},{9... | collective-permute-start | bytes 196616 | tf_op jit(solution)/shard_map/ppermute | solution.py:241
  121.4 5.3 %collective-permute-done.6.late_ref = bf16[2,128,768]{2,1,0:T(8,128)(2,1)S(1)} collective-permute-done((bf16[2,128,768]{2,1,0:T(8,128)(2,1)S(1)}, bf16[2,128,768]{2,1,0:T(8,128)(2,1)S(1)}, u32[]{:S(2)}, u32[]{:S(2)}) %collective-permute-start.6) | collective-permute-done | bytes 393248 | tf_op jit(solution)/shard_map/ppermute | solution.py:241
  126.6 1.1 shard_map.36
  127.8 1.9 %collective-permute-start.11 = (bf16[2,2,2,64,128]{4,3,2,1,0:T(8,128)(2,1)S(1)}, bf16[2,2,2,64,128]{4,3,2,1,0:T(8,128)(2,1)S(1)}, u32[]{:S(2)}, u32[]{:S(2)}) collective-permute-start(bf16[2,2,2,64,128]{4,3,2,1,0:T(8,128)(2,1)S(1)} %get-tuple-element.43), channel_id=1, source_target_pairs={{0,8},{1,9},{2,10},{3,11},{4,508},{5,509},{6,510},{7,511},{8,16},{... | collective-permute-start | bytes 393224 | tf_op jit(solution)/shard_map/ppermute | solution.py:241
  129.7 1.9 %collective-permute-start.12 = (bf16[2,2,2,64,128]{4,3,2,1,0:T(8,128)(2,1)S(1)}, bf16[2,2,2,64,128]{4,3,2,1,0:T(8,128)(2,1)S(1)}, u32[]{:S(2)}, u32[]{:S(2)}) collective-permute-start(bf16[2,2,2,64,128]{4,3,2,1,0:T(8,128)(2,1)S(1)} %get-tuple-element.44), channel_id=1, source_target_pairs={{0,9},{1,8},{2,11},{3,10},{4,511},{5,510},{6,509},{7,508},{8,17},{... | collective-permute-start | bytes 393224 | tf_op jit(solution)/shard_map/ppermute | solution.py:241
  131.6 7.2 %collective-permute-start.7 = (bf16[2,2,64,128]{3,2,1,0:T(8,128)(2,1)S(1)}, bf16[2,2,64,128]{3,2,1,0:T(8,128)(2,1)S(1)}, u32[]{:S(2)}, u32[]{:S(2)}) collective-permute-start(bf16[2,2,64,128]{3,2,1,0:T(8,128)(2,1)S(1)} %get-tuple-element.39), channel_id=1, source_target_pairs={{0,4},{1,5},{2,6},{3,7},{4,0},{5,1},{6,2},{7,3},{8,12},{9,13},{10,... | collective-permute-start | bytes 196616 | tf_op jit(solution)/shard_map/ppermute | solution.py:241
  138.8 6.1 %collective-permute-start.8 = (bf16[2,2,64,128]{3,2,1,0:T(8,128)(2,1)S(1)}, bf16[2,2,64,128]{3,2,1,0:T(8,128)(2,1)S(1)}, u32[]{:S(2)}, u32[]{:S(2)}) collective-permute-start(bf16[2,2,64,128]{3,2,1,0:T(8,128)(2,1)S(1)} %get-tuple-element.40), channel_id=1, source_target_pairs={{0,5},{1,4},{2,7},{3,6},{4,3},{5,2},{6,1},{7,0},{8,13},{9,12},{10,... | collective-permute-start | bytes 196616 | tf_op jit(solution)/shard_map/ppermute | solution.py:241
  145.0 0.0 collective-permute-done.10.next_first_ref
  145.0 2.4 %collective-permute-start.9 = (bf16[2,2,64,128]{3,2,1,0:T(8,128)(2,1)S(1)}, bf16[2,2,64,128]{3,2,1,0:T(8,128)(2,1)S(1)}, u32[]{:S(2)}, u32[]{:S(2)}) collective-permute-start(bf16[2,2,64,128]{3,2,1,0:T(8,128)(2,1)S(1)} %get-tuple-element.41), channel_id=1, source_target_pairs={{0,508},{1,509},{2,510},{3,511},{4,8},{5,9},{6,10},{7,11},{8,4},{9... | collective-permute-start | bytes 196616 | tf_op jit(solution)/shard_map/ppermute | solution.py:241
  147.4 0.0 collective-permute-done.7.mate_same_ref
  147.4 1.6 collective-permute-done.8.mate_first_ref
  149.0 6.4 %collective-permute-done.9.next_same_ref = bf16[2,2,64,128]{3,2,1,0:T(8,128)(2,1)S(1)} collective-permute-done((bf16[2,2,64,128]{3,2,1,0:T(8,128)(2,1)S(1)}, bf16[2,2,64,128]{3,2,1,0:T(8,128)(2,1)S(1)}, u32[]{:S(2)}, u32[]{:S(2)}) %collective-permute-start.9) | collective-permute-done | bytes 65568 | tf_op jit(solution)/shard_map/ppermute | solution.py:241
  155.4 0.0 collective-permute-done.11.far_same_ref
  155.4 0.0 collective-permute-done.12.far_first_ref
  155.4 1.3 shard_map.37
  156.6 2.0 %copy.3 = bf16[4,128,2,512]{3,2,1,0:T(2,128)(2,1)} copy(bf16[4,128,2,512]{3,1,2,0:T(8,128)(2,1)S(1)} %bitcast.13) | data formatting | bytes 2097152 | tf_op jit(solution)/shard_map/transpose | solution.py:310
  (1 shorter events, 0.0 us)
Async XLA Ops:
  0.0 24.8 %copy-start = (f32[512]{0:T(512)S(1)}, f32[512]{0:T(512)}, u32[]{:S(2)}) copy-start(f32[512]{0:T(512)} %param.3) | copy-start | bytes 6148
  1.8 20.9 %collective-permute-start.1 = (bf16[2,256,1024]{2,1,0:T(8,128)(2,1)S(1)}, bf16[2,256,1024]{2,1,0:T(8,128)(2,1)S(1)}, u32[]{:S(2)}, u32[]{:S(2)}) collective-permute-start(bf16[2,256,1024]{2,1,0:T(8,128)(2,1)S(1)} %reshape.39.plain_ref), channel_id=1, source_target_pairs={{0,508},{4,8},{8,4},{12,16},{16,12},{20,24},{24,20},{28,32},{32,28... | collective-permute-start | bytes 3145736 | tf_op jit(solution)/shard_map/ppermute | solution.py:230
  10.2 15.6 %collective-permute-start = (bf16[2,256,1024]{2,1,0:T(8,128)(2,1)S(1)}, bf16[2,256,1024]{2,1,0:T(8,128)(2,1)}, u32[]{:S(2)}, u32[]{:S(2)}) collective-permute-start(bf16[2,256,1024]{2,1,0:T(8,128)(2,1)S(1)} %reshape.39.plain_ref), channel_id=1, source_target_pairs={{0,4},{4,0},{8,12},{12,8},{16,20},{20,16},{24,28},{28,24},{32,36},... | collective-permute-start | bytes 3145736 | tf_op jit(solution)/shard_map/ppermute | solution.py:230
  22.7 14.1 %collective-permute-start.3 = (bf16[2,256,1024]{2,1,0:T(8,128)(2,1)S(1)}, bf16[2,256,1024]{2,1,0:T(8,128)(2,1)S(1)}, u32[]{:S(2)}, u32[]{:S(2)}) collective-permute-start(bf16[2,256,1024]{2,1,0:T(8,128)(2,1)S(1)} %collective-permute-done.1.next_ref), channel_id=1, source_target_pairs={{0,4},{4,0},{8,12},{12,8},{16,20},{20,16},{24,28},{28,24},{32,36},... | collective-permute-start | bytes 3145736 | tf_op jit(solution)/shard_map/ppermute | solution.py:230
  27.8 53.3 %collective-permute-start.2 = (bf16[2,256,512]{2,1,0:T(8,128)(2,1)S(1)}, bf16[2,256,512]{2,1,0:T(8,128)(2,1)S(1)}, u32[]{:S(2)}, u32[]{:S(2)}) collective-permute-start(bf16[2,256,512]{2,1,0:T(8,128)(2,1)S(1)} %shard_map.29), channel_id=1, source_target_pairs={{0,1},{1,0},{2,3},{3,2},{4,7},{5,6},{6,5},{7,4},{8,9},{9,8},{10,11... | collective-permute-start | bytes 1572872 | tf_op jit(solution)/shard_map/ppermute | solution.py:241
  37.6 55.6 %collective-permute-start.5 = (bf16[2,256,512]{2,1,0:T(8,128)(2,1)S(1)}, bf16[2,256,512]{2,1,0:T(8,128)(2,1)S(1)}, u32[]{:S(2)}, u32[]{:S(2)}) collective-permute-start(bf16[2,256,512]{2,1,0:T(8,128)(2,1)S(1)} %shard_map.30), channel_id=1, source_target_pairs={{0,1},{1,0},{2,3},{3,2},{4,7},{5,6},{6,5},{7,4},{8,9},{9,8},{10,11... | collective-permute-start | bytes 1572872 | tf_op jit(solution)/shard_map/ppermute | solution.py:241
  81.9 34.5 %collective-permute-start.4 = (bf16[2,128,768]{2,1,0:T(8,128)(2,1)S(1)}, bf16[2,128,768]{2,1,0:T(8,128)(2,1)S(1)}, u32[]{:S(2)}, u32[]{:S(2)}) collective-permute-start(bf16[2,128,768]{2,1,0:T(8,128)(2,1)S(1)} %shard_map.33.second_ref), channel_id=1, source_target_pairs={{0,3},{1,2},{2,1},{3,0},{4,5},{5,4},{6,7},{7,6},{8,11},{9,10},{10,... | collective-permute-start | bytes 1179656 | tf_op jit(solution)/shard_map/ppermute | solution.py:241
  94.1 32.5 %collective-permute-start.6 = (bf16[2,128,768]{2,1,0:T(8,128)(2,1)S(1)}, bf16[2,128,768]{2,1,0:T(8,128)(2,1)S(1)}, u32[]{:S(2)}, u32[]{:S(2)}) collective-permute-start(bf16[2,128,768]{2,1,0:T(8,128)(2,1)S(1)} %shard_map.34.second_ref), channel_id=1, source_target_pairs={{0,3},{1,2},{2,1},{3,0},{4,5},{5,4},{6,7},{7,6},{8,11},{9,10},{10,... | collective-permute-start | bytes 1179656 | tf_op jit(solution)/shard_map/ppermute | solution.py:241
  117.5 27.5 %collective-permute-start.10 = (bf16[2,2,64,128]{3,2,1,0:T(8,128)(2,1)S(1)}, bf16[2,2,64,128]{3,2,1,0:T(8,128)(2,1)S(1)}, u32[]{:S(2)}, u32[]{:S(2)}) collective-permute-start(bf16[2,2,64,128]{3,2,1,0:T(8,128)(2,1)S(1)} %get-tuple-element.42), channel_id=1, source_target_pairs={{0,509},{1,508},{2,511},{3,510},{4,11},{5,10},{6,9},{7,8},{8,5},{9... | collective-permute-start | bytes 196616 | tf_op jit(solution)/shard_map/ppermute | solution.py:241
  127.8 27.6 %collective-permute-start.11 = (bf16[2,2,2,64,128]{4,3,2,1,0:T(8,128)(2,1)S(1)}, bf16[2,2,2,64,128]{4,3,2,1,0:T(8,128)(2,1)S(1)}, u32[]{:S(2)}, u32[]{:S(2)}) collective-permute-start(bf16[2,2,2,64,128]{4,3,2,1,0:T(8,128)(2,1)S(1)} %get-tuple-element.43), channel_id=1, source_target_pairs={{0,8},{1,9},{2,10},{3,11},{4,508},{5,509},{6,510},{7,511},{8,16},{... | collective-permute-start | bytes 393224 | tf_op jit(solution)/shard_map/ppermute | solution.py:241
  129.7 25.7 %collective-permute-start.12 = (bf16[2,2,2,64,128]{4,3,2,1,0:T(8,128)(2,1)S(1)}, bf16[2,2,2,64,128]{4,3,2,1,0:T(8,128)(2,1)S(1)}, u32[]{:S(2)}, u32[]{:S(2)}) collective-permute-start(bf16[2,2,2,64,128]{4,3,2,1,0:T(8,128)(2,1)S(1)} %get-tuple-element.44), channel_id=1, source_target_pairs={{0,9},{1,8},{2,11},{3,10},{4,511},{5,510},{6,509},{7,508},{8,17},{... | collective-permute-start | bytes 393224 | tf_op jit(solution)/shard_map/ppermute | solution.py:241
  131.6 15.8 %collective-permute-start.7 = (bf16[2,2,64,128]{3,2,1,0:T(8,128)(2,1)S(1)}, bf16[2,2,64,128]{3,2,1,0:T(8,128)(2,1)S(1)}, u32[]{:S(2)}, u32[]{:S(2)}) collective-permute-start(bf16[2,2,64,128]{3,2,1,0:T(8,128)(2,1)S(1)} %get-tuple-element.39), channel_id=1, source_target_pairs={{0,4},{1,5},{2,6},{3,7},{4,0},{5,1},{6,2},{7,3},{8,12},{9,13},{10,... | collective-permute-start | bytes 196616 | tf_op jit(solution)/shard_map/ppermute | solution.py:241
  138.8 10.2 %collective-permute-start.8 = (bf16[2,2,64,128]{3,2,1,0:T(8,128)(2,1)S(1)}, bf16[2,2,64,128]{3,2,1,0:T(8,128)(2,1)S(1)}, u32[]{:S(2)}, u32[]{:S(2)}) collective-permute-start(bf16[2,2,64,128]{3,2,1,0:T(8,128)(2,1)S(1)} %get-tuple-element.40), channel_id=1, source_target_pairs={{0,5},{1,4},{2,7},{3,6},{4,3},{5,2},{6,1},{7,0},{8,13},{9,12},{10,... | collective-permute-start | bytes 196616 | tf_op jit(solution)/shard_map/ppermute | solution.py:241
  145.0 10.4 %collective-permute-start.9 = (bf16[2,2,64,128]{3,2,1,0:T(8,128)(2,1)S(1)}, bf16[2,2,64,128]{3,2,1,0:T(8,128)(2,1)S(1)}, u32[]{:S(2)}, u32[]{:S(2)}) collective-permute-start(bf16[2,2,64,128]{3,2,1,0:T(8,128)(2,1)S(1)} %get-tuple-element.41), channel_id=1, source_target_pairs={{0,508},{1,509},{2,510},{3,511},{4,8},{5,9},{6,10},{7,11},{8,4},{9... | collective-permute-start | bytes 196616 | tf_op jit(solution)/shard_map/ppermute | solution.py:241

commit v12 on v11

--- a/solution.py
+++ b/solution.py
@@ -37,20 +37,22 @@
     return value.astype(jnp.float32)
 
 
-def left_kernel(order_ref, plain_ref, weight_ref, left_ref):
+def left_kernel(order_ref, plain_ref, weight_ref, away_ref, rest_ref):
     points, transitions, depth = plain_ref.shape
     owners = order_ref.shape[0] - 1
     blocks = transitions // (owners * BLOCK)
     weight = weight_ref[...]
     for point in range(points):
         for slot in range(owners):
+            out_ref = (away_ref, rest_ref)[slot // 2]
             for block in range(blocks):
                 start = pl.multiple_of((block * owners + order_ref[slot]) * BLOCK, BLOCK)
                 rows = wide(plain_ref[point, pl.ds(start, BLOCK), :]) * weight
-                place = pl.ds(block * BLOCK, BLOCK)
-                left_ref[point, slot, 0, place, :] = low(rows)
-                left_ref[point, slot, 1, place, : depth // 2] = low(-rows[:, depth // 2 :])
-                left_ref[point, slot, 1, place, depth // 2 :] = low(rows[:, : depth // 2])
+                real = pl.ds((slot % 2 * 2 * blocks + block) * BLOCK, BLOCK)
+                imag = pl.ds(((slot % 2 * 2 + 1) * blocks + block) * BLOCK, BLOCK)
+                out_ref[point, real, :] = low(rows)
+                out_ref[point, imag, : depth // 2] = low(-rows[:, depth // 2 :])
+                out_ref[point, imag, depth // 2 :] = low(rows[:, : depth // 2])
 
 
 def agreeing(order_ref, point):
@@ -120,7 +122,7 @@
             out_ref[point, :, place[0] : place[1]] = low(dots(own[:, part * half : (part + 1) * half], pick))
 
 
-def turned_part(order_ref, block_ref, second_ref, late_ref, part, same_ref, first_ref, index):
+def turned_part(order_ref, block_ref, second_ref, late_ref, part, same_ref, first_ref, place):
     points, count, columns = block_ref.shape
     half = columns // 2
     rows = count // 2
@@ -142,35 +144,40 @@
     for source, out in enumerate((dots(pick, own), dots(same, other))):
         for to, ref in enumerate((same_ref, first_ref)):
             piece = out[to * rows : (to + 1) * rows]
-            ref[source, *index, 0] = low(piece[:, : points * rows])
-            ref[source, *index, 1] = low(-piece[:, points * rows :])
-
-
-def finish(order_ref, rest_ref, got_ref, second_ref, late_ref, block_ref):
+            both = jnp.concatenate([low(piece[:, : points * rows]), low(-piece[:, points * rows :])], axis=0)
+            if place is None:
+                ref[source] = both
+            else:
+                ref[source, place] = both
+
+
+def finish(rest_ref, got_ref, late_ref, block_ref):
     points, count, columns = block_ref.shape
     for point in range(points):
         total = wide(rest_ref[1, point]) + wide(got_ref[point, :count, :]) + wide(late_ref[point, :, :columns])
         block_ref[point] = low(total)
 
 
-def finish_pair_kernel(
-    order_ref, rest_ref, got_ref, second_ref, late_ref,
-    block_ref, mate_same_ref, mate_first_ref, next_same_ref, next_first_ref,
+def finish_kernel(
+    order_ref, rest_pair_ref, got_pair_ref, second_pair_ref, late_pair_ref,
+    rest_far_ref, got_far_ref, second_far_ref, late_far_ref,
+    block_ref, mate_same_ref, mate_first_ref, next_same_ref, next_first_ref, far_ref,
 ):
-    finish(order_ref, rest_ref, got_ref, second_ref, late_ref, block_ref)
-    turned_part(order_ref, block_ref, second_ref, late_ref, 0, mate_same_ref, mate_first_ref, ())
-    turned_part(order_ref, block_ref, second_ref, late_ref, 1, next_same_ref, next_first_ref, ())
-
-
-def finish_far_kernel(order_ref, rest_ref, got_ref, second_ref, late_ref, block_ref, same_ref, first_ref):
-    finish(order_ref, rest_ref, got_ref, second_ref, late_ref, block_ref)
-    for part in range(block_ref.shape[0]):
-        turned_part(order_ref, block_ref, second_ref, late_ref, part, same_ref, first_ref, (part,))
+    points, count, columns = block_ref.shape
+    finish(rest_pair_ref, got_pair_ref, late_pair_ref, block_ref)
+    finish(rest_far_ref, got_far_ref, late_far_ref, far_ref)
+    strips = columns // count
+    for point in range(points):
+        for strip in range(strips):
+            mate_same_ref[2 + point * strips + strip] = far_ref[point, :, strip * count : (strip + 1) * count]
+    turned_part(order_ref, block_ref, second_pair_ref, late_pair_ref, 0, mate_same_ref, mate_first_ref, None)
+    turned_part(order_ref, block_ref, second_pair_ref, late_pair_ref, 1, next_same_ref, next_first_ref, 0)
+    for part in range(points):
+        turned_part(order_ref, far_ref, second_far_ref, late_far_ref, part, next_same_ref, next_first_ref, 1 + part)
 
 
 def merge_kernel(
-    order_ref, pair_ref, far_ref, mate_same_ref, mate_first_ref, next_same_ref, next_first_ref,
-    far_same_ref, far_first_ref, out_ref,
+    order_ref, pair_ref, mate_same_ref, mate_first_ref, next_same_ref, next_first_ref, out_ref
 ):
     points, count, columns = pair_ref.shape
     rows = count // 2
@@ -178,20 +185,20 @@
     owners = order_ref.shape[0] - 1
     even = order_ref[owners]
     lanes = points * rows
+    strips = columns // count
     n = lax.broadcasted_iota(jnp.int32, (lanes, columns), 0)
     column = lax.broadcasted_iota(jnp.int32, (lanes, columns), 1)
     target = (n // BLOCK * owners) * BLOCK + n % BLOCK
     sources = [
-        (mate_same_ref, 1, next_same_ref, 1, far_first_ref, 0),
-        (mate_first_ref, 1, next_first_ref, 1, far_first_ref, 1),
-        (mate_first_ref, 0, next_first_ref, 0, far_same_ref, 1),
-        (mate_same_ref, 0, next_same_ref, 0, far_same_ref, 0),
+        (mate_same_ref, next_same_ref, 1),
+        (mate_first_ref, next_first_ref, 1),
+        (mate_first_ref, next_first_ref, 0),
+        (mate_same_ref, next_same_ref, 0),
     ]
     total = 0.0
-    for slot, (mate_piece, i, next_piece, j, far_piece, k) in enumerate(sources):
+    for slot, (mate_piece, next_piece, source) in enumerate(sources):
         pick = low(jnp.where(column == target + order_ref[slot] * BLOCK, 1.0, 0.0))
-        tiles = [mate_piece[i, p] for p in range(2)] + [next_piece[j, p] for p in range(2)]
-        tiles += [far_piece[k, part, p] for part in range(points) for p in range(2)]
+        tiles = [mate_piece[source]] + [next_piece[source, place] for place in range(1 + points)]
         total = total + lax.dot_general(
             jnp.concatenate(tiles, axis=0), pick, (((1,), (0,)), ((), ())), preferred_element_type=jnp.float32
         )
@@ -209,7 +216,9 @@
                     ] = jnp.where(mine, here, there)
         for point in range(points):
             span = slice(point * rows, (point + 1) * rows)
-            out_ref[1 + 2 * even, p, span, :] = far_ref[point, p * rows : (p + 1) * rows, :]
+            for strip in range(strips):
+                tile = mate_same_ref[2 + point * strips + strip, p * rows : (p + 1) * rows, :]
+                out_ref[1 + 2 * even, p, span, strip * count : (strip + 1) * count] = tile
             first = (4 + 2 * point + p) * rows
             out_ref[3 - 2 * even, p, span, :] = back[first : first + rows]
 
@@ -249,9 +258,6 @@
     def across(i):
         return i - 1 if i % 2 == 0 else i + 1
 
-    def second_next(i):
-        return i + 2 if i % 2 == 0 else i - 2
-
     near_flip, far_flip = 1 + 2 * parity, 3 - 2 * parity
     relative = jnp.stack([me ^ near_flip, me ^ 2, me ^ far_flip, me, 1 - parity])
 
@@ -260,51 +266,51 @@
     next_right = exchange_kp(plain, across)
 
     weights = (jnp.concatenate([coulomb, coulomb]) * scale).reshape(1, depth)
-    left = local(left_kernel, [(points, owners, 2, rows, depth)], relative, plain, weights, scalars=1, moved=4 << 20)
-    left_away = left[:, :2].reshape(points, 4 * rows, depth)
-    left_rest = left[:, 2:].reshape(points, 4 * rows, depth)
-
-    left_away, left_rest, mate_right = lax.optimization_barrier((left_away, left_rest, mate_right))
+    left_shape = [(points, 4 * rows, depth)] * 2
+    left_away, left_rest = local(left_kernel, left_shape, relative, plain, weights, scalars=1, moved=4 << 20)
+    mate_away, mate_rest = local(left_kernel, left_shape, relative, mate_right, weights, scalars=1, moved=4 << 20)
+    next_right, left_away, mate_away = lax.optimization_barrier((next_right, left_away, mate_away))
+
     columns = points * transitions
     away_shape = [(points, 4 * rows, columns)]
+    rest_shape = [(2, points, 2 * rows, columns)]
     second_shape = [(points, 2 * rows, columns + 4 * rows)]
-    block_shape = (points, 2 * rows, columns)
-    pair_back = (2, 2, rows, points * rows)
-    far_back = (2, points, 2, rows, points * rows)
-
-    rest_shape = [(2, points, 2 * rows, columns)]
-
-    far_right = exchange_kp(next_right, mate)
+
     away_pair = local(away_pair_kernel, away_shape, relative, left_away, mate_right, next_right, scalars=1)
     got_pair = exchange_own(away_pair, True)
-    far_right, _ = lax.optimization_barrier((far_right, away_pair))
-    away_far = local(away_far_kernel, away_shape, left_away, far_right)
+    mate_away, _ = lax.optimization_barrier((mate_away, away_pair))
+    away_far = local(away_far_kernel, away_shape, mate_away, next_right)
     got_far = exchange_own(away_far, True)
-    late_left, mate_right, next_right, far_right, _ = lax.optimization_barrier(
-        (left_rest, mate_right, next_right, far_right, away_far)
-    )
+    left_rest, mate_rest, _ = lax.optimization_barrier((left_rest, mate_rest, away_far))
     rest_pair = local(
-        rest_pair_kernel, rest_shape, relative, late_left, mate_right, next_right, scalars=1, moved=8 << 20
-    )
-    rest_far = local(rest_far_kernel, rest_shape, late_left, far_right, moved=8 << 20)
+        rest_pair_kernel, rest_shape, relative, left_rest, mate_right, next_right, scalars=1, moved=8 << 20
+    )
+    rest_far = local(rest_far_kernel, rest_shape, mate_rest, next_right, moved=8 << 20)
     got_pair, rest_pair, rest_far = lax.optimization_barrier((got_pair, rest_pair, rest_far))
     second_pair = local(second_kernel, second_shape, relative, rest_pair, got_pair, scalars=1)
     late_pair = exchange_own(second_pair, False)
+    got_far, _ = lax.optimization_barrier((got_far, second_pair))
     second_far = local(second_kernel, second_shape, relative, rest_far, got_far, scalars=1)
-    late_pair, _ = lax.optimization_barrier((late_pair, second_far))
     late_far = exchange_own(second_far, False)
-    block_pair, mate_same, mate_first, next_same, next_first = local(
-        finish_pair_kernel, [block_shape] + [pair_back] * 4, relative, rest_pair, got_pair, second_pair, late_pair, scalars=1
-    )
-    block_far, far_same, far_first = local(
-        finish_far_kernel, [block_shape, far_back, far_back], relative, rest_far, got_far, second_far, late_far, scalars=1
+    tile = (2 * rows, points * rows)
+    strips = points * columns // tile[1]
+    block_pair, mate_same, mate_first, next_same, next_first, _ = local(
+        finish_kernel,
+        [
+            (points, 2 * rows, columns),
+            (2 + strips, *tile),
+            (2, *tile),
+            (2, 1 + points, *tile),
+            (2, 1 + points, *tile),
+            (points, 2 * rows, columns),
+        ],
+        relative, rest_pair, got_pair, second_pair, late_pair, rest_far, got_far, second_far, late_far, scalars=1,
     )
     out = local(
         merge_kernel, [(4, 2, points * rows, columns)],
-        relative, block_pair, block_far,
+        relative, block_pair,
         exchange(mate_same, 3, mate), exchange(mate_first, 0, mate),
         exchange(next_same, 3, across), exchange(next_first, 0, across),
-        exchange(far_same, 3, second_next), exchange(far_first, 0, second_next),
         scalars=1,
     )
     return out.transpose(0, 2, 1, 3)

time: 159 us -> 159 us (level)
  the two profiles are of different devices: /device:TPU:24 before, /device:TPU:128 now
where the time goes in v12:
time: 159 us; the launch traced here: 158 us
  waiting for transfers between devices  91.2 us (57%)
  starting transfers between devices  51.7 us (33%)
  Pallas kernels  10.7 us (7%)
  local copies, waits for them, and re-layouts  4.51 us (3%)
    ppermute x8, waiting for transfers between devices, exchange(): return lax.ppermute(value, ('kp', 'own'), pairs)  81 us
    ppermute x8, starting transfers between devices, exchange(): return lax.ppermute(value, ('kp', 'own'), pairs)  38.5 us
    ppermute x2, starting transfers between devices, exchange_kp(): lax.ppermute(value, 'kp', [(i, partner(i) % groups) for i in range(groups)])  13.2 us
    pallas_call x10, Pallas kernels, local(): pl.pallas_call(kernel, out_shape=out_shape if several else out_shape[0],...  10.7 us
    ppermute x2, waiting for transfers between devices, exchange_kp(): lax.ppermute(value, 'kp', [(i, partner(i) % groups) for i in range(groups)])  10.2 us
  transfers between devices with their start and end apart: 10, of which 6 were waited for; matrix products, arithmetic and copies ran while one was open for 0% of the time, Pallas kernels for 4%

profile of v12, /device:TPU:128, one launch (start us, length us, event | category | flops | bytes accessed | tf_op | source)
XLA Modules:
  0.0 158.3 jit_solution(5816794901663153275)
XLA Ops:
  0.0 1.8 %reshape.33.plain_ref = bf16[2,256,1024]{2,1,0:T(8,128)(2,1)S(1)} reshape(bf16[2,256,2,512]{3,2,1,0:T(2,128)(2,1)} %param.2) | data formatting | bytes 2097152 | tf_op jit(solution)/shard_map/reshape | solution.py:264
  1.8 1.9 %collective-permute-start.1 = (bf16[2,256,1024]{2,1,0:T(8,128)(2,1)S(1)}, bf16[2,256,1024]{2,1,0:T(8,128)(2,1)S(1)}, u32[]{:S(2)}, u32[]{:S(2)}) collective-permute-start(bf16[2,256,1024]{2,1,0:T(8,128)(2,1)S(1)} %reshape.33.plain_ref), channel_id=1, source_target_pairs={{0,4},{4,0},{8,12},{12,8},{16,20},{20,16},{24,28},{28,24},{32,36},... | collective-permute-start | bytes 3145736 | tf_op jit(solution)/shard_map/ppermute | solution.py:239
  3.7 11.3 %collective-permute-start = (bf16[2,256,1024]{2,1,0:T(8,128)(2,1)S(1)}, bf16[2,256,1024]{2,1,0:T(8,128)(2,1)S(1)}, u32[]{:S(2)}, u32[]{:S(2)}) collective-permute-start(bf16[2,256,1024]{2,1,0:T(8,128)(2,1)S(1)} %reshape.33.plain_ref), channel_id=1, source_target_pairs={{0,508},{4,8},{8,4},{12,16},{16,12},{20,24},{24,20},{28,32},{32,28... | collective-permute-start | bytes 3145736 | tf_op jit(solution)/shard_map/ppermute | solution.py:239
  15.0 0.0 copy-start
  15.0 0.1 stack.23.order_ref
  15.1 0.6 copy-done
  15.7 0.8 shard_map.28
  16.5 0.0 collective-permute-done.1.plain_ref.mate_ref
  16.5 0.8 shard_map.29
  17.3 10.2 %collective-permute-done.next_ref.right_ref = bf16[2,256,1024]{2,1,0:T(8,128)(2,1)S(1)} collective-permute-done((bf16[2,256,1024]{2,1,0:T(8,128)(2,1)S(1)}, bf16[2,256,1024]{2,1,0:T(8,128)(2,1)S(1)}, u32[]{:S(2)}, u32[]{:S(2)}) %collective-permute-start) | collective-permute-done | bytes 1048608 | tf_op jit(solution)/shard_map/ppermute | solution.py:239
  27.5 1.3 shard_map.30
  28.8 4.4 %collective-permute-start.2 = (bf16[2,256,512]{2,1,0:T(8,128)(2,1)S(1)}, bf16[2,256,512]{2,1,0:T(8,128)(2,1)S(1)}, u32[]{:S(2)}, u32[]{:S(2)}) collective-permute-start(bf16[2,256,512]{2,1,0:T(8,128)(2,1)S(1)} %shard_map.30), channel_id=1, source_target_pairs={{0,1},{1,0},{2,3},{3,2},{4,7},{5,6},{6,5},{7,4},{8,9},{9,8},{10,11... | collective-permute-start | bytes 1572872 | tf_op jit(solution)/shard_map/ppermute | solution.py:250
  33.2 0.7 shard_map.31
  33.9 5.3 %collective-permute-start.4 = (bf16[2,256,512]{2,1,0:T(8,128)(2,1)S(1)}, bf16[2,256,512]{2,1,0:T(8,128)(2,1)S(1)}, u32[]{:S(2)}, u32[]{:S(2)}) collective-permute-start(bf16[2,256,512]{2,1,0:T(8,128)(2,1)S(1)} %shard_map.31), channel_id=1, source_target_pairs={{0,1},{1,0},{2,3},{3,2},{4,7},{5,6},{6,5},{7,4},{8,9},{9,8},{10,11... | collective-permute-start | bytes 1572872 | tf_op jit(solution)/shard_map/ppermute | solution.py:250
  39.3 0.8 shard_map.33.rest_ref.rest_far_ref
  40.1 1.3 shard_map.32.rest_ref.rest_pair_ref
  41.4 26.9 %collective-permute-done.2.got_ref.got_pair_ref = bf16[2,256,512]{2,1,0:T(8,128)(2,1)S(1)} collective-permute-done((bf16[2,256,512]{2,1,0:T(8,128)(2,1)S(1)}, bf16[2,256,512]{2,1,0:T(8,128)(2,1)S(1)}, u32[]{:S(2)}, u32[]{:S(2)}) %collective-permute-start.2) | collective-permute-done | bytes 524320 | tf_op jit(solution)/shard_map/ppermute | solution.py:250
  68.2 0.8 shard_map.34.second_pair_ref
  69.1 13.1 %collective-permute-start.3 = (bf16[2,128,768]{2,1,0:T(8,128)(2,1)S(1)}, bf16[2,128,768]{2,1,0:T(8,128)(2,1)S(1)}, u32[]{:S(2)}, u32[]{:S(2)}) collective-permute-start(bf16[2,128,768]{2,1,0:T(8,128)(2,1)S(1)} %shard_map.34.second_pair_ref), channel_id=1, source_target_pairs={{0,3},{1,2},{2,1},{3,0},{4,5},{5,4},{6,7},{7,6},{8,11},{9,10},{10,... | collective-permute-start | bytes 1179656 | tf_op jit(solution)/shard_map/ppermute | solution.py:250
  82.1 28.4 %collective-permute-done.4.got_ref.got_far_ref = bf16[2,256,512]{2,1,0:T(8,128)(2,1)S(1)} collective-permute-done((bf16[2,256,512]{2,1,0:T(8,128)(2,1)S(1)}, bf16[2,256,512]{2,1,0:T(8,128)(2,1)S(1)}, u32[]{:S(2)}, u32[]{:S(2)}) %collective-permute-start.4) | collective-permute-done | bytes 524320 | tf_op jit(solution)/shard_map/ppermute | solution.py:250
  110.5 0.8 shard_map.35.second_far_ref
  111.3 1.9 %collective-permute-start.5 = (bf16[2,128,768]{2,1,0:T(8,128)(2,1)S(1)}, bf16[2,128,768]{2,1,0:T(8,128)(2,1)S(1)}, u32[]{:S(2)}, u32[]{:S(2)}) collective-permute-start(bf16[2,128,768]{2,1,0:T(8,128)(2,1)S(1)} %shard_map.35.second_far_ref), channel_id=1, source_target_pairs={{0,3},{1,2},{2,1},{3,0},{4,5},{5,4},{6,7},{7,6},{8,11},{9,10},{10,... | collective-permute-start | bytes 1179656 | tf_op jit(solution)/shard_map/ppermute | solution.py:250
  113.3 0.0 collective-permute-done.3.late_pair_ref
  113.3 11.8 %collective-permute-done.5.late_far_ref = bf16[2,128,768]{2,1,0:T(8,128)(2,1)S(1)} collective-permute-done((bf16[2,128,768]{2,1,0:T(8,128)(2,1)S(1)}, bf16[2,128,768]{2,1,0:T(8,128)(2,1)S(1)}, u32[]{:S(2)}, u32[]{:S(2)}) %collective-permute-start.5) | collective-permute-done | bytes 393248 | tf_op jit(solution)/shard_map/ppermute | solution.py:250
  125.1 2.1 %shard_map.36 = (bf16[2,128,512]{2,1,0:T(8,128)(2,1)S(1)}, bf16[10,128,128]{2,1,0:T(8,128)(2,1)S(1)}, bf16[2,128,128]{2,1,0:T(8,128)(2,1)S(1)}, bf16[2,3,128,128...) custom-call(s32[5]{0:T(128)S(1)} %stack.23.order_ref, ...), custom_call_target="tpu_custom_call" | custom-call | tf_op jit(solution)/shard_map/pallas_call | solution.py:18
  127.2 1.9 %collective-permute-start.6 = (bf16[10,128,128]{2,1,0:T(8,128)(2,1)S(1)}, bf16[10,128,128]{2,1,0:T(8,128)(2,1)S(1)}, u32[]{:S(2)}, u32[]{:S(2)}) collective-permute-start(bf16[10,128,128]{2,1,0:T(8,128)(2,1)S(1)} %get-tuple-element.39), channel_id=1, source_target_pairs={{0,4},{1,5},{2,6},{3,7},{4,0},{5,1},{6,2},{7,3},{8,12},{9,13},{10,... | collective-permute-start | bytes 983048 | tf_op jit(solution)/shard_map/ppermute | solution.py:250
  129.1 8.0 %collective-permute-start.8 = (bf16[2,3,128,128]{3,2,1,0:T(8,128)(2,1)S(1)}, bf16[2,3,128,128]{3,2,1,0:T(8,128)(2,1)S(1)}, u32[]{:S(2)}, u32[]{:S(2)}) collective-permute-start(bf16[2,3,128,128]{3,2,1,0:T(8,128)(2,1)S(1)} %get-tuple-element.41), channel_id=1, source_target_pairs={{0,508},{1,509},{2,510},{3,511},{4,8},{5,9},{6,10},{7,11},{8,4},{9... | collective-permute-start | bytes 589832 | tf_op jit(solution)/shard_map/ppermute | solution.py:250
  137.1 1.9 %collective-permute-start.9 = (bf16[2,3,128,128]{3,2,1,0:T(8,128)(2,1)S(1)}, bf16[2,3,128,128]{3,2,1,0:T(8,128)(2,1)S(1)}, u32[]{:S(2)}, u32[]{:S(2)}) collective-permute-start(bf16[2,3,128,128]{3,2,1,0:T(8,128)(2,1)S(1)} %get-tuple-element.42), channel_id=1, source_target_pairs={{0,509},{1,508},{2,511},{3,510},{4,11},{5,10},{6,9},{7,8},{8,5},{9... | collective-permute-start | bytes 589832 | tf_op jit(solution)/shard_map/ppermute | solution.py:250
  139.1 1.9 %collective-permute-start.7 = (bf16[2,128,128]{2,1,0:T(8,128)(2,1)S(1)}, bf16[2,128,128]{2,1,0:T(8,128)(2,1)S(1)}, u32[]{:S(2)}, u32[]{:S(2)}) collective-permute-start(bf16[2,128,128]{2,1,0:T(8,128)(2,1)S(1)} %get-tuple-element.40), channel_id=1, source_target_pairs={{0,5},{1,4},{2,7},{3,6},{4,3},{5,2},{6,1},{7,0},{8,13},{9,12},{10,... | collective-permute-start | bytes 196616 | tf_op jit(solution)/shard_map/ppermute | solution.py:250
  141.0 7.6 %collective-permute-done.7.mate_first_ref = bf16[2,128,128]{2,1,0:T(8,128)(2,1)S(1)} collective-permute-done((bf16[2,128,128]{2,1,0:T(8,128)(2,1)S(1)}, bf16[2,128,128]{2,1,0:T(8,128)(2,1)S(1)}, u32[]{:S(2)}, u32[]{:S(2)}) %collective-permute-start.7) | collective-permute-done | bytes 65568 | tf_op jit(solution)/shard_map/ppermute | solution.py:250
  148.6 0.0 collective-permute-done.8.next_same_ref
  148.6 6.4 %collective-permute-done.9.next_first_ref = bf16[2,3,128,128]{3,2,1,0:T(8,128)(2,1)S(1)} collective-permute-done((bf16[2,3,128,128]{3,2,1,0:T(8,128)(2,1)S(1)}, bf16[2,3,128,128]{3,2,1,0:T(8,128)(2,1)S(1)}, u32[]{:S(2)}, u32[]{:S(2)}) %collective-permute-start.9) | collective-permute-done | bytes 196640 | tf_op jit(solution)/shard_map/ppermute | solution.py:250
  154.9 0.0 collective-permute-done.6.mate_same_ref
  155.0 1.3 shard_map.37
  156.2 2.0 %copy.3 = bf16[4,128,2,512]{3,2,1,0:T(2,128)(2,1)} copy(bf16[4,128,2,512]{3,1,2,0:T(8,128)(2,1)S(1)} %bitcast.7) | data formatting | bytes 2097152 | tf_op jit(solution)/shard_map/transpose | solution.py:316
  (1 shorter events, 0.0 us)
Async XLA Ops:
  1.8 14.7 %collective-permute-start.1 = (bf16[2,256,1024]{2,1,0:T(8,128)(2,1)S(1)}, bf16[2,256,1024]{2,1,0:T(8,128)(2,1)S(1)}, u32[]{:S(2)}, u32[]{:S(2)}) collective-permute-start(bf16[2,256,1024]{2,1,0:T(8,128)(2,1)S(1)} %reshape.33.plain_ref), channel_id=1, source_target_pairs={{0,4},{4,0},{8,12},{12,8},{16,20},{20,16},{24,28},{28,24},{32,36},... | collective-permute-start | bytes 3145736 | tf_op jit(solution)/shard_map/ppermute | solution.py:239
  3.7 23.8 %collective-permute-start = (bf16[2,256,1024]{2,1,0:T(8,128)(2,1)S(1)}, bf16[2,256,1024]{2,1,0:T(8,128)(2,1)S(1)}, u32[]{:S(2)}, u32[]{:S(2)}) collective-permute-start(bf16[2,256,1024]{2,1,0:T(8,128)(2,1)S(1)} %reshape.33.plain_ref), channel_id=1, source_target_pairs={{0,508},{4,8},{8,4},{12,16},{16,12},{20,24},{24,20},{28,32},{32,28... | collective-permute-start | bytes 3145736 | tf_op jit(solution)/shard_map/ppermute | solution.py:239
  15.0 0.7 copy-start
  28.8 39.4 %collective-permute-start.2 = (bf16[2,256,512]{2,1,0:T(8,128)(2,1)S(1)}, bf16[2,256,512]{2,1,0:T(8,128)(2,1)S(1)}, u32[]{:S(2)}, u32[]{:S(2)}) collective-permute-start(bf16[2,256,512]{2,1,0:T(8,128)(2,1)S(1)} %shard_map.30), channel_id=1, source_target_pairs={{0,1},{1,0},{2,3},{3,2},{4,7},{5,6},{6,5},{7,4},{8,9},{9,8},{10,11... | collective-permute-start | bytes 1572872 | tf_op jit(solution)/shard_map/ppermute | solution.py:250
  33.9 76.5 %collective-permute-start.4 = (bf16[2,256,512]{2,1,0:T(8,128)(2,1)S(1)}, bf16[2,256,512]{2,1,0:T(8,128)(2,1)S(1)}, u32[]{:S(2)}, u32[]{:S(2)}) collective-permute-start(bf16[2,256,512]{2,1,0:T(8,128)(2,1)S(1)} %shard_map.31), channel_id=1, source_target_pairs={{0,1},{1,0},{2,3},{3,2},{4,7},{5,6},{6,5},{7,4},{8,9},{9,8},{10,11... | collective-permute-start | bytes 1572872 | tf_op jit(solution)/shard_map/ppermute | solution.py:250
  69.1 44.2 %collective-permute-start.3 = (bf16[2,128,768]{2,1,0:T(8,128)(2,1)S(1)}, bf16[2,128,768]{2,1,0:T(8,128)(2,1)S(1)}, u32[]{:S(2)}, u32[]{:S(2)}) collective-permute-start(bf16[2,128,768]{2,1,0:T(8,128)(2,1)S(1)} %shard_map.34.second_pair_ref), channel_id=1, source_target_pairs={{0,3},{1,2},{2,1},{3,0},{4,5},{5,4},{6,7},{7,6},{8,11},{9,10},{10,... | collective-permute-start | bytes 1179656 | tf_op jit(solution)/shard_map/ppermute | solution.py:250
  111.3 13.8 %collective-permute-start.5 = (bf16[2,128,768]{2,1,0:T(8,128)(2,1)S(1)}, bf16[2,128,768]{2,1,0:T(8,128)(2,1)S(1)}, u32[]{:S(2)}, u32[]{:S(2)}) collective-permute-start(bf16[2,128,768]{2,1,0:T(8,128)(2,1)S(1)} %shard_map.35.second_far_ref), channel_id=1, source_target_pairs={{0,3},{1,2},{2,1},{3,0},{4,5},{5,4},{6,7},{7,6},{8,11},{9,10},{10,... | collective-permute-start | bytes 1179656 | tf_op jit(solution)/shard_map/ppermute | solution.py:250
  127.2 27.7 %collective-permute-start.6 = (bf16[10,128,128]{2,1,0:T(8,128)(2,1)S(1)}, bf16[10,128,128]{2,1,0:T(8,128)(2,1)S(1)}, u32[]{:S(2)}, u32[]{:S(2)}) collective-permute-start(bf16[10,128,128]{2,1,0:T(8,128)(2,1)S(1)} %get-tuple-element.39), channel_id=1, source_target_pairs={{0,4},{1,5},{2,6},{3,7},{4,0},{5,1},{6,2},{7,3},{8,12},{9,13},{10,... | collective-permute-start | bytes 983048 | tf_op jit(solution)/shard_map/ppermute | solution.py:250
  129.1 19.4 %collective-permute-start.8 = (bf16[2,3,128,128]{3,2,1,0:T(8,128)(2,1)S(1)}, bf16[2,3,128,128]{3,2,1,0:T(8,128)(2,1)S(1)}, u32[]{:S(2)}, u32[]{:S(2)}) collective-permute-start(bf16[2,3,128,128]{3,2,1,0:T(8,128)(2,1)S(1)} %get-tuple-element.41), channel_id=1, source_target_pairs={{0,508},{1,509},{2,510},{3,511},{4,8},{5,9},{6,10},{7,11},{8,4},{9... | collective-permute-start | bytes 589832 | tf_op jit(solution)/shard_map/ppermute | solution.py:250
  137.1 17.8 %collective-permute-start.9 = (bf16[2,3,128,128]{3,2,1,0:T(8,128)(2,1)S(1)}, bf16[2,3,128,128]{3,2,1,0:T(8,128)(2,1)S(1)}, u32[]{:S(2)}, u32[]{:S(2)}) collective-permute-start(bf16[2,3,128,128]{3,2,1,0:T(8,128)(2,1)S(1)} %get-tuple-element.42), channel_id=1, source_target_pairs={{0,509},{1,508},{2,511},{3,510},{4,11},{5,10},{6,9},{7,8},{8,5},{9... | collective-permute-start | bytes 589832 | tf_op jit(solution)/shard_map/ppermute | solution.py:250
  139.1 9.5 %collective-permute-start.7 = (bf16[2,128,128]{2,1,0:T(8,128)(2,1)S(1)}, bf16[2,128,128]{2,1,0:T(8,128)(2,1)S(1)}, u32[]{:S(2)}, u32[]{:S(2)}) collective-permute-start(bf16[2,128,128]{2,1,0:T(8,128)(2,1)S(1)} %get-tuple-element.40), channel_id=1, source_target_pairs={{0,5},{1,4},{2,7},{3,6},{4,3},{5,2},{6,1},{7,0},{8,13},{9,12},{10,... | collective-permute-start | bytes 196616 | tf_op jit(solution)/shard_map/ppermute | solution.py:250

commit v13 on v12

--- a/solution.py
+++ b/solution.py
@@ -122,7 +122,7 @@
             out_ref[point, :, place[0] : place[1]] = low(dots(own[:, part * half : (part + 1) * half], pick))
 
 
-def turned_part(order_ref, block_ref, second_ref, late_ref, part, same_ref, first_ref, place):
+def turned_part(order_ref, block_ref, second_ref, late_ref, part):
     points, count, columns = block_ref.shape
     half = columns // 2
     rows = count // 2
@@ -141,14 +141,12 @@
     )
     n = lax.broadcasted_iota(jnp.int32, (count, count), 0)
     same = low(jnp.where(n == lax.broadcasted_iota(jnp.int32, (count, count), 1), 1.0, 0.0))
-    for source, out in enumerate((dots(pick, own), dots(same, other))):
-        for to, ref in enumerate((same_ref, first_ref)):
+    pieces = []
+    for out in (dots(pick, own), dots(same, other)):
+        for to in range(2):
             piece = out[to * rows : (to + 1) * rows]
-            both = jnp.concatenate([low(piece[:, : points * rows]), low(-piece[:, points * rows :])], axis=0)
-            if place is None:
-                ref[source] = both
-            else:
-                ref[source, place] = both
+            pieces.append(jnp.concatenate([low(piece[:, : points * rows]), low(-piece[:, points * rows :])], axis=0))
+    return (pieces[0], pieces[2]), (pieces[1], pieces[3])
 
 
 def finish(rest_ref, got_ref, late_ref, block_ref):
@@ -158,51 +156,66 @@
         block_ref[point] = low(total)
 
 
-def finish_kernel(
-    order_ref, rest_pair_ref, got_pair_ref, second_pair_ref, late_pair_ref,
-    rest_far_ref, got_far_ref, second_far_ref, late_far_ref,
-    block_ref, mate_same_ref, mate_first_ref, next_same_ref, next_first_ref, far_ref,
+def finish_pair_kernel(
+    order_ref, rest_ref, got_ref, second_ref, late_ref, block_ref, same_ref, first_ref
 ):
-    points, count, columns = block_ref.shape
-    finish(rest_pair_ref, got_pair_ref, late_pair_ref, block_ref)
-    finish(rest_far_ref, got_far_ref, late_far_ref, far_ref)
+    finish(rest_ref, got_ref, late_ref, block_ref)
+    for part in range(2):
+        same, first = turned_part(order_ref, block_ref, second_ref, late_ref, part)
+        for source in range(2):
+            same_ref[part, source] = same[source]
+            first_ref[part, source] = first[source]
+
+
+def finish_far_kernel(order_ref, rest_ref, got_ref, second_ref, late_ref, block_ref, same_ref, first_ref):
+    finish(rest_ref, got_ref, late_ref, block_ref)
+    for part in range(block_ref.shape[0]):
+        same, first = turned_part(order_ref, block_ref, second_ref, late_ref, part)
+        for source in range(2):
+            same_ref[part, source] = same[source]
+            first_ref[part, source] = first[source]
+
+
+def pack_kernel(pair_same_ref, passed_ref, far_same_ref, far_ref, to_mate_ref, to_next_ref):
+    points, count, columns = far_ref.shape
     strips = columns // count
-    for point in range(points):
+    for part, ref in enumerate((to_mate_ref, to_next_ref)):
+        ref[0:2] = pair_same_ref[part]
+        ref[2:4] = passed_ref[part]
+    for point in range(points):
+        to_next_ref[4 + 2 * point : 6 + 2 * point] = far_same_ref[point]
         for strip in range(strips):
-            mate_same_ref[2 + point * strips + strip] = far_ref[point, :, strip * count : (strip + 1) * count]
-    turned_part(order_ref, block_ref, second_pair_ref, late_pair_ref, 0, mate_same_ref, mate_first_ref, None)
-    turned_part(order_ref, block_ref, second_pair_ref, late_pair_ref, 1, next_same_ref, next_first_ref, 0)
-    for part in range(points):
-        turned_part(order_ref, far_ref, second_far_ref, late_far_ref, part, next_same_ref, next_first_ref, 1 + part)
-
-
-def merge_kernel(
-    order_ref, pair_ref, mate_same_ref, mate_first_ref, next_same_ref, next_first_ref, out_ref
-):
+            to_mate_ref[4 + point * strips + strip] = far_ref[point, :, strip * count : (strip + 1) * count]
+
+
+def spread(order_ref, slot, lanes, columns):
+    n = lax.broadcasted_iota(jnp.int32, (lanes, columns), 0)
+    column = lax.broadcasted_iota(jnp.int32, (lanes, columns), 1)
+    target = (n // BLOCK * (order_ref.shape[0] - 1) + order_ref[slot]) * BLOCK + n % BLOCK
+    return low(jnp.where(column == target, 1.0, 0.0))
+
+
+def merge_kernel(order_ref, pair_ref, far_first_ref, from_next_ref, from_mate_ref, out_ref):
     points, count, columns = pair_ref.shape
     rows = count // 2
     half = columns // 2
-    owners = order_ref.shape[0] - 1
-    even = order_ref[owners]
+    even = order_ref[order_ref.shape[0] - 1]
     lanes = points * rows
     strips = columns // count
-    n = lax.broadcasted_iota(jnp.int32, (lanes, columns), 0)
-    column = lax.broadcasted_iota(jnp.int32, (lanes, columns), 1)
-    target = (n // BLOCK * owners) * BLOCK + n % BLOCK
-    sources = [
-        (mate_same_ref, next_same_ref, 1),
-        (mate_first_ref, next_first_ref, 1),
-        (mate_first_ref, next_first_ref, 0),
-        (mate_same_ref, next_same_ref, 0),
-    ]
-    total = 0.0
-    for slot, (mate_piece, next_piece, source) in enumerate(sources):
-        pick = low(jnp.where(column == target + order_ref[slot] * BLOCK, 1.0, 0.0))
-        tiles = [mate_piece[source]] + [next_piece[source, place] for place in range(1 + points)]
-        total = total + lax.dot_general(
-            jnp.concatenate(tiles, axis=0), pick, (((1,), (0,)), ((), ())), preferred_element_type=jnp.float32
+    back = 0.0
+    for slot, source in enumerate((1, 3, 2, 0)):
+        tiles = [from_mate_ref[source], from_next_ref[source]]
+        if source < 2:
+            tiles += [from_next_ref[4 + 2 * part + source] for part in range(points)]
+        else:
+            tiles += [far_first_ref[part, source - 2] for part in range(points)]
+        back = back + lax.dot_general(
+            jnp.concatenate(tiles, axis=0),
+            spread(order_ref, slot, lanes, columns),
+            (((1,), (0,)), ((), ())),
+            preferred_element_type=jnp.float32,
         )
-    back = low(total)
+    back = low(back)
     for p in range(2):
         for part, place in ((0, 2 * even), (1, 2 - 2 * even)):
             natural = back[(2 * part + p) * rows : (2 * part + p + 1) * rows]
@@ -217,9 +230,9 @@
         for point in range(points):
             span = slice(point * rows, (point + 1) * rows)
             for strip in range(strips):
-                tile = mate_same_ref[2 + point * strips + strip, p * rows : (p + 1) * rows, :]
+                tile = from_mate_ref[4 + point * strips + strip, p * rows : (p + 1) * rows, :]
                 out_ref[1 + 2 * even, p, span, strip * count : (strip + 1) * count] = tile
-            first = (4 + 2 * point + p) * rows
+            first = (2 + point) * count + p * rows
             out_ref[3 - 2 * even, p, span, :] = back[first : first + rows]
 
 
@@ -262,14 +275,13 @@
     relative = jnp.stack([me ^ near_flip, me ^ 2, me ^ far_flip, me, 1 - parity])
 
     plain = pair_density.reshape(points, transitions, depth)
+    next_right = exchange_kp(plain, across)
     mate_right = exchange_kp(plain, mate)
-    next_right = exchange_kp(plain, across)
 
     weights = (jnp.concatenate([coulomb, coulomb]) * scale).reshape(1, depth)
     left_shape = [(points, 4 * rows, depth)] * 2
     left_away, left_rest = local(left_kernel, left_shape, relative, plain, weights, scalars=1, moved=4 << 20)
-    mate_away, mate_rest = local(left_kernel, left_shape, relative, mate_right, weights, scalars=1, moved=4 << 20)
-    next_right, left_away, mate_away = lax.optimization_barrier((next_right, left_away, mate_away))
+    next_right, left_away = lax.optimization_barrier((next_right, left_away))
 
     columns = points * transitions
     away_shape = [(points, 4 * rows, columns)]
@@ -278,7 +290,8 @@
 
     away_pair = local(away_pair_kernel, away_shape, relative, left_away, mate_right, next_right, scalars=1)
     got_pair = exchange_own(away_pair, True)
-    mate_away, _ = lax.optimization_barrier((mate_away, away_pair))
+    mate_left, _ = lax.optimization_barrier((mate_right, away_pair))
+    mate_away, mate_rest = local(left_kernel, left_shape, relative, mate_left, weights, scalars=1)
     away_far = local(away_far_kernel, away_shape, mate_away, next_right)
     got_far = exchange_own(away_far, True)
     left_rest, mate_rest, _ = lax.optimization_barrier((left_rest, mate_rest, away_far))
@@ -294,24 +307,27 @@
     late_far = exchange_own(second_far, False)
     tile = (2 * rows, points * rows)
     strips = points * columns // tile[1]
-    block_pair, mate_same, mate_first, next_same, next_first, _ = local(
-        finish_kernel,
-        [
-            (points, 2 * rows, columns),
-            (2 + strips, *tile),
-            (2, *tile),
-            (2, 1 + points, *tile),
-            (2, 1 + points, *tile),
-            (points, 2 * rows, columns),
-        ],
-        relative, rest_pair, got_pair, second_pair, late_pair, rest_far, got_far, second_far, late_far, scalars=1,
-    )
+    block_shape = (points, 2 * rows, columns)
+    late_pair, _ = lax.optimization_barrier((late_pair, second_far))
+    block_pair, same_pair, first_pair = local(
+        finish_pair_kernel, [block_shape, (2, 2, *tile), (2, 2, *tile)],
+        relative, rest_pair, got_pair, second_pair, late_pair, scalars=1,
+    )
+    passed_pair = exchange_own(first_pair, True)
+    late_far, _ = lax.optimization_barrier((late_far, first_pair))
+    block_far, far_same, far_first = local(
+        finish_far_kernel, [block_shape, (points, 2, *tile), (points, 2, *tile)],
+        relative, rest_far, got_far, second_far, late_far, scalars=1,
+    )
+    to_mate, to_next = local(
+        pack_kernel, [(4 + strips, *tile), (4 + 2 * points, *tile)],
+        same_pair, passed_pair, far_same, block_far, moved=16 << 20,
+    )
+    far_first = exchange(far_first, 0, across)
+    from_next = exchange_kp(to_next, across)
+    from_mate = exchange_kp(to_mate, mate)
     out = local(
-        merge_kernel, [(4, 2, points * rows, columns)],
-        relative, block_pair,
-        exchange(mate_same, 3, mate), exchange(mate_first, 0, mate),
-        exchange(next_same, 3, across), exchange(next_first, 0, across),
-        scalars=1,
+        merge_kernel, [(4, 2, points * rows, columns)], relative, block_pair, far_first, from_next, from_mate, scalars=1
     )
     return out.transpose(0, 2, 1, 3)
 

time: 159 us -> 155 us (0.975)
  waiting for transfers between devices: 91.2 us -> 78.4 us
  starting transfers between devices: 51.7 us -> 60.4 us
    ppermute x2 -> x4, starting transfers between devices: 13.2 us -> 25.3 us  [exchange_kp(): lax.ppermute(value, 'kp', [(i, partner(i) % groups) for i in range(groups)])]
    ppermute x8 -> x6, waiting for transfers between devices: 81 us -> 69.3 us  [exchange(): return lax.ppermute(value, ('kp', 'own'), pairs)]
    ppermute x8 -> x6, starting transfers between devices: 38.5 us -> 35.1 us  [exchange(): return lax.ppermute(value, ('kp', 'own'), pairs)]
    ppermute x2 -> x4, waiting for transfers between devices: 10.2 us -> 9.06 us  [exchange_kp(): lax.ppermute(value, 'kp', [(i, partner(i) % groups) for i in range(groups)])]
    pallas_call x10 -> x12, Pallas kernels: 10.7 us -> 10.9 us  [local(): pl.pallas_call(kernel, out_shape=out_shape if several else out_shape[0],...]
  transfers between devices with their start and end apart: 10 -> 10, of which waited for: 6 -> 5; matrix products, arithmetic and copies ran while one was open for 0% -> 0% of each run, Pallas kernels for 4% -> 5%
where the time goes in v13:
time: 155 us; the launch traced here: 154 us
  waiting for transfers between devices  78.4 us (51%)
  starting transfers between devices  60.4 us (39%)
  Pallas kernels  10.9 us (7%)
  local copies, waits for them, and re-layouts  4.51 us (3%)
    ppermute x6, waiting for transfers between devices, exchange(): return lax.ppermute(value, ('kp', 'own'), pairs)  69.3 us
    ppermute x6, starting transfers between devices, exchange(): return lax.ppermute(value, ('kp', 'own'), pairs)  35.1 us
    ppermute x4, starting transfers between devices, exchange_kp(): lax.ppermute(value, 'kp', [(i, partner(i) % groups) for i in range(groups)])  25.3 us
    pallas_call x12, Pallas kernels, local(): pl.pallas_call(kernel, out_shape=out_shape if several else out_shape[0],...  10.9 us
    ppermute x4, waiting for transfers between devices, exchange_kp(): lax.ppermute(value, 'kp', [(i, partner(i) % groups) for i in range(groups)])  9.06 us
  transfers between devices with their start and end apart: 10, of which 5 were waited for; matrix products, arithmetic and copies ran while one was open for 0% of the time, Pallas kernels for 5%

profile of v13, /device:TPU:128, one launch (start us, length us, event | category | flops | bytes accessed | tf_op | source)
XLA Modules:
  0.0 154.4 jit_solution(17620896729431546019)
XLA Ops:
  0.0 1.8 %reshape.33.plain_ref = bf16[2,256,1024]{2,1,0:T(8,128)(2,1)S(1)} reshape(bf16[2,256,2,512]{3,2,1,0:T(2,128)(2,1)} %param.2) | data formatting | bytes 2097152 | tf_op jit(solution)/shard_map/reshape | solution.py:277
  1.8 10.6 %collective-permute-start = (bf16[2,256,1024]{2,1,0:T(8,128)(2,1)S(1)}, bf16[2,256,1024]{2,1,0:T(8,128)(2,1)S(1)}, u32[]{:S(2)}, u32[]{:S(2)}) collective-permute-start(bf16[2,256,1024]{2,1,0:T(8,128)(2,1)S(1)} %reshape.33.plain_ref), channel_id=1, source_target_pairs={{0,508},{4,8},{8,4},{12,16},{16,12},{20,24},{24,20},{28,32},{32,28... | collective-permute-start | bytes 3145736 | tf_op jit(solution)/shard_map/ppermute | solution.py:252
  12.4 1.9 %collective-permute-start.1 = (bf16[2,256,1024]{2,1,0:T(8,128)(2,1)S(1)}, bf16[2,256,1024]{2,1,0:T(8,128)(2,1)S(1)}, u32[]{:S(2)}, u32[]{:S(2)}) collective-permute-start(bf16[2,256,1024]{2,1,0:T(8,128)(2,1)S(1)} %reshape.33.plain_ref), channel_id=1, source_target_pairs={{0,4},{4,0},{8,12},{12,8},{16,20},{20,16},{24,28},{28,24},{32,36},... | collective-permute-start | bytes 3145736 | tf_op jit(solution)/shard_map/ppermute | solution.py:252
  14.4 0.0 copy-start
  14.4 0.1 stack.23.order_ref
  14.5 0.6 copy-done
  15.1 0.8 shard_map.28
  15.8 9.1 %collective-permute-done.next_ref.right_ref = bf16[2,256,1024]{2,1,0:T(8,128)(2,1)S(1)} collective-permute-done((bf16[2,256,1024]{2,1,0:T(8,128)(2,1)S(1)}, bf16[2,256,1024]{2,1,0:T(8,128)(2,1)S(1)}, u32[]{:S(2)}, u32[]{:S(2)}) %collective-permute-start) | collective-permute-done | bytes 1048608 | tf_op jit(solution)/shard_map/ppermute | solution.py:252
  24.9 0.0 collective-permute-done.1.mate_ref.plain_ref
  24.9 1.3 shard_map.29
  26.2 5.1 %collective-permute-start.2 = (bf16[2,256,512]{2,1,0:T(8,128)(2,1)S(1)}, bf16[2,256,512]{2,1,0:T(8,128)(2,1)S(1)}, u32[]{:S(2)}, u32[]{:S(2)}) collective-permute-start(bf16[2,256,512]{2,1,0:T(8,128)(2,1)S(1)} %shard_map.29), channel_id=1, source_target_pairs={{0,1},{1,0},{2,3},{3,2},{4,7},{5,6},{6,5},{7,4},{8,9},{9,8},{10,11... | collective-permute-start | bytes 1572872 | tf_op jit(solution)/shard_map/ppermute | solution.py:263
  31.3 0.8 shard_map.30
  32.0 0.7 shard_map.31
  32.8 4.7 %collective-permute-start.4 = (bf16[2,256,512]{2,1,0:T(8,128)(2,1)S(1)}, bf16[2,256,512]{2,1,0:T(8,128)(2,1)S(1)}, u32[]{:S(2)}, u32[]{:S(2)}) collective-permute-start(bf16[2,256,512]{2,1,0:T(8,128)(2,1)S(1)} %shard_map.31), channel_id=1, source_target_pairs={{0,1},{1,0},{2,3},{3,2},{4,7},{5,6},{6,5},{7,4},{8,9},{9,8},{10,11... | collective-permute-start | bytes 1572872 | tf_op jit(solution)/shard_map/ppermute | solution.py:263
  37.5 0.8 shard_map.33.rest_ref
  38.2 1.3 shard_map.32.rest_ref
  39.5 26.5 %collective-permute-done.2.got_ref = bf16[2,256,512]{2,1,0:T(8,128)(2,1)S(1)} collective-permute-done((bf16[2,256,512]{2,1,0:T(8,128)(2,1)S(1)}, bf16[2,256,512]{2,1,0:T(8,128)(2,1)S(1)}, u32[]{:S(2)}, u32[]{:S(2)}) %collective-permute-start.2) | collective-permute-done | bytes 524320 | tf_op jit(solution)/shard_map/ppermute | solution.py:263
  66.0 0.8 shard_map.34.second_ref
  66.8 13.1 %collective-permute-start.3 = (bf16[2,128,768]{2,1,0:T(8,128)(2,1)S(1)}, bf16[2,128,768]{2,1,0:T(8,128)(2,1)S(1)}, u32[]{:S(2)}, u32[]{:S(2)}) collective-permute-start(bf16[2,128,768]{2,1,0:T(8,128)(2,1)S(1)} %shard_map.34.second_ref), channel_id=1, source_target_pairs={{0,3},{1,2},{2,1},{3,0},{4,5},{5,4},{6,7},{7,6},{8,11},{9,10},{10,... | collective-permute-start | bytes 1179656 | tf_op jit(solution)/shard_map/ppermute | solution.py:263
  79.9 13.6 %collective-permute-done.4.got_ref = bf16[2,256,512]{2,1,0:T(8,128)(2,1)S(1)} collective-permute-done((bf16[2,256,512]{2,1,0:T(8,128)(2,1)S(1)}, bf16[2,256,512]{2,1,0:T(8,128)(2,1)S(1)}, u32[]{:S(2)}, u32[]{:S(2)}) %collective-permute-start.4) | collective-permute-done | bytes 524320 | tf_op jit(solution)/shard_map/ppermute | solution.py:263
  93.6 0.8 shard_map.35.second_ref
  94.4 6.0 %collective-permute-start.5 = (bf16[2,128,768]{2,1,0:T(8,128)(2,1)S(1)}, bf16[2,128,768]{2,1,0:T(8,128)(2,1)S(1)}, u32[]{:S(2)}, u32[]{:S(2)}) collective-permute-start(bf16[2,128,768]{2,1,0:T(8,128)(2,1)S(1)} %shard_map.35.second_ref), channel_id=1, source_target_pairs={{0,3},{1,2},{2,1},{3,0},{4,5},{5,4},{6,7},{7,6},{8,11},{9,10},{10,... | collective-permute-start | bytes 1179656 | tf_op jit(solution)/shard_map/ppermute | solution.py:263
  100.4 0.0 collective-permute-done.3.late_ref
  100.4 1.1 shard_map.36
  101.5 4.4 %collective-permute-start.7 = (bf16[2,2,128,128]{3,2,1,0:T(8,128)(2,1)S(1)}, bf16[2,2,128,128]{3,2,1,0:T(8,128)(2,1)S(1)}, u32[]{:S(2)}, u32[]{:S(2)}) collective-permute-start(bf16[2,2,128,128]{3,2,1,0:T(8,128)(2,1)S(1)} %get-tuple-element.43), channel_id=1, source_target_pairs={{0,1},{1,0},{2,3},{3,2},{4,7},{5,6},{6,5},{7,4},{8,9},{9,8},{10,11... | collective-permute-start | bytes 393224 | tf_op jit(solution)/shard_map/ppermute | solution.py:263
  105.9 14.0 %collective-permute-done.5.late_ref = bf16[2,128,768]{2,1,0:T(8,128)(2,1)S(1)} collective-permute-done((bf16[2,128,768]{2,1,0:T(8,128)(2,1)S(1)}, bf16[2,128,768]{2,1,0:T(8,128)(2,1)S(1)}, u32[]{:S(2)}, u32[]{:S(2)}) %collective-permute-start.5) | collective-permute-done | bytes 393248 | tf_op jit(solution)/shard_map/ppermute | solution.py:263
  120.0 1.1 shard_map.37
  121.1 0.0 collective-permute-done.7.passed_ref
  121.1 0.1 shard_map.38
  121.2 3.1 %collective-permute-start.9 = (bf16[12,128,128]{2,1,0:T(8,128)(2,1)S(1)}, bf16[12,128,128]{2,1,0:T(8,128)(2,1)S(1)}, u32[]{:S(2)}, u32[]{:S(2)}) collective-permute-start(bf16[12,128,128]{2,1,0:T(8,128)(2,1)S(1)} %get-tuple-element.50), channel_id=1, source_target_pairs={{0,4},{4,0},{8,12},{12,8},{16,20},{20,16},{24,28},{28,24},{32,36},... | collective-permute-start | bytes 1179656 | tf_op jit(solution)/shard_map/ppermute | solution.py:252
  124.2 9.8 %collective-permute-start.8 = (bf16[8,128,128]{2,1,0:T(8,128)(2,1)S(1)}, bf16[8,128,128]{2,1,0:T(8,128)(2,1)S(1)}, u32[]{:S(2)}, u32[]{:S(2)}) collective-permute-start(bf16[8,128,128]{2,1,0:T(8,128)(2,1)S(1)} %get-tuple-element.49), channel_id=1, source_target_pairs={{0,508},{4,8},{8,4},{12,16},{16,12},{20,24},{24,20},{28,32},{32,28... | collective-permute-start | bytes 786440 | tf_op jit(solution)/shard_map/ppermute | solution.py:252
  134.0 1.9 %collective-permute-start.6 = (bf16[2,2,128,128]{3,2,1,0:T(8,128)(2,1)S(1)}, bf16[2,2,128,128]{3,2,1,0:T(8,128)(2,1)S(1)}, u32[]{:S(2)}, u32[]{:S(2)}) collective-permute-start(bf16[2,2,128,128]{3,2,1,0:T(8,128)(2,1)S(1)} %get-tuple-element.45), channel_id=1, source_target_pairs={{0,509},{1,508},{2,511},{3,510},{4,11},{5,10},{6,9},{7,8},{8,5},{9... | collective-permute-start | bytes 393224 | tf_op jit(solution)/shard_map/ppermute | solution.py:263
  135.9 15.2 %collective-permute-done.6.far_first_ref = bf16[2,2,128,128]{3,2,1,0:T(8,128)(2,1)S(1)} collective-permute-done((bf16[2,2,128,128]{3,2,1,0:T(8,128)(2,1)S(1)}, bf16[2,2,128,128]{3,2,1,0:T(8,128)(2,1)S(1)}, u32[]{:S(2)}, u32[]{:S(2)}) %collective-permute-start.6) | collective-permute-done | bytes 131104 | tf_op jit(solution)/shard_map/ppermute | solution.py:263
  151.1 0.0 collective-permute-done.8.from_next_ref
  151.1 0.0 collective-permute-done.9.from_mate_ref
  151.1 1.3 shard_map.39
  152.4 2.0 %copy.3 = bf16[4,128,2,512]{3,2,1,0:T(2,128)(2,1)} copy(bf16[4,128,2,512]{3,1,2,0:T(8,128)(2,1)S(1)} %bitcast.7) | data formatting | bytes 2097152 | tf_op jit(solution)/shard_map/transpose | solution.py:332
  (1 shorter events, 0.0 us)
Async XLA Ops:
  1.8 23.1 %collective-permute-start = (bf16[2,256,1024]{2,1,0:T(8,128)(2,1)S(1)}, bf16[2,256,1024]{2,1,0:T(8,128)(2,1)S(1)}, u32[]{:S(2)}, u32[]{:S(2)}) collective-permute-start(bf16[2,256,1024]{2,1,0:T(8,128)(2,1)S(1)} %reshape.33.plain_ref), channel_id=1, source_target_pairs={{0,508},{4,8},{8,4},{12,16},{16,12},{20,24},{24,20},{28,32},{32,28... | collective-permute-start | bytes 3145736 | tf_op jit(solution)/shard_map/ppermute | solution.py:252
  12.4 12.5 %collective-permute-start.1 = (bf16[2,256,1024]{2,1,0:T(8,128)(2,1)S(1)}, bf16[2,256,1024]{2,1,0:T(8,128)(2,1)S(1)}, u32[]{:S(2)}, u32[]{:S(2)}) collective-permute-start(bf16[2,256,1024]{2,1,0:T(8,128)(2,1)S(1)} %reshape.33.plain_ref), channel_id=1, source_target_pairs={{0,4},{4,0},{8,12},{12,8},{16,20},{20,16},{24,28},{28,24},{32,36},... | collective-permute-start | bytes 3145736 | tf_op jit(solution)/shard_map/ppermute | solution.py:252
  14.4 0.7 copy-start
  26.2 39.8 %collective-permute-start.2 = (bf16[2,256,512]{2,1,0:T(8,128)(2,1)S(1)}, bf16[2,256,512]{2,1,0:T(8,128)(2,1)S(1)}, u32[]{:S(2)}, u32[]{:S(2)}) collective-permute-start(bf16[2,256,512]{2,1,0:T(8,128)(2,1)S(1)} %shard_map.29), channel_id=1, source_target_pairs={{0,1},{1,0},{2,3},{3,2},{4,7},{5,6},{6,5},{7,4},{8,9},{9,8},{10,11... | collective-permute-start | bytes 1572872 | tf_op jit(solution)/shard_map/ppermute | solution.py:263
  32.8 60.8 %collective-permute-start.4 = (bf16[2,256,512]{2,1,0:T(8,128)(2,1)S(1)}, bf16[2,256,512]{2,1,0:T(8,128)(2,1)S(1)}, u32[]{:S(2)}, u32[]{:S(2)}) collective-permute-start(bf16[2,256,512]{2,1,0:T(8,128)(2,1)S(1)} %shard_map.31), channel_id=1, source_target_pairs={{0,1},{1,0},{2,3},{3,2},{4,7},{5,6},{6,5},{7,4},{8,9},{9,8},{10,11... | collective-permute-start | bytes 1572872 | tf_op jit(solution)/shard_map/ppermute | solution.py:263
  66.8 33.5 %collective-permute-start.3 = (bf16[2,128,768]{2,1,0:T(8,128)(2,1)S(1)}, bf16[2,128,768]{2,1,0:T(8,128)(2,1)S(1)}, u32[]{:S(2)}, u32[]{:S(2)}) collective-permute-start(bf16[2,128,768]{2,1,0:T(8,128)(2,1)S(1)} %shard_map.34.second_ref), channel_id=1, source_target_pairs={{0,3},{1,2},{2,1},{3,0},{4,5},{5,4},{6,7},{7,6},{8,11},{9,10},{10,... | collective-permute-start | bytes 1179656 | tf_op jit(solution)/shard_map/ppermute | solution.py:263
  94.4 25.6 %collective-permute-start.5 = (bf16[2,128,768]{2,1,0:T(8,128)(2,1)S(1)}, bf16[2,128,768]{2,1,0:T(8,128)(2,1)S(1)}, u32[]{:S(2)}, u32[]{:S(2)}) collective-permute-start(bf16[2,128,768]{2,1,0:T(8,128)(2,1)S(1)} %shard_map.35.second_ref), channel_id=1, source_target_pairs={{0,3},{1,2},{2,1},{3,0},{4,5},{5,4},{6,7},{7,6},{8,11},{9,10},{10,... | collective-permute-start | bytes 1179656 | tf_op jit(solution)/shard_map/ppermute | solution.py:263
  101.5 19.6 %collective-permute-start.7 = (bf16[2,2,128,128]{3,2,1,0:T(8,128)(2,1)S(1)}, bf16[2,2,128,128]{3,2,1,0:T(8,128)(2,1)S(1)}, u32[]{:S(2)}, u32[]{:S(2)}) collective-permute-start(bf16[2,2,128,128]{3,2,1,0:T(8,128)(2,1)S(1)} %get-tuple-element.43), channel_id=1, source_target_pairs={{0,1},{1,0},{2,3},{3,2},{4,7},{5,6},{6,5},{7,4},{8,9},{9,8},{10,11... | collective-permute-start | bytes 393224 | tf_op jit(solution)/shard_map/ppermute | solution.py:263
  121.2 29.9 %collective-permute-start.9 = (bf16[12,128,128]{2,1,0:T(8,128)(2,1)S(1)}, bf16[12,128,128]{2,1,0:T(8,128)(2,1)S(1)}, u32[]{:S(2)}, u32[]{:S(2)}) collective-permute-start(bf16[12,128,128]{2,1,0:T(8,128)(2,1)S(1)} %get-tuple-element.50), channel_id=1, source_target_pairs={{0,4},{4,0},{8,12},{12,8},{16,20},{20,16},{24,28},{28,24},{32,36},... | collective-permute-start | bytes 1179656 | tf_op jit(solution)/shard_map/ppermute | solution.py:252
  124.2 26.9 %collective-permute-start.8 = (bf16[8,128,128]{2,1,0:T(8,128)(2,1)S(1)}, bf16[8,128,128]{2,1,0:T(8,128)(2,1)S(1)}, u32[]{:S(2)}, u32[]{:S(2)}) collective-permute-start(bf16[8,128,128]{2,1,0:T(8,128)(2,1)S(1)} %get-tuple-element.49), channel_id=1, source_target_pairs={{0,508},{4,8},{8,4},{12,16},{16,12},{20,24},{24,20},{28,32},{32,28... | collective-permute-start | bytes 786440 | tf_op jit(solution)/shard_map/ppermute | solution.py:252
  134.0 17.1 %collective-permute-start.6 = (bf16[2,2,128,128]{3,2,1,0:T(8,128)(2,1)S(1)}, bf16[2,2,128,128]{3,2,1,0:T(8,128)(2,1)S(1)}, u32[]{:S(2)}, u32[]{:S(2)}) collective-permute-start(bf16[2,2,128,128]{3,2,1,0:T(8,128)(2,1)S(1)} %get-tuple-element.45), channel_id=1, source_target_pairs={{0,509},{1,508},{2,511},{3,510},{4,11},{5,10},{6,9},{7,8},{8,5},{9... | collective-permute-start | bytes 393224 | tf_op jit(solution)/shard_map/ppermute | solution.py:263

commit v14 on v13

--- a/solution.py
+++ b/solution.py
@@ -60,44 +60,37 @@
     return point + even - 2 * even * point
 
 
-def away_pair_kernel(order_ref, left_ref, mate_ref, next_ref, out_ref):
-    points, _, columns = out_ref.shape
-    half = columns // 2
-    for point in range(points):
-        for part, right_ref in enumerate((mate_ref, next_ref)):
-            out_ref[point, :, part * half : (part + 1) * half] = low(
-                dots(left_ref[point], right_ref[agreeing(order_ref, point)])
-            )
-
-
-def away_far_kernel(left_ref, right_ref, out_ref):
-    points, _, columns = out_ref.shape
-    half = columns // points
-    for point in range(points):
-        for part in range(points):
-            out_ref[point, :, part * half : (part + 1) * half] = low(dots(left_ref[point], right_ref[part]))
-
-
-def rest_pair_kernel(order_ref, left_ref, mate_ref, next_ref, out_ref):
-    _, points, count, columns = out_ref.shape
-    half = columns // 2
-    for point in range(points):
-        rows = left_ref[point].reshape(2 * count, -1)
-        for part, right_ref in enumerate((mate_ref, next_ref)):
-            out = low(dots(rows, right_ref[agreeing(order_ref, point)]))
-            out_ref[0, point, :, part * half : (part + 1) * half] = out[:count]
-            out_ref[1, point, :, part * half : (part + 1) * half] = out[count:]
-
-
-def rest_far_kernel(left_ref, right_ref, out_ref):
-    _, points, count, columns = out_ref.shape
-    half = columns // points
-    for point in range(points):
-        rows = left_ref[point].reshape(2 * count, -1)
-        for part in range(points):
-            out = low(dots(rows, right_ref[part]))
-            out_ref[0, point, :, part * half : (part + 1) * half] = out[:count]
-            out_ref[1, point, :, part * half : (part + 1) * half] = out[count:]
+def first_right(order_ref, point, mate_ref, near_ref):
+    return mate_ref[agreeing(order_ref, point)], near_ref[...]
+
+
+def second_right(order_ref, point, near_ref, later_ref):
+    return jnp.where(agreeing(order_ref, point) == 0, near_ref[...], later_ref[...]), later_ref[...]
+
+
+def away_kernel(rights):
+    def kernel(order_ref, left_ref, mate_left_ref, one_ref, other_ref, out_ref):
+        points, _, columns = out_ref.shape
+        half = columns // 2
+        for point in range(points):
+            for part, right in enumerate(rights(order_ref, point, one_ref, other_ref)):
+                rows = (left_ref, mate_left_ref)[part][point]
+                out_ref[point, :, part * half : (part + 1) * half] = low(dots(rows, right))
+
+    return kernel
+
+
+def rest_kernel(rights):
+    def kernel(order_ref, left_ref, mate_left_ref, one_ref, other_ref, out_ref):
+        _, points, count, columns = out_ref.shape
+        half = columns // 2
+        for point in range(points):
+            for part, right in enumerate(rights(order_ref, point, one_ref, other_ref)):
+                out = low(dots((left_ref, mate_left_ref)[part][point], right))
+                out_ref[0, point, :, part * half : (part + 1) * half] = out[:count]
+                out_ref[1, point, :, part * half : (part + 1) * half] = out[count:]
+
+    return kernel
 
 
 def picked(order_ref, slots, rows, owners, transitions):
@@ -156,9 +149,7 @@
         block_ref[point] = low(total)
 
 
-def finish_pair_kernel(
-    order_ref, rest_ref, got_ref, second_ref, late_ref, block_ref, same_ref, first_ref
-):
+def finish_kernel(order_ref, rest_ref, got_ref, second_ref, late_ref, block_ref, same_ref, first_ref):
     finish(rest_ref, got_ref, late_ref, block_ref)
     for part in range(2):
         same, first = turned_part(order_ref, block_ref, second_ref, late_ref, part)
@@ -167,25 +158,18 @@
             first_ref[part, source] = first[source]
 
 
-def finish_far_kernel(order_ref, rest_ref, got_ref, second_ref, late_ref, block_ref, same_ref, first_ref):
-    finish(rest_ref, got_ref, late_ref, block_ref)
-    for part in range(block_ref.shape[0]):
-        same, first = turned_part(order_ref, block_ref, second_ref, late_ref, part)
-        for source in range(2):
-            same_ref[part, source] = same[source]
-            first_ref[part, source] = first[source]
-
-
-def pack_kernel(pair_same_ref, passed_ref, far_same_ref, far_ref, to_mate_ref, to_next_ref):
-    points, count, columns = far_ref.shape
-    strips = columns // count
+def pack_kernel(same_0_ref, passed_0_ref, same_1_ref, block_0_ref, block_1_ref, to_mate_ref, to_next_ref):
+    points, count, columns = block_0_ref.shape
+    strips = columns // 2 // count
     for part, ref in enumerate((to_mate_ref, to_next_ref)):
-        ref[0:2] = pair_same_ref[part]
-        ref[2:4] = passed_ref[part]
-    for point in range(points):
-        to_next_ref[4 + 2 * point : 6 + 2 * point] = far_same_ref[point]
-        for strip in range(strips):
-            to_mate_ref[4 + point * strips + strip] = far_ref[point, :, strip * count : (strip + 1) * count]
+        ref[0:2] = same_0_ref[part]
+        ref[2:4] = passed_0_ref[part]
+        to_next_ref[4 + 2 * part : 6 + 2 * part] = same_1_ref[part]
+    for point in range(points):
+        for stream, ref in enumerate((block_0_ref, block_1_ref)):
+            for strip in range(strips):
+                tile = ref[point, :, columns // 2 + strip * count : columns // 2 + (strip + 1) * count]
+                to_mate_ref[4 + (point * 2 + stream) * strips + strip] = tile
 
 
 def spread(order_ref, slot, lanes, columns):
@@ -195,8 +179,8 @@
     return low(jnp.where(column == target, 1.0, 0.0))
 
 
-def merge_kernel(order_ref, pair_ref, far_first_ref, from_next_ref, from_mate_ref, out_ref):
-    points, count, columns = pair_ref.shape
+def merge_kernel(order_ref, block_0_ref, block_1_ref, first_1_ref, from_next_ref, from_mate_ref, out_ref):
+    points, count, columns = block_0_ref.shape
     rows = count // 2
     half = columns // 2
     even = order_ref[order_ref.shape[0] - 1]
@@ -205,10 +189,8 @@
     back = 0.0
     for slot, source in enumerate((1, 3, 2, 0)):
         tiles = [from_mate_ref[source], from_next_ref[source]]
-        if source < 2:
-            tiles += [from_next_ref[4 + 2 * part + source] for part in range(points)]
-        else:
-            tiles += [far_first_ref[part, source - 2] for part in range(points)]
+        for part in range(2):
+            tiles += [from_next_ref[4 + 2 * part + source] if source < 2 else first_1_ref[part, source - 2]]
         back = back + lax.dot_general(
             jnp.concatenate(tiles, axis=0),
             spread(order_ref, slot, lanes, columns),
@@ -217,10 +199,10 @@
         )
     back = low(back)
     for p in range(2):
-        for part, place in ((0, 2 * even), (1, 2 - 2 * even)):
-            natural = back[(2 * part + p) * rows : (2 * part + p + 1) * rows]
+        for kind, block_ref, place in ((0, block_0_ref, 2 * even), (2, block_1_ref, 2 - 2 * even)):
+            natural = back[kind * count + p * rows : kind * count + (p + 1) * rows]
             for row_point in range(points):
-                here = pair_ref[row_point, p * rows : (p + 1) * rows, part * half : (part + 1) * half]
+                here = block_ref[row_point, p * rows : (p + 1) * rows, :half]
                 for column_point in range(points):
                     there = natural[:, column_point * half : (column_point + 1) * half]
                     mine = even == (0 if row_point == column_point else 1)
@@ -232,8 +214,8 @@
             for strip in range(strips):
                 tile = from_mate_ref[4 + point * strips + strip, p * rows : (p + 1) * rows, :]
                 out_ref[1 + 2 * even, p, span, strip * count : (strip + 1) * count] = tile
-            first = (2 + point) * count + p * rows
-            out_ref[3 - 2 * even, p, span, :] = back[first : first + rows]
+            begin = (1 + 2 * point) * count + p * rows
+            out_ref[3 - 2 * even, p, span, :] = back[begin : begin + rows]
 
 
 def body(pair_density, coulomb):
@@ -275,59 +257,58 @@
     relative = jnp.stack([me ^ near_flip, me ^ 2, me ^ far_flip, me, 1 - parity])
 
     plain = pair_density.reshape(points, transitions, depth)
-    next_right = exchange_kp(plain, across)
+    near = exchange_kp(plain[0], across)
     mate_right = exchange_kp(plain, mate)
 
     weights = (jnp.concatenate([coulomb, coulomb]) * scale).reshape(1, depth)
     left_shape = [(points, 4 * rows, depth)] * 2
     left_away, left_rest = local(left_kernel, left_shape, relative, plain, weights, scalars=1, moved=4 << 20)
-    next_right, left_away = lax.optimization_barrier((next_right, left_away))
+    held, _ = lax.optimization_barrier((plain, left_away))
+    later = exchange_kp(held[1], across)
+    mate_away, mate_rest = local(left_kernel, left_shape, relative, mate_right, weights, scalars=1, moved=4 << 20)
+    near, mate_away = lax.optimization_barrier((near, mate_away))
 
     columns = points * transitions
     away_shape = [(points, 4 * rows, columns)]
     rest_shape = [(2, points, 2 * rows, columns)]
     second_shape = [(points, 2 * rows, columns + 4 * rows)]
-
-    away_pair = local(away_pair_kernel, away_shape, relative, left_away, mate_right, next_right, scalars=1)
-    got_pair = exchange_own(away_pair, True)
-    mate_left, _ = lax.optimization_barrier((mate_right, away_pair))
-    mate_away, mate_rest = local(left_kernel, left_shape, relative, mate_left, weights, scalars=1)
-    away_far = local(away_far_kernel, away_shape, mate_away, next_right)
-    got_far = exchange_own(away_far, True)
-    left_rest, mate_rest, _ = lax.optimization_barrier((left_rest, mate_rest, away_far))
-    rest_pair = local(
-        rest_pair_kernel, rest_shape, relative, left_rest, mate_right, next_right, scalars=1, moved=8 << 20
-    )
-    rest_far = local(rest_far_kernel, rest_shape, mate_rest, next_right, moved=8 << 20)
-    got_pair, rest_pair, rest_far = lax.optimization_barrier((got_pair, rest_pair, rest_far))
-    second_pair = local(second_kernel, second_shape, relative, rest_pair, got_pair, scalars=1)
-    late_pair = exchange_own(second_pair, False)
-    got_far, _ = lax.optimization_barrier((got_far, second_pair))
-    second_far = local(second_kernel, second_shape, relative, rest_far, got_far, scalars=1)
-    late_far = exchange_own(second_far, False)
+    block_shape = (points, 2 * rows, columns)
     tile = (2 * rows, points * rows)
     strips = points * columns // tile[1]
-    block_shape = (points, 2 * rows, columns)
-    late_pair, _ = lax.optimization_barrier((late_pair, second_far))
-    block_pair, same_pair, first_pair = local(
-        finish_pair_kernel, [block_shape, (2, 2, *tile), (2, 2, *tile)],
-        relative, rest_pair, got_pair, second_pair, late_pair, scalars=1,
-    )
-    passed_pair = exchange_own(first_pair, True)
-    late_far, _ = lax.optimization_barrier((late_far, first_pair))
-    block_far, far_same, far_first = local(
-        finish_far_kernel, [block_shape, (points, 2, *tile), (points, 2, *tile)],
-        relative, rest_far, got_far, second_far, late_far, scalars=1,
-    )
+
+    away_0 = local(away_kernel(first_right), away_shape, relative, left_away, mate_away, mate_right, near, scalars=1)
+    got_0 = exchange_own(away_0, True)
+    later, _ = lax.optimization_barrier((later, away_0))
+    away_1 = local(away_kernel(second_right), away_shape, relative, left_away, mate_away, near, later, scalars=1)
+    got_1 = exchange_own(away_1, True)
+    left_rest, mate_rest, _ = lax.optimization_barrier((left_rest, mate_rest, away_1))
+    rest_0 = local(
+        rest_kernel(first_right), rest_shape, relative, left_rest, mate_rest, mate_right, near, scalars=1, moved=8 << 20
+    )
+    rest_1 = local(
+        rest_kernel(second_right), rest_shape, relative, left_rest, mate_rest, near, later, scalars=1, moved=8 << 20
+    )
+    got_0, rest_0, rest_1 = lax.optimization_barrier((got_0, rest_0, rest_1))
+    second_0 = local(second_kernel, second_shape, relative, rest_0, got_0, scalars=1)
+    late_0 = exchange_own(second_0, False)
+    got_1, _ = lax.optimization_barrier((got_1, second_0))
+    second_1 = local(second_kernel, second_shape, relative, rest_1, got_1, scalars=1)
+    late_1 = exchange_own(second_1, False)
+    late_0, _ = lax.optimization_barrier((late_0, second_1))
+    finish_shape = [block_shape, (2, 2, *tile), (2, 2, *tile)]
+    block_0, same_0, first_0 = local(finish_kernel, finish_shape, relative, rest_0, got_0, second_0, late_0, scalars=1)
+    passed_0 = exchange_own(first_0, True)
+    late_1, _ = lax.optimization_barrier((late_1, first_0))
+    block_1, same_1, first_1 = local(finish_kernel, finish_shape, relative, rest_1, got_1, second_1, late_1, scalars=1)
     to_mate, to_next = local(
-        pack_kernel, [(4 + strips, *tile), (4 + 2 * points, *tile)],
-        same_pair, passed_pair, far_same, block_far, moved=16 << 20,
-    )
-    far_first = exchange(far_first, 0, across)
+        pack_kernel, [(4 + strips, *tile), (8, *tile)], same_0, passed_0, same_1, block_0, block_1, moved=16 << 20
+    )
+    first_1 = exchange(first_1, 0, across)
     from_next = exchange_kp(to_next, across)
     from_mate = exchange_kp(to_mate, mate)
     out = local(
-        merge_kernel, [(4, 2, points * rows, columns)], relative, block_pair, far_first, from_next, from_mate, scalars=1
+        merge_kernel, [(4, 2, points * rows, columns)],
+        relative, block_0, block_1, first_1, from_next, from_mate, scalars=1,
     )
     return out.transpose(0, 2, 1, 3)
 

time: 155 us -> 164 us (1.058)
  the two profiles are of different devices: /device:TPU:128 before, /device:TPU:56 now
where the time goes in v14:
time: 164 us
  starting transfers between devices  87.3 us (53%)
  waiting for transfers between devices  59.3 us (36%)
  Pallas kernels  12 us (7%)
  local copies, waits for them, and re-layouts  4.62 us (3%)
    ppermute x6, waiting for transfers between devices, exchange(): return lax.ppermute(value, ('kp', 'own'), pairs)  56.7 us
    ppermute x6, starting transfers between devices, exchange(): return lax.ppermute(value, ('kp', 'own'), pairs)  44.9 us
    ppermute x5, starting transfers between devices, exchange_kp(): lax.ppermute(value, 'kp', [(i, partner(i) % groups) for i in range(groups)])  42.4 us
    pallas_call x12, Pallas kernels, local(): pl.pallas_call(kernel, out_shape=out_shape if several else out_shape[0],...  12 us
  transfers between devices with their start and end apart: 11, of which 5 were waited for; matrix products, arithmetic and copies ran while one was open for 0% of the time, Pallas kernels for 7%

profile of v14, /device:TPU:56, one launch (start us, length us, event | category | flops | bytes accessed | tf_op | source)
XLA Modules:
  0.0 163.6 jit_solution(811751551690945851)
XLA Ops:
  0.0 1.8 %reshape.35.plain_ref = bf16[2,256,1024]{2,1,0:T(8,128)(2,1)S(1)} reshape(bf16[2,256,2,512]{3,2,1,0:T(2,128)(2,1)} %param.2) | data formatting | bytes 2097152 | tf_op jit(solution)/shard_map/reshape | solution.py:259
  1.8 0.0 slice-start
  1.8 2.1 %collective-permute-start.1 = (bf16[2,256,1024]{2,1,0:T(8,128)(2,1)S(1)}, bf16[2,256,1024]{2,1,0:T(8,128)(2,1)S(1)}, u32[]{:S(2)}, u32[]{:S(2)}) collective-permute-start(bf16[2,256,1024]{2,1,0:T(8,128)(2,1)S(1)} %reshape.35.plain_ref), channel_id=1, source_target_pairs={{0,4},{4,0},{8,12},{12,8},{16,20},{20,16},{24,28},{28,24},{32,36},... | collective-permute-start | bytes 3145736 | tf_op jit(solution)/shard_map/ppermute | solution.py:234
  3.9 0.0 slice-done
  3.9 0.1 copy.4
  4.0 4.3 %collective-permute-start = (bf16[256,1024]{1,0:T(8,128)(2,1)S(1)}, bf16[256,1024]{1,0:T(8,128)(2,1)S(1)}, u32[]{:S(2)}, u32[]{:S(2)}) collective-permute-start(bf16[256,1024]{1,0:T(8,128)(2,1)S(1)} %bitcast.14), channel_id=1, source_target_pairs={{0,508},{4,8},{8,4},{12,16},{16,12},{20,24},{24,20},{28,32},{32,28... | collective-permute-start | bytes 1572872 | tf_op jit(solution)/shard_map/ppermute | solution.py:234
  8.3 0.0 copy-start
  8.3 0.1 stack.23.order_ref
  8.4 0.6 copy-done
  9.0 0.8 shard_map.28
  9.8 3.4 %collective-permute-start.3 = (bf16[256,1024]{1,0:T(8,128)(2,1)S(1)}, bf16[256,1024]{1,0:T(8,128)(2,1)S(1)}, u32[]{:S(2)}, u32[]{:S(2)}) collective-permute-start(bf16[256,1024]{1,0:T(8,128)(2,1)S(1)} %slice_bitcast_fusion), channel_id=1, source_target_pairs={{0,508},{4,8},{8,4},{12,16},{16,12},{20,24},{24,20},{28,32},{32,28... | collective-permute-start | bytes 1572872 | tf_op jit(solution)/shard_map/ppermute | solution.py:234
  13.2 0.0 collective-permute-done.1.plain_ref.one_ref
  13.2 0.8 shard_map.29
  14.0 2.6 %collective-permute-done.other_ref.one_ref = bf16[256,1024]{1,0:T(8,128)(2,1)S(1)} collective-permute-done((bf16[256,1024]{1,0:T(8,128)(2,1)S(1)}, bf16[256,1024]{1,0:T(8,128)(2,1)S(1)}, u32[]{:S(2)}, u32[]{:S(2)}) %collective-permute-start) | collective-permute-done | bytes 524320 | tf_op jit(solution)/shard_map/ppermute | solution.py:234
  16.6 1.3 shard_map.30
  17.9 9.1 %collective-permute-start.2 = (bf16[2,256,512]{2,1,0:T(8,128)(2,1)S(1)}, bf16[2,256,512]{2,1,0:T(8,128)(2,1)S(1)}, u32[]{:S(2)}, u32[]{:S(2)}) collective-permute-start(bf16[2,256,512]{2,1,0:T(8,128)(2,1)S(1)} %shard_map.30), channel_id=1, source_target_pairs={{0,1},{1,0},{2,3},{3,2},{4,7},{5,6},{6,5},{7,4},{8,9},{9,8},{10,11... | collective-permute-start | bytes 1572872 | tf_op jit(solution)/shard_map/ppermute | solution.py:245
  27.0 0.0 collective-permute-done.3.other_ref
  27.0 1.3 shard_map.31
  28.3 4.5 %collective-permute-start.5 = (bf16[2,256,512]{2,1,0:T(8,128)(2,1)S(1)}, bf16[2,256,512]{2,1,0:T(8,128)(2,1)S(1)}, u32[]{:S(2)}, u32[]{:S(2)}) collective-permute-start(bf16[2,256,512]{2,1,0:T(8,128)(2,1)S(1)} %shard_map.31), channel_id=1, source_target_pairs={{0,1},{1,0},{2,3},{3,2},{4,7},{5,6},{6,5},{7,4},{8,9},{9,8},{10,11... | collective-permute-start | bytes 1572872 | tf_op jit(solution)/shard_map/ppermute | solution.py:245
  32.8 1.3 shard_map.33.rest_ref
  34.1 1.3 shard_map.32.rest_ref
  35.4 36.5 %collective-permute-done.2.got_ref = bf16[2,256,512]{2,1,0:T(8,128)(2,1)S(1)} collective-permute-done((bf16[2,256,512]{2,1,0:T(8,128)(2,1)S(1)}, bf16[2,256,512]{2,1,0:T(8,128)(2,1)S(1)}, u32[]{:S(2)}, u32[]{:S(2)}) %collective-permute-start.2) | collective-permute-done | bytes 524320 | tf_op jit(solution)/shard_map/ppermute | solution.py:245
  71.9 0.8 shard_map.34.second_ref
  72.8 9.3 %collective-permute-start.4 = (bf16[2,128,768]{2,1,0:T(8,128)(2,1)S(1)}, bf16[2,128,768]{2,1,0:T(8,128)(2,1)S(1)}, u32[]{:S(2)}, u32[]{:S(2)}) collective-permute-start(bf16[2,128,768]{2,1,0:T(8,128)(2,1)S(1)} %shard_map.34.second_ref), channel_id=1, source_target_pairs={{0,3},{1,2},{2,1},{3,0},{4,5},{5,4},{6,7},{7,6},{8,11},{9,10},{10,... | collective-permute-start | bytes 1179656 | tf_op jit(solution)/shard_map/ppermute | solution.py:245
  82.1 0.0 collective-permute-done.5.got_ref
  82.1 0.8 shard_map.35.second_ref
  82.9 14.6 %collective-permute-start.6 = (bf16[2,128,768]{2,1,0:T(8,128)(2,1)S(1)}, bf16[2,128,768]{2,1,0:T(8,128)(2,1)S(1)}, u32[]{:S(2)}, u32[]{:S(2)}) collective-permute-start(bf16[2,128,768]{2,1,0:T(8,128)(2,1)S(1)} %shard_map.35.second_ref), channel_id=1, source_target_pairs={{0,3},{1,2},{2,1},{3,0},{4,5},{5,4},{6,7},{7,6},{8,11},{9,10},{10,... | collective-permute-start | bytes 1179656 | tf_op jit(solution)/shard_map/ppermute | solution.py:245
  97.6 4.3 %collective-permute-done.4.late_ref = bf16[2,128,768]{2,1,0:T(8,128)(2,1)S(1)} collective-permute-done((bf16[2,128,768]{2,1,0:T(8,128)(2,1)S(1)}, bf16[2,128,768]{2,1,0:T(8,128)(2,1)S(1)}, u32[]{:S(2)}, u32[]{:S(2)}) %collective-permute-start.4) | collective-permute-done | bytes 393248 | tf_op jit(solution)/shard_map/ppermute | solution.py:245
  101.9 1.1 shard_map.36
  103.0 5.0 %collective-permute-start.8 = (bf16[2,2,128,128]{3,2,1,0:T(8,128)(2,1)S(1)}, bf16[2,2,128,128]{3,2,1,0:T(8,128)(2,1)S(1)}, u32[]{:S(2)}, u32[]{:S(2)}) collective-permute-start(bf16[2,2,128,128]{3,2,1,0:T(8,128)(2,1)S(1)} %get-tuple-element.45), channel_id=1, source_target_pairs={{0,1},{1,0},{2,3},{3,2},{4,7},{5,6},{6,5},{7,4},{8,9},{9,8},{10,11... | collective-permute-start | bytes 393224 | tf_op jit(solution)/shard_map/ppermute | solution.py:245
  108.0 5.0 %collective-permute-done.6.late_ref = bf16[2,128,768]{2,1,0:T(8,128)(2,1)S(1)} collective-permute-done((bf16[2,128,768]{2,1,0:T(8,128)(2,1)S(1)}, bf16[2,128,768]{2,1,0:T(8,128)(2,1)S(1)}, u32[]{:S(2)}, u32[]{:S(2)}) %collective-permute-start.6) | collective-permute-done | bytes 393248 | tf_op jit(solution)/shard_map/ppermute | solution.py:245
  113.1 1.1 shard_map.37
  114.2 0.0 collective-permute-done.8.passed_0_ref
  114.2 0.1 shard_map.38
  114.3 1.9 %collective-permute-start.10 = (bf16[12,128,128]{2,1,0:T(8,128)(2,1)S(1)}, bf16[12,128,128]{2,1,0:T(8,128)(2,1)S(1)}, u32[]{:S(2)}, u32[]{:S(2)}) collective-permute-start(bf16[12,128,128]{2,1,0:T(8,128)(2,1)S(1)} %get-tuple-element.52), channel_id=1, source_target_pairs={{0,4},{4,0},{8,12},{12,8},{16,20},{20,16},{24,28},{28,24},{32,36},... | collective-permute-start | bytes 1179656 | tf_op jit(solution)/shard_map/ppermute | solution.py:234
  116.2 30.8 %collective-permute-start.9 = (bf16[8,128,128]{2,1,0:T(8,128)(2,1)S(1)}, bf16[8,128,128]{2,1,0:T(8,128)(2,1)S(1)}, u32[]{:S(2)}, u32[]{:S(2)}) collective-permute-start(bf16[8,128,128]{2,1,0:T(8,128)(2,1)S(1)} %get-tuple-element.51), channel_id=1, source_target_pairs={{0,508},{4,8},{8,4},{12,16},{16,12},{20,24},{24,20},{28,32},{32,28... | collective-permute-start | bytes 786440 | tf_op jit(solution)/shard_map/ppermute | solution.py:234
  147.0 2.3 %collective-permute-start.7 = (bf16[2,2,128,128]{3,2,1,0:T(8,128)(2,1)S(1)}, bf16[2,2,128,128]{3,2,1,0:T(8,128)(2,1)S(1)}, u32[]{:S(2)}, u32[]{:S(2)}) collective-permute-start(bf16[2,2,128,128]{3,2,1,0:T(8,128)(2,1)S(1)} %get-tuple-element.48), channel_id=1, source_target_pairs={{0,509},{1,508},{2,511},{3,510},{4,11},{5,10},{6,9},{7,8},{8,5},{9... | collective-permute-start | bytes 393224 | tf_op jit(solution)/shard_map/ppermute | solution.py:245
  149.4 10.9 %collective-permute-done.7.first_1_ref = bf16[2,2,128,128]{3,2,1,0:T(8,128)(2,1)S(1)} collective-permute-done((bf16[2,2,128,128]{3,2,1,0:T(8,128)(2,1)S(1)}, bf16[2,2,128,128]{3,2,1,0:T(8,128)(2,1)S(1)}, u32[]{:S(2)}, u32[]{:S(2)}) %collective-permute-start.7) | collective-permute-done | bytes 131104 | tf_op jit(solution)/shard_map/ppermute | solution.py:245
  160.2 0.0 collective-permute-done.9.from_next_ref
  160.2 0.0 collective-permute-done.10.from_mate_ref
  160.2 1.3 shard_map.39
  161.5 2.0 %copy.3 = bf16[4,128,2,512]{3,2,1,0:T(2,128)(2,1)} copy(bf16[4,128,2,512]{3,1,2,0:T(8,128)(2,1)S(1)} %bitcast.12) | data formatting | bytes 2097152 | tf_op jit(solution)/shard_map/transpose | solution.py:313
  (2 shorter events, 0.0 us)
Async XLA Ops:
  1.8 2.1 %slice-start = ((bf16[2,256,2,512]{3,2,1,0:T(2,128)(2,1)}), bf16[1,256,2,512]{3,2,1,0:T(2,128)(2,1)S(1)}, s32[]{:S(2)}) async-start(bf16[2,256,2,512]{3,2,1,0:T(2,128)(2,1)} %param.2), calls=%async_computation | async-start | bytes 1048576 | tf_op jit(solution)/shard_map/slice | solution.py:260
  1.8 11.4 %collective-permute-start.1 = (bf16[2,256,1024]{2,1,0:T(8,128)(2,1)S(1)}, bf16[2,256,1024]{2,1,0:T(8,128)(2,1)S(1)}, u32[]{:S(2)}, u32[]{:S(2)}) collective-permute-start(bf16[2,256,1024]{2,1,0:T(8,128)(2,1)S(1)} %reshape.35.plain_ref), channel_id=1, source_target_pairs={{0,4},{4,0},{8,12},{12,8},{16,20},{20,16},{24,28},{28,24},{32,36},... | collective-permute-start | bytes 3145736 | tf_op jit(solution)/shard_map/ppermute | solution.py:234
  4.0 12.6 %collective-permute-start = (bf16[256,1024]{1,0:T(8,128)(2,1)S(1)}, bf16[256,1024]{1,0:T(8,128)(2,1)S(1)}, u32[]{:S(2)}, u32[]{:S(2)}) collective-permute-start(bf16[256,1024]{1,0:T(8,128)(2,1)S(1)} %bitcast.14), channel_id=1, source_target_pairs={{0,508},{4,8},{8,4},{12,16},{16,12},{20,24},{24,20},{28,32},{32,28... | collective-permute-start | bytes 1572872 | tf_op jit(solution)/shard_map/ppermute | solution.py:234
  8.3 0.7 copy-start
  9.8 17.2 %collective-permute-start.3 = (bf16[256,1024]{1,0:T(8,128)(2,1)S(1)}, bf16[256,1024]{1,0:T(8,128)(2,1)S(1)}, u32[]{:S(2)}, u32[]{:S(2)}) collective-permute-start(bf16[256,1024]{1,0:T(8,128)(2,1)S(1)} %slice_bitcast_fusion), channel_id=1, source_target_pairs={{0,508},{4,8},{8,4},{12,16},{16,12},{20,24},{24,20},{28,32},{32,28... | collective-permute-start | bytes 1572872 | tf_op jit(solution)/shard_map/ppermute | solution.py:234
  17.9 54.1 %collective-permute-start.2 = (bf16[2,256,512]{2,1,0:T(8,128)(2,1)S(1)}, bf16[2,256,512]{2,1,0:T(8,128)(2,1)S(1)}, u32[]{:S(2)}, u32[]{:S(2)}) collective-permute-start(bf16[2,256,512]{2,1,0:T(8,128)(2,1)S(1)} %shard_map.30), channel_id=1, source_target_pairs={{0,1},{1,0},{2,3},{3,2},{4,7},{5,6},{6,5},{7,4},{8,9},{9,8},{10,11... | collective-permute-start | bytes 1572872 | tf_op jit(solution)/shard_map/ppermute | solution.py:245
  28.3 53.8 %collective-permute-start.5 = (bf16[2,256,512]{2,1,0:T(8,128)(2,1)S(1)}, bf16[2,256,512]{2,1,0:T(8,128)(2,1)S(1)}, u32[]{:S(2)}, u32[]{:S(2)}) collective-permute-start(bf16[2,256,512]{2,1,0:T(8,128)(2,1)S(1)} %shard_map.31), channel_id=1, source_target_pairs={{0,1},{1,0},{2,3},{3,2},{4,7},{5,6},{6,5},{7,4},{8,9},{9,8},{10,11... | collective-permute-start | bytes 1572872 | tf_op jit(solution)/shard_map/ppermute | solution.py:245
  72.8 29.1 %collective-permute-start.4 = (bf16[2,128,768]{2,1,0:T(8,128)(2,1)S(1)}, bf16[2,128,768]{2,1,0:T(8,128)(2,1)S(1)}, u32[]{:S(2)}, u32[]{:S(2)}) collective-permute-start(bf16[2,128,768]{2,1,0:T(8,128)(2,1)S(1)} %shard_map.34.second_ref), channel_id=1, source_target_pairs={{0,3},{1,2},{2,1},{3,0},{4,5},{5,4},{6,7},{7,6},{8,11},{9,10},{10,... | collective-permute-start | bytes 1179656 | tf_op jit(solution)/shard_map/ppermute | solution.py:245
  82.9 30.1 %collective-permute-start.6 = (bf16[2,128,768]{2,1,0:T(8,128)(2,1)S(1)}, bf16[2,128,768]{2,1,0:T(8,128)(2,1)S(1)}, u32[]{:S(2)}, u32[]{:S(2)}) collective-permute-start(bf16[2,128,768]{2,1,0:T(8,128)(2,1)S(1)} %shard_map.35.second_ref), channel_id=1, source_target_pairs={{0,3},{1,2},{2,1},{3,0},{4,5},{5,4},{6,7},{7,6},{8,11},{9,10},{10,... | collective-permute-start | bytes 1179656 | tf_op jit(solution)/shard_map/ppermute | solution.py:245
  103.0 11.2 %collective-permute-start.8 = (bf16[2,2,128,128]{3,2,1,0:T(8,128)(2,1)S(1)}, bf16[2,2,128,128]{3,2,1,0:T(8,128)(2,1)S(1)}, u32[]{:S(2)}, u32[]{:S(2)}) collective-permute-start(bf16[2,2,128,128]{3,2,1,0:T(8,128)(2,1)S(1)} %get-tuple-element.45), channel_id=1, source_target_pairs={{0,1},{1,0},{2,3},{3,2},{4,7},{5,6},{6,5},{7,4},{8,9},{9,8},{10,11... | collective-permute-start | bytes 393224 | tf_op jit(solution)/shard_map/ppermute | solution.py:245
  114.3 46.0 %collective-permute-start.10 = (bf16[12,128,128]{2,1,0:T(8,128)(2,1)S(1)}, bf16[12,128,128]{2,1,0:T(8,128)(2,1)S(1)}, u32[]{:S(2)}, u32[]{:S(2)}) collective-permute-start(bf16[12,128,128]{2,1,0:T(8,128)(2,1)S(1)} %get-tuple-element.52), channel_id=1, source_target_pairs={{0,4},{4,0},{8,12},{12,8},{16,20},{20,16},{24,28},{28,24},{32,36},... | collective-permute-start | bytes 1179656 | tf_op jit(solution)/shard_map/ppermute | solution.py:234
  116.2 44.0 %collective-permute-start.9 = (bf16[8,128,128]{2,1,0:T(8,128)(2,1)S(1)}, bf16[8,128,128]{2,1,0:T(8,128)(2,1)S(1)}, u32[]{:S(2)}, u32[]{:S(2)}) collective-permute-start(bf16[8,128,128]{2,1,0:T(8,128)(2,1)S(1)} %get-tuple-element.51), channel_id=1, source_target_pairs={{0,508},{4,8},{8,4},{12,16},{16,12},{20,24},{24,20},{28,32},{32,28... | collective-permute-start | bytes 786440 | tf_op jit(solution)/shard_map/ppermute | solution.py:234
  147.0 13.2 %collective-permute-start.7 = (bf16[2,2,128,128]{3,2,1,0:T(8,128)(2,1)S(1)}, bf16[2,2,128,128]{3,2,1,0:T(8,128)(2,1)S(1)}, u32[]{:S(2)}, u32[]{:S(2)}) collective-permute-start(bf16[2,2,128,128]{3,2,1,0:T(8,128)(2,1)S(1)} %get-tuple-element.48), channel_id=1, source_target_pairs={{0,509},{1,508},{2,511},{3,510},{4,11},{5,10},{6,9},{7,8},{8,5},{9... | collective-permute-start | bytes 393224 | tf_op jit(solution)/shard_map/ppermute | solution.py:245

commit v15 on v14

--- a/solution.py
+++ b/solution.py
@@ -256,15 +256,14 @@
     near_flip, far_flip = 1 + 2 * parity, 3 - 2 * parity
     relative = jnp.stack([me ^ near_flip, me ^ 2, me ^ far_flip, me, 1 - parity])
 
-    plain = pair_density.reshape(points, transitions, depth)
+    plain = lax.optimization_barrier(pair_density.reshape(points, transitions, depth))
     near = exchange_kp(plain[0], across)
+    later = exchange_kp(plain[1], across)
     mate_right = exchange_kp(plain, mate)
 
     weights = (jnp.concatenate([coulomb, coulomb]) * scale).reshape(1, depth)
     left_shape = [(points, 4 * rows, depth)] * 2
     left_away, left_rest = local(left_kernel, left_shape, relative, plain, weights, scalars=1, moved=4 << 20)
-    held, _ = lax.optimization_barrier((plain, left_away))
-    later = exchange_kp(held[1], across)
     mate_away, mate_rest = local(left_kernel, left_shape, relative, mate_right, weights, scalars=1, moved=4 << 20)
     near, mate_away = lax.optimization_barrier((near, mate_away))
 

time: 164 us -> 154 us (0.939)
  the two profiles are of different devices: /device:TPU:56 before, /device:TPU:24 now
where the time goes in v15:
time: 154 us; the launch traced here: 151 us
  starting transfers between devices  105 us (68%)
  waiting for transfers between devices  28.3 us (18%)
  Pallas kernels  12.1 us (8%)
  local copies, waits for them, and re-layouts  5.54 us (4%)
    ppermute x6, starting transfers between devices, exchange(): return lax.ppermute(value, ('kp', 'own'), pairs)  88.5 us
    ppermute x6, waiting for transfers between devices, exchange(): return lax.ppermute(value, ('kp', 'own'), pairs)  25.4 us
    ppermute x5, starting transfers between devices, exchange_kp(): lax.ppermute(value, 'kp', [(i, partner(i) % groups) for i in range(groups)])  16.7 us
    pallas_call x12, Pallas kernels, local(): pl.pallas_call(kernel, out_shape=out_shape if several else out_shape[0],...  12.1 us
  transfers between devices with their start and end apart: 11, of which 5 were waited for; matrix products, arithmetic and copies ran while one was open for 1% of the time, Pallas kernels for 7%

profile of v15, /device:TPU:24, one launch (start us, length us, event | category | flops | bytes accessed | tf_op | source)
XLA Modules:
  0.0 151.3 jit_solution(17385026364644585628)
XLA Ops:
  0.0 1.8 %reshape.33.plain_ref = bf16[2,256,1024]{2,1,0:T(8,128)(2,1)S(1)} reshape(bf16[2,256,2,512]{3,2,1,0:T(2,128)(2,1)} %param.2) | data formatting | bytes 2097152 | tf_op jit(solution)/shard_map/reshape | solution.py:259
  1.8 1.9 %collective-permute-start.1 = (bf16[2,256,1024]{2,1,0:T(8,128)(2,1)S(1)}, bf16[2,256,1024]{2,1,0:T(8,128)(2,1)S(1)}, u32[]{:S(2)}, u32[]{:S(2)}) collective-permute-start(bf16[2,256,1024]{2,1,0:T(8,128)(2,1)S(1)} %reshape.33.plain_ref), channel_id=1, source_target_pairs={{0,4},{4,0},{8,12},{12,8},{16,20},{20,16},{24,28},{28,24},{32,36},... | collective-permute-start | bytes 3145736 | tf_op jit(solution)/shard_map/ppermute | solution.py:234
  3.7 1.0 slice_bitcast_fusion
  4.8 9.0 %collective-permute-start = (bf16[256,1024]{1,0:T(8,128)(2,1)}, bf16[256,1024]{1,0:T(8,128)(2,1)S(1)}, u32[]{:S(2)}, u32[]{:S(2)}) collective-permute-start(bf16[256,1024]{1,0:T(8,128)(2,1)} %get-tuple-element.52), channel_id=1, source_target_pairs={{0,508},{4,8},{8,4},{12,16},{16,12},{20,24},{24,20},{28,32},{32,28... | collective-permute-start | bytes 1572872 | tf_op jit(solution)/shard_map/ppermute | solution.py:234
  13.8 1.9 %collective-permute-start.3 = (bf16[256,1024]{1,0:T(8,128)(2,1)}, bf16[256,1024]{1,0:T(8,128)(2,1)S(1)}, u32[]{:S(2)}, u32[]{:S(2)}) collective-permute-start(bf16[256,1024]{1,0:T(8,128)(2,1)} %get-tuple-element.51), channel_id=1, source_target_pairs={{0,508},{4,8},{8,4},{12,16},{16,12},{20,24},{24,20},{28,32},{32,28... | collective-permute-start | bytes 1572872 | tf_op jit(solution)/shard_map/ppermute | solution.py:234
  15.7 0.0 copy-start
  15.7 0.1 stack.23.order_ref
  15.8 0.6 copy-done
  16.4 0.8 shard_map.28
  17.2 0.0 collective-permute-done.1.plain_ref.one_ref
  17.2 0.8 shard_map.29
  18.0 2.9 %collective-permute-done.other_ref.one_ref = bf16[256,1024]{1,0:T(8,128)(2,1)S(1)} collective-permute-done((bf16[256,1024]{1,0:T(8,128)(2,1)}, bf16[256,1024]{1,0:T(8,128)(2,1)S(1)}, u32[]{:S(2)}, u32[]{:S(2)}) %collective-permute-start) | collective-permute-done | bytes 524320 | tf_op jit(solution)/shard_map/ppermute | solution.py:234
  20.8 1.3 shard_map.30
  22.1 9.1 %collective-permute-start.2 = (bf16[2,256,512]{2,1,0:T(8,128)(2,1)S(1)}, bf16[2,256,512]{2,1,0:T(8,128)(2,1)S(1)}, u32[]{:S(2)}, u32[]{:S(2)}) collective-permute-start(bf16[2,256,512]{2,1,0:T(8,128)(2,1)S(1)} %shard_map.30), channel_id=1, source_target_pairs={{0,1},{1,0},{2,3},{3,2},{4,7},{5,6},{6,5},{7,4},{8,9},{9,8},{10,11... | collective-permute-start | bytes 1572872 | tf_op jit(solution)/shard_map/ppermute | solution.py:245
  31.2 0.0 collective-permute-done.3.other_ref
  31.2 1.3 shard_map.31
  32.5 9.4 %collective-permute-start.5 = (bf16[2,256,512]{2,1,0:T(8,128)(2,1)S(1)}, bf16[2,256,512]{2,1,0:T(8,128)(2,1)S(1)}, u32[]{:S(2)}, u32[]{:S(2)}) collective-permute-start(bf16[2,256,512]{2,1,0:T(8,128)(2,1)S(1)} %shard_map.31), channel_id=1, source_target_pairs={{0,1},{1,0},{2,3},{3,2},{4,7},{5,6},{6,5},{7,4},{8,9},{9,8},{10,11... | collective-permute-start | bytes 1572872 | tf_op jit(solution)/shard_map/ppermute | solution.py:245
  41.9 1.3 shard_map.33.rest_ref
  43.3 1.3 shard_map.32.rest_ref
  44.6 10.1 %collective-permute-done.2.got_ref = bf16[2,256,512]{2,1,0:T(8,128)(2,1)S(1)} collective-permute-done((bf16[2,256,512]{2,1,0:T(8,128)(2,1)S(1)}, bf16[2,256,512]{2,1,0:T(8,128)(2,1)S(1)}, u32[]{:S(2)}, u32[]{:S(2)}) %collective-permute-start.2) | collective-permute-done | bytes 524320 | tf_op jit(solution)/shard_map/ppermute | solution.py:245
  54.7 0.8 shard_map.34.second_ref
  55.5 11.6 %collective-permute-start.4 = (bf16[2,128,768]{2,1,0:T(8,128)(2,1)S(1)}, bf16[2,128,768]{2,1,0:T(8,128)(2,1)S(1)}, u32[]{:S(2)}, u32[]{:S(2)}) collective-permute-start(bf16[2,128,768]{2,1,0:T(8,128)(2,1)S(1)} %shard_map.34.second_ref), channel_id=1, source_target_pairs={{0,3},{1,2},{2,1},{3,0},{4,5},{5,4},{6,7},{7,6},{8,11},{9,10},{10,... | collective-permute-start | bytes 1179656 | tf_op jit(solution)/shard_map/ppermute | solution.py:245
  67.1 9.7 %collective-permute-done.5.got_ref = bf16[2,256,512]{2,1,0:T(8,128)(2,1)S(1)} collective-permute-done((bf16[2,256,512]{2,1,0:T(8,128)(2,1)S(1)}, bf16[2,256,512]{2,1,0:T(8,128)(2,1)S(1)}, u32[]{:S(2)}, u32[]{:S(2)}) %collective-permute-start.5) | collective-permute-done | bytes 524320 | tf_op jit(solution)/shard_map/ppermute | solution.py:245
  76.8 0.8 shard_map.35.second_ref
  77.6 37.5 %collective-permute-start.6 = (bf16[2,128,768]{2,1,0:T(8,128)(2,1)S(1)}, bf16[2,128,768]{2,1,0:T(8,128)(2,1)S(1)}, u32[]{:S(2)}, u32[]{:S(2)}) collective-permute-start(bf16[2,128,768]{2,1,0:T(8,128)(2,1)S(1)} %shard_map.35.second_ref), channel_id=1, source_target_pairs={{0,3},{1,2},{2,1},{3,0},{4,5},{5,4},{6,7},{7,6},{8,11},{9,10},{10,... | collective-permute-start | bytes 1179656 | tf_op jit(solution)/shard_map/ppermute | solution.py:245
  115.1 0.0 collective-permute-done.4.late_ref
  115.1 1.1 shard_map.36
  116.3 8.5 %collective-permute-start.8 = (bf16[2,2,128,128]{3,2,1,0:T(8,128)(2,1)S(1)}, bf16[2,2,128,128]{3,2,1,0:T(8,128)(2,1)S(1)}, u32[]{:S(2)}, u32[]{:S(2)}) collective-permute-start(bf16[2,2,128,128]{3,2,1,0:T(8,128)(2,1)S(1)} %get-tuple-element.43), channel_id=1, source_target_pairs={{0,1},{1,0},{2,3},{3,2},{4,7},{5,6},{6,5},{7,4},{8,9},{9,8},{10,11... | collective-permute-start | bytes 393224 | tf_op jit(solution)/shard_map/ppermute | solution.py:245
  124.8 3.1 %collective-permute-done.6.late_ref = bf16[2,128,768]{2,1,0:T(8,128)(2,1)S(1)} collective-permute-done((bf16[2,128,768]{2,1,0:T(8,128)(2,1)S(1)}, bf16[2,128,768]{2,1,0:T(8,128)(2,1)S(1)}, u32[]{:S(2)}, u32[]{:S(2)}) %collective-permute-start.6) | collective-permute-done | bytes 393248 | tf_op jit(solution)/shard_map/ppermute | solution.py:245
  127.9 1.1 shard_map.37
  129.1 0.0 collective-permute-done.8.passed_0_ref
  129.1 0.1 shard_map.38
  129.1 1.9 %collective-permute-start.10 = (bf16[12,128,128]{2,1,0:T(8,128)(2,1)S(1)}, bf16[12,128,128]{2,1,0:T(8,128)(2,1)S(1)}, u32[]{:S(2)}, u32[]{:S(2)}) collective-permute-start(bf16[12,128,128]{2,1,0:T(8,128)(2,1)S(1)} %get-tuple-element.50), channel_id=1, source_target_pairs={{0,4},{4,0},{8,12},{12,8},{16,20},{20,16},{24,28},{28,24},{32,36},... | collective-permute-start | bytes 1179656 | tf_op jit(solution)/shard_map/ppermute | solution.py:234
  131.1 1.9 %collective-permute-start.9 = (bf16[8,128,128]{2,1,0:T(8,128)(2,1)S(1)}, bf16[8,128,128]{2,1,0:T(8,128)(2,1)S(1)}, u32[]{:S(2)}, u32[]{:S(2)}) collective-permute-start(bf16[8,128,128]{2,1,0:T(8,128)(2,1)S(1)} %get-tuple-element.49), channel_id=1, source_target_pairs={{0,508},{4,8},{8,4},{12,16},{16,12},{20,24},{24,20},{28,32},{32,28... | collective-permute-start | bytes 786440 | tf_op jit(solution)/shard_map/ppermute | solution.py:234
  133.0 12.5 %collective-permute-start.7 = (bf16[2,2,128,128]{3,2,1,0:T(8,128)(2,1)S(1)}, bf16[2,2,128,128]{3,2,1,0:T(8,128)(2,1)S(1)}, u32[]{:S(2)}, u32[]{:S(2)}) collective-permute-start(bf16[2,2,128,128]{3,2,1,0:T(8,128)(2,1)S(1)} %get-tuple-element.46), channel_id=1, source_target_pairs={{0,509},{1,508},{2,511},{3,510},{4,11},{5,10},{6,9},{7,8},{8,5},{9... | collective-permute-start | bytes 393224 | tf_op jit(solution)/shard_map/ppermute | solution.py:245
  145.5 2.5 %collective-permute-done.7.first_1_ref = bf16[2,2,128,128]{3,2,1,0:T(8,128)(2,1)S(1)} collective-permute-done((bf16[2,2,128,128]{3,2,1,0:T(8,128)(2,1)S(1)}, bf16[2,2,128,128]{3,2,1,0:T(8,128)(2,1)S(1)}, u32[]{:S(2)}, u32[]{:S(2)}) %collective-permute-start.7) | collective-permute-done | bytes 131104 | tf_op jit(solution)/shard_map/ppermute | solution.py:245
  148.0 0.0 collective-permute-done.9.from_next_ref
  148.0 0.0 collective-permute-done.10.from_mate_ref
  148.0 1.3 shard_map.39
  149.3 2.0 %copy.3 = bf16[4,128,2,512]{3,2,1,0:T(2,128)(2,1)} copy(bf16[4,128,2,512]{3,1,2,0:T(8,128)(2,1)S(1)} %bitcast.11) | data formatting | bytes 2097152 | tf_op jit(solution)/shard_map/transpose | solution.py:312
  (1 shorter events, 0.0 us)
Async XLA Ops:
  1.8 15.4 %collective-permute-start.1 = (bf16[2,256,1024]{2,1,0:T(8,128)(2,1)S(1)}, bf16[2,256,1024]{2,1,0:T(8,128)(2,1)S(1)}, u32[]{:S(2)}, u32[]{:S(2)}) collective-permute-start(bf16[2,256,1024]{2,1,0:T(8,128)(2,1)S(1)} %reshape.33.plain_ref), channel_id=1, source_target_pairs={{0,4},{4,0},{8,12},{12,8},{16,20},{20,16},{24,28},{28,24},{32,36},... | collective-permute-start | bytes 3145736 | tf_op jit(solution)/shard_map/ppermute | solution.py:234
  4.8 16.1 %collective-permute-start = (bf16[256,1024]{1,0:T(8,128)(2,1)}, bf16[256,1024]{1,0:T(8,128)(2,1)S(1)}, u32[]{:S(2)}, u32[]{:S(2)}) collective-permute-start(bf16[256,1024]{1,0:T(8,128)(2,1)} %get-tuple-element.52), channel_id=1, source_target_pairs={{0,508},{4,8},{8,4},{12,16},{16,12},{20,24},{24,20},{28,32},{32,28... | collective-permute-start | bytes 1572872 | tf_op jit(solution)/shard_map/ppermute | solution.py:234
  13.8 17.5 %collective-permute-start.3 = (bf16[256,1024]{1,0:T(8,128)(2,1)}, bf16[256,1024]{1,0:T(8,128)(2,1)S(1)}, u32[]{:S(2)}, u32[]{:S(2)}) collective-permute-start(bf16[256,1024]{1,0:T(8,128)(2,1)} %get-tuple-element.51), channel_id=1, source_target_pairs={{0,508},{4,8},{8,4},{12,16},{16,12},{20,24},{24,20},{28,32},{32,28... | collective-permute-start | bytes 1572872 | tf_op jit(solution)/shard_map/ppermute | solution.py:234
  15.7 0.7 copy-start
  22.1 32.5 %collective-permute-start.2 = (bf16[2,256,512]{2,1,0:T(8,128)(2,1)S(1)}, bf16[2,256,512]{2,1,0:T(8,128)(2,1)S(1)}, u32[]{:S(2)}, u32[]{:S(2)}) collective-permute-start(bf16[2,256,512]{2,1,0:T(8,128)(2,1)S(1)} %shard_map.30), channel_id=1, source_target_pairs={{0,1},{1,0},{2,3},{3,2},{4,7},{5,6},{6,5},{7,4},{8,9},{9,8},{10,11... | collective-permute-start | bytes 1572872 | tf_op jit(solution)/shard_map/ppermute | solution.py:245
  32.5 44.2 %collective-permute-start.5 = (bf16[2,256,512]{2,1,0:T(8,128)(2,1)S(1)}, bf16[2,256,512]{2,1,0:T(8,128)(2,1)S(1)}, u32[]{:S(2)}, u32[]{:S(2)}) collective-permute-start(bf16[2,256,512]{2,1,0:T(8,128)(2,1)S(1)} %shard_map.31), channel_id=1, source_target_pairs={{0,1},{1,0},{2,3},{3,2},{4,7},{5,6},{6,5},{7,4},{8,9},{9,8},{10,11... | collective-permute-start | bytes 1572872 | tf_op jit(solution)/shard_map/ppermute | solution.py:245
  55.5 59.6 %collective-permute-start.4 = (bf16[2,128,768]{2,1,0:T(8,128)(2,1)S(1)}, bf16[2,128,768]{2,1,0:T(8,128)(2,1)S(1)}, u32[]{:S(2)}, u32[]{:S(2)}) collective-permute-start(bf16[2,128,768]{2,1,0:T(8,128)(2,1)S(1)} %shard_map.34.second_ref), channel_id=1, source_target_pairs={{0,3},{1,2},{2,1},{3,0},{4,5},{5,4},{6,7},{7,6},{8,11},{9,10},{10,... | collective-permute-start | bytes 1179656 | tf_op jit(solution)/shard_map/ppermute | solution.py:245
  77.6 50.3 %collective-permute-start.6 = (bf16[2,128,768]{2,1,0:T(8,128)(2,1)S(1)}, bf16[2,128,768]{2,1,0:T(8,128)(2,1)S(1)}, u32[]{:S(2)}, u32[]{:S(2)}) collective-permute-start(bf16[2,128,768]{2,1,0:T(8,128)(2,1)S(1)} %shard_map.35.second_ref), channel_id=1, source_target_pairs={{0,3},{1,2},{2,1},{3,0},{4,5},{5,4},{6,7},{7,6},{8,11},{9,10},{10,... | collective-permute-start | bytes 1179656 | tf_op jit(solution)/shard_map/ppermute | solution.py:245
  116.3 12.8 %collective-permute-start.8 = (bf16[2,2,128,128]{3,2,1,0:T(8,128)(2,1)S(1)}, bf16[2,2,128,128]{3,2,1,0:T(8,128)(2,1)S(1)}, u32[]{:S(2)}, u32[]{:S(2)}) collective-permute-start(bf16[2,2,128,128]{3,2,1,0:T(8,128)(2,1)S(1)} %get-tuple-element.43), channel_id=1, source_target_pairs={{0,1},{1,0},{2,3},{3,2},{4,7},{5,6},{6,5},{7,4},{8,9},{9,8},{10,11... | collective-permute-start | bytes 393224 | tf_op jit(solution)/shard_map/ppermute | solution.py:245
  129.1 18.8 %collective-permute-start.10 = (bf16[12,128,128]{2,1,0:T(8,128)(2,1)S(1)}, bf16[12,128,128]{2,1,0:T(8,128)(2,1)S(1)}, u32[]{:S(2)}, u32[]{:S(2)}) collective-permute-start(bf16[12,128,128]{2,1,0:T(8,128)(2,1)S(1)} %get-tuple-element.50), channel_id=1, source_target_pairs={{0,4},{4,0},{8,12},{12,8},{16,20},{20,16},{24,28},{28,24},{32,36},... | collective-permute-start | bytes 1179656 | tf_op jit(solution)/shard_map/ppermute | solution.py:234
  131.1 16.9 %collective-permute-start.9 = (bf16[8,128,128]{2,1,0:T(8,128)(2,1)S(1)}, bf16[8,128,128]{2,1,0:T(8,128)(2,1)S(1)}, u32[]{:S(2)}, u32[]{:S(2)}) collective-permute-start(bf16[8,128,128]{2,1,0:T(8,128)(2,1)S(1)} %get-tuple-element.49), channel_id=1, source_target_pairs={{0,508},{4,8},{8,4},{12,16},{16,12},{20,24},{24,20},{28,32},{32,28... | collective-permute-start | bytes 786440 | tf_op jit(solution)/shard_map/ppermute | solution.py:234
  133.0 15.0 %collective-permute-start.7 = (bf16[2,2,128,128]{3,2,1,0:T(8,128)(2,1)S(1)}, bf16[2,2,128,128]{3,2,1,0:T(8,128)(2,1)S(1)}, u32[]{:S(2)}, u32[]{:S(2)}) collective-permute-start(bf16[2,2,128,128]{3,2,1,0:T(8,128)(2,1)S(1)} %get-tuple-element.46), channel_id=1, source_target_pairs={{0,509},{1,508},{2,511},{3,510},{4,11},{5,10},{6,9},{7,8},{8,5},{9... | collective-permute-start | bytes 393224 | tf_op jit(solution)/shard_map/ppermute | solution.py:245

commit v16 on v15

--- a/solution.py
+++ b/solution.py
@@ -179,9 +179,11 @@
     return low(jnp.where(column == target, 1.0, 0.0))
 
 
-def merge_kernel(order_ref, block_0_ref, block_1_ref, first_1_ref, from_next_ref, from_mate_ref, out_ref):
-    points, count, columns = block_0_ref.shape
+def merge_kernel(order_ref, held_ref, first_1_ref, from_next_ref, from_mate_ref, out_ref):
+    _, _, height, columns = out_ref.shape
+    _, count, lanes = from_mate_ref.shape
     rows = count // 2
+    points = height // rows
     half = columns // 2
     even = order_ref[order_ref.shape[0] - 1]
     lanes = points * rows
@@ -199,16 +201,15 @@
         )
     back = low(back)
     for p in range(2):
-        for kind, block_ref, place in ((0, block_0_ref, 2 * even), (2, block_1_ref, 2 - 2 * even)):
+        for kind, place in ((0, 2 * even), (2, 2 - 2 * even)):
             natural = back[kind * count + p * rows : kind * count + (p + 1) * rows]
             for row_point in range(points):
-                here = block_ref[row_point, p * rows : (p + 1) * rows, :half]
                 for column_point in range(points):
                     there = natural[:, column_point * half : (column_point + 1) * half]
-                    mine = even == (0 if row_point == column_point else 1)
-                    out_ref[
-                        place, p, row_point * rows : (row_point + 1) * rows, column_point * half : (column_point + 1) * half
-                    ] = jnp.where(mine, here, there)
+                    other = even == (1 if row_point == column_point else 0)
+                    down = slice(row_point * rows, (row_point + 1) * rows)
+                    along = slice(column_point * half, (column_point + 1) * half)
+                    out_ref[place, p, down, along] = jnp.where(other, there, held_ref[place, p, down, along])
         for point in range(points):
             span = slice(point * rows, (point + 1) * rows)
             for strip in range(strips):
@@ -305,9 +306,20 @@
     first_1 = exchange(first_1, 0, across)
     from_next = exchange_kp(to_next, across)
     from_mate = exchange_kp(to_mate, mate)
+    def quadrants(block):
+        own = block[..., :transitions].reshape(points, 2, rows, transitions)
+        lines = []
+        for row_point in range(points):
+            here = [odd if row_point == column_point else ~odd for column_point in range(points)]
+            lines.append(jnp.concatenate([jnp.where(h, own[row_point], 0) for h in here], axis=-1))
+        return jnp.concatenate(lines, axis=1)
+
+    with_mate, with_next = quadrants(block_0), quadrants(block_1)
+    nothing = jnp.zeros_like(with_mate)
+    held = jnp.stack([jnp.where(odd, with_mate, with_next), nothing, jnp.where(odd, with_next, with_mate), nothing])
+    held = lax.optimization_barrier(held)
     out = local(
-        merge_kernel, [(4, 2, points * rows, columns)],
-        relative, block_0, block_1, first_1, from_next, from_mate, scalars=1,
+        merge_kernel, [(4, 2, points * rows, columns)], relative, held, first_1, from_next, from_mate, scalars=1
     )
     return out.transpose(0, 2, 1, 3)
 

time: 154 us -> 160 us (1.039)
  the two profiles are of different devices: /device:TPU:24 before, /device:TPU:1 now
where the time goes in v16:
time: 160 us; the launch traced here: 159 us
  waiting for transfers between devices  77.6 us (48%)
  starting transfers between devices  61.2 us (38%)
  Pallas kernels  12.5 us (8%)
  local copies, waits for them, and re-layouts  7.41 us (5%)
    ppermute x6, waiting for transfers between devices, exchange(): return lax.ppermute(value, ('kp', 'own'), pairs)  69 us
    ppermute x5, starting transfers between devices, exchange_kp(): lax.ppermute(value, 'kp', [(i, partner(i) % groups) for i in range(groups)])  41.7 us
    ppermute x6, starting transfers between devices, exchange(): return lax.ppermute(value, ('kp', 'own'), pairs)  19.5 us
    pallas_call x12, Pallas kernels, local(): pl.pallas_call(kernel, out_shape=out_shape if several else out_shape[0],...  12.5 us
    ppermute x5, waiting for transfers between devices, exchange_kp(): lax.ppermute(value, 'kp', [(i, partner(i) % groups) for i in range(groups)])  8.64 us
  transfers between devices with their start and end apart: 11, of which 6 were waited for; matrix products, arithmetic and copies ran while one was open for 1% of the time, Pallas kernels for 7%

profile of v16, /device:TPU:1, one launch (start us, length us, event | category | flops | bytes accessed | tf_op | source)
XLA Modules:
  0.0 159.4 jit_solution(16895823154153614893)
XLA Ops:
  0.0 1.8 %reshape.177.plain_ref = bf16[2,256,1024]{2,1,0:T(8,128)(2,1)S(1)} reshape(bf16[2,256,2,512]{3,2,1,0:T(2,128)(2,1)} %param.2) | data formatting | bytes 2097152 | tf_op jit(solution)/shard_map/reshape | solution.py:260
  1.8 8.8 %collective-permute-start.1 = (bf16[2,256,1024]{2,1,0:T(8,128)(2,1)S(1)}, bf16[2,256,1024]{2,1,0:T(8,128)(2,1)S(1)}, u32[]{:S(2)}, u32[]{:S(2)}) collective-permute-start(bf16[2,256,1024]{2,1,0:T(8,128)(2,1)S(1)} %reshape.177.plain_ref), channel_id=1, source_target_pairs={{0,4},{4,0},{8,12},{12,8},{16,20},{20,16},{24,28},{28,24},{32,36},... | collective-permute-start | bytes 3145736 | tf_op jit(solution)/shard_map/ppermute | solution.py:235
  10.6 1.0 slice_bitcast_fusion
  11.6 1.9 %collective-permute-start = (bf16[256,1024]{1,0:T(8,128)(2,1)}, bf16[256,1024]{1,0:T(8,128)(2,1)S(1)}, u32[]{:S(2)}, u32[]{:S(2)}) collective-permute-start(bf16[256,1024]{1,0:T(8,128)(2,1)} %get-tuple-element.52), channel_id=1, source_target_pairs={{0,508},{4,8},{8,4},{12,16},{16,12},{20,24},{24,20},{28,32},{32,28... | collective-permute-start | bytes 1572872 | tf_op jit(solution)/shard_map/ppermute | solution.py:235
  13.5 3.6 %collective-permute-start.3 = (bf16[256,1024]{1,0:T(8,128)(2,1)}, bf16[256,1024]{1,0:T(8,128)(2,1)S(1)}, u32[]{:S(2)}, u32[]{:S(2)}) collective-permute-start(bf16[256,1024]{1,0:T(8,128)(2,1)} %get-tuple-element.51), channel_id=1, source_target_pairs={{0,508},{4,8},{8,4},{12,16},{16,12},{20,24},{24,20},{28,32},{32,28... | collective-permute-start | bytes 1572872 | tf_op jit(solution)/shard_map/ppermute | solution.py:235
  17.2 0.0 copy-start.4
  17.2 0.1 stack.28.order_ref
  17.3 0.6 copy-done.4
  17.9 0.8 shard_map.28
  18.7 0.0 collective-permute-done.1.plain_ref.one_ref
  18.7 0.8 shard_map.29
  19.5 3.2 %collective-permute-done.other_ref.one_ref = bf16[256,1024]{1,0:T(8,128)(2,1)S(1)} collective-permute-done((bf16[256,1024]{1,0:T(8,128)(2,1)}, bf16[256,1024]{1,0:T(8,128)(2,1)S(1)}, u32[]{:S(2)}, u32[]{:S(2)}) %collective-permute-start) | collective-permute-done | bytes 524320 | tf_op jit(solution)/shard_map/ppermute | solution.py:235
  22.6 1.3 shard_map.30
  23.9 7.1 %collective-permute-start.2 = (bf16[2,256,512]{2,1,0:T(8,128)(2,1)S(1)}, bf16[2,256,512]{2,1,0:T(8,128)(2,1)S(1)}, u32[]{:S(2)}, u32[]{:S(2)}) collective-permute-start(bf16[2,256,512]{2,1,0:T(8,128)(2,1)S(1)} %shard_map.30), channel_id=1, source_target_pairs={{0,1},{1,0},{2,3},{3,2},{4,7},{5,6},{6,5},{7,4},{8,9},{9,8},{10,11... | collective-permute-start | bytes 1572872 | tf_op jit(solution)/shard_map/ppermute | solution.py:246
  31.0 0.0 collective-permute-done.3.other_ref
  31.0 1.3 shard_map.31
  32.3 0.0 copy-start.2
  32.3 0.8 copy-done.2
  33.1 4.0 %collective-permute-start.5 = (bf16[2,256,512]{2,1,0:T(8,128)(2,1)S(1)}, bf16[2,256,512]{2,1,0:T(8,128)(2,1)S(1)}, u32[]{:S(2)}, u32[]{:S(2)}) collective-permute-start(bf16[2,256,512]{2,1,0:T(8,128)(2,1)S(1)} %shard_map.31), channel_id=1, source_target_pairs={{0,1},{1,0},{2,3},{3,2},{4,7},{5,6},{6,5},{7,4},{8,9},{9,8},{10,11... | collective-permute-start | bytes 1572872 | tf_op jit(solution)/shard_map/ppermute | solution.py:246
  37.1 0.0 copy-start.3
  37.2 1.0 copy-done.3
  38.2 1.3 shard_map.33.rest_ref
  39.5 1.3 shard_map.32.rest_ref
  40.9 27.0 %collective-permute-done.2.got_ref = bf16[2,256,512]{2,1,0:T(8,128)(2,1)S(1)} collective-permute-done((bf16[2,256,512]{2,1,0:T(8,128)(2,1)S(1)}, bf16[2,256,512]{2,1,0:T(8,128)(2,1)S(1)}, u32[]{:S(2)}, u32[]{:S(2)}) %collective-permute-start.2) | collective-permute-done | bytes 524320 | tf_op jit(solution)/shard_map/ppermute | solution.py:246
  67.9 0.8 shard_map.34.second_ref
  68.7 0.0 copy-done
  68.7 1.9 %collective-permute-start.4 = (bf16[2,128,768]{2,1,0:T(8,128)(2,1)S(1)}, bf16[2,128,768]{2,1,0:T(8,128)(2,1)}, u32[]{:S(2)}, u32[]{:S(2)}) collective-permute-start(bf16[2,128,768]{2,1,0:T(8,128)(2,1)S(1)} %shard_map.34.second_ref), channel_id=1, source_target_pairs={{0,3},{1,2},{2,1},{3,0},{4,5},{5,4},{6,7},{7,6},{8,11},{9,10},{10,... | collective-permute-start | bytes 1179656 | tf_op jit(solution)/shard_map/ppermute | solution.py:246
  70.7 0.0 copy-start.1
  70.7 24.4 %collective-permute-done.5.got_ref = bf16[2,256,512]{2,1,0:T(8,128)(2,1)S(1)} collective-permute-done((bf16[2,256,512]{2,1,0:T(8,128)(2,1)S(1)}, bf16[2,256,512]{2,1,0:T(8,128)(2,1)S(1)}, u32[]{:S(2)}, u32[]{:S(2)}) %collective-permute-start.5) | collective-permute-done | bytes 524320 | tf_op jit(solution)/shard_map/ppermute | solution.py:246
  95.1 0.8 shard_map.35.second_ref
  95.9 1.9 %collective-permute-start.6 = (bf16[2,128,768]{2,1,0:T(8,128)(2,1)S(1)}, bf16[2,128,768]{2,1,0:T(8,128)(2,1)S(1)}, u32[]{:S(2)}, u32[]{:S(2)}) collective-permute-start(bf16[2,128,768]{2,1,0:T(8,128)(2,1)S(1)} %shard_map.35.second_ref), channel_id=1, source_target_pairs={{0,3},{1,2},{2,1},{3,0},{4,5},{5,4},{6,7},{7,6},{8,11},{9,10},{10,... | collective-permute-start | bytes 1179656 | tf_op jit(solution)/shard_map/ppermute | solution.py:246
  97.8 6.9 %collective-permute-done.4.late_ref = bf16[2,128,768]{2,1,0:T(8,128)(2,1)} collective-permute-done((bf16[2,128,768]{2,1,0:T(8,128)(2,1)S(1)}, bf16[2,128,768]{2,1,0:T(8,128)(2,1)}, u32[]{:S(2)}, u32[]{:S(2)}) %collective-permute-start.4) | collective-permute-done | bytes 393248 | tf_op jit(solution)/shard_map/ppermute | solution.py:246
  104.7 1.6 shard_map.36
  106.3 1.9 %collective-permute-start.8 = (bf16[2,2,128,128]{3,2,1,0:T(8,128)(2,1)S(1)}, bf16[2,2,128,128]{3,2,1,0:T(8,128)(2,1)S(1)}, u32[]{:S(2)}, u32[]{:S(2)}) collective-permute-start(bf16[2,2,128,128]{3,2,1,0:T(8,128)(2,1)S(1)} %get-tuple-element.43), channel_id=1, source_target_pairs={{0,1},{1,0},{2,3},{3,2},{4,7},{5,6},{6,5},{7,4},{8,9},{9,8},{10,11... | collective-permute-start | bytes 393224 | tf_op jit(solution)/shard_map/ppermute | solution.py:246
  108.2 10.7 %collective-permute-done.6.late_ref = bf16[2,128,768]{2,1,0:T(8,128)(2,1)S(1)} collective-permute-done((bf16[2,128,768]{2,1,0:T(8,128)(2,1)S(1)}, bf16[2,128,768]{2,1,0:T(8,128)(2,1)S(1)}, u32[]{:S(2)}, u32[]{:S(2)}) %collective-permute-start.6) | collective-permute-done | bytes 393248 | tf_op jit(solution)/shard_map/ppermute | solution.py:246
  118.9 1.1 shard_map.37
  120.0 2.6 %collective-permute-start.7 = (bf16[2,2,128,128]{3,2,1,0:T(8,128)(2,1)S(1)}, bf16[2,2,128,128]{3,2,1,0:T(8,128)(2,1)S(1)}, u32[]{:S(2)}, u32[]{:S(2)}) collective-permute-start(bf16[2,2,128,128]{3,2,1,0:T(8,128)(2,1)S(1)} %get-tuple-element.46), channel_id=1, source_target_pairs={{0,509},{1,508},{2,511},{3,510},{4,11},{5,10},{6,9},{7,8},{8,5},{9... | collective-permute-start | bytes 393224 | tf_op jit(solution)/shard_map/ppermute | solution.py:246
  122.8 0.0 collective-permute-done.8.passed_0_ref
  122.8 0.1 shard_map.38
  122.8 25.5 %collective-permute-start.10 = (bf16[12,128,128]{2,1,0:T(8,128)(2,1)S(1)}, bf16[12,128,128]{2,1,0:T(8,128)(2,1)S(1)}, u32[]{:S(2)}, u32[]{:S(2)}) collective-permute-start(bf16[12,128,128]{2,1,0:T(8,128)(2,1)S(1)} %get-tuple-element.50), channel_id=1, source_target_pairs={{0,4},{4,0},{8,12},{12,8},{16,20},{20,16},{24,28},{28,24},{32,36},... | collective-permute-start | bytes 1179656 | tf_op jit(solution)/shard_map/ppermute | solution.py:235
  148.4 1.9 %collective-permute-start.9 = (bf16[8,128,128]{2,1,0:T(8,128)(2,1)S(1)}, bf16[8,128,128]{2,1,0:T(8,128)(2,1)S(1)}, u32[]{:S(2)}, u32[]{:S(2)}) collective-permute-start(bf16[8,128,128]{2,1,0:T(8,128)(2,1)S(1)} %get-tuple-element.49), channel_id=1, source_target_pairs={{0,508},{4,8},{8,4},{12,16},{16,12},{20,24},{24,20},{28,32},{32,28... | collective-permute-start | bytes 786440 | tf_op jit(solution)/shard_map/ppermute | solution.py:235
  150.3 0.1 broadcast_select_fusion.1
  150.4 0.1 pad_maximum_fusion.held_ref
  150.6 0.0 collective-permute-done.7.first_1_ref
  150.6 5.5 %collective-permute-done.9.from_next_ref = bf16[8,128,128]{2,1,0:T(8,128)(2,1)S(1)} collective-permute-done((bf16[8,128,128]{2,1,0:T(8,128)(2,1)S(1)}, bf16[8,128,128]{2,1,0:T(8,128)(2,1)S(1)}, u32[]{:S(2)}, u32[]{:S(2)}) %collective-permute-start.9) | collective-permute-done | bytes 262176 | tf_op jit(solution)/shard_map/ppermute | solution.py:235
  156.1 0.0 collective-permute-done.10.from_mate_ref
  156.1 1.3 shard_map.39
  157.4 2.0 %copy.3 = bf16[4,128,2,512]{3,2,1,0:T(2,128)(2,1)} copy(bf16[4,128,2,512]{3,1,2,0:T(8,128)(2,1)S(1)} %bitcast.27) | data formatting | bytes 2097152 | tf_op jit(solution)/shard_map/transpose | solution.py:324
  (8 shorter events, 0.1 us)
Async XLA Ops:
  1.8 16.9 %collective-permute-start.1 = (bf16[2,256,1024]{2,1,0:T(8,128)(2,1)S(1)}, bf16[2,256,1024]{2,1,0:T(8,128)(2,1)S(1)}, u32[]{:S(2)}, u32[]{:S(2)}) collective-permute-start(bf16[2,256,1024]{2,1,0:T(8,128)(2,1)S(1)} %reshape.177.plain_ref), channel_id=1, source_target_pairs={{0,4},{4,0},{8,12},{12,8},{16,20},{20,16},{24,28},{28,24},{32,36},... | collective-permute-start | bytes 3145736 | tf_op jit(solution)/shard_map/ppermute | solution.py:235
  11.6 11.0 %collective-permute-start = (bf16[256,1024]{1,0:T(8,128)(2,1)}, bf16[256,1024]{1,0:T(8,128)(2,1)S(1)}, u32[]{:S(2)}, u32[]{:S(2)}) collective-permute-start(bf16[256,1024]{1,0:T(8,128)(2,1)} %get-tuple-element.52), channel_id=1, source_target_pairs={{0,508},{4,8},{8,4},{12,16},{16,12},{20,24},{24,20},{28,32},{32,28... | collective-permute-start | bytes 1572872 | tf_op jit(solution)/shard_map/ppermute | solution.py:235
  13.5 17.5 %collective-permute-start.3 = (bf16[256,1024]{1,0:T(8,128)(2,1)}, bf16[256,1024]{1,0:T(8,128)(2,1)S(1)}, u32[]{:S(2)}, u32[]{:S(2)}) collective-permute-start(bf16[256,1024]{1,0:T(8,128)(2,1)} %get-tuple-element.51), channel_id=1, source_target_pairs={{0,508},{4,8},{8,4},{12,16},{16,12},{20,24},{24,20},{28,32},{32,28... | collective-permute-start | bytes 1572872 | tf_op jit(solution)/shard_map/ppermute | solution.py:235
  17.2 0.7 copy-start.4
  23.9 44.0 %collective-permute-start.2 = (bf16[2,256,512]{2,1,0:T(8,128)(2,1)S(1)}, bf16[2,256,512]{2,1,0:T(8,128)(2,1)S(1)}, u32[]{:S(2)}, u32[]{:S(2)}) collective-permute-start(bf16[2,256,512]{2,1,0:T(8,128)(2,1)S(1)} %shard_map.30), channel_id=1, source_target_pairs={{0,1},{1,0},{2,3},{3,2},{4,7},{5,6},{6,5},{7,4},{8,9},{9,8},{10,11... | collective-permute-start | bytes 1572872 | tf_op jit(solution)/shard_map/ppermute | solution.py:246
  32.3 0.8 copy-start.2
  33.1 61.9 %collective-permute-start.5 = (bf16[2,256,512]{2,1,0:T(8,128)(2,1)S(1)}, bf16[2,256,512]{2,1,0:T(8,128)(2,1)S(1)}, u32[]{:S(2)}, u32[]{:S(2)}) collective-permute-start(bf16[2,256,512]{2,1,0:T(8,128)(2,1)S(1)} %shard_map.31), channel_id=1, source_target_pairs={{0,1},{1,0},{2,3},{3,2},{4,7},{5,6},{6,5},{7,4},{8,9},{9,8},{10,11... | collective-permute-start | bytes 1572872 | tf_op jit(solution)/shard_map/ppermute | solution.py:246
  37.1 1.0 copy-start.3
  67.9 0.8 copy-start
  68.7 35.9 %collective-permute-start.4 = (bf16[2,128,768]{2,1,0:T(8,128)(2,1)S(1)}, bf16[2,128,768]{2,1,0:T(8,128)(2,1)}, u32[]{:S(2)}, u32[]{:S(2)}) collective-permute-start(bf16[2,128,768]{2,1,0:T(8,128)(2,1)S(1)} %shard_map.34.second_ref), channel_id=1, source_target_pairs={{0,3},{1,2},{2,1},{3,0},{4,5},{5,4},{6,7},{7,6},{8,11},{9,10},{10,... | collective-permute-start | bytes 1179656 | tf_op jit(solution)/shard_map/ppermute | solution.py:246
  70.7 34.0 %copy-start.1 = (bf16[2,256,512]{2,1,0:T(8,128)(2,1)S(1)}, bf16[2,256,512]{2,1,0:T(8,128)(2,1)}, u32[]{:S(2)}) copy-start(bf16[2,256,512]{2,1,0:T(8,128)(2,1)} %copy-done) | copy-start | bytes 1572868
  95.9 23.0 %collective-permute-start.6 = (bf16[2,128,768]{2,1,0:T(8,128)(2,1)S(1)}, bf16[2,128,768]{2,1,0:T(8,128)(2,1)S(1)}, u32[]{:S(2)}, u32[]{:S(2)}) collective-permute-start(bf16[2,128,768]{2,1,0:T(8,128)(2,1)S(1)} %shard_map.35.second_ref), channel_id=1, source_target_pairs={{0,3},{1,2},{2,1},{3,0},{4,5},{5,4},{6,7},{7,6},{8,11},{9,10},{10,... | collective-permute-start | bytes 1179656 | tf_op jit(solution)/shard_map/ppermute | solution.py:246
  106.3 16.5 %collective-permute-start.8 = (bf16[2,2,128,128]{3,2,1,0:T(8,128)(2,1)S(1)}, bf16[2,2,128,128]{3,2,1,0:T(8,128)(2,1)S(1)}, u32[]{:S(2)}, u32[]{:S(2)}) collective-permute-start(bf16[2,2,128,128]{3,2,1,0:T(8,128)(2,1)S(1)} %get-tuple-element.43), channel_id=1, source_target_pairs={{0,1},{1,0},{2,3},{3,2},{4,7},{5,6},{6,5},{7,4},{8,9},{9,8},{10,11... | collective-permute-start | bytes 393224 | tf_op jit(solution)/shard_map/ppermute | solution.py:246
  120.0 30.5 %collective-permute-start.7 = (bf16[2,2,128,128]{3,2,1,0:T(8,128)(2,1)S(1)}, bf16[2,2,128,128]{3,2,1,0:T(8,128)(2,1)S(1)}, u32[]{:S(2)}, u32[]{:S(2)}) collective-permute-start(bf16[2,2,128,128]{3,2,1,0:T(8,128)(2,1)S(1)} %get-tuple-element.46), channel_id=1, source_target_pairs={{0,509},{1,508},{2,511},{3,510},{4,11},{5,10},{6,9},{7,8},{8,5},{9... | collective-permute-start | bytes 393224 | tf_op jit(solution)/shard_map/ppermute | solution.py:246
  122.8 33.2 %collective-permute-start.10 = (bf16[12,128,128]{2,1,0:T(8,128)(2,1)S(1)}, bf16[12,128,128]{2,1,0:T(8,128)(2,1)S(1)}, u32[]{:S(2)}, u32[]{:S(2)}) collective-permute-start(bf16[12,128,128]{2,1,0:T(8,128)(2,1)S(1)} %get-tuple-element.50), channel_id=1, source_target_pairs={{0,4},{4,0},{8,12},{12,8},{16,20},{20,16},{24,28},{28,24},{32,36},... | collective-permute-start | bytes 1179656 | tf_op jit(solution)/shard_map/ppermute | solution.py:235
  148.4 7.7 %collective-permute-start.9 = (bf16[8,128,128]{2,1,0:T(8,128)(2,1)S(1)}, bf16[8,128,128]{2,1,0:T(8,128)(2,1)S(1)}, u32[]{:S(2)}, u32[]{:S(2)}) collective-permute-start(bf16[8,128,128]{2,1,0:T(8,128)(2,1)S(1)} %get-tuple-element.49), channel_id=1, source_target_pairs={{0,508},{4,8},{8,4},{12,16},{16,12},{20,24},{24,20},{28,32},{32,28... | collective-permute-start | bytes 786440 | tf_op jit(solution)/shard_map/ppermute | solution.py:235

commit v17 on v14

v17 whole, which is shorter than its diff:
```python
import math

import jax
import jax.numpy as jnp
from jax import lax
from jax.experimental import pallas as pl
from jax.experimental.pallas import tpu as pltpu
from jax.sharding import PartitionSpec as P

BLOCK = 32
PARTS = 4


def local(kernel, shapes, *operands, scalars=0, moved=0):
    vmem = pl.BlockSpec(memory_space=pltpu.VMEM)
    smem = pl.BlockSpec(memory_space=pltpu.SMEM)
    several = len(shapes) > 1
    out_shape = [jax.ShapeDtypeStruct(s, jnp.bfloat16) for s in shapes]
    return pl.pallas_call(
        kernel,
        out_shape=out_shape if several else out_shape[0],
        in_specs=[smem] * scalars + [vmem] * (len(operands) - scalars),
        out_specs=[vmem] * len(shapes) if several else vmem,
        compiler_params=pltpu.CompilerParams(vmem_limit_bytes=40 * 1024 * 1024),
        cost_estimate=pl.CostEstimate(flops=0, transcendentals=0, bytes_accessed=moved),
    )(*operands)


def dots(left, right):
    return lax.dot_general(left, right, (((1,), (1,)), ((), ())), preferred_element_type=jnp.float32)


def low(value):
    return value.astype(jnp.bfloat16)


def wide(value):
    return value.astype(jnp.float32)


def left_kernel(order_ref, plain_ref, weight_ref, away_ref, rest_ref):
    points, transitions, depth = plain_ref.shape
    owners = order_ref.shape[0] - 1
    blocks = transitions // (owners * BLOCK)
    weight = weight_ref[...]
    for point in range(points):
        for slot in range(owners):
            out_ref = (away_ref, rest_ref)[slot // 2]
            for block in range(blocks):
                start = pl.multiple_of((block * owners + order_ref[slot]) * BLOCK, BLOCK)
                rows = wide(plain_ref[point, pl.ds(start, BLOCK), :]) * weight
                real = pl.ds((slot % 2 * 2 * blocks + block) * BLOCK, BLOCK)
                imag = pl.ds(((slot % 2 * 2 + 1) * blocks + block) * BLOCK, BLOCK)
                out_ref[point, real, :] = low(rows)
                out_ref[point, imag, : depth // 2] = low(-rows[:, depth // 2 :])
                out_ref[point, imag, depth // 2 :] = low(rows[:, : depth // 2])


def agreeing(order_ref, point):
    even = order_ref[order_ref.shape[0] - 1]
    return point + even - 2 * even * point


def sides(order_ref, point, left_ref, mate_left_ref, mate_ref, next_ref):
    agreed = agreeing(order_ref, point)
    own, far = left_ref[point], mate_left_ref[point]
    return (own, mate_ref[agreed]), (own, next_ref[agreed]), (far, next_ref[0]), (far, next_ref[1])


def away_kernel(order_ref, left_ref, mate_left_ref, mate_ref, next_ref, out_ref):
    for point in range(out_ref.shape[0]):
        for part, (rows, right) in enumerate(sides(order_ref, point, left_ref, mate_left_ref, mate_ref, next_ref)):
            half = right.shape[0]
            out_ref[point, :, part * half : (part + 1) * half] = low(dots(rows, right))


def rest_kernel(order_ref, left_ref, mate_left_ref, mate_ref, next_ref, out_ref):
    _, points, count, _ = out_ref.shape
    for point in range(points):
        for part, (rows, right) in enumerate(sides(order_ref, point, left_ref, mate_left_ref, mate_ref, next_ref)):
            half = right.shape[0]
            out = low(dots(rows, right))
            out_ref[0, point, :, part * half : (part + 1) * half] = out[:count]
            out_ref[1, point, :, part * half : (part + 1) * half] = out[count:]


def picked(order_ref, slots, rows, owners, transitions):
    n = lax.broadcasted_iota(jnp.int32, (rows, transitions), 0)
    column = lax.broadcasted_iota(jnp.int32, (rows, transitions), 1)
    target = (n // BLOCK * owners) * BLOCK + n % BLOCK
    return jnp.concatenate(
        [low(jnp.where(column == target + order_ref[slot] * BLOCK, 1.0, 0.0)) for slot in slots], axis=0
    )


def second_kernel(order_ref, rest_ref, got_ref, out_ref):
    points, count, _ = out_ref.shape
    columns = rest_ref.shape[3]
    half = columns // PARTS
    owners = order_ref.shape[0] - 1
    pick = picked(order_ref, (2, 1), count // 2, owners, half)
    for point in range(points):
        out_ref[point, :, :columns] = low(wide(rest_ref[0, point]) + wide(got_ref[point, count:, :]))
        own = low(wide(rest_ref[1, point]) + wide(got_ref[point, :count, :]))
        for part in range(PARTS):
            place = (columns + part * count, columns + (part + 1) * count)
            out_ref[point, :, place[0] : place[1]] = low(dots(own[:, part * half : (part + 1) * half], pick))


def turned_part(order_ref, block_ref, second_ref, late_ref, part):
    points, count, columns = block_ref.shape
    half = columns // PARTS
    rows = count // 2
    owners = order_ref.shape[0] - 1
    span = pl.ds(part * half, half)
    own = jnp.concatenate(
        [block_ref[point, p * rows : (p + 1) * rows, span] for p in range(2) for point in range(points)], axis=0
    )
    pick = picked(order_ref, (3, 0), rows, owners, half)
    others = []
    for point in range(points):
        other = dots(second_ref[point, :, span], pick) + wide(late_ref[point, :, pl.ds(columns + part * count, count)])
        others.append(low(other))
    other = jnp.concatenate(
        [others[point][p * rows : (p + 1) * rows] for p in range(2) for point in range(points)], axis=0
    )
    n = lax.broadcasted_iota(jnp.int32, (count, count), 0)
    same = low(jnp.where(n == lax.broadcasted_iota(jnp.int32, (count, count), 1), 1.0, 0.0))
    pieces = []
    for out in (dots(pick, own), dots(same, other)):
        for to in range(2):
            piece = out[to * rows : (to + 1) * rows]
            pieces.append(jnp.concatenate([low(piece[:, : points * rows]), low(-piece[:, points * rows :])], axis=0))
    return (pieces[0], pieces[2]), (pieces[1], pieces[3])


def finish(rest_ref, got_ref, late_ref, block_ref):
    points, count, columns = block_ref.shape
    for point in range(points):
        total = wide(rest_ref[1, point]) + wide(got_ref[point, :count, :]) + wide(late_ref[point, :, :columns])
        block_ref[point] = low(total)


def finish_kernel(
    order_ref, rest_ref, got_ref, second_ref, late_ref,
    block_ref, mate_same_ref, mate_first_ref, next_same_ref, next_first_ref,
):
    points, count, columns = block_ref.shape
    finish(rest_ref, got_ref, late_ref, block_ref)
    strips = columns // 2 // count
    for part in range(PARTS):
        same, first = turned_part(order_ref, block_ref, second_ref, late_ref, part)
        for source in range(2):
            if part == 0:
                mate_same_ref[source] = same[source]
                mate_first_ref[source] = first[source]
            else:
                next_same_ref[part - 1, source] = same[source]
                next_first_ref[part - 1, source] = first[source]
    for point in range(points):
        for strip in range(strips):
            tile = block_ref[point, :, columns // 2 + strip * count : columns // 2 + (strip + 1) * count]
            mate_same_ref[2 + point * strips + strip] = tile


def spread(order_ref, slot, lanes, columns):
    n = lax.broadcasted_iota(jnp.int32, (lanes, columns), 0)
    column = lax.broadcasted_iota(jnp.int32, (lanes, columns), 1)
    target = (n // BLOCK * (order_ref.shape[0] - 1) + order_ref[slot]) * BLOCK + n % BLOCK
    return low(jnp.where(column == target, 1.0, 0.0))


def merge_kernel(order_ref, block_ref, mate_first_ref, next_first_ref, next_same_ref, mate_same_ref, out_ref):
    points, count, _ = block_ref.shape
    columns = out_ref.shape[3]
    rows = count // 2
    half = columns // 2
    even = order_ref[order_ref.shape[0] - 1]
    lanes = points * rows
    strips = columns // count
    back = 0.0
    for slot, (mate_ref, next_ref, source) in enumerate(
        (
            (mate_same_ref, next_same_ref, 1),
            (mate_first_ref, next_first_ref, 1),
            (mate_first_ref, next_first_ref, 0),
            (mate_same_ref, next_same_ref, 0),
        )
    ):
        tiles = [mate_ref[source]] + [next_ref[part, source] for part in range(PARTS - 1)]
        back = back + lax.dot_general(
            jnp.concatenate(tiles, axis=0),
            spread(order_ref, slot, lanes, columns),
            (((1,), (0,)), ((), ())),
            preferred_element_type=jnp.float32,
        )
    back = low(back)
    for p in range(2):
        for part, place in ((0, 2 * even), (1, 2 - 2 * even)):
            natural = back[part * count + p * rows : part * count + (p + 1) * rows]
            for row_point in range(points):
                here = block_ref[row_point, p * rows : (p + 1) * rows, part * half : (part + 1) * half]
                for column_point in range(points):
                    there = natural[:, column_point * half : (column_point + 1) * half]
                    mine = even == (0 if row_point == column_point else 1)
                    out_ref[
                        place, p, row_point * rows : (row_point + 1) * rows, column_point * half : (column_point + 1) * half
                    ] = jnp.where(mine, here, there)
        for point in range(points):
            span = slice(point * rows, (point + 1) * rows)
            for strip in range(strips):
                tile = mate_same_ref[2 + point * strips + strip, p * rows : (p + 1) * rows, :]
                out_ref[1 + 2 * even, p, span, strip * count : (strip + 1) * count] = tile
            begin = (2 + point) * count + p * rows
            out_ref[3 - 2 * even, p, span, :] = back[begin : begin + rows]


def body(pair_density, coulomb):
    points, transitions, _, g_local = pair_density.shape
    owners = lax.axis_size("own")
    groups = lax.axis_size("kp")
    blocks = transitions // (owners * BLOCK)
    rows = blocks * BLOCK
    depth = 2 * g_local
    scale = 1.0 / math.sqrt(g_local * owners)
    me = lax.axis_index("own")
    odd = lax.axis_index("kp") % 2 == 1
    parity = odd.astype(jnp.int32)

    def exchange_kp(value, partner):
        return lax.ppermute(value, "kp", [(i, partner(i) % groups) for i in range(groups)])

    def flips(i):
        return [1, 2, 3, 0] if i % 2 == 0 else [3, 2, 1, 0]

    def exchange(value, slot, partner):
        pairs = [
            (i * owners + o, partner(i) % groups * owners + (o ^ flips(i)[slot]))
            for i in range(groups)
            for o in range(owners)
        ]
        return lax.ppermute(value, ("kp", "own"), pairs)

    def exchange_own(value, first):
        return exchange(value, 0 if first else 2, lambda i: i)

    def mate(i):
        return i + 1 if i % 2 == 0 else i - 1

    def across(i):
        return i - 1 if i % 2 == 0 else i + 1

    near_flip, far_flip = 1 + 2 * parity, 3 - 2 * parity
    relative = jnp.stack([me ^ near_flip, me ^ 2, me ^ far_flip, me, 1 - parity])

    plain = pair_density.reshape(points, transitions, depth)
    next_right = exchange_kp(plain, across)
    mate_right = exchange_kp(plain, mate)

    weights = (jnp.concatenate([coulomb, coulomb]) * scale).reshape(1, depth)
    left_shape = [(points, 4 * rows, depth)] * 2
    left_away, left_rest = local(left_kernel, left_shape, relative, plain, weights, scalars=1, moved=4 << 20)
    next_right, left_away = lax.optimization_barrier((next_right, left_away))
    mate_left, _ = lax.optimization_barrier((mate_right, next_right))
    mate_away, mate_rest = local(left_kernel, left_shape, relative, mate_left, weights, scalars=1)

    columns = points * transitions
    tile = (2 * rows, points * rows)
    strips = points * columns // tile[1]
    width = PARTS * transitions
    away_shape = [(points, 4 * rows, width)]
    rest_shape = [(2, points, 2 * rows, width)]
    second_shape = [(points, 2 * rows, width + PARTS * 2 * rows)]

    away = local(away_kernel, away_shape, relative, left_away, mate_away, mate_right, next_right, scalars=1)
    got = exchange_own(away, True)
    left_rest, mate_rest, _ = lax.optimization_barrier((left_rest, mate_rest, away))
    rest = local(
        rest_kernel, rest_shape, relative, left_rest, mate_rest, mate_right, next_right, scalars=1, moved=8 << 20
    )
    got, rest = lax.optimization_barrier((got, rest))
    second = local(second_kernel, second_shape, relative, rest, got, scalars=1)
    late = exchange_own(second, False)
    block, mate_same, mate_first, next_same, next_first = local(
        finish_kernel,
        [
            (points, 2 * rows, width),
            (2 + strips, *tile),
            (2, *tile),
            (PARTS - 1, 2, *tile),
            (PARTS - 1, 2, *tile),
        ],
        relative, rest, got, second, late, scalars=1,
    )
    mate_first = exchange(mate_first, 0, mate)
    next_first = exchange(next_first, 0, across)
    next_same = exchange_kp(next_same, across)
    mate_same = exchange_kp(mate_same, mate)
    out = local(
        merge_kernel, [(4, 2, points * rows, columns)],
        relative, block, mate_first, next_first, next_same, mate_same, scalars=1,
    )
    return out.transpose(0, 2, 1, 3)


def solution(mesh):
    placed = (P("kp", None, None, "own"), P("own"))
    return jax.shard_map(
        body,
        mesh=mesh,
        in_specs=placed,
        out_specs=P(None, ("kp", "own"), None, None),
        check_vma=False,
    )
```

time: 164 us -> 173 us (1.055)
  the two profiles are of different devices: /device:TPU:56 before, /device:TPU:24 now
where the time goes in v17:
time: 173 us; the launch traced here: 172 us
  waiting for transfers between devices  84.4 us (49%)
  starting transfers between devices  73.8 us (43%)
  Pallas kernels  9.14 us (5%)
  local copies, waits for them, and re-layouts  4.51 us (3%)
    ppermute x4, waiting for transfers between devices, exchange(): return lax.ppermute(value, ('kp', 'own'), pairs)  75.3 us
    ppermute x4, starting transfers between devices, exchange(): return lax.ppermute(value, ('kp', 'own'), pairs)  47.1 us
    ppermute x4, starting transfers between devices, exchange_kp(): lax.ppermute(value, 'kp', [(i, partner(i) % groups) for i in range(groups)])  26.6 us
    ppermute x4, waiting for transfers between devices, exchange_kp(): lax.ppermute(value, 'kp', [(i, partner(i) % groups) for i in range(groups)])  9.16 us
    pallas_call x7, Pallas kernels, local(): pl.pallas_call(kernel, out_shape=out_shape if several else out_shape[0],...  9.14 us
  transfers between devices with their start and end apart: 8, of which 4 were waited for; matrix products, arithmetic and copies ran while one was open for 0% of the time, Pallas kernels for 2%

profile of v17, /device:TPU:24, one launch (start us, length us, event | category | flops | bytes accessed | tf_op | source)
XLA Modules:
  0.0 172.0 jit_solution(993299906806564224)
XLA Ops:
  0.0 1.8 %reshape.33.plain_ref = bf16[2,256,1024]{2,1,0:T(8,128)(2,1)S(1)} reshape(bf16[2,256,2,512]{3,2,1,0:T(2,128)(2,1)} %param.2) | data formatting | bytes 2097152 | tf_op jit(solution)/shard_map/reshape | solution.py:256
  1.8 8.3 %collective-permute-start = (bf16[2,256,1024]{2,1,0:T(8,128)(2,1)S(1)}, bf16[2,256,1024]{2,1,0:T(8,128)(2,1)S(1)}, u32[]{:S(2)}, u32[]{:S(2)}) collective-permute-start(bf16[2,256,1024]{2,1,0:T(8,128)(2,1)S(1)} %reshape.33.plain_ref), channel_id=1, source_target_pairs={{0,508},{4,8},{8,4},{12,16},{16,12},{20,24},{24,20},{28,32},{32,28... | collective-permute-start | bytes 3145736 | tf_op jit(solution)/shard_map/ppermute | solution.py:231
  10.1 1.9 %collective-permute-start.1 = (bf16[2,256,1024]{2,1,0:T(8,128)(2,1)S(1)}, bf16[2,256,1024]{2,1,0:T(8,128)(2,1)S(1)}, u32[]{:S(2)}, u32[]{:S(2)}) collective-permute-start(bf16[2,256,1024]{2,1,0:T(8,128)(2,1)S(1)} %reshape.33.plain_ref), channel_id=1, source_target_pairs={{0,4},{4,0},{8,12},{12,8},{16,20},{20,16},{24,28},{28,24},{32,36},... | collective-permute-start | bytes 3145736 | tf_op jit(solution)/shard_map/ppermute | solution.py:231
  12.1 0.0 copy-start
  12.1 0.1 stack.23.order_ref
  12.2 0.6 copy-done
  12.8 0.8 shard_map.28
  13.6 9.2 %collective-permute-done.next_ref = bf16[2,256,1024]{2,1,0:T(8,128)(2,1)S(1)} collective-permute-done((bf16[2,256,1024]{2,1,0:T(8,128)(2,1)S(1)}, bf16[2,256,1024]{2,1,0:T(8,128)(2,1)S(1)}, u32[]{:S(2)}, u32[]{:S(2)}) %collective-permute-start) | collective-permute-done | bytes 1048608 | tf_op jit(solution)/shard_map/ppermute | solution.py:231
  22.7 0.0 collective-permute-done.1.plain_ref.mate_ref
  22.7 0.8 shard_map.29
  23.5 1.8 %shard_map.30 = bf16[2,256,1024]{2,1,0:T(8,128)(2,1)S(1)} custom-call(s32[5]{0:T(128)S(1)} %stack.23.order_ref, bf16[2,256,1024]{2,1,0:T(8,128)(2,1)S(1)} %get-tuple-element.22.left_ref, bf16[2,256,1024]{2,1,0:T(8,128)(2,1)S(1)} %get-tuple-element.25.mate_left_ref, bf16[2,256,1024]{2,1,0:T(8,128)(2,1)S(1)} %collective-permute-done.1.plain_ref.mate_ref, ...), custom_call_target="tpu_custom_call" | custom-call | tf_op jit(solution)/shard_map/pallas_call | solution.py:19
  25.3 9.1 %collective-permute-start.2 = (bf16[2,256,1024]{2,1,0:T(8,128)(2,1)S(1)}, bf16[2,256,1024]{2,1,0:T(8,128)(2,1)S(1)}, u32[]{:S(2)}, u32[]{:S(2)}) collective-permute-start(bf16[2,256,1024]{2,1,0:T(8,128)(2,1)S(1)} %shard_map.30), channel_id=1, source_target_pairs={{0,1},{1,0},{2,3},{3,2},{4,7},{5,6},{6,5},{7,4},{8,9},{9,8},{10,11... | collective-permute-start | bytes 3145736 | tf_op jit(solution)/shard_map/ppermute | solution.py:242
  34.4 1.8 %shard_map.31.rest_ref = bf16[2,2,128,1024]{3,2,1,0:T(8,128)(2,1)S(1)} custom-call(s32[5]{0:T(128)S(1)} %stack.23.order_ref, bf16[2,256,1024]{2,1,0:T(8,128)(2,1)S(1)} %get-tuple-element.28.left_ref, bf16[2,256,1024]{2,1,0:T(8,128)(2,1)S(1)} %get-tuple-element.29.mate_left_ref, bf16[2,256,1024]{2,1,0:T(8,128)(2,1)S(1)} %collective-permute-done.1.plain_ref.mate_ref, ...), custom_call_target="tpu_custom_call" | custom-call | bytes 8388608 | tf_op jit(solution)/shard_map/pallas_call | solution.py:19
  36.3 43.5 %collective-permute-done.2.got_ref = bf16[2,256,1024]{2,1,0:T(8,128)(2,1)S(1)} collective-permute-done((bf16[2,256,1024]{2,1,0:T(8,128)(2,1)S(1)}, bf16[2,256,1024]{2,1,0:T(8,128)(2,1)S(1)}, u32[]{:S(2)}, u32[]{:S(2)}) %collective-permute-start.2) | collective-permute-done | bytes 1048608 | tf_op jit(solution)/shard_map/ppermute | solution.py:242
  79.8 1.1 shard_map.32.second_ref
  80.9 34.2 %collective-permute-start.3 = (bf16[2,128,1536]{2,1,0:T(8,128)(2,1)S(1)}, bf16[2,128,1536]{2,1,0:T(8,128)(2,1)S(1)}, u32[]{:S(2)}, u32[]{:S(2)}) collective-permute-start(bf16[2,128,1536]{2,1,0:T(8,128)(2,1)S(1)} %shard_map.32.second_ref), channel_id=1, source_target_pairs={{0,3},{1,2},{2,1},{3,0},{4,5},{5,4},{6,7},{7,6},{8,11},{9,10},{10,... | collective-permute-start | bytes 2359304 | tf_op jit(solution)/shard_map/ppermute | solution.py:242
  115.1 24.2 %collective-permute-done.3.late_ref = bf16[2,128,1536]{2,1,0:T(8,128)(2,1)S(1)} collective-permute-done((bf16[2,128,1536]{2,1,0:T(8,128)(2,1)S(1)}, bf16[2,128,1536]{2,1,0:T(8,128)(2,1)S(1)}, u32[]{:S(2)}, u32[]{:S(2)}) %collective-permute-start.3) | collective-permute-done | bytes 786464 | tf_op jit(solution)/shard_map/ppermute | solution.py:242
  139.3 1.6 shard_map.33
  140.8 1.9 %collective-permute-start.7 = (bf16[10,128,128]{2,1,0:T(8,128)(2,1)S(1)}, bf16[10,128,128]{2,1,0:T(8,128)(2,1)S(1)}, u32[]{:S(2)}, u32[]{:S(2)}) collective-permute-start(bf16[10,128,128]{2,1,0:T(8,128)(2,1)S(1)} %get-tuple-element.36), channel_id=1, source_target_pairs={{0,4},{4,0},{8,12},{12,8},{16,20},{20,16},{24,28},{28,24},{32,36},... | collective-permute-start | bytes 983048 | tf_op jit(solution)/shard_map/ppermute | solution.py:231
  142.8 1.9 %collective-permute-start.5 = (bf16[3,2,128,128]{3,2,1,0:T(8,128)(2,1)S(1)}, bf16[3,2,128,128]{3,2,1,0:T(8,128)(2,1)S(1)}, u32[]{:S(2)}, u32[]{:S(2)}) collective-permute-start(bf16[3,2,128,128]{3,2,1,0:T(8,128)(2,1)S(1)} %get-tuple-element.34), channel_id=1, source_target_pairs={{0,509},{1,508},{2,511},{3,510},{4,11},{5,10},{6,9},{7,8},{8,5},{9... | collective-permute-start | bytes 589832 | tf_op jit(solution)/shard_map/ppermute | solution.py:242
  144.7 14.4 %collective-permute-start.6 = (bf16[3,2,128,128]{3,2,1,0:T(8,128)(2,1)S(1)}, bf16[3,2,128,128]{3,2,1,0:T(8,128)(2,1)S(1)}, u32[]{:S(2)}, u32[]{:S(2)}) collective-permute-start(bf16[3,2,128,128]{3,2,1,0:T(8,128)(2,1)S(1)} %get-tuple-element.35), channel_id=1, source_target_pairs={{0,508},{4,8},{8,4},{12,16},{16,12},{20,24},{24,20},{28,32},{32,28... | collective-permute-start | bytes 589832 | tf_op jit(solution)/shard_map/ppermute | solution.py:231
  159.1 1.9 %collective-permute-start.4 = (bf16[2,128,128]{2,1,0:T(8,128)(2,1)S(1)}, bf16[2,128,128]{2,1,0:T(8,128)(2,1)S(1)}, u32[]{:S(2)}, u32[]{:S(2)}) collective-permute-start(bf16[2,128,128]{2,1,0:T(8,128)(2,1)S(1)} %get-tuple-element.33), channel_id=1, source_target_pairs={{0,5},{1,4},{2,7},{3,6},{4,3},{5,2},{6,1},{7,0},{8,13},{9,12},{10,... | collective-permute-start | bytes 196616 | tf_op jit(solution)/shard_map/ppermute | solution.py:242
  161.1 7.6 %collective-permute-done.4.mate_first_ref = bf16[2,128,128]{2,1,0:T(8,128)(2,1)S(1)} collective-permute-done((bf16[2,128,128]{2,1,0:T(8,128)(2,1)S(1)}, bf16[2,128,128]{2,1,0:T(8,128)(2,1)S(1)}, u32[]{:S(2)}, u32[]{:S(2)}) %collective-permute-start.4) | collective-permute-done | bytes 65568 | tf_op jit(solution)/shard_map/ppermute | solution.py:242
  168.6 0.0 collective-permute-done.5.next_first_ref
  168.6 0.0 collective-permute-done.6.next_same_ref
  168.6 0.0 collective-permute-done.7.mate_same_ref
  168.7 1.3 shard_map.34
  169.9 2.0 %copy.3 = bf16[4,128,2,512]{3,2,1,0:T(2,128)(2,1)} copy(bf16[4,128,2,512]{3,1,2,0:T(8,128)(2,1)S(1)} %bitcast.7) | data formatting | bytes 2097152 | tf_op jit(solution)/shard_map/transpose | solution.py:303
  (1 shorter events, 0.0 us)
Async XLA Ops:
  1.8 20.9 %collective-permute-start = (bf16[2,256,1024]{2,1,0:T(8,128)(2,1)S(1)}, bf16[2,256,1024]{2,1,0:T(8,128)(2,1)S(1)}, u32[]{:S(2)}, u32[]{:S(2)}) collective-permute-start(bf16[2,256,1024]{2,1,0:T(8,128)(2,1)S(1)} %reshape.33.plain_ref), channel_id=1, source_target_pairs={{0,508},{4,8},{8,4},{12,16},{16,12},{20,24},{24,20},{28,32},{32,28... | collective-permute-start | bytes 3145736 | tf_op jit(solution)/shard_map/ppermute | solution.py:231
  10.1 12.6 %collective-permute-start.1 = (bf16[2,256,1024]{2,1,0:T(8,128)(2,1)S(1)}, bf16[2,256,1024]{2,1,0:T(8,128)(2,1)S(1)}, u32[]{:S(2)}, u32[]{:S(2)}) collective-permute-start(bf16[2,256,1024]{2,1,0:T(8,128)(2,1)S(1)} %reshape.33.plain_ref), channel_id=1, source_target_pairs={{0,4},{4,0},{8,12},{12,8},{16,20},{20,16},{24,28},{28,24},{32,36},... | collective-permute-start | bytes 3145736 | tf_op jit(solution)/shard_map/ppermute | solution.py:231
  12.1 0.7 copy-start
  25.3 54.5 %collective-permute-start.2 = (bf16[2,256,1024]{2,1,0:T(8,128)(2,1)S(1)}, bf16[2,256,1024]{2,1,0:T(8,128)(2,1)S(1)}, u32[]{:S(2)}, u32[]{:S(2)}) collective-permute-start(bf16[2,256,1024]{2,1,0:T(8,128)(2,1)S(1)} %shard_map.30), channel_id=1, source_target_pairs={{0,1},{1,0},{2,3},{3,2},{4,7},{5,6},{6,5},{7,4},{8,9},{9,8},{10,11... | collective-permute-start | bytes 3145736 | tf_op jit(solution)/shard_map/ppermute | solution.py:242
  80.9 58.4 %collective-permute-start.3 = (bf16[2,128,1536]{2,1,0:T(8,128)(2,1)S(1)}, bf16[2,128,1536]{2,1,0:T(8,128)(2,1)S(1)}, u32[]{:S(2)}, u32[]{:S(2)}) collective-permute-start(bf16[2,128,1536]{2,1,0:T(8,128)(2,1)S(1)} %shard_map.32.second_ref), channel_id=1, source_target_pairs={{0,3},{1,2},{2,1},{3,0},{4,5},{5,4},{6,7},{7,6},{8,11},{9,10},{10,... | collective-permute-start | bytes 2359304 | tf_op jit(solution)/shard_map/ppermute | solution.py:242
  140.8 27.8 %collective-permute-start.7 = (bf16[10,128,128]{2,1,0:T(8,128)(2,1)S(1)}, bf16[10,128,128]{2,1,0:T(8,128)(2,1)S(1)}, u32[]{:S(2)}, u32[]{:S(2)}) collective-permute-start(bf16[10,128,128]{2,1,0:T(8,128)(2,1)S(1)} %get-tuple-element.36), channel_id=1, source_target_pairs={{0,4},{4,0},{8,12},{12,8},{16,20},{20,16},{24,28},{28,24},{32,36},... | collective-permute-start | bytes 983048 | tf_op jit(solution)/shard_map/ppermute | solution.py:231
  142.8 25.9 %collective-permute-start.5 = (bf16[3,2,128,128]{3,2,1,0:T(8,128)(2,1)S(1)}, bf16[3,2,128,128]{3,2,1,0:T(8,128)(2,1)S(1)}, u32[]{:S(2)}, u32[]{:S(2)}) collective-permute-start(bf16[3,2,128,128]{3,2,1,0:T(8,128)(2,1)S(1)} %get-tuple-element.34), channel_id=1, source_target_pairs={{0,509},{1,508},{2,511},{3,510},{4,11},{5,10},{6,9},{7,8},{8,5},{9... | collective-permute-start | bytes 589832 | tf_op jit(solution)/shard_map/ppermute | solution.py:242
  144.7 23.9 %collective-permute-start.6 = (bf16[3,2,128,128]{3,2,1,0:T(8,128)(2,1)S(1)}, bf16[3,2,128,128]{3,2,1,0:T(8,128)(2,1)S(1)}, u32[]{:S(2)}, u32[]{:S(2)}) collective-permute-start(bf16[3,2,128,128]{3,2,1,0:T(8,128)(2,1)S(1)} %get-tuple-element.35), channel_id=1, source_target_pairs={{0,508},{4,8},{8,4},{12,16},{16,12},{20,24},{24,20},{28,32},{32,28... | collective-permute-start | bytes 589832 | tf_op jit(solution)/shard_map/ppermute | solution.py:231
  159.1 9.5 %collective-permute-start.4 = (bf16[2,128,128]{2,1,0:T(8,128)(2,1)S(1)}, bf16[2,128,128]{2,1,0:T(8,128)(2,1)S(1)}, u32[]{:S(2)}, u32[]{:S(2)}) collective-permute-start(bf16[2,128,128]{2,1,0:T(8,128)(2,1)S(1)} %get-tuple-element.33), channel_id=1, source_target_pairs={{0,5},{1,4},{2,7},{3,6},{4,3},{5,2},{6,1},{7,0},{8,13},{9,12},{10,... | collective-permute-start | bytes 196616 | tf_op jit(solution)/shard_map/ppermute | solution.py:242

commit v18 on v15

--- a/solution.py
+++ b/solution.py
@@ -179,43 +179,94 @@
     return low(jnp.where(column == target, 1.0, 0.0))
 
 
-def merge_kernel(order_ref, block_0_ref, block_1_ref, first_1_ref, from_next_ref, from_mate_ref, out_ref):
-    points, count, columns = block_0_ref.shape
-    rows = count // 2
-    half = columns // 2
-    even = order_ref[order_ref.shape[0] - 1]
-    lanes = points * rows
-    strips = columns // count
+def gathered(order_ref, sources, lanes, columns):
     back = 0.0
-    for slot, source in enumerate((1, 3, 2, 0)):
-        tiles = [from_mate_ref[source], from_next_ref[source]]
-        for part in range(2):
-            tiles += [from_next_ref[4 + 2 * part + source] if source < 2 else first_1_ref[part, source - 2]]
+    for slot, tiles in enumerate(sources):
         back = back + lax.dot_general(
             jnp.concatenate(tiles, axis=0),
             spread(order_ref, slot, lanes, columns),
             (((1,), (0,)), ((), ())),
             preferred_element_type=jnp.float32,
         )
-    back = low(back)
+    return low(back)
+
+
+def early_kernel(order_ref, block_0_ref, from_next_ref, from_mate_ref, out_ref):
+    points, count, columns = block_0_ref.shape
+    rows = count // 2
+    half = columns // 2
+    even = order_ref[order_ref.shape[0] - 1]
+    strips = columns // count
+    sources = [[from_mate_ref[source], from_next_ref[source]] for source in (1, 3, 2, 0)]
+    back = gathered(order_ref, sources, points * rows, columns)
     for p in range(2):
-        for kind, block_ref, place in ((0, block_0_ref, 2 * even), (2, block_1_ref, 2 - 2 * even)):
-            natural = back[kind * count + p * rows : kind * count + (p + 1) * rows]
-            for row_point in range(points):
-                here = block_ref[row_point, p * rows : (p + 1) * rows, :half]
-                for column_point in range(points):
-                    there = natural[:, column_point * half : (column_point + 1) * half]
-                    mine = even == (0 if row_point == column_point else 1)
-                    out_ref[
-                        place, p, row_point * rows : (row_point + 1) * rows, column_point * half : (column_point + 1) * half
-                    ] = jnp.where(mine, here, there)
-        for point in range(points):
-            span = slice(point * rows, (point + 1) * rows)
+        for row_point in range(points):
+            down = slice(row_point * rows, (row_point + 1) * rows)
+            here = block_0_ref[row_point, p * rows : (p + 1) * rows, :half]
+            for column_point in range(points):
+                along = slice(column_point * half, (column_point + 1) * half)
+                mine = even == (0 if row_point == column_point else 1)
+                out_ref[2 * even, down, p, along] = jnp.where(mine, here, back[p * rows : (p + 1) * rows, along])
             for strip in range(strips):
-                tile = from_mate_ref[4 + point * strips + strip, p * rows : (p + 1) * rows, :]
-                out_ref[1 + 2 * even, p, span, strip * count : (strip + 1) * count] = tile
-            begin = (1 + 2 * point) * count + p * rows
-            out_ref[3 - 2 * even, p, span, :] = back[begin : begin + rows]
+                tile = from_mate_ref[4 + row_point * strips + strip, p * rows : (p + 1) * rows, :]
+                out_ref[1 + 2 * even, down, p, strip * count : (strip + 1) * count] = tile
+        out_ref[3 - 2 * even, :rows, p, :] = back[count + p * rows : count + (p + 1) * rows]
+
+
+def last_kernel(order_ref, early_ref, block_1_ref, first_1_ref, from_next_ref, out_ref, back_ref):
+    del early_ref
+    points, count, columns = block_1_ref.shape
+    rows = count // 2
+    half = columns // 2
+    even = order_ref[order_ref.shape[0] - 1]
+    step = pl.program_id(0)
+
+    @pl.when(step == 0)
+    def _():
+        same = [[from_next_ref[4 + 2 * part + source] for part in range(2)] for source in range(2)]
+        first = [[first_1_ref[part, source] for part in range(2)] for source in range(2)]
+        back_ref[...] = gathered(order_ref, [same[1], first[1], first[0], same[0]], points * rows, columns)
+
+    for p in range(2):
+
+        @pl.when(step < points)
+        def _():
+            here = block_1_ref[jnp.minimum(step, points - 1), p * rows : (p + 1) * rows, :half]
+            for column_point in range(points):
+                along = slice(column_point * half, (column_point + 1) * half)
+                mine = even == jnp.where(step == column_point, 0, 1)
+                there = back_ref[p * rows : (p + 1) * rows, along]
+                out_ref[0, :, p, along] = jnp.where(mine, here, there)
+
+        @pl.when(step == points)
+        def _():
+            out_ref[0, :, p, :] = back_ref[count + p * rows : count + (p + 1) * rows, :]
+
+
+def last(order, early, block_1, first_1, from_next):
+    points, count, columns = block_1.shape
+    rows = count // 2
+
+    def place(step, order_ref):
+        even = order_ref[order_ref.shape[0] - 1]
+        far = step // points
+        return (2 - 2 * even) * (1 - far) + (3 - 2 * even) * far, step * (1 - far) + (points - 1) * far, 0, 0
+
+    vmem = pl.BlockSpec(memory_space=pltpu.VMEM)
+    return pl.pallas_call(
+        last_kernel,
+        out_shape=jax.ShapeDtypeStruct(early.shape, early.dtype),
+        grid_spec=pltpu.PrefetchScalarGridSpec(
+            num_scalar_prefetch=1,
+            grid=(points + 1,),
+            in_specs=[pl.BlockSpec(memory_space=pl.ANY), vmem, vmem, vmem],
+            out_specs=pl.BlockSpec((1, rows, 2, columns), place),
+            scratch_shapes=[pltpu.VMEM((2 * count, columns), jnp.bfloat16)],
+        ),
+        input_output_aliases={1: 0},
+        compiler_params=pltpu.CompilerParams(vmem_limit_bytes=40 * 1024 * 1024),
+        cost_estimate=pl.CostEstimate(flops=0, transcendentals=0, bytes_accessed=0),
+    )(order, early, block_1, first_1, from_next)
 
 
 def body(pair_density, coulomb):
@@ -305,11 +356,10 @@
     first_1 = exchange(first_1, 0, across)
     from_next = exchange_kp(to_next, across)
     from_mate = exchange_kp(to_mate, mate)
-    out = local(
-        merge_kernel, [(4, 2, points * rows, columns)],
-        relative, block_0, block_1, first_1, from_next, from_mate, scalars=1,
-    )
-    return out.transpose(0, 2, 1, 3)
+    early = local(
+        early_kernel, [(4, points * rows, 2, columns)], relative, block_0, from_next, from_mate, scalars=1, moved=8 << 20
+    )
+    return last(relative, early, block_1, first_1, from_next)
 
 
 def solution(mesh):

time: 154 us -> 153 us (level)
  Pallas kernels: 12.1 us -> 16.2 us
  waiting for transfers between devices: 28.3 us -> 25.8 us
  local copies, waits for them, and re-layouts: 5.54 us -> 3.49 us
    pallas_call x0 -> x1, Pallas kernels: none -> 2.57 us  [last(): pl.pallas_call(last_kernel, out_shape=jax.ShapeDtypeStruct(early.shape, e...]
    ppermute x6, waiting for transfers between devices: 25.4 us -> 22.9 us  [exchange(): return lax.ppermute(value, ('kp', 'own'), pairs)]
    transpose x1 -> x0, local copies, waits for them, and re-layouts: 2.05 us -> none  [body(): return out.transpose(0, 2, 1, 3)]
    pallas_call x12, Pallas kernels: 12.1 us -> 13.7 us  [local(): pl.pallas_call(kernel, out_shape=out_shape if several else out_shape[0],...]
  transfers between devices with their start and end apart: 11 -> 11, of which waited for: 5 -> 4; matrix products, arithmetic and copies ran while one was open for 1% -> 1% of each run, Pallas kernels for 7% -> 9%
where the time goes in v18:
time: 153 us; the launch traced here: 151 us
  starting transfers between devices  105 us (69%)
  waiting for transfers between devices  25.8 us (17%)
  Pallas kernels  16.2 us (11%)
  local copies, waits for them, and re-layouts  3.49 us (2%)
    ppermute x6, starting transfers between devices, exchange(): return lax.ppermute(value, ('kp', 'own'), pairs)  88.5 us
    ppermute x6, waiting for transfers between devices, exchange(): return lax.ppermute(value, ('kp', 'own'), pairs)  22.9 us
    ppermute x5, starting transfers between devices, exchange_kp(): lax.ppermute(value, 'kp', [(i, partner(i) % groups) for i in range(groups)])  16.7 us
    pallas_call x12, Pallas kernels, local(): pl.pallas_call(kernel, out_shape=out_shape if several else out_shape[0],...  13.7 us
  transfers between devices with their start and end apart: 11, of which 4 were waited for; matrix products, arithmetic and copies ran while one was open for 1% of the time, Pallas kernels for 9%

profile of v18, /device:TPU:24, one launch (start us, length us, event | category | flops | bytes accessed | tf_op | source)
XLA Modules:
  0.0 151.0 jit_solution(8476971652069415621)
XLA Ops:
  0.0 1.8 %reshape.33.plain_ref = bf16[2,256,1024]{2,1,0:T(8,128)(2,1)S(1)} reshape(bf16[2,256,2,512]{3,2,1,0:T(2,128)(2,1)} %param.2) | data formatting | bytes 2097152 | tf_op jit(solution)/shard_map/reshape | solution.py:310
  1.8 1.9 %collective-permute-start.1 = (bf16[2,256,1024]{2,1,0:T(8,128)(2,1)S(1)}, bf16[2,256,1024]{2,1,0:T(8,128)(2,1)S(1)}, u32[]{:S(2)}, u32[]{:S(2)}) collective-permute-start(bf16[2,256,1024]{2,1,0:T(8,128)(2,1)S(1)} %reshape.33.plain_ref), channel_id=1, source_target_pairs={{0,4},{4,0},{8,12},{12,8},{16,20},{20,16},{24,28},{28,24},{32,36},... | collective-permute-start | bytes 3145736 | tf_op jit(solution)/shard_map/ppermute | solution.py:285
  3.7 1.0 slice_bitcast_fusion
  4.8 9.0 %collective-permute-start = (bf16[256,1024]{1,0:T(8,128)(2,1)}, bf16[256,1024]{1,0:T(8,128)(2,1)S(1)}, u32[]{:S(2)}, u32[]{:S(2)}) collective-permute-start(bf16[256,1024]{1,0:T(8,128)(2,1)} %get-tuple-element.52), channel_id=1, source_target_pairs={{0,508},{4,8},{8,4},{12,16},{16,12},{20,24},{24,20},{28,32},{32,28... | collective-permute-start | bytes 1572872 | tf_op jit(solution)/shard_map/ppermute | solution.py:285
  13.8 1.9 %collective-permute-start.3 = (bf16[256,1024]{1,0:T(8,128)(2,1)}, bf16[256,1024]{1,0:T(8,128)(2,1)S(1)}, u32[]{:S(2)}, u32[]{:S(2)}) collective-permute-start(bf16[256,1024]{1,0:T(8,128)(2,1)} %get-tuple-element.51), channel_id=1, source_target_pairs={{0,508},{4,8},{8,4},{12,16},{16,12},{20,24},{24,20},{28,32},{32,28... | collective-permute-start | bytes 1572872 | tf_op jit(solution)/shard_map/ppermute | solution.py:285
  15.7 0.0 copy-start
  15.7 0.1 stack.23.order_ref
  15.8 0.6 copy-done
  16.4 0.8 shard_map.28
  17.2 0.0 collective-permute-done.1.plain_ref.one_ref
  17.2 0.8 shard_map.29
  18.0 2.9 %collective-permute-done.other_ref.one_ref = bf16[256,1024]{1,0:T(8,128)(2,1)S(1)} collective-permute-done((bf16[256,1024]{1,0:T(8,128)(2,1)}, bf16[256,1024]{1,0:T(8,128)(2,1)S(1)}, u32[]{:S(2)}, u32[]{:S(2)}) %collective-permute-start) | collective-permute-done | bytes 524320 | tf_op jit(solution)/shard_map/ppermute | solution.py:285
  20.8 1.3 shard_map.30
  22.1 9.1 %collective-permute-start.2 = (bf16[2,256,512]{2,1,0:T(8,128)(2,1)S(1)}, bf16[2,256,512]{2,1,0:T(8,128)(2,1)S(1)}, u32[]{:S(2)}, u32[]{:S(2)}) collective-permute-start(bf16[2,256,512]{2,1,0:T(8,128)(2,1)S(1)} %shard_map.30), channel_id=1, source_target_pairs={{0,1},{1,0},{2,3},{3,2},{4,7},{5,6},{6,5},{7,4},{8,9},{9,8},{10,11... | collective-permute-start | bytes 1572872 | tf_op jit(solution)/shard_map/ppermute | solution.py:296
  31.2 0.0 collective-permute-done.3.other_ref
  31.2 1.3 shard_map.31
  32.5 9.4 %collective-permute-start.5 = (bf16[2,256,512]{2,1,0:T(8,128)(2,1)S(1)}, bf16[2,256,512]{2,1,0:T(8,128)(2,1)S(1)}, u32[]{:S(2)}, u32[]{:S(2)}) collective-permute-start(bf16[2,256,512]{2,1,0:T(8,128)(2,1)S(1)} %shard_map.31), channel_id=1, source_target_pairs={{0,1},{1,0},{2,3},{3,2},{4,7},{5,6},{6,5},{7,4},{8,9},{9,8},{10,11... | collective-permute-start | bytes 1572872 | tf_op jit(solution)/shard_map/ppermute | solution.py:296
  41.9 1.3 shard_map.33.rest_ref
  43.3 1.3 shard_map.32.rest_ref
  44.6 10.1 %collective-permute-done.2.got_ref = bf16[2,256,512]{2,1,0:T(8,128)(2,1)S(1)} collective-permute-done((bf16[2,256,512]{2,1,0:T(8,128)(2,1)S(1)}, bf16[2,256,512]{2,1,0:T(8,128)(2,1)S(1)}, u32[]{:S(2)}, u32[]{:S(2)}) %collective-permute-start.2) | collective-permute-done | bytes 524320 | tf_op jit(solution)/shard_map/ppermute | solution.py:296
  54.7 0.8 shard_map.34.second_ref
  55.5 11.6 %collective-permute-start.4 = (bf16[2,128,768]{2,1,0:T(8,128)(2,1)S(1)}, bf16[2,128,768]{2,1,0:T(8,128)(2,1)S(1)}, u32[]{:S(2)}, u32[]{:S(2)}) collective-permute-start(bf16[2,128,768]{2,1,0:T(8,128)(2,1)S(1)} %shard_map.34.second_ref), channel_id=1, source_target_pairs={{0,3},{1,2},{2,1},{3,0},{4,5},{5,4},{6,7},{7,6},{8,11},{9,10},{10,... | collective-permute-start | bytes 1179656 | tf_op jit(solution)/shard_map/ppermute | solution.py:296
  67.1 9.7 %collective-permute-done.5.got_ref = bf16[2,256,512]{2,1,0:T(8,128)(2,1)S(1)} collective-permute-done((bf16[2,256,512]{2,1,0:T(8,128)(2,1)S(1)}, bf16[2,256,512]{2,1,0:T(8,128)(2,1)S(1)}, u32[]{:S(2)}, u32[]{:S(2)}) %collective-permute-start.5) | collective-permute-done | bytes 524320 | tf_op jit(solution)/shard_map/ppermute | solution.py:296
  76.8 0.8 shard_map.35.second_ref
  77.6 37.5 %collective-permute-start.7 = (bf16[2,128,768]{2,1,0:T(8,128)(2,1)S(1)}, bf16[2,128,768]{2,1,0:T(8,128)(2,1)S(1)}, u32[]{:S(2)}, u32[]{:S(2)}) collective-permute-start(bf16[2,128,768]{2,1,0:T(8,128)(2,1)S(1)} %shard_map.35.second_ref), channel_id=1, source_target_pairs={{0,3},{1,2},{2,1},{3,0},{4,5},{5,4},{6,7},{7,6},{8,11},{9,10},{10,... | collective-permute-start | bytes 1179656 | tf_op jit(solution)/shard_map/ppermute | solution.py:296
  115.1 0.0 collective-permute-done.4.late_ref
  115.1 1.1 shard_map.36
  116.3 8.5 %collective-permute-start.6 = (bf16[2,2,128,128]{3,2,1,0:T(8,128)(2,1)S(1)}, bf16[2,2,128,128]{3,2,1,0:T(8,128)(2,1)S(1)}, u32[]{:S(2)}, u32[]{:S(2)}) collective-permute-start(bf16[2,2,128,128]{3,2,1,0:T(8,128)(2,1)S(1)} %get-tuple-element.44), channel_id=1, source_target_pairs={{0,1},{1,0},{2,3},{3,2},{4,7},{5,6},{6,5},{7,4},{8,9},{9,8},{10,11... | collective-permute-start | bytes 393224 | tf_op jit(solution)/shard_map/ppermute | solution.py:296
  124.8 3.1 %collective-permute-done.7.late_ref = bf16[2,128,768]{2,1,0:T(8,128)(2,1)S(1)} collective-permute-done((bf16[2,128,768]{2,1,0:T(8,128)(2,1)S(1)}, bf16[2,128,768]{2,1,0:T(8,128)(2,1)S(1)}, u32[]{:S(2)}, u32[]{:S(2)}) %collective-permute-start.7) | collective-permute-done | bytes 393248 | tf_op jit(solution)/shard_map/ppermute | solution.py:296
  127.9 1.1 shard_map.37
  129.1 0.0 collective-permute-done.6.passed_0_ref
  129.1 0.1 shard_map.38
  129.1 1.9 %collective-permute-start.9 = (bf16[12,128,128]{2,1,0:T(8,128)(2,1)S(1)}, bf16[12,128,128]{2,1,0:T(8,128)(2,1)S(1)}, u32[]{:S(2)}, u32[]{:S(2)}) collective-permute-start(bf16[12,128,128]{2,1,0:T(8,128)(2,1)S(1)} %get-tuple-element.49), channel_id=1, source_target_pairs={{0,4},{4,0},{8,12},{12,8},{16,20},{20,16},{24,28},{28,24},{32,36},... | collective-permute-start | bytes 1179656 | tf_op jit(solution)/shard_map/ppermute | solution.py:285
  131.1 1.9 %collective-permute-start.8 = (bf16[8,128,128]{2,1,0:T(8,128)(2,1)S(1)}, bf16[8,128,128]{2,1,0:T(8,128)(2,1)S(1)}, u32[]{:S(2)}, u32[]{:S(2)}) collective-permute-start(bf16[8,128,128]{2,1,0:T(8,128)(2,1)S(1)} %get-tuple-element.48), channel_id=1, source_target_pairs={{0,508},{4,8},{8,4},{12,16},{16,12},{20,24},{24,20},{28,32},{32,28... | collective-permute-start | bytes 786440 | tf_op jit(solution)/shard_map/ppermute | solution.py:285
  133.0 12.5 %collective-permute-start.10 = (bf16[2,2,128,128]{3,2,1,0:T(8,128)(2,1)S(1)}, bf16[2,2,128,128]{3,2,1,0:T(8,128)(2,1)S(1)}, u32[]{:S(2)}, u32[]{:S(2)}) collective-permute-start(bf16[2,2,128,128]{3,2,1,0:T(8,128)(2,1)S(1)} %get-tuple-element.50), channel_id=1, source_target_pairs={{0,509},{1,508},{2,511},{3,510},{4,11},{5,10},{6,9},{7,8},{8,5},{9... | collective-permute-start | bytes 393224 | tf_op jit(solution)/shard_map/ppermute | solution.py:296
  145.5 0.0 collective-permute-done.8.from_next_ref
  145.5 0.0 collective-permute-done.9.from_mate_ref
  145.5 2.9 %shard_map.39.early_ref = bf16[4,128,2,512]{3,2,1,0:T(2,128)(2,1)} custom-call(s32[5]{0:T(128)S(1)} %stack.23.order_ref, bf16[2,128,512]{2,1,0:T(8,128)(2,1)S(1)} %get-tuple-element.42.block_0_ref, bf16[8,128,128]{2,1,0:T(8,128)(2,1)S(1)} %collective-permute-done.8.from_next_ref, bf16[12,128,128]{2,1,0:T(8,128)(2,1)S(1)} %collective-permute-done.9.from_mate_ref), custom_call_target="tpu_custom_call" | custom-call | bytes 8388608 | tf_op jit(solution)/shard_map/pallas_call | solution.py:18
  148.4 0.0 collective-permute-done.10.first_1_ref
  148.4 2.6 %shard_map.40 = bf16[4,128,2,512]{3,2,1,0:T(2,128)(2,1)} custom-call(s32[5]{0:T(128)S(1)} %stack.23.order_ref, bf16[4,128,2,512]{3,2,1,0:T(2,128)(2,1)} %shard_map.39.early_ref, bf16[2,128,512]{2,1,0:T(8,128)(2,1)S(1)} %get-tuple-element.47.block_1_ref, ...), custom_call_target="tpu_custom_call", output_to_operand_aliasing={{}: (1, {})} | custom-call | tf_op jit(solution)/shard_map/pallas_call | solution.py:256
  (1 shorter events, 0.0 us)
Async XLA Ops:
  1.8 15.4 %collective-permute-start.1 = (bf16[2,256,1024]{2,1,0:T(8,128)(2,1)S(1)}, bf16[2,256,1024]{2,1,0:T(8,128)(2,1)S(1)}, u32[]{:S(2)}, u32[]{:S(2)}) collective-permute-start(bf16[2,256,1024]{2,1,0:T(8,128)(2,1)S(1)} %reshape.33.plain_ref), channel_id=1, source_target_pairs={{0,4},{4,0},{8,12},{12,8},{16,20},{20,16},{24,28},{28,24},{32,36},... | collective-permute-start | bytes 3145736 | tf_op jit(solution)/shard_map/ppermute | solution.py:285
  4.8 16.1 %collective-permute-start = (bf16[256,1024]{1,0:T(8,128)(2,1)}, bf16[256,1024]{1,0:T(8,128)(2,1)S(1)}, u32[]{:S(2)}, u32[]{:S(2)}) collective-permute-start(bf16[256,1024]{1,0:T(8,128)(2,1)} %get-tuple-element.52), channel_id=1, source_target_pairs={{0,508},{4,8},{8,4},{12,16},{16,12},{20,24},{24,20},{28,32},{32,28... | collective-permute-start | bytes 1572872 | tf_op jit(solution)/shard_map/ppermute | solution.py:285
  13.8 17.5 %collective-permute-start.3 = (bf16[256,1024]{1,0:T(8,128)(2,1)}, bf16[256,1024]{1,0:T(8,128)(2,1)S(1)}, u32[]{:S(2)}, u32[]{:S(2)}) collective-permute-start(bf16[256,1024]{1,0:T(8,128)(2,1)} %get-tuple-element.51), channel_id=1, source_target_pairs={{0,508},{4,8},{8,4},{12,16},{16,12},{20,24},{24,20},{28,32},{32,28... | collective-permute-start | bytes 1572872 | tf_op jit(solution)/shard_map/ppermute | solution.py:285
  15.7 0.7 copy-start
  22.1 32.5 %collective-permute-start.2 = (bf16[2,256,512]{2,1,0:T(8,128)(2,1)S(1)}, bf16[2,256,512]{2,1,0:T(8,128)(2,1)S(1)}, u32[]{:S(2)}, u32[]{:S(2)}) collective-permute-start(bf16[2,256,512]{2,1,0:T(8,128)(2,1)S(1)} %shard_map.30), channel_id=1, source_target_pairs={{0,1},{1,0},{2,3},{3,2},{4,7},{5,6},{6,5},{7,4},{8,9},{9,8},{10,11... | collective-permute-start | bytes 1572872 | tf_op jit(solution)/shard_map/ppermute | solution.py:296
  32.5 44.2 %collective-permute-start.5 = (bf16[2,256,512]{2,1,0:T(8,128)(2,1)S(1)}, bf16[2,256,512]{2,1,0:T(8,128)(2,1)S(1)}, u32[]{:S(2)}, u32[]{:S(2)}) collective-permute-start(bf16[2,256,512]{2,1,0:T(8,128)(2,1)S(1)} %shard_map.31), channel_id=1, source_target_pairs={{0,1},{1,0},{2,3},{3,2},{4,7},{5,6},{6,5},{7,4},{8,9},{9,8},{10,11... | collective-permute-start | bytes 1572872 | tf_op jit(solution)/shard_map/ppermute | solution.py:296
  55.5 59.6 %collective-permute-start.4 = (bf16[2,128,768]{2,1,0:T(8,128)(2,1)S(1)}, bf16[2,128,768]{2,1,0:T(8,128)(2,1)S(1)}, u32[]{:S(2)}, u32[]{:S(2)}) collective-permute-start(bf16[2,128,768]{2,1,0:T(8,128)(2,1)S(1)} %shard_map.34.second_ref), channel_id=1, source_target_pairs={{0,3},{1,2},{2,1},{3,0},{4,5},{5,4},{6,7},{7,6},{8,11},{9,10},{10,... | collective-permute-start | bytes 1179656 | tf_op jit(solution)/shard_map/ppermute | solution.py:296
  77.6 50.3 %collective-permute-start.7 = (bf16[2,128,768]{2,1,0:T(8,128)(2,1)S(1)}, bf16[2,128,768]{2,1,0:T(8,128)(2,1)S(1)}, u32[]{:S(2)}, u32[]{:S(2)}) collective-permute-start(bf16[2,128,768]{2,1,0:T(8,128)(2,1)S(1)} %shard_map.35.second_ref), channel_id=1, source_target_pairs={{0,3},{1,2},{2,1},{3,0},{4,5},{5,4},{6,7},{7,6},{8,11},{9,10},{10,... | collective-permute-start | bytes 1179656 | tf_op jit(solution)/shard_map/ppermute | solution.py:296
  116.3 12.8 %collective-permute-start.6 = (bf16[2,2,128,128]{3,2,1,0:T(8,128)(2,1)S(1)}, bf16[2,2,128,128]{3,2,1,0:T(8,128)(2,1)S(1)}, u32[]{:S(2)}, u32[]{:S(2)}) collective-permute-start(bf16[2,2,128,128]{3,2,1,0:T(8,128)(2,1)S(1)} %get-tuple-element.44), channel_id=1, source_target_pairs={{0,1},{1,0},{2,3},{3,2},{4,7},{5,6},{6,5},{7,4},{8,9},{9,8},{10,11... | collective-permute-start | bytes 393224 | tf_op jit(solution)/shard_map/ppermute | solution.py:296
  129.1 16.3 %collective-permute-start.9 = (bf16[12,128,128]{2,1,0:T(8,128)(2,1)S(1)}, bf16[12,128,128]{2,1,0:T(8,128)(2,1)S(1)}, u32[]{:S(2)}, u32[]{:S(2)}) collective-permute-start(bf16[12,128,128]{2,1,0:T(8,128)(2,1)S(1)} %get-tuple-element.49), channel_id=1, source_target_pairs={{0,4},{4,0},{8,12},{12,8},{16,20},{20,16},{24,28},{28,24},{32,36},... | collective-permute-start | bytes 1179656 | tf_op jit(solution)/shard_map/ppermute | solution.py:285
  131.1 14.4 %collective-permute-start.8 = (bf16[8,128,128]{2,1,0:T(8,128)(2,1)S(1)}, bf16[8,128,128]{2,1,0:T(8,128)(2,1)S(1)}, u32[]{:S(2)}, u32[]{:S(2)}) collective-permute-start(bf16[8,128,128]{2,1,0:T(8,128)(2,1)S(1)} %get-tuple-element.48), channel_id=1, source_target_pairs={{0,508},{4,8},{8,4},{12,16},{16,12},{20,24},{24,20},{28,32},{32,28... | collective-permute-start | bytes 786440 | tf_op jit(solution)/shard_map/ppermute | solution.py:285
  133.0 15.4 %collective-permute-start.10 = (bf16[2,2,128,128]{3,2,1,0:T(8,128)(2,1)S(1)}, bf16[2,2,128,128]{3,2,1,0:T(8,128)(2,1)S(1)}, u32[]{:S(2)}, u32[]{:S(2)}) collective-permute-start(bf16[2,2,128,128]{3,2,1,0:T(8,128)(2,1)S(1)} %get-tuple-element.50), channel_id=1, source_target_pairs={{0,509},{1,508},{2,511},{3,510},{4,11},{5,10},{6,9},{7,8},{8,5},{9... | collective-permute-start | bytes 393224 | tf_op jit(solution)/shard_map/ppermute | solution.py:296
